TPU v7x, 128 devices: a whole 4x4x4 slice. The times are simulated.
128 devices in a mesh: span: 16 (over z, x_lo, core), head: 8 (over y, x_hi).
Axes of the slice: x: 4 (x_hi: 2, x_lo: 2; x = x_hi * 2 + x_lo), y: 4, z: 4, core: 2. Of those that a mesh axis runs over, the one named last changes fastest.
Arguments:
- queries: bfloat16 [16384, 3072], P(('span', 'head')), may hold values from -15 to 15
- keys: bfloat16 [16384, 3072], P(('span', 'head')), may hold values from -6 to 6
- values: bfloat16 [16384, 3072], P(('span', 'head')), may hold values from -6 to 6
- span_ids: int32 [16384], P(('span', 'head')), may hold values from 0 to 23, never falling along the last dimension, each value on 1 to 1365 neighbouring positions
- timesteps: int32 [24], replicated, may hold values from 0 to 999
- time_weight: bfloat16 [256, 3072], replicated, may hold values from -0.375 to 0.375
Outputs:
- gated: bfloat16 [16384, 3072], P(('span', 'head'))
Inputs may be any that keep to these rules, and one draw needn't show every extreme that they name: span_ids never fall along the tokens; each span holds 1 to 1365 tokens.
All inputs are finite; a program needn't handle non-finite values.
Results may differ from a plain program's by a relative error of at most 0.0057.
Values may be sent and summed in bfloat16 or wider, within the bound.
No kernel may reach another device: no remote copies, remote signals or barrier semaphores. Data moves between devices by JAX's collectives and lax.ppermute only.
A program may use at most 128 MiB of HBM per device.

v0:
```python
import math

import jax
import jax.numpy as jnp
from jax import lax
from jax.sharding import PartitionSpec as P

HEAD_DIM = 128


def absorb(totals, portion, group_rows, group_ids, group_tops):
    key_part, value_part, id_part = portion
    heads_local = group_rows.shape[2]
    head_size = group_rows.shape[3]
    length = key_part.shape[0]
    width = math.gcd(length, 1024)
    count = length // width
    key_blocks = key_part.reshape(count, width, heads_local, head_size)
    value_blocks = value_part.reshape(count, width, heads_local, head_size)
    id_blocks = id_part.reshape(count, width)
    score_scale = head_size ** (-0.5)

    def one_group(unused_carry, group_inputs):
        query_rows, query_ids, query_top, best0, total0, accum0 = group_inputs

        def visit(state, inputs):
            key_block, value_block, id_block = inputs

            def attend(current):
                best, total, accum = current
                scores = (
                    jnp.einsum(
                        "qhd,khd->hqk", query_rows, key_block, preferred_element_type=jnp.float32
                    )
                    * score_scale
                )
                visible = id_block[None, None, :] <= query_ids[None, :, None]
                scores = jnp.where(visible, scores, -1e30)
                new_best = jnp.maximum(best, jnp.max(scores, axis=2))
                weights = jnp.where(visible, jnp.exp(scores - new_best[:, :, None]), 0.0)
                factor = jnp.exp(best - new_best)
                total = total * factor + jnp.sum(weights, axis=2)
                update = jnp.einsum(
                    "hqk,khd->hqd",
                    weights.astype(jnp.bfloat16),
                    value_block,
                    preferred_element_type=jnp.float32,
                )
                accum = accum * factor[:, :, None] + update
                return (new_best, total, accum)

            def untouched(current):
                return current

            return (lax.cond(id_block[0] > query_top, untouched, attend, state), None)

        result, unused = lax.scan(
            visit, (best0, total0, accum0), (key_blocks, value_blocks, id_blocks)
        )
        return (unused_carry, result)

    best, total, accum = totals
    unused, result = lax.scan(
        one_group, jnp.zeros((), jnp.int32), (group_rows, group_ids, group_tops, best, total, accum)
    )
    return result


def gate_rows(span_ids, timesteps, time_weight):
    half = time_weight.shape[0] // 2
    freqs = jnp.exp(-math.log(10000.0) * jnp.arange(half, dtype=jnp.float32) / half)
    angles = timesteps.astype(jnp.float32)[:, None] * freqs[None, :]
    embed = jnp.concatenate([jnp.cos(angles), jnp.sin(angles)], axis=1).astype(jnp.bfloat16)
    gate_table = jnp.dot(embed, time_weight, preferred_element_type=jnp.float32)
    onehot = (span_ids[:, None] == jnp.arange(timesteps.shape[0], dtype=jnp.int32)[None, :]).astype(
        jnp.float32
    )
    return jnp.dot(onehot, gate_table, precision=lax.Precision.HIGHEST)


def per_device(queries, keys, values, span_ids, timesteps, time_weight):
    groups = lax.axis_size("head")
    tok_local = queries.shape[0]
    tiled_ids = jnp.broadcast_to(span_ids[:, None], (tok_local, groups))
    head_q, head_k, head_v, row_ids = (
        lax.all_to_all(queries, "head", split_axis=1, concat_axis=0, tiled=True),
        lax.all_to_all(keys, "head", split_axis=1, concat_axis=0, tiled=True),
        lax.all_to_all(values, "head", split_axis=1, concat_axis=0, tiled=True),
        lax.all_to_all(tiled_ids, "head", split_axis=1, concat_axis=0, tiled=True),
    )
    row_ids = row_ids[:, 0]
    heads_local = head_q.shape[1] // HEAD_DIM
    query_flat, query_ids = (head_q, row_ids)
    sources = 1
    rows_here = query_flat.shape[0]
    rows_group = rows_here // sources
    group_rows = query_flat.reshape(sources, rows_group, heads_local, HEAD_DIM)
    group_ids = query_ids.reshape(sources, rows_group)
    group_tops = jnp.max(group_ids, axis=1)
    initial = (
        jnp.full((sources, heads_local, rows_group), -1e30, jnp.float32),
        jnp.zeros((sources, heads_local, rows_group), jnp.float32),
        jnp.zeros((sources, heads_local, rows_group, HEAD_DIM), jnp.float32),
    )
    best, total, accum = absorb(
        initial,
        (
            lax.all_gather(head_k, "span", axis=0, tiled=True),
            lax.all_gather(head_v, "span", axis=0, tiled=True),
            lax.all_gather(row_ids, "span", axis=0, tiled=True),
        ),
        group_rows,
        group_ids,
        group_tops,
    )
    attended = (
        (accum / total[:, :, :, None])
        .transpose(0, 2, 1, 3)
        .reshape(rows_here, heads_local * HEAD_DIM)
        .astype(jnp.bfloat16)
    )
    mixed = lax.all_to_all(attended, "head", split_axis=0, concat_axis=1, tiled=True)
    gates = gate_rows(span_ids, timesteps, time_weight)
    return (gates * mixed.astype(jnp.float32)).astype(jnp.bfloat16)


def solution(mesh):
    return jax.shard_map(
        per_device,
        mesh=mesh,
        in_specs=(
            P(("span", "head"), None),
            P(("span", "head"), None),
            P(("span", "head"), None),
            P(("span", "head")),
            P(),
            P(),
        ),
        out_specs=P(("span", "head"), None),
        check_vma=False,
    )
```

profile of v0, /device:TPU:98, one launch (start us, length us, event | category | flops | bytes accessed | tf_op | source)
XLA Modules:
  0.0 533.9 jit_solution(7467406423629827842)
XLA Ops:
  8.2 20.3 %all_to_all.77 = bf16[128,8,384]{0,2,1:T(8,128)(2,1)S(1)} all-to-all(bf16[128,8,384]{0,2,1:T(8,128)(2,1)S(1)} %bitcast.64), channel_id=1, replica_groups=mesh['span'=16,'head'=8] {'head'}, dimensions={1} | all-to-all | bytes 1572864 | tf_op jit(solution)/shard_map/all_to_all | solution.py:87
  31.2 23.9 %all_to_all.78 = bf16[128,8,384]{0,2,1:T(8,128)(2,1)S(1)} all-to-all(bf16[128,8,384]{0,2,1:T(8,128)(2,1)S(1)} %bitcast.65), channel_id=1, replica_groups=mesh['span'=16,'head'=8] {'head'}, dimensions={1} | all-to-all | bytes 1572864 | tf_op jit(solution)/shard_map/all_to_all | solution.py:88
  63.1 5.3 all-to-all-done
  68.4 3.5 all-to-all-start.2
  72.0 27.7 %all_gather.9 = s32[16384]{0:T(1024)S(1)} all-gather(s32[1024]{0:T(1024)S(1)} %bitcast.67), channel_id=1, replica_groups=mesh['span'=16,'head'=8] {'span'}, dimensions={0}, use_global_device_ids=true | all-gather | bytes 69632 | tf_op jit(solution)/shard_map/all_gather | solution.py:110
  102.3 10.6 %all-gather.3.cloned.1.call-done = bf16[16384,384]{1,0:T(8,128)(2,1)} async-done(((bf16[1024,384]{1,0:T(8,128)(2,1)}), bf16[16384,384]{1,0:T(8,128)(2,1)}) %all-gather.3.cloned.1.call-update) | async-done | bytes 12582928 | tf_op jit(solution)/shard_map/all_gather | solution.py:108
  112.9 32.3 %reshape.98 = bf16[16,1024,3,128]{3,2,1,0:T(4,128)(2,1)} reshape(bf16[16384,384]{1,0:T(8,128)(2,1)} %all-gather.3.cloned.1.call-done) | data formatting | bytes 25165824 | tf_op jit(solution)/shard_map/reshape | solution.py:18
  145.2 12.9 %copy.40 = bf16[16,1024,3,128]{3,1,2,0:T(8,128)(2,1)} copy(bf16[16,1024,3,128]{3,2,1,0:T(4,128)(2,1)} %reshape.98) | data formatting | bytes 25165824 | tf_op jit(solution)/shard_map/while/body/eval_jaxpr/while | solution.py:57
  158.1 29.7 %all-gather.5.cloned.1.call-done = bf16[16384,384]{1,0:T(8,128)(2,1)} async-done(((bf16[1024,384]{1,0:T(8,128)(2,1)}), bf16[16384,384]{1,0:T(8,128)(2,1)}) %all-gather.5.cloned.1.call-update) | async-done | bytes 12582928 | tf_op jit(solution)/shard_map/all_gather | solution.py:109
  187.8 32.1 %reshape.99 = bf16[16,1024,3,128]{3,2,1,0:T(4,128)(2,1)} reshape(bf16[16384,384]{1,0:T(8,128)(2,1)} %all-gather.5.cloned.1.call-done) | data formatting | bytes 25165824 | tf_op jit(solution)/shard_map/reshape | solution.py:19
  219.9 12.8 %copy.42 = bf16[16,1024,3,128]{3,1,2,0:T(8,128)(2,1)} copy(bf16[16,1024,3,128]{3,2,1,0:T(4,128)(2,1)} %reshape.99) | data formatting | bytes 25165824 | tf_op jit(solution)/shard_map/while/body/eval_jaxpr/while | solution.py:57
  232.8 264.9 %while.23 = (s32[]{:T(128)}, f32[3,1024]{1,0:T(4,128)S(1)}, f32[3,1024]{1,0:T(4,128)S(1)}, f32[3,1024,128]{2,1,0:T(8,128)S(1)}, s32[16,1024]{1,0:T(8,128)S(1)}, ...) while((s32[]{:T(128)}, f32[3,1024]{1,0:T(4,128)S(1)}, ...), condition=%wide.region_6.7_spmd, body=%wide.region_1.6_spmd.sunk | while | flops 1653348352 | bytes 47662336 | solution.py:57
  234.5 14.8 %conditional.2 = (f32[3,1024]{1,0:T(4,128)S(1)}, f32[3,1024]{1,0:T(4,128)S(1)}, f32[3,1024,128]{2,1,0:T(8,128)S(1)}) conditional(s32[]{:T(128)} %convert_element_type.58, (s32[1,1024]{1,0:T(1,128)S(1)}, s32[1024]{0:T(1024)S(1)}, bf16[16,1024,3,128]{3,1,2,0:T(8,128)(2,1)}, s32[]{:T(128)}, bf16[1024,3,128]{2,0,1:T(8,128)(2,1)}, ...), branch_computations={%region_2.4_spmd, %region_5.5_spmd} | conditional | flops 1653348352 | bytes 47629336 | solution.py:55
  235.2 4.0 fusion
  239.2 3.3 fusion.2
  242.6 6.7 %multiply_add_fusion = f32[3,1024,128]{2,1,0:T(8,128)S(1)} fusion(f32[3,1024,128]{2,1,0:T(8,128)S(1)} %get-tuple-element.151, f32[3,1024,1024]{2,1,0:T(8,128)S(1)} %get-tuple-element.224, f32[3,1024]{1,0:T(4,128)S(1)} %max.4, pred[1024,1024]{0,1:T(8,128)(4,1)S(1)} %broadcast_compare_fusion, bf16[16,1024,3,128]{3,1,2,0:T(8,128)(2,1)} %get-tuple-element.152, ...), kind=kOutput, calls=%fused_computation.8 | convolution fusion | flops 821821440 | bytes 17588736 | tf_op jit(solution)/shard_map/while/body/eval_jaxpr/while/body/eval_jaxpr/cond/branch_0_fun/hqk,khd->hqd/dot_general | solution.py:43
  251.1 14.8 %conditional.2 = (f32[3,1024]{1,0:T(4,128)S(1)}, f32[3,1024]{1,0:T(4,128)S(1)}, f32[3,1024,128]{2,1,0:T(8,128)S(1)}) conditional(s32[]{:T(128)} %convert_element_type.58, (s32[1,1024]{1,0:T(1,128)S(1)}, s32[1024]{0:T(1024)S(1)}, bf16[16,1024,3,128]{3,1,2,0:T(8,128)(2,1)}, s32[]{:T(128)}, bf16[1024,3,128]{2,0,1:T(8,128)(2,1)}, ...), branch_computations={%region_2.4_spmd, %region_5.5_spmd} | conditional | flops 1653348352 | bytes 47629336 | solution.py:55
  251.8 4.0 fusion
  259.1 6.7 %multiply_add_fusion = f32[3,1024,128]{2,1,0:T(8,128)S(1)} fusion(f32[3,1024,128]{2,1,0:T(8,128)S(1)} %get-tuple-element.151, f32[3,1024,1024]{2,1,0:T(8,128)S(1)} %get-tuple-element.224, f32[3,1024]{1,0:T(4,128)S(1)} %max.4, pred[1024,1024]{0,1:T(8,128)(4,1)S(1)} %broadcast_compare_fusion, bf16[16,1024,3,128]{3,1,2,0:T(8,128)(2,1)} %get-tuple-element.152, ...), kind=kOutput, calls=%fused_computation.8 | convolution fusion | flops 821821440 | bytes 17588736 | tf_op jit(solution)/shard_map/while/body/eval_jaxpr/while/body/eval_jaxpr/cond/branch_0_fun/hqk,khd->hqd/dot_general | solution.py:43
  267.6 14.8 %conditional.2 = (f32[3,1024]{1,0:T(4,128)S(1)}, f32[3,1024]{1,0:T(4,128)S(1)}, f32[3,1024,128]{2,1,0:T(8,128)S(1)}) conditional(s32[]{:T(128)} %convert_element_type.58, (s32[1,1024]{1,0:T(1,128)S(1)}, s32[1024]{0:T(1024)S(1)}, bf16[16,1024,3,128]{3,1,2,0:T(8,128)(2,1)}, s32[]{:T(128)}, bf16[1024,3,128]{2,0,1:T(8,128)(2,1)}, ...), branch_computations={%region_2.4_spmd, %region_5.5_spmd} | conditional | flops 1653348352 | bytes 47629336 | solution.py:55
  268.3 4.0 fusion
  275.7 6.7 %multiply_add_fusion = f32[3,1024,128]{2,1,0:T(8,128)S(1)} fusion(f32[3,1024,128]{2,1,0:T(8,128)S(1)} %get-tuple-element.151, f32[3,1024,1024]{2,1,0:T(8,128)S(1)} %get-tuple-element.224, f32[3,1024]{1,0:T(4,128)S(1)} %max.4, pred[1024,1024]{0,1:T(8,128)(4,1)S(1)} %broadcast_compare_fusion, bf16[16,1024,3,128]{3,1,2,0:T(8,128)(2,1)} %get-tuple-element.152, ...), kind=kOutput, calls=%fused_computation.8 | convolution fusion | flops 821821440 | bytes 17588736 | tf_op jit(solution)/shard_map/while/body/eval_jaxpr/while/body/eval_jaxpr/cond/branch_0_fun/hqk,khd->hqd/dot_general | solution.py:43
  284.2 14.8 %conditional.2 = (f32[3,1024]{1,0:T(4,128)S(1)}, f32[3,1024]{1,0:T(4,128)S(1)}, f32[3,1024,128]{2,1,0:T(8,128)S(1)}) conditional(s32[]{:T(128)} %convert_element_type.58, (s32[1,1024]{1,0:T(1,128)S(1)}, s32[1024]{0:T(1024)S(1)}, bf16[16,1024,3,128]{3,1,2,0:T(8,128)(2,1)}, s32[]{:T(128)}, bf16[1024,3,128]{2,0,1:T(8,128)(2,1)}, ...), branch_computations={%region_2.4_spmd, %region_5.5_spmd} | conditional | flops 1653348352 | bytes 47629336 | solution.py:55
  284.8 4.0 fusion
  288.9 3.3 fusion.2
  292.2 6.7 %multiply_add_fusion = f32[3,1024,128]{2,1,0:T(8,128)S(1)} fusion(f32[3,1024,128]{2,1,0:T(8,128)S(1)} %get-tuple-element.151, f32[3,1024,1024]{2,1,0:T(8,128)S(1)} %get-tuple-element.224, f32[3,1024]{1,0:T(4,128)S(1)} %max.4, pred[1024,1024]{0,1:T(8,128)(4,1)S(1)} %broadcast_compare_fusion, bf16[16,1024,3,128]{3,1,2,0:T(8,128)(2,1)} %get-tuple-element.152, ...), kind=kOutput, calls=%fused_computation.8 | convolution fusion | flops 821821440 | bytes 17588736 | tf_op jit(solution)/shard_map/while/body/eval_jaxpr/while/body/eval_jaxpr/cond/branch_0_fun/hqk,khd->hqd/dot_general | solution.py:43
  300.7 14.8 %conditional.2 = (f32[3,1024]{1,0:T(4,128)S(1)}, f32[3,1024]{1,0:T(4,128)S(1)}, f32[3,1024,128]{2,1,0:T(8,128)S(1)}) conditional(s32[]{:T(128)} %convert_element_type.58, (s32[1,1024]{1,0:T(1,128)S(1)}, s32[1024]{0:T(1024)S(1)}, bf16[16,1024,3,128]{3,1,2,0:T(8,128)(2,1)}, s32[]{:T(128)}, bf16[1024,3,128]{2,0,1:T(8,128)(2,1)}, ...), branch_computations={%region_2.4_spmd, %region_5.5_spmd} | conditional | flops 1653348352 | bytes 47629336 | solution.py:55
  301.4 4.0 fusion
  308.8 6.7 %multiply_add_fusion = f32[3,1024,128]{2,1,0:T(8,128)S(1)} fusion(f32[3,1024,128]{2,1,0:T(8,128)S(1)} %get-tuple-element.151, f32[3,1024,1024]{2,1,0:T(8,128)S(1)} %get-tuple-element.224, f32[3,1024]{1,0:T(4,128)S(1)} %max.4, pred[1024,1024]{0,1:T(8,128)(4,1)S(1)} %broadcast_compare_fusion, bf16[16,1024,3,128]{3,1,2,0:T(8,128)(2,1)} %get-tuple-element.152, ...), kind=kOutput, calls=%fused_computation.8 | convolution fusion | flops 821821440 | bytes 17588736 | tf_op jit(solution)/shard_map/while/body/eval_jaxpr/while/body/eval_jaxpr/cond/branch_0_fun/hqk,khd->hqd/dot_general | solution.py:43
  317.2 14.8 %conditional.2 = (f32[3,1024]{1,0:T(4,128)S(1)}, f32[3,1024]{1,0:T(4,128)S(1)}, f32[3,1024,128]{2,1,0:T(8,128)S(1)}) conditional(s32[]{:T(128)} %convert_element_type.58, (s32[1,1024]{1,0:T(1,128)S(1)}, s32[1024]{0:T(1024)S(1)}, bf16[16,1024,3,128]{3,1,2,0:T(8,128)(2,1)}, s32[]{:T(128)}, bf16[1024,3,128]{2,0,1:T(8,128)(2,1)}, ...), branch_computations={%region_2.4_spmd, %region_5.5_spmd} | conditional | flops 1653348352 | bytes 47629336 | solution.py:55
  317.9 4.0 fusion
  325.3 6.7 %multiply_add_fusion = f32[3,1024,128]{2,1,0:T(8,128)S(1)} fusion(f32[3,1024,128]{2,1,0:T(8,128)S(1)} %get-tuple-element.151, f32[3,1024,1024]{2,1,0:T(8,128)S(1)} %get-tuple-element.224, f32[3,1024]{1,0:T(4,128)S(1)} %max.4, pred[1024,1024]{0,1:T(8,128)(4,1)S(1)} %broadcast_compare_fusion, bf16[16,1024,3,128]{3,1,2,0:T(8,128)(2,1)} %get-tuple-element.152, ...), kind=kOutput, calls=%fused_computation.8 | convolution fusion | flops 821821440 | bytes 17588736 | tf_op jit(solution)/shard_map/while/body/eval_jaxpr/while/body/eval_jaxpr/cond/branch_0_fun/hqk,khd->hqd/dot_general | solution.py:43
  333.8 14.8 %conditional.2 = (f32[3,1024]{1,0:T(4,128)S(1)}, f32[3,1024]{1,0:T(4,128)S(1)}, f32[3,1024,128]{2,1,0:T(8,128)S(1)}) conditional(s32[]{:T(128)} %convert_element_type.58, (s32[1,1024]{1,0:T(1,128)S(1)}, s32[1024]{0:T(1024)S(1)}, bf16[16,1024,3,128]{3,1,2,0:T(8,128)(2,1)}, s32[]{:T(128)}, bf16[1024,3,128]{2,0,1:T(8,128)(2,1)}, ...), branch_computations={%region_2.4_spmd, %region_5.5_spmd} | conditional | flops 1653348352 | bytes 47629336 | solution.py:55
  334.4 4.0 fusion
  341.8 6.7 %multiply_add_fusion = f32[3,1024,128]{2,1,0:T(8,128)S(1)} fusion(f32[3,1024,128]{2,1,0:T(8,128)S(1)} %get-tuple-element.151, f32[3,1024,1024]{2,1,0:T(8,128)S(1)} %get-tuple-element.224, f32[3,1024]{1,0:T(4,128)S(1)} %max.4, pred[1024,1024]{0,1:T(8,128)(4,1)S(1)} %broadcast_compare_fusion, bf16[16,1024,3,128]{3,1,2,0:T(8,128)(2,1)} %get-tuple-element.152, ...), kind=kOutput, calls=%fused_computation.8 | convolution fusion | flops 821821440 | bytes 17588736 | tf_op jit(solution)/shard_map/while/body/eval_jaxpr/while/body/eval_jaxpr/cond/branch_0_fun/hqk,khd->hqd/dot_general | solution.py:43
  350.3 14.8 %conditional.2 = (f32[3,1024]{1,0:T(4,128)S(1)}, f32[3,1024]{1,0:T(4,128)S(1)}, f32[3,1024,128]{2,1,0:T(8,128)S(1)}) conditional(s32[]{:T(128)} %convert_element_type.58, (s32[1,1024]{1,0:T(1,128)S(1)}, s32[1024]{0:T(1024)S(1)}, bf16[16,1024,3,128]{3,1,2,0:T(8,128)(2,1)}, s32[]{:T(128)}, bf16[1024,3,128]{2,0,1:T(8,128)(2,1)}, ...), branch_computations={%region_2.4_spmd, %region_5.5_spmd} | conditional | flops 1653348352 | bytes 47629336 | solution.py:55
  351.0 4.0 fusion
  358.4 6.7 %multiply_add_fusion = f32[3,1024,128]{2,1,0:T(8,128)S(1)} fusion(f32[3,1024,128]{2,1,0:T(8,128)S(1)} %get-tuple-element.151, f32[3,1024,1024]{2,1,0:T(8,128)S(1)} %get-tuple-element.224, f32[3,1024]{1,0:T(4,128)S(1)} %max.4, pred[1024,1024]{0,1:T(8,128)(4,1)S(1)} %broadcast_compare_fusion, bf16[16,1024,3,128]{3,1,2,0:T(8,128)(2,1)} %get-tuple-element.152, ...), kind=kOutput, calls=%fused_computation.8 | convolution fusion | flops 821821440 | bytes 17588736 | tf_op jit(solution)/shard_map/while/body/eval_jaxpr/while/body/eval_jaxpr/cond/branch_0_fun/hqk,khd->hqd/dot_general | solution.py:43
  366.9 14.8 %conditional.2 = (f32[3,1024]{1,0:T(4,128)S(1)}, f32[3,1024]{1,0:T(4,128)S(1)}, f32[3,1024,128]{2,1,0:T(8,128)S(1)}) conditional(s32[]{:T(128)} %convert_element_type.58, (s32[1,1024]{1,0:T(1,128)S(1)}, s32[1024]{0:T(1024)S(1)}, bf16[16,1024,3,128]{3,1,2,0:T(8,128)(2,1)}, s32[]{:T(128)}, bf16[1024,3,128]{2,0,1:T(8,128)(2,1)}, ...), branch_computations={%region_2.4_spmd, %region_5.5_spmd} | conditional | flops 1653348352 | bytes 47629336 | solution.py:55
  367.5 4.0 fusion
  374.9 6.7 %multiply_add_fusion = f32[3,1024,128]{2,1,0:T(8,128)S(1)} fusion(f32[3,1024,128]{2,1,0:T(8,128)S(1)} %get-tuple-element.151, f32[3,1024,1024]{2,1,0:T(8,128)S(1)} %get-tuple-element.224, f32[3,1024]{1,0:T(4,128)S(1)} %max.4, pred[1024,1024]{0,1:T(8,128)(4,1)S(1)} %broadcast_compare_fusion, bf16[16,1024,3,128]{3,1,2,0:T(8,128)(2,1)} %get-tuple-element.152, ...), kind=kOutput, calls=%fused_computation.8 | convolution fusion | flops 821821440 | bytes 17588736 | tf_op jit(solution)/shard_map/while/body/eval_jaxpr/while/body/eval_jaxpr/cond/branch_0_fun/hqk,khd->hqd/dot_general | solution.py:43
  383.4 14.8 %conditional.2 = (f32[3,1024]{1,0:T(4,128)S(1)}, f32[3,1024]{1,0:T(4,128)S(1)}, f32[3,1024,128]{2,1,0:T(8,128)S(1)}) conditional(s32[]{:T(128)} %convert_element_type.58, (s32[1,1024]{1,0:T(1,128)S(1)}, s32[1024]{0:T(1024)S(1)}, bf16[16,1024,3,128]{3,1,2,0:T(8,128)(2,1)}, s32[]{:T(128)}, bf16[1024,3,128]{2,0,1:T(8,128)(2,1)}, ...), branch_computations={%region_2.4_spmd, %region_5.5_spmd} | conditional | flops 1653348352 | bytes 47629336 | solution.py:55
  384.1 4.0 fusion
  391.5 6.7 %multiply_add_fusion = f32[3,1024,128]{2,1,0:T(8,128)S(1)} fusion(f32[3,1024,128]{2,1,0:T(8,128)S(1)} %get-tuple-element.151, f32[3,1024,1024]{2,1,0:T(8,128)S(1)} %get-tuple-element.224, f32[3,1024]{1,0:T(4,128)S(1)} %max.4, pred[1024,1024]{0,1:T(8,128)(4,1)S(1)} %broadcast_compare_fusion, bf16[16,1024,3,128]{3,1,2,0:T(8,128)(2,1)} %get-tuple-element.152, ...), kind=kOutput, calls=%fused_computation.8 | convolution fusion | flops 821821440 | bytes 17588736 | tf_op jit(solution)/shard_map/while/body/eval_jaxpr/while/body/eval_jaxpr/cond/branch_0_fun/hqk,khd->hqd/dot_general | solution.py:43
  399.9 14.8 %conditional.2 = (f32[3,1024]{1,0:T(4,128)S(1)}, f32[3,1024]{1,0:T(4,128)S(1)}, f32[3,1024,128]{2,1,0:T(8,128)S(1)}) conditional(s32[]{:T(128)} %convert_element_type.58, (s32[1,1024]{1,0:T(1,128)S(1)}, s32[1024]{0:T(1024)S(1)}, bf16[16,1024,3,128]{3,1,2,0:T(8,128)(2,1)}, s32[]{:T(128)}, bf16[1024,3,128]{2,0,1:T(8,128)(2,1)}, ...), branch_computations={%region_2.4_spmd, %region_5.5_spmd} | conditional | flops 1653348352 | bytes 47629336 | solution.py:55
  400.6 4.0 fusion
  408.0 6.7 %multiply_add_fusion = f32[3,1024,128]{2,1,0:T(8,128)S(1)} fusion(f32[3,1024,128]{2,1,0:T(8,128)S(1)} %get-tuple-element.151, f32[3,1024,1024]{2,1,0:T(8,128)S(1)} %get-tuple-element.224, f32[3,1024]{1,0:T(4,128)S(1)} %max.4, pred[1024,1024]{0,1:T(8,128)(4,1)S(1)} %broadcast_compare_fusion, bf16[16,1024,3,128]{3,1,2,0:T(8,128)(2,1)} %get-tuple-element.152, ...), kind=kOutput, calls=%fused_computation.8 | convolution fusion | flops 821821440 | bytes 17588736 | tf_op jit(solution)/shard_map/while/body/eval_jaxpr/while/body/eval_jaxpr/cond/branch_0_fun/hqk,khd->hqd/dot_general | solution.py:43
  416.5 14.8 %conditional.2 = (f32[3,1024]{1,0:T(4,128)S(1)}, f32[3,1024]{1,0:T(4,128)S(1)}, f32[3,1024,128]{2,1,0:T(8,128)S(1)}) conditional(s32[]{:T(128)} %convert_element_type.58, (s32[1,1024]{1,0:T(1,128)S(1)}, s32[1024]{0:T(1024)S(1)}, bf16[16,1024,3,128]{3,1,2,0:T(8,128)(2,1)}, s32[]{:T(128)}, bf16[1024,3,128]{2,0,1:T(8,128)(2,1)}, ...), branch_computations={%region_2.4_spmd, %region_5.5_spmd} | conditional | flops 1653348352 | bytes 47629336 | solution.py:55
  417.1 4.0 fusion
  424.5 6.7 %multiply_add_fusion = f32[3,1024,128]{2,1,0:T(8,128)S(1)} fusion(f32[3,1024,128]{2,1,0:T(8,128)S(1)} %get-tuple-element.151, f32[3,1024,1024]{2,1,0:T(8,128)S(1)} %get-tuple-element.224, f32[3,1024]{1,0:T(4,128)S(1)} %max.4, pred[1024,1024]{0,1:T(8,128)(4,1)S(1)} %broadcast_compare_fusion, bf16[16,1024,3,128]{3,1,2,0:T(8,128)(2,1)} %get-tuple-element.152, ...), kind=kOutput, calls=%fused_computation.8 | convolution fusion | flops 821821440 | bytes 17588736 | tf_op jit(solution)/shard_map/while/body/eval_jaxpr/while/body/eval_jaxpr/cond/branch_0_fun/hqk,khd->hqd/dot_general | solution.py:43
  433.0 14.8 %conditional.2 = (f32[3,1024]{1,0:T(4,128)S(1)}, f32[3,1024]{1,0:T(4,128)S(1)}, f32[3,1024,128]{2,1,0:T(8,128)S(1)}) conditional(s32[]{:T(128)} %convert_element_type.58, (s32[1,1024]{1,0:T(1,128)S(1)}, s32[1024]{0:T(1024)S(1)}, bf16[16,1024,3,128]{3,1,2,0:T(8,128)(2,1)}, s32[]{:T(128)}, bf16[1024,3,128]{2,0,1:T(8,128)(2,1)}, ...), branch_computations={%region_2.4_spmd, %region_5.5_spmd} | conditional | flops 1653348352 | bytes 47629336 | solution.py:55
  433.7 4.0 fusion
  441.1 6.7 %multiply_add_fusion = f32[3,1024,128]{2,1,0:T(8,128)S(1)} fusion(f32[3,1024,128]{2,1,0:T(8,128)S(1)} %get-tuple-element.151, f32[3,1024,1024]{2,1,0:T(8,128)S(1)} %get-tuple-element.224, f32[3,1024]{1,0:T(4,128)S(1)} %max.4, pred[1024,1024]{0,1:T(8,128)(4,1)S(1)} %broadcast_compare_fusion, bf16[16,1024,3,128]{3,1,2,0:T(8,128)(2,1)} %get-tuple-element.152, ...), kind=kOutput, calls=%fused_computation.8 | convolution fusion | flops 821821440 | bytes 17588736 | tf_op jit(solution)/shard_map/while/body/eval_jaxpr/while/body/eval_jaxpr/cond/branch_0_fun/hqk,khd->hqd/dot_general | solution.py:43
  449.5 14.8 %conditional.2 = (f32[3,1024]{1,0:T(4,128)S(1)}, f32[3,1024]{1,0:T(4,128)S(1)}, f32[3,1024,128]{2,1,0:T(8,128)S(1)}) conditional(s32[]{:T(128)} %convert_element_type.58, (s32[1,1024]{1,0:T(1,128)S(1)}, s32[1024]{0:T(1024)S(1)}, bf16[16,1024,3,128]{3,1,2,0:T(8,128)(2,1)}, s32[]{:T(128)}, bf16[1024,3,128]{2,0,1:T(8,128)(2,1)}, ...), branch_computations={%region_2.4_spmd, %region_5.5_spmd} | conditional | flops 1653348352 | bytes 47629336 | solution.py:55
  450.2 4.0 fusion
  457.6 6.7 %multiply_add_fusion = f32[3,1024,128]{2,1,0:T(8,128)S(1)} fusion(f32[3,1024,128]{2,1,0:T(8,128)S(1)} %get-tuple-element.151, f32[3,1024,1024]{2,1,0:T(8,128)S(1)} %get-tuple-element.224, f32[3,1024]{1,0:T(4,128)S(1)} %max.4, pred[1024,1024]{0,1:T(8,128)(4,1)S(1)} %broadcast_compare_fusion, bf16[16,1024,3,128]{3,1,2,0:T(8,128)(2,1)} %get-tuple-element.152, ...), kind=kOutput, calls=%fused_computation.8 | convolution fusion | flops 821821440 | bytes 17588736 | tf_op jit(solution)/shard_map/while/body/eval_jaxpr/while/body/eval_jaxpr/cond/branch_0_fun/hqk,khd->hqd/dot_general | solution.py:43
  466.1 14.8 %conditional.2 = (f32[3,1024]{1,0:T(4,128)S(1)}, f32[3,1024]{1,0:T(4,128)S(1)}, f32[3,1024,128]{2,1,0:T(8,128)S(1)}) conditional(s32[]{:T(128)} %convert_element_type.58, (s32[1,1024]{1,0:T(1,128)S(1)}, s32[1024]{0:T(1024)S(1)}, bf16[16,1024,3,128]{3,1,2,0:T(8,128)(2,1)}, s32[]{:T(128)}, bf16[1024,3,128]{2,0,1:T(8,128)(2,1)}, ...), branch_computations={%region_2.4_spmd, %region_5.5_spmd} | conditional | flops 1653348352 | bytes 47629336 | solution.py:55
  466.8 4.0 fusion
  474.1 6.7 %multiply_add_fusion = f32[3,1024,128]{2,1,0:T(8,128)S(1)} fusion(f32[3,1024,128]{2,1,0:T(8,128)S(1)} %get-tuple-element.151, f32[3,1024,1024]{2,1,0:T(8,128)S(1)} %get-tuple-element.224, f32[3,1024]{1,0:T(4,128)S(1)} %max.4, pred[1024,1024]{0,1:T(8,128)(4,1)S(1)} %broadcast_compare_fusion, bf16[16,1024,3,128]{3,1,2,0:T(8,128)(2,1)} %get-tuple-element.152, ...), kind=kOutput, calls=%fused_computation.8 | convolution fusion | flops 821821440 | bytes 17588736 | tf_op jit(solution)/shard_map/while/body/eval_jaxpr/while/body/eval_jaxpr/cond/branch_0_fun/hqk,khd->hqd/dot_general | solution.py:43
  482.6 14.8 %conditional.2 = (f32[3,1024]{1,0:T(4,128)S(1)}, f32[3,1024]{1,0:T(4,128)S(1)}, f32[3,1024,128]{2,1,0:T(8,128)S(1)}) conditional(s32[]{:T(128)} %convert_element_type.58, (s32[1,1024]{1,0:T(1,128)S(1)}, s32[1024]{0:T(1024)S(1)}, bf16[16,1024,3,128]{3,1,2,0:T(8,128)(2,1)}, s32[]{:T(128)}, bf16[1024,3,128]{2,0,1:T(8,128)(2,1)}, ...), branch_computations={%region_2.4_spmd, %region_5.5_spmd} | conditional | flops 1653348352 | bytes 47629336 | solution.py:55
  483.3 4.0 fusion
  490.7 6.7 %multiply_add_fusion = f32[3,1024,128]{2,1,0:T(8,128)S(1)} fusion(f32[3,1024,128]{2,1,0:T(8,128)S(1)} %get-tuple-element.151, f32[3,1024,1024]{2,1,0:T(8,128)S(1)} %get-tuple-element.224, f32[3,1024]{1,0:T(4,128)S(1)} %max.4, pred[1024,1024]{0,1:T(8,128)(4,1)S(1)} %broadcast_compare_fusion, bf16[16,1024,3,128]{3,1,2,0:T(8,128)(2,1)} %get-tuple-element.152, ...), kind=kOutput, calls=%fused_computation.8 | convolution fusion | flops 821821440 | bytes 17588736 | tf_op jit(solution)/shard_map/while/body/eval_jaxpr/while/body/eval_jaxpr/cond/branch_0_fun/hqk,khd->hqd/dot_general | solution.py:43
  501.6 5.8 %all-to-all-start.4 = ((bf16[8,128,384]{1,2,0:T(8,128)(2,1)}), bf16[8,128,384]{1,2,0:T(8,128)(2,1)S(1)}, u32[]{:S(2)}, u32[]{:S(2)}) async-start(bf16[8,128,384]{1,2,0:T(8,128)(2,1)} %copy.44), calls=%async_computation.4 | async-start | bytes 1572864 | tf_op jit(solution)/shard_map/all_to_all | solution.py:122
  507.9 14.3 %all-to-all-done.4 = bf16[8,128,384]{1,2,0:T(8,128)(2,1)S(1)} async-done(((bf16[8,128,384]{1,2,0:T(8,128)(2,1)}), bf16[8,128,384]{1,2,0:T(8,128)(2,1)S(1)}, u32[]{:S(2)}, u32[]{:S(2)}) %all-to-all-start.4) | async-done | bytes 786464 | tf_op jit(solution)/shard_map/all_to_all | solution.py:122
  (147 shorter events, 90.5 us)
Async XLA Ops:
  6.5 501.0 %copy-start = (bf16[256,3072]{1,0:T(8,128)(2,1)S(1)}, bf16[256,3072]{1,0:T(8,128)(2,1)}, u32[]{:S(2)}) copy-start(bf16[256,3072]{1,0:T(8,128)(2,1)} %param.15) | copy-start | bytes 4718596
  6.5 106.3 %all-gather.3.cloned.1.call-start = ((), (), s32[]{:S(2)}) async-start(), calls=%async_computation.5 | async-start | bytes 13369344 | tf_op jit(solution)/shard_map/all_gather | solution.py:108
  29.6 158.2 %all-gather.5.cloned.1.call-start = ((), (), s32[]{:S(2)}) async-start(), calls=%async_computation.6 | async-start | bytes 13369344 | tf_op jit(solution)/shard_map/all_gather | solution.py:109
  57.5 10.9 %all-to-all-start = ((s32[128,8,1]{0,2,1:T(1,128)}), s32[128,8,1]{0,2,1:T(1,128)S(1)}, u32[]{:S(2)}, u32[]{:S(2)}) async-start(s32[128,8,1]{0,2,1:T(1,128)} %broadcast_in_dim.48), calls=%async_computation | async-start | bytes 8192 | tf_op jit(solution)/shard_map/all_to_all | solution.py:89
  68.4 31.9 %all-to-all-start.2 = ((bf16[128,8,384]{0,2,1:T(8,128)(2,1)}), bf16[128,8,384]{0,2,1:T(8,128)(2,1)S(1)}, u32[]{:S(2)}, u32[]{:S(2)}) async-start(bf16[128,8,384]{0,2,1:T(8,128)(2,1)} %bitcast.11), calls=%async_computation.2 | async-start | bytes 1572864 | tf_op jit(solution)/shard_map/all_to_all | solution.py:86
  232.8 274.7 %copy-start.2 = (s32[24]{0:T(128)S(1)}, s32[24]{0:T(128)}, u32[]{:S(2)}) copy-start(s32[24]{0:T(128)} %param.14) | copy-start | bytes 292
  497.6 27.7 %copy-start.1 = (s32[128]{0:T(128)S(1)}, s32[128]{0:T(128)}, u32[]{:S(2)}) copy-start(s32[128]{0:T(128)} %param.13) | copy-start | bytes 1540
  501.6 20.6 %all-to-all-start.4 = ((bf16[8,128,384]{1,2,0:T(8,128)(2,1)}), bf16[8,128,384]{1,2,0:T(8,128)(2,1)S(1)}, u32[]{:S(2)}, u32[]{:S(2)}) async-start(bf16[8,128,384]{1,2,0:T(8,128)(2,1)} %copy.44), calls=%async_computation.4 | async-start | bytes 1572864 | tf_op jit(solution)/shard_map/all_to_all | solution.py:122
Sparse Core Ops, SparseCore 0:
  29.7 83.0 all-gather.2
  114.6 73.1 all-gather.4
where the time goes:
time: 538 us; the launch traced here: 534 us
  matrix products  173 us (32%)
  local copies, waits for them, and re-layouts  114 us (21%)
  blocking collectives  71.8 us (13%)
  other arithmetic  67.5 us (13%)
  waiting for transfers between devices  60 us (11%)
  loops' own time  20.9 us (4%)
  between operations  13.6 us (3%)
  starting transfers between devices  12.6 us (2%)
    dot_general x16, matrix products, attend(): jnp.einsum('hqk,khd->hqd', weights.astype(jnp.bfloat16), value_block, pre...  107 us
    dot_general x16, matrix products, attend(): jnp.einsum('qhd,khd->hqk', query_rows, key_block, preferred_element_type=...  64.2 us
    reduce_sum x16, other arithmetic, attend(): total = total * factor + jnp.sum(weights, axis=2)  53.2 us
    reshape x1, local copies, waits for them, and re-layouts, absorb(): key_blocks = key_part.reshape(count, width, heads_local, head_size)  32.3 us
    reshape x1, local copies, waits for them, and re-layouts, absorb(): value_blocks = value_part.reshape(count, width, heads_local, head_size)  32.1 us
    all_gather x1, waiting for transfers between devices, per_device(): lax.all_gather(head_v, 'span', axis=0, tiled=True)  29.7 us
    all_gather x1, blocking collectives, per_device(): lax.all_gather(row_ids, 'span', axis=0, tiled=True)  27.7 us
    while x3, local copies, waits for them, and re-layouts, one_group(): lax.scan(visit, (best0, total0, accum0), (key_blocks, value_blocks, id_bl...  26.8 us
  transfers between devices with their start and end apart: 5, of which 4 were waited for; matrix products, arithmetic and copies ran while one was open for 10% of the time, Pallas kernels for 0%

commit v1 on v0

v1 whole, which is shorter than its diff:
```python
import functools
import math

import jax
import jax.numpy as jnp
from jax import lax
from jax.experimental import pallas as pl
from jax.experimental.pallas import tpu as pltpu
from jax.sharding import PartitionSpec as P

HEAD_DIM = 128
SCALE = HEAD_DIM**-0.5
BOTH = ("span", "head")
ZONES = 4
SEGMENT = 256
WIDE = 1024
WIDTH = 512
ITEMS = 4
K_NORM, Q_NORM = 32, 40
NOTE = 16
PLAIN_LIMIT = 70.0
LOW = -1e30


def dot(a, b):
    return jnp.dot(a, b, preferred_element_type=jnp.float32)


def attend_kernel(head, ringed, info_ref, own_q, their_q, end_ref, *refs):
    sources, refs = refs[: 4 if ringed else 1], refs[4 if ringed else 1 :]
    own_out, their_out, kv_ref, qt_ref, weight_ref, acc_ref, top_ref, sems = refs
    core, rank, side = info_ref[0], info_ref[1], info_ref[2]
    blocks = 2 * ZONES

    copies = []
    if ringed:
        near, near_last, far, far_last = sources
        for j, (src, last, c) in enumerate(((near, near_last, core), (far, far_last, 1 - core))):
            pieces = [(src.at[0], 0), (src.at[1], 1), (last.at[0], 2), (src.at[2], 3)]
            for piece, step in pieces:
                copies.append(
                    pltpu.make_async_copy(
                        piece.at[:, :, pl.ds(0, 2 * HEAD_DIM)],
                        kv_ref.at[(rank + step) % 4, c],
                        sems.at[4 * j + step],
                    )
                )
    else:
        copies.append(pltpu.make_async_copy(sources[0], kv_ref, sems.at[0]))
    for copy in copies:
        copy.start()

    for zone in range(ZONES):
        for q_ref, half in ((own_q, side), (their_q, 1 - side)):
            qt_ref[2 * zone + half] = q_ref[zone].astype(jnp.float32).T.astype(jnp.bfloat16)
    acc_ref[...] = jnp.zeros_like(acc_ref)
    top_ref[...] = jnp.zeros_like(top_ref)
    ones = jnp.ones((NOTE, WIDTH), jnp.bfloat16)
    for copy in copies:
        copy.wait()

    def part(i, rows):
        return kv_ref[pl.ds((i % 2) * 2, 2), (i // 2) % 2, i // 4, :, rows]

    def keys_at(i):
        return part(i, slice(0, HEAD_DIM)).reshape(WIDTH, HEAD_DIM)

    def values_at(i):
        block = part(i, slice(HEAD_DIM, 2 * HEAD_DIM))
        block = jnp.concatenate([block[y, x] for y in range(2) for x in range(2)], axis=1)
        return jnp.concatenate([block, ones], axis=0)

    def visible_at(r, i):
        row = i * WIDTH + lax.broadcasted_iota(jnp.int32, (WIDTH, SEGMENT), 0)
        return row < end_ref[r]

    def weigh(slot, r, i):
        r = jnp.minimum(r, blocks - 1)
        weights = jnp.exp(dot(keys_at(i), qt_ref[r]) * SCALE)
        weights = jnp.where(visible_at(r, i), weights, 0.0)
        weight_ref[slot] = weights.astype(jnp.bfloat16)

    def absorb(slot, r, i):
        acc_ref[r] += dot(values_at(i), weight_ref[slot])

    def careful(r, i):
        scores = dot(keys_at(i), qt_ref[r]) * SCALE
        visible = visible_at(r, i)
        scores = jnp.where(visible, scores, LOW)
        old = top_ref[r, :1]
        new = jnp.maximum(old, jnp.max(scores, axis=0, keepdims=True))
        weights = jnp.where(visible, jnp.exp(scores - new), 0.0).astype(jnp.bfloat16)
        acc_ref[r] = acc_ref[r] * jnp.exp(old - new) + dot(values_at(i), weights)
        top_ref[r] = jnp.broadcast_to(new, top_ref.shape[1:])

    def count(r):
        return info_ref[3 + r]

    plain = info_ref[3 + blocks + head] == 1

    @pl.when(plain)
    def _():
        def following(item):
            r, i = item
            over = i + 1 >= count(jnp.minimum(r, blocks - 1))
            over = jnp.logical_or(over, r >= blocks)
            return jnp.where(over, jnp.minimum(r + 1, blocks), r), jnp.where(over, 0, i + 1)

        def run(item):
            items = [item]
            for _ in range(ITEMS - 1):
                items.append(following(items[-1]))
            return tuple(items)

        def step(_, items):
            later = run(following(items[-1]))
            for slot in range(ITEMS):
                absorb(slot, *items[slot])
                weigh(slot, *later[slot])
            return later

        items = run((jnp.int32(0), jnp.int32(0)))
        for slot in range(ITEMS):
            weigh(slot, *items[slot])
        total = sum(count(r) for r in range(blocks))
        items = lax.fori_loop(0, (total + ITEMS - 1) // ITEMS - 1, step, items)
        for slot in range(ITEMS):
            absorb(slot, *items[slot])

    @pl.when(jnp.logical_not(plain))
    def _():
        top_ref[...] = jnp.full_like(top_ref, LOW)

        def over_block(r, carry):
            def over_chunk(i, carry):
                careful(r, i)
                return carry

            return lax.fori_loop(0, count(r), over_chunk, carry)

        lax.fori_loop(0, blocks, over_block, 0)

    for zone in range(ZONES):
        for out, half in ((own_out, side), (their_out, 1 - side)):
            r = 2 * zone + half
            acc = acc_ref[r]
            total = acc[HEAD_DIM : HEAD_DIM + 1]
            some = total > 0.0
            safe = jnp.where(some, total, 1.0)
            mean = (acc[:HEAD_DIM] * jnp.where(some, 1.0 / safe, 0.0)).T
            level = jnp.where(some, top_ref[r, :1] + jnp.log(safe), LOW)
            level = jnp.concatenate([level[:, :HEAD_DIM], level[:, HEAD_DIM:]], axis=0)
            high = level.astype(jnp.bfloat16).astype(jnp.float32)
            middle = (level - high).astype(jnp.bfloat16).astype(jnp.float32)
            low = level - high - middle
            spare = jnp.zeros((NOTE - 6, HEAD_DIM), jnp.float32)
            out[zone, :SEGMENT, :] = mean.astype(jnp.bfloat16)
            out[zone, SEGMENT:, :] = jnp.concatenate([high, middle, low, spare]).astype(jnp.bfloat16)


def attend(info, own_q, their_q, ends, sources, head):
    rows = 2 * ZONES * SEGMENT
    tokens = 2 * ZONES * WIDE
    blocks = 2 * ZONES
    out = jax.ShapeDtypeStruct((ZONES, SEGMENT + NOTE, HEAD_DIM), jnp.bfloat16)
    q_spec = pl.BlockSpec((ZONES, SEGMENT, HEAD_DIM), lambda i, *_: (0, 0, head))
    whole = pl.BlockSpec(memory_space=pltpu.VMEM)
    return pl.pallas_call(
        functools.partial(attend_kernel, head, len(sources) > 1),
        grid_spec=pltpu.PrefetchScalarGridSpec(
            num_scalar_prefetch=1,
            grid=(1,),
            in_specs=[q_spec, q_spec, whole] + [pl.BlockSpec(memory_space=pl.ANY)] * len(sources),
            out_specs=[whole, whole],
            scratch_shapes=[
                pltpu.VMEM((4, 2, ZONES, 2, 2 * HEAD_DIM, HEAD_DIM), jnp.bfloat16),
                pltpu.VMEM((blocks, HEAD_DIM, SEGMENT), jnp.bfloat16),
                pltpu.VMEM((ITEMS, WIDTH, SEGMENT), jnp.bfloat16),
                pltpu.VMEM((blocks + 1, HEAD_DIM + NOTE, SEGMENT), jnp.float32),
                pltpu.VMEM((blocks, 8, SEGMENT), jnp.float32),
                pltpu.SemaphoreType.DMA((8,)),
            ],
        ),
        out_shape=[out, out],
        compiler_params=pltpu.CompilerParams(vmem_limit_bytes=58 << 20),
        cost_estimate=pl.CostEstimate(
            flops=4 * rows * tokens * HEAD_DIM,
            bytes_accessed=4 * tokens * HEAD_DIM + 4 * rows * HEAD_DIM,
            transcendentals=rows * tokens // 2,
        ),
    )(info, own_q, their_q, ends, *sources)


def pack_first_kernel(queries_ref, keys_ref, values_ref, ids_ref, out_ref):
    groups = out_ref.shape[0]
    heads = keys_ref.shape[1] // HEAD_DIM // groups
    ids = jnp.broadcast_to(ids_ref[...].astype(jnp.float32), (HEAD_DIM, HEAD_DIM)).T
    lane = lax.broadcasted_iota(jnp.int32, (HEAD_DIM, HEAD_DIM), 1)
    counts = jnp.sum(jnp.where(ids <= lane.astype(jnp.float32), 1.0, 0.0), axis=0, keepdims=True)
    ones = jnp.ones((HEAD_DIM, HEAD_DIM), jnp.bfloat16)
    lane = lane[:1]
    for g in range(groups):
        at = slice(g * heads * HEAD_DIM, (g * heads + 1) * HEAD_DIM)
        out_ref[g, :HEAD_DIM] = keys_ref[:, at]
        out_ref[g, HEAD_DIM : 2 * HEAD_DIM] = values_ref[:, at].T
        note = counts
        for first, ref in ((K_NORM, keys_ref), (Q_NORM, queries_ref)):
            for head in range(heads):
                start = (g * heads + head) * HEAD_DIM
                rows = ref[:, start : start + HEAD_DIM].astype(jnp.float32)
                norm = jnp.max(dot((rows * rows).astype(jnp.bfloat16), ones), axis=0, keepdims=True)
                note = jnp.where(lane == first + head, norm * 1.02, note)
        out_ref[g, 2 * HEAD_DIM :] = jnp.broadcast_to(note, (NOTE, HEAD_DIM)).astype(jnp.bfloat16)


def pack_rest_kernel(keys_ref, values_ref, queries_ref, one_ref, two_ref, q_ref):
    groups = q_ref.shape[0]
    local = q_ref.shape[2]
    for g in range(groups):
        q_ref[g] = queries_ref[:, g * local : (g + 1) * local]
        for head, out_ref in ((1, one_ref), (2, two_ref)):
            start = g * local + head * HEAD_DIM
            out_ref[g, :HEAD_DIM] = keys_ref[:, start : start + HEAD_DIM]
            out_ref[g, HEAD_DIM:] = values_ref[:, start : start + HEAD_DIM].T


def packed(groups, rows, columns):
    return jax.ShapeDtypeStruct((groups, rows, columns), jnp.bfloat16)


def pack_first(queries, keys, values, span_ids, groups):
    return pl.pallas_call(
        pack_first_kernel, out_shape=packed(groups, 2 * HEAD_DIM + NOTE, HEAD_DIM)
    )(queries, keys, values, span_ids.reshape(1, -1))


def pack_rest(keys, values, queries, groups):
    chunk, width = keys.shape
    pair = packed(groups, 2 * HEAD_DIM, HEAD_DIM)
    return pl.pallas_call(
        pack_rest_kernel, out_shape=[pair, pair, packed(groups, chunk, width // groups)]
    )(keys, values, queries)


def merge_kernel(*refs):
    out = refs[-1]
    pieces = SEGMENT // HEAD_DIM

    def level(note, j):
        parts = [note[k * pieces + j : k * pieces + j + 1] for k in range(3)]
        return parts[0] + parts[1] + parts[2]

    for head in range(len(refs) // 2):
        one, two = refs[2 * head], refs[2 * head + 1]
        for zone in range(ZONES):
            note_one = one[zone, SEGMENT:, :].astype(jnp.float32)
            note_two = two[zone, SEGMENT:, :].astype(jnp.float32)
            for j in range(pieces):
                at = slice(j * HEAD_DIM, (j + 1) * HEAD_DIM)
                share = 1.0 / (1.0 + jnp.exp(level(note_two, j) - level(note_one, j)))
                share = jnp.broadcast_to(share, (HEAD_DIM, HEAD_DIM)).T
                a, b = one[zone, at, :].astype(jnp.float32), two[zone, at, :].astype(jnp.float32)
                merged = (b + (a - b) * share).astype(jnp.bfloat16)
                out[zone * pieces + j, :, head * HEAD_DIM : (head + 1) * HEAD_DIM] = merged


def merge(parts):
    heads = len(parts) // 2
    shape = (ZONES * SEGMENT // HEAD_DIM, HEAD_DIM, heads * HEAD_DIM)
    return pl.pallas_call(merge_kernel, out_shape=jax.ShapeDtypeStruct(shape, jnp.bfloat16))(*parts)


def gate_kernel(gate_ref, mixed_ref, out_ref):
    groups, _, local = mixed_ref.shape
    for g in range(groups):
        at = slice(g * local, (g + 1) * local)
        out_ref[:, at] = (gate_ref[:, at] * mixed_ref[g].astype(jnp.float32)).astype(jnp.bfloat16)


def gate_rows(span_ids, timesteps, time_weight):
    half = time_weight.shape[0] // 2
    freqs = jnp.exp(-math.log(10000.0) * jnp.arange(half, dtype=jnp.float32) / half)
    angles = timesteps.astype(jnp.float32)[:, None] * freqs[None, :]
    embed = jnp.concatenate([jnp.cos(angles), jnp.sin(angles)], axis=1).astype(jnp.bfloat16)
    gate_table = jnp.dot(embed, time_weight, preferred_element_type=jnp.float32)
    onehot = (span_ids[:, None] == jnp.arange(timesteps.shape[0], dtype=jnp.int32)[None, :]).astype(
        jnp.float32
    )
    return jnp.dot(onehot, gate_table, precision=lax.Precision.HIGHEST)


def per_device(queries, keys, values, span_ids, timesteps, time_weight):
    runs, groups = lax.axis_size("span"), lax.axis_size("head")
    run, rank = lax.axis_index("span"), lax.axis_index("head")
    spans = timesteps.shape[0]
    chunk, width = queries.shape
    local = width // groups
    heads = local // HEAD_DIM

    across = [
        [(4 * z + xc) * groups + 2 * y + x for z in range(ZONES) for x in range(2)]
        for xc in range(4)
        for y in range(4)
    ]
    along_y = [
        [(4 * z + 2 * side + c) * groups + 2 * y + x for y in range(4) for c in range(2)]
        for z in range(ZONES)
        for side in range(2)
        for x in range(2)
    ]
    up = [(h, (h + 2) % groups) for h in range(groups)]
    down = [(h, (h - 2) % groups) for h in range(groups)]
    core_swap = [(s, s ^ 1) for s in range(runs)]
    partner = [(s, s ^ 2) for s in range(runs)]
    other = [(s, s ^ 3) for s in range(runs)]

    def exchange(parts):
        return lax.all_to_all(
            parts, BOTH, split_axis=0, concat_axis=0, axis_index_groups=across, tiled=True
        )

    def after(*values):
        return lax.optimization_barrier(values)

    def sides(block):
        return lax.ppermute(block, "head", up), lax.ppermute(block, "head", down)

    def opposite(below, above):
        half = below.shape[0] // 2
        return lax.ppermute(below[:half], "head", up), lax.ppermute(above[half:], "head", down)

    def zoned(block):
        return block.reshape((-1, ZONES, 2) + block.shape[1:])

    def swapped(block):
        return [block, lax.ppermute(block, "span", core_swap)]

    block = exchange(pack_first(queries, keys, values, span_ids, groups))
    below, above = sides(block)
    queries, block = after(queries, block)
    one, two, split_q = pack_rest(keys, values, queries, groups)
    block_one = exchange(one)
    split_q, block_one, below, above = after(split_q, block_one, below, above)
    last = zoned(jnp.concatenate(opposite(below, above)))
    near = zoned(jnp.concatenate([block, above, below]))
    own_q = exchange(split_q)
    two, own_q = after(two, own_q)
    block_two = exchange(two)
    own_q = own_q.reshape(ZONES, SEGMENT, local)
    their_q = lax.ppermute(own_q, "span", partner)
    gathered = [
        lax.all_gather(x, BOTH, axis_index_groups=along_y, axis=0, tiled=True)
        for x in (block_one, block_two)
    ]
    gathered = [x.reshape(4, 2, ZONES, 2, 2 * HEAD_DIM, HEAD_DIM) for x in gathered]

    def combined(notes):
        is_count = jnp.arange(HEAD_DIM) < K_NORM
        return jnp.where(is_count, jnp.sum(notes, axis=0), jnp.max(notes, axis=0))

    notes = jnp.concatenate([x[:, :, :, 2 * HEAD_DIM].reshape(-1, HEAD_DIM) for x in (near, last)])
    note = combined(notes.astype(jnp.float32))[None]
    notes = [note] + [lax.ppermute(note, "span", move) for move in (core_swap, partner, other)]
    note = combined(jnp.concatenate(notes))
    squares = note[K_NORM : K_NORM + heads] * note[Q_NORM : Q_NORM + heads]
    plain = (squares * (1.05 * SCALE**2) < PLAIN_LIMIT**2).astype(jnp.int32)
    ends = note[:spans].astype(jnp.int32)

    core, side = run % 2, (run // 2) % 2
    zone_start = jnp.arange(ZONES)[:, None, None] * 4096
    inside = core * 1024 + (rank // 2) * SEGMENT + jnp.arange(SEGMENT)[None, None, :]
    position = zone_start + jnp.arange(2)[None, :, None] * 2048 + inside
    reach = jnp.min(
        jnp.where(ends > position[..., None], ends, runs * groups * chunk), axis=3
    )
    starts = (jnp.arange(ZONES)[:, None] * 4096 + side * 2048 + jnp.arange(2)[None, :] * 1024).reshape(-1)
    seen = jnp.sum(jnp.clip(reach[..., None] - starts, 0, 1024), axis=3).astype(jnp.int32)
    counts = jnp.maximum((seen[:, :, -1].reshape(-1) + WIDTH - 1) // WIDTH, 1)
    info = jnp.concatenate([jnp.stack([core, rank // 2, side]), counts, plain]).astype(jnp.int32)
    seen = seen.reshape(2 * ZONES, 1, SEGMENT)

    (near, near_other), (last, last_other) = swapped(near), swapped(last)
    sources = [(near, last, near_other, last_other), (gathered[0],), (gathered[1],)]
    info, block_two = after(info, block_two)
    parts = []
    for head in range(heads):
        mine, theirs = attend(info, own_q, their_q, seen, sources[head], head)
        info, theirs = after(info, theirs)
        parts += [mine, lax.ppermute(theirs, "span", partner)]
    mixed = exchange(merge(parts))
    gates = gate_rows(span_ids, timesteps, time_weight)
    return pl.pallas_call(
        gate_kernel, out_shape=jax.ShapeDtypeStruct((chunk, width), jnp.bfloat16)
    )(gates, mixed)


def solution(mesh):
    return jax.shard_map(
        per_device,
        mesh=mesh,
        in_specs=(
            P(("span", "head"), None),
            P(("span", "head"), None),
            P(("span", "head"), None),
            P(("span", "head")),
            P(),
            P(),
        ),
        out_specs=P(("span", "head"), None),
        check_vma=False,
    )
```

time: 538 us -> 300 us (0.56)
  the two profiles are of different devices: /device:TPU:98 before, /device:TPU:25 now
where the time goes in v1:
time: 300 us; the launch traced here: 299 us
  Pallas kernels  164 us (55%)
  blocking collectives  58.6 us (20%)
  waiting for transfers between devices  31.8 us (11%)
  starting transfers between devices  21.7 us (7%)
  between operations  13.7 us (5%)
  local copies, waits for them, and re-layouts  3.91 us (1%)
  other arithmetic  3.3 us (1%)
    pallas_call x3, Pallas kernels, attend(): pl.pallas_call(functools.partial(attend_kernel, head, len(sources) > 1),...  152 us
    all_to_all x4, blocking collectives, exchange(): lax.all_to_all(parts, BOTH, split_axis=0, concat_axis=0, axis_index_group...  58.6 us
    ppermute x1, waiting for transfers between devices, per_device(): their_q = lax.ppermute(own_q, 'span', partner)  16.1 us
    all_to_all x1, waiting for transfers between devices, exchange(): lax.all_to_all(parts, BOTH, split_axis=0, concat_axis=0, axis_index_group...  7.92 us
    ppermute x2, starting transfers between devices, swapped(): return [block, lax.ppermute(block, 'span', core_swap)]  6.76 us
    ppermute x3, starting transfers between devices, per_device(): lax.ppermute(note, 'span', move)  6.68 us
    ppermute x3, waiting for transfers between devices, per_device(): parts += [mine, lax.ppermute(theirs, 'span', partner)]  6.46 us
  transfers between devices with their start and end apart: 16, of which 5 were waited for; matrix products, arithmetic and copies ran while one was open for 2% of the time, Pallas kernels for 52%

profile of v1, /device:TPU:25, one launch (start us, length us, event | category | flops | bytes accessed | tf_op | source)
XLA Modules:
  0.0 299.1 jit_solution(907406065885184897)
XLA Ops:
  6.5 3.1 %shard_map.64 = bf16[8,272,128]{2,1,0:T(8,128)(2,1)} custom-call(bf16[128,3072]{1,0:T(8,128)(2,1)} %queries_ref.2, bf16[128,3072]{1,0:T(8,128)(2,1)} %keys_ref.3, bf16[128,3072]{1,0:T(8,128)(2,1)} %values_ref.3, s32[1,128]{1,0:T(1,128)} %bitcast.47), custom_call_target="tpu_custom_call" | custom-call | tf_op jit(solution)/shard_map/pallas_call | solution.py:232
  9.7 18.3 %all_to_all.25 = bf16[8,272,128]{2,1,0:T(8,128)(2,1)S(1)} all-to-all(bf16[8,272,128]{2,1,0:T(8,128)(2,1)} %shard_map.64), channel_id=1, replica_groups={{0,1,32,33,64,65,96,97},{2,3,34,35,66,67,98,99},{4,5,36,37,68,69,100,10..., dimensions={0} | all-to-all | bytes 1114112 | tf_op jit(solution)/shard_map/all_to_all | solution.py:318
  28.0 0.0 collective-permute-start
  28.0 1.5 collective-permute-start.1
  29.5 3.1 %shard_map.65 = (bf16[8,256,128]{2,1,0:T(8,128)(2,1)}, bf16[8,256,128]{2,1,0:T(8,128)(2,1)}, bf16[8,128,384]{2,1,0:T(8,128)(2,1)}) custom-call(bf16[128,3072]{1,0:T(8,128)(2,1)} %keys_ref.3, bf16[128,3072]{1,0:T(8,128)(2,1)} %values_ref.3, bf16[128,3072]{1,0:T(8,128)(2,1)} %queries_ref.2), custom_call_target="tpu_custom_call" | custom-call | tf_op jit(solution)/shard_map/pallas_call | solution.py:240
  32.6 13.3 %all_to_all.26 = bf16[8,256,128]{2,1,0:T(8,128)(2,1)} all-to-all(bf16[8,256,128]{2,1,0:T(8,128)(2,1)} %get-tuple-element.31), channel_id=1, replica_groups={{0,1,32,33,64,65,96,97},{2,3,34,35,66,67,98,99},{4,5,36,37,68,69,100,10..., dimensions={0} | all-to-all | bytes 1048576 | tf_op jit(solution)/shard_map/all_to_all | solution.py:318
  45.9 0.0 collective-permute-done
  45.9 0.0 collective-permute-done.1
  45.9 0.0 all-gather.3.cloned.1.call-update
  45.9 0.0 all-gather.5.cloned.1.call-start
  46.0 14.8 %all_to_all.27 = bf16[8,128,384]{2,1,0:T(8,128)(2,1)} all-to-all(bf16[8,128,384]{2,1,0:T(8,128)(2,1)} %get-tuple-element.35), channel_id=1, replica_groups={{0,1,32,33,64,65,96,97},{2,3,34,35,66,67,98,99},{4,5,36,37,68,69,100,10..., dimensions={0} | all-to-all | bytes 1572864 | tf_op jit(solution)/shard_map/all_to_all | solution.py:318
  60.8 12.1 %all_to_all.28 = bf16[8,256,128]{2,1,0:T(8,128)(2,1)} all-to-all(bf16[8,256,128]{2,1,0:T(8,128)(2,1)S(1)} %copy-done.3), channel_id=1, replica_groups={{0,1,32,33,64,65,96,97},{2,3,34,35,66,67,98,99},{4,5,36,37,68,69,100,10..., dimensions={0} | all-to-all | bytes 1048576 | tf_op jit(solution)/shard_map/all_to_all | solution.py:318
  73.0 0.0 all-gather.5.cloned.1.call-update
  73.1 0.1 broadcast_add_fusion.2
  73.2 0.1 broadcast_add_fusion
  73.3 1.2 collective-permute-start.2
  74.5 0.4 collective-permute-start.3
  74.9 1.4 pad_maximum_fusion
  76.3 6.6 %collective-permute-start.8 = (bf16[3,4,2,272,128]{4,3,2,1,0:T(8,128)(2,1)}, bf16[3,4,2,272,128]{4,3,2,1,0:T(8,128)(2,1)}, u32[]{:S(2)}, u32[]{:S(2)}) collective-permute-start(bf16[3,4,2,272,128]{4,3,2,1,0:T(8,128)(2,1)} %bitcast.4.refs_0_), channel_id=1, source_target_pairs={{0,8},{8,0},{16,24},{24,16},{32,40},{40,32},{48,56},{56,48},{64,72... | collective-permute-start | bytes 5013512 | tf_op jit(solution)/shard_map/ppermute | solution.py:336
  82.9 0.8 slice_reduce_fusion.1
  83.8 0.0 collective-permute-done.2
  83.8 0.0 collective-permute-done.3
  83.8 0.1 pad_maximum_fusion.1
  83.9 5.0 %collective-permute-start.4 = (f32[1,128]{1,0:T(1,128)S(1)}, f32[1,128]{1,0:T(1,128)S(1)}, u32[]{:S(2)}, u32[]{:S(2)}) collective-permute-start(f32[1,128]{1,0:T(1,128)S(1)} %compare_select_fusion), channel_id=1, source_target_pairs={{0,8},{8,0},{16,24},{24,16},{32,40},{40,32},{48,56},{56,48},{64,72... | collective-permute-start | bytes 1544 | tf_op jit(solution)/shard_map/ppermute | solution.py:363
  88.9 0.3 collective-permute-start.5
  89.2 1.4 collective-permute-start.6
  90.6 0.1 broadcast_add_fusion.1
  90.7 0.1 add.111
  90.8 0.2 collective-permute-start.9
  90.9 0.0 collective-permute-done.4
  90.9 0.4 collective-permute-done.5
  91.3 0.9 collective-permute-done.6
  92.2 1.2 collective-permute-start.7
  93.4 0.1 select_reduce_fusion
  93.6 0.1 clamp_reduce_fusion
  93.7 0.6 reshape.148.end_ref
  94.3 0.2 fusion.8
  94.5 0.1 sub.41
  94.6 0.1 compare_convert_fusion
  94.7 0.6 concatenate.21.info_ref
  95.3 0.0 collective-permute-done.9.refs_3_
  95.3 16.1 %collective-permute-done.7.their_q = bf16[4,256,384]{2,1,0:T(8,128)(2,1)S(1)} collective-permute-done((bf16[4,256,384]{2,1,0:T(8,128)(2,1)}, bf16[4,256,384]{2,1,0:T(8,128)(2,1)S(1)}, u32[]{:S(2)}, u32[]{:S(2)}) %collective-permute-start.7) | collective-permute-done | bytes 786464 | tf_op jit(solution)/shard_map/ppermute | solution.py:350
  111.4 0.9 copy-done.8
  112.3 50.7 %shard_map.66 = (bf16[4,272,128]{2,1,0:T(8,128)(2,1)}, bf16[4,272,128]{2,1,0:T(8,128)(2,1)}) custom-call(s32[14]{0:T(128)} %concatenate.21.info_ref, bf16[4,256,384]{2,1,0:T(8,128)(2,1)} %bitcast.39, bf16[4,256,384]{2,1,0:T(8,128)(2,1)} %copy-done.8, s32[8,1,256]{2,1,0:T(1,128)} %reshape.148.end_ref, bf16[3,4,2,272,128]{4,3,2,1,0:T(8,128)(2,1)} %bitcast.4.refs_0_, ...), custom_call_target="tpu_custom_call" | custom-call | flops 8589934592 | bytes 5242880 | tf_op jit(solution)/shard_map/pallas_call | solution.py:168
  162.9 0.1 collective-permute-start.10
  163.0 0.0 all-gather.3.cloned.1.call-done
  163.1 50.6 %shard_map.67 = (bf16[4,272,128]{2,1,0:T(8,128)(2,1)}, bf16[4,272,128]{2,1,0:T(8,128)(2,1)}) custom-call(s32[14]{0:T(128)} %concatenate.21.info_ref, bf16[4,256,384]{2,1,0:T(8,128)(2,1)} %bitcast.40, bf16[4,256,384]{2,1,0:T(8,128)(2,1)} %copy-done.8, s32[8,1,256]{2,1,0:T(1,128)} %reshape.148.end_ref, bf16[4,2,4,2,256,128]{5,4,3,2,1,0:T(8,128)(2,1)} %bitcast.48), custom_call_target="tpu_custom_call" | custom-call | flops 8589934592 | bytes 5242880 | tf_op jit(solution)/shard_map/pallas_call | solution.py:168
  213.7 0.1 collective-permute-start.11
  213.8 0.0 all-gather.5.cloned.1.call-done
  213.8 0.0 copy-start.9
  213.8 50.8 %shard_map.68 = (bf16[4,272,128]{2,1,0:T(8,128)(2,1)}, bf16[4,272,128]{2,1,0:T(8,128)(2,1)}) custom-call(s32[14]{0:T(128)} %concatenate.21.info_ref, bf16[4,256,384]{2,1,0:T(8,128)(2,1)} %bitcast.41, bf16[4,256,384]{2,1,0:T(8,128)(2,1)} %copy-done.8, s32[8,1,256]{2,1,0:T(1,128)} %reshape.148.end_ref, bf16[4,2,4,2,256,128]{5,4,3,2,1,0:T(8,128)(2,1)} %bitcast.49), custom_call_target="tpu_custom_call" | custom-call | flops 8589934592 | bytes 5242880 | tf_op jit(solution)/shard_map/pallas_call | solution.py:168
  264.6 0.1 collective-permute-start.12
  264.7 0.0 collective-permute-done.10.refs_1_
  264.7 0.0 collective-permute-done.11.refs_3_
  264.7 6.5 %collective-permute-done.12.refs_5_ = bf16[4,272,128]{2,1,0:T(8,128)(2,1)S(1)} collective-permute-done((bf16[4,272,128]{2,1,0:T(8,128)(2,1)}, bf16[4,272,128]{2,1,0:T(8,128)(2,1)S(1)}, u32[]{:S(2)}, u32[]{:S(2)}) %collective-permute-start.12) | collective-permute-done | bytes 278560 | tf_op jit(solution)/shard_map/ppermute | solution.py:389
  271.2 0.7 copy-done.6
  271.9 2.8 shard_map.69
  274.7 3.7 %all-to-all-start.4 = ((bf16[8,128,384]{2,1,0:T(8,128)(2,1)}), bf16[8,128,384]{2,1,0:T(8,128)(2,1)S(1)}, u32[]{:S(2)}, u32[]{:S(2)}) async-start(bf16[8,128,384]{2,1,0:T(8,128)(2,1)} %shard_map.69), calls=%async_computation.4 | async-start | bytes 1572864 | tf_op jit(solution)/shard_map/all_to_all | solution.py:318
  278.3 0.1 fusion.2
  278.5 0.3 fusion.4
  278.8 2.0 fusion.gate_ref
  280.8 7.9 %all-to-all-done.4.mixed_ref = bf16[8,128,384]{2,1,0:T(8,128)(2,1)S(1)} async-done(((bf16[8,128,384]{2,1,0:T(8,128)(2,1)}), bf16[8,128,384]{2,1,0:T(8,128)(2,1)S(1)}, u32[]{:S(2)}, u32[]{:S(2)}) %all-to-all-start.4) | async-done | bytes 786464 | tf_op jit(solution)/shard_map/all_to_all | solution.py:318
  288.7 0.9 copy-done.1
  289.6 2.6 shard_map.70
  (35 shorter events, 0.2 us)
Async XLA Ops:
  6.5 271.9 %copy-start = (bf16[256,3072]{1,0:T(8,128)(2,1)S(1)}, bf16[256,3072]{1,0:T(8,128)(2,1)}, u32[]{:S(2)}) copy-start(bf16[256,3072]{1,0:T(8,128)(2,1)} %param.11) | copy-start | bytes 4718596
  6.5 156.5 %all-gather.3.cloned.1.call-start = ((), (), s32[]{:S(2)}) async-start(), calls=%async_computation.5 | async-start | bytes 4718592 | tf_op jit(solution)/shard_map/all_gather | solution.py:352
  28.0 17.9 %collective-permute-start = (bf16[8,272,128]{2,1,0:T(8,128)(2,1)S(1)}, bf16[8,272,128]{2,1,0:T(8,128)(2,1)S(1)}, u32[]{:S(2)}, u32[]{:S(2)}) collective-permute-start(bf16[8,272,128]{2,1,0:T(8,128)(2,1)S(1)} %all_to_all.25), channel_id=1, source_target_pairs={{0,2},{1,3},{2,4},{3,5},{4,6},{5,7},{6,0},{7,1},{8,10},{9,11},{10,... | collective-permute-start | bytes 1671176 | tf_op jit(solution)/shard_map/ppermute | solution.py:326
  28.0 17.9 %collective-permute-start.1 = (bf16[8,272,128]{2,1,0:T(8,128)(2,1)S(1)}, bf16[8,272,128]{2,1,0:T(8,128)(2,1)S(1)}, u32[]{:S(2)}, u32[]{:S(2)}) collective-permute-start(bf16[8,272,128]{2,1,0:T(8,128)(2,1)S(1)} %all_to_all.25), channel_id=1, source_target_pairs={{0,6},{1,7},{2,0},{3,1},{4,2},{5,3},{6,4},{7,5},{8,14},{9,15},{10,... | collective-permute-start | bytes 1671176 | tf_op jit(solution)/shard_map/ppermute | solution.py:326
  45.9 167.9 %all-gather.5.cloned.1.call-start = ((), (), s32[]{:S(2)}) async-start(), calls=%async_computation.6 | async-start | bytes 4718592 | tf_op jit(solution)/shard_map/all_gather | solution.py:352
  46.0 14.9 %copy-start.3 = (bf16[8,256,128]{2,1,0:T(8,128)(2,1)S(1)}, bf16[8,256,128]{2,1,0:T(8,128)(2,1)}, u32[]{:S(2)}) copy-start(bf16[8,256,128]{2,1,0:T(8,128)(2,1)} %get-tuple-element.36) | copy-start | bytes 1572868
  73.3 10.5 %collective-permute-start.2 = (bf16[4,272,128]{2,1,0:T(8,128)(2,1)S(1)}, bf16[4,272,128]{2,1,0:T(8,128)(2,1)S(1)}, u32[]{:S(2)}, u32[]{:S(2)}) collective-permute-start(bf16[4,272,128]{2,1,0:T(8,128)(2,1)S(1)} %slice.25), channel_id=1, source_target_pairs={{0,2},{1,3},{2,4},{3,5},{4,6},{5,7},{6,0},{7,1},{8,10},{9,11},{10,... | collective-permute-start | bytes 835592 | tf_op jit(solution)/shard_map/ppermute | solution.py:330
  74.5 9.3 %collective-permute-start.3 = (bf16[4,272,128]{2,1,0:T(8,128)(2,1)S(1)}, bf16[4,272,128]{2,1,0:T(8,128)(2,1)S(1)}, u32[]{:S(2)}, u32[]{:S(2)}) collective-permute-start(bf16[4,272,128]{2,1,0:T(8,128)(2,1)S(1)} %slice.26), channel_id=1, source_target_pairs={{0,6},{1,7},{2,0},{3,1},{4,2},{5,3},{6,4},{7,5},{8,14},{9,15},{10,... | collective-permute-start | bytes 835592 | tf_op jit(solution)/shard_map/ppermute | solution.py:330
  76.3 35.1 %collective-permute-start.8 = (bf16[3,4,2,272,128]{4,3,2,1,0:T(8,128)(2,1)}, bf16[3,4,2,272,128]{4,3,2,1,0:T(8,128)(2,1)}, u32[]{:S(2)}, u32[]{:S(2)}) collective-permute-start(bf16[3,4,2,272,128]{4,3,2,1,0:T(8,128)(2,1)} %bitcast.4.refs_0_), channel_id=1, source_target_pairs={{0,8},{8,0},{16,24},{24,16},{32,40},{40,32},{48,56},{56,48},{64,72... | collective-permute-start | bytes 5013512 | tf_op jit(solution)/shard_map/ppermute | solution.py:336
  83.9 27.5 %copy-start.2 = (bf16[8,272,128]{2,1,0:T(8,128)(2,1)}, bf16[8,272,128]{2,1,0:T(8,128)(2,1)S(1)}, u32[]{:S(2)}) copy-start(bf16[8,272,128]{2,1,0:T(8,128)(2,1)S(1)} %pad_maximum_fusion.1) | copy-start | bytes 1671172
  83.9 7.0 %collective-permute-start.4 = (f32[1,128]{1,0:T(1,128)S(1)}, f32[1,128]{1,0:T(1,128)S(1)}, u32[]{:S(2)}, u32[]{:S(2)}) collective-permute-start(f32[1,128]{1,0:T(1,128)S(1)} %compare_select_fusion), channel_id=1, source_target_pairs={{0,8},{8,0},{16,24},{24,16},{32,40},{40,32},{48,56},{56,48},{64,72... | collective-permute-start | bytes 1544 | tf_op jit(solution)/shard_map/ppermute | solution.py:363
  88.9 2.4 collective-permute-start.5
  89.2 3.0 collective-permute-start.6
  90.8 4.5 %collective-permute-start.9 = (bf16[1,4,2,272,128]{4,3,2,1,0:T(8,128)(2,1)S(1)}, bf16[1,4,2,272,128]{4,3,2,1,0:T(8,128)(2,1)}, u32[]{:S(2)}, u32[]{:S(2)}) collective-permute-start(bf16[1,4,2,272,128]{4,3,2,1,0:T(8,128)(2,1)S(1)} %bitcast.43), channel_id=1, source_target_pairs={{0,8},{8,0},{16,24},{24,16},{32,40},{40,32},{48,56},{56,48},{64,72... | collective-permute-start | bytes 1671176 | tf_op jit(solution)/shard_map/ppermute | solution.py:336
  92.2 19.2 %collective-permute-start.7 = (bf16[4,256,384]{2,1,0:T(8,128)(2,1)}, bf16[4,256,384]{2,1,0:T(8,128)(2,1)S(1)}, u32[]{:S(2)}, u32[]{:S(2)}) collective-permute-start(bf16[4,256,384]{2,1,0:T(8,128)(2,1)} %bitcast.38), channel_id=1, source_target_pairs={{0,16},{8,24},{16,0},{24,8},{32,48},{40,56},{48,32},{56,40},{64,80... | collective-permute-start | bytes 2359304 | tf_op jit(solution)/shard_map/ppermute | solution.py:350
  111.4 0.9 copy-start.8
  162.9 101.8 %collective-permute-start.10 = (bf16[4,272,128]{2,1,0:T(8,128)(2,1)}, bf16[4,272,128]{2,1,0:T(8,128)(2,1)S(1)}, u32[]{:S(2)}, u32[]{:S(2)}) collective-permute-start(bf16[4,272,128]{2,1,0:T(8,128)(2,1)} %get-tuple-element.41), channel_id=1, source_target_pairs={{0,16},{8,24},{16,0},{24,8},{32,48},{40,56},{48,32},{56,40},{64,80... | collective-permute-start | bytes 835592 | tf_op jit(solution)/shard_map/ppermute | solution.py:389
  213.7 51.0 %collective-permute-start.11 = (bf16[4,272,128]{2,1,0:T(8,128)(2,1)}, bf16[4,272,128]{2,1,0:T(8,128)(2,1)S(1)}, u32[]{:S(2)}, u32[]{:S(2)}) collective-permute-start(bf16[4,272,128]{2,1,0:T(8,128)(2,1)} %get-tuple-element.46), channel_id=1, source_target_pairs={{0,16},{8,24},{16,0},{24,8},{32,48},{40,56},{48,32},{56,40},{64,80... | collective-permute-start | bytes 835592 | tf_op jit(solution)/shard_map/ppermute | solution.py:389
  213.8 50.9 %copy-start.9 = (s32[24]{0:T(128)S(1)}, s32[24]{0:T(128)}, u32[]{:S(2)}) copy-start(s32[24]{0:T(128)} %param.10) | copy-start | bytes 292
  264.6 6.6 %collective-permute-start.12 = (bf16[4,272,128]{2,1,0:T(8,128)(2,1)}, bf16[4,272,128]{2,1,0:T(8,128)(2,1)S(1)}, u32[]{:S(2)}, u32[]{:S(2)}) collective-permute-start(bf16[4,272,128]{2,1,0:T(8,128)(2,1)} %get-tuple-element.50), channel_id=1, source_target_pairs={{0,16},{8,24},{16,0},{24,8},{32,48},{40,56},{48,32},{56,40},{64,80... | collective-permute-start | bytes 835592 | tf_op jit(solution)/shard_map/ppermute | solution.py:389
  264.7 6.5 %copy-start.4 = (bf16[4,272,128]{2,1,0:T(8,128)(2,1)}, bf16[4,272,128]{2,1,0:T(8,128)(2,1)S(1)}, u32[]{:S(2)}) copy-start(bf16[4,272,128]{2,1,0:T(8,128)(2,1)S(1)} %collective-permute-done.10.refs_1_) | copy-start | bytes 835588
  264.7 6.5 %copy-start.5 = (bf16[4,272,128]{2,1,0:T(8,128)(2,1)}, bf16[4,272,128]{2,1,0:T(8,128)(2,1)S(1)}, u32[]{:S(2)}) copy-start(bf16[4,272,128]{2,1,0:T(8,128)(2,1)S(1)} %collective-permute-done.11.refs_3_) | copy-start | bytes 835588
  271.2 0.7 copy-start.6
  274.7 4.1 %copy-start.7 = (s32[128]{0:T(128)S(1)}, s32[128]{0:T(128)}, u32[]{:S(2)}) copy-start(s32[128]{0:T(128)} %param.9) | copy-start | bytes 1540
  274.7 14.1 %all-to-all-start.4 = ((bf16[8,128,384]{2,1,0:T(8,128)(2,1)}), bf16[8,128,384]{2,1,0:T(8,128)(2,1)S(1)}, u32[]{:S(2)}, u32[]{:S(2)}) async-start(bf16[8,128,384]{2,1,0:T(8,128)(2,1)} %shard_map.69), calls=%async_computation.4 | async-start | bytes 1572864 | tf_op jit(solution)/shard_map/all_to_all | solution.py:318
  288.7 0.9 copy-start.1
Sparse Core Ops, SparseCore 0:
  46.1 30.8 all-gather.2
  78.6 35.2 all-gather.4

commit v2 on v1

v2 whole, which is shorter than its diff:
```python
import functools
import math

import jax
import jax.numpy as jnp
from jax import lax
from jax.experimental import pallas as pl
from jax.experimental.pallas import tpu as pltpu
from jax.sharding import PartitionSpec as P

HEAD_DIM = 128
SCALE = HEAD_DIM**-0.5
SCALE_LOG2 = SCALE * math.log2(math.e)
BOTH = ("span", "head")
ZONES = 8
SEGMENT = 2 * HEAD_DIM
KEYS = 8192
WIDTH = 512
ITEMS = 4
K_NORM, Q_NORM = 32, 40
NOTE = 16
PLAIN_LIMIT = 70.0
LOW = -1e30


def dot(a, b):
    return jnp.dot(a, b, preferred_element_type=jnp.float32)


def attend_kernel(head, ringed, info_ref, own_q, their_q, end_ref, *refs):
    sources, refs = refs[: 4 if ringed else 1], refs[4 if ringed else 1 :]
    own_out, their_out, kv_ref, qt_ref, weight_ref, acc_ref, top_ref, sems = refs
    core, rank = info_ref[0], info_ref[1]
    blocks = ZONES

    copies = []
    if ringed:
        near, near_last, far, far_last = sources
        for j, (src, last, c) in enumerate(((near, near_last, core), (far, far_last, 1 - core))):
            pieces = [(src.at[0], 0), (src.at[1], 1), (last.at[0], 2), (src.at[2], 3)]
            for piece, step in pieces:
                copies.append(
                    pltpu.make_async_copy(
                        piece, kv_ref.at[(rank + step) % 4, c], sems.at[4 * j + step]
                    )
                )
    else:
        whole = sources[0].at[:, :, :, pl.ds(0, 2 * HEAD_DIM)]
        copies.append(pltpu.make_async_copy(whole, kv_ref, sems.at[0]))
    for copy in copies:
        copy.start()

    for zone in range(ZONES):
        qt_ref[zone] = jnp.concatenate([own_q[zone], their_q[zone]], axis=1)
    acc_ref[...] = jnp.zeros_like(acc_ref)
    top_ref[...] = jnp.zeros_like(top_ref)
    ones = jnp.ones((NOTE, WIDTH), jnp.bfloat16)
    for copy in copies:
        copy.wait()

    def part(i, rows):
        return kv_ref[:, i % 2, i // 2, rows]

    def keys_at(i):
        return part(i, slice(0, HEAD_DIM)).reshape(WIDTH, HEAD_DIM)

    def values_at(i):
        block = part(i, slice(HEAD_DIM, 2 * HEAD_DIM))
        block = jnp.concatenate([block[y] for y in range(4)], axis=1)
        return jnp.concatenate([block, ones], axis=0)

    def visible_at(r, i):
        row = lax.broadcasted_iota(jnp.int32, (WIDTH, SEGMENT), 0)
        return row < end_ref[r] - i * WIDTH

    def weigh(slot, r, i):
        r = jnp.minimum(r, blocks - 1)
        weights = jnp.exp2(dot(keys_at(i), qt_ref[r]) * SCALE_LOG2)
        weights = jnp.where(visible_at(r, i), weights, 0.0)
        weight_ref[slot] = weights.astype(jnp.bfloat16)

    def absorb(slot, r, i):
        acc_ref[r] += dot(values_at(i), weight_ref[slot])

    def careful(r, i):
        scores = dot(keys_at(i), qt_ref[r]) * SCALE_LOG2
        visible = visible_at(r, i)
        scores = jnp.where(visible, scores, LOW)
        old = top_ref[r, :1]
        new = jnp.maximum(old, jnp.max(scores, axis=0, keepdims=True))
        weights = jnp.where(visible, jnp.exp2(scores - new), 0.0).astype(jnp.bfloat16)
        acc_ref[r] = acc_ref[r] * jnp.exp2(old - new) + dot(values_at(i), weights)
        top_ref[r] = jnp.broadcast_to(new, top_ref.shape[1:])

    def count(r):
        return info_ref[2 + r]

    plain = info_ref[2 + blocks + head] == 1

    @pl.when(plain)
    def _():
        def following(item):
            r, i = item
            over = i + 1 >= count(jnp.minimum(r, blocks - 1))
            over = jnp.logical_or(over, r >= blocks)
            return jnp.where(over, jnp.minimum(r + 1, blocks), r), jnp.where(over, 0, i + 1)

        def run(item):
            items = [item]
            for _ in range(ITEMS - 1):
                items.append(following(items[-1]))
            return tuple(items)

        def step(_, items):
            later = run(following(items[-1]))
            for slot in range(ITEMS):
                absorb(slot, *items[slot])
                weigh(slot, *later[slot])
            return later

        items = run((jnp.int32(0), jnp.int32(0)))
        for slot in range(ITEMS):
            weigh(slot, *items[slot])
        total = sum(count(r) for r in range(blocks))
        items = lax.fori_loop(0, (total + ITEMS - 1) // ITEMS - 1, step, items)
        for slot in range(ITEMS):
            absorb(slot, *items[slot])

    @pl.when(jnp.logical_not(plain))
    def _():
        top_ref[...] = jnp.full_like(top_ref, LOW)

        def over_block(r, carry):
            def over_chunk(i, carry):
                careful(r, i)
                return carry

            return lax.fori_loop(0, count(r), over_chunk, carry)

        lax.fori_loop(0, blocks, over_block, 0)

    for r in range(blocks):
        acc = acc_ref[r]
        total = acc[HEAD_DIM : HEAD_DIM + 1]
        some = total > 0.0
        safe = jnp.where(some, total, 1.0)
        mean = (acc[:HEAD_DIM] * jnp.where(some, 1.0 / safe, 0.0)).astype(jnp.bfloat16)
        level = jnp.where(some, top_ref[r, :1] + jnp.log2(safe), LOW)
        high = level.astype(jnp.bfloat16).astype(jnp.float32)
        middle = (level - high).astype(jnp.bfloat16).astype(jnp.float32)
        low = level - high - middle
        spare = jnp.zeros((NOTE - 3, SEGMENT), jnp.float32)
        note = jnp.concatenate([high, middle, low, spare]).astype(jnp.bfloat16)
        for out, at in ((own_out, slice(0, HEAD_DIM)), (their_out, slice(HEAD_DIM, SEGMENT))):
            out[r, :HEAD_DIM, :] = mean[:, at]
            out[r, HEAD_DIM:, :] = note[:, at]


def attend(info, own_q, their_q, ends, sources, head):
    rows = ZONES * SEGMENT
    out = jax.ShapeDtypeStruct((ZONES, HEAD_DIM + NOTE, HEAD_DIM), jnp.bfloat16)
    first = own_q.shape[1] // HEAD_DIM - 3
    own_spec = pl.BlockSpec((ZONES, HEAD_DIM, HEAD_DIM), lambda i, *_: (0, first + head, 0))
    whole = pl.BlockSpec(memory_space=pltpu.VMEM)
    return pl.pallas_call(
        functools.partial(attend_kernel, head, len(sources) > 1),
        grid_spec=pltpu.PrefetchScalarGridSpec(
            num_scalar_prefetch=1,
            grid=(1,),
            in_specs=[own_spec, whole, whole]
            + [pl.BlockSpec(memory_space=pl.ANY)] * len(sources),
            out_specs=[whole, whole],
            scratch_shapes=[
                pltpu.VMEM((4, 2, ZONES, 2 * HEAD_DIM, HEAD_DIM), jnp.bfloat16),
                pltpu.VMEM((ZONES, HEAD_DIM, SEGMENT), jnp.bfloat16),
                pltpu.VMEM((ITEMS, WIDTH, SEGMENT), jnp.bfloat16),
                pltpu.VMEM((ZONES + 1, HEAD_DIM + NOTE, SEGMENT), jnp.float32),
                pltpu.VMEM((ZONES, 8, SEGMENT), jnp.float32),
                pltpu.SemaphoreType.DMA((8,)),
            ],
        ),
        out_shape=[out, out],
        compiler_params=pltpu.CompilerParams(vmem_limit_bytes=58 << 20),
        cost_estimate=pl.CostEstimate(
            flops=4 * rows * KEYS * HEAD_DIM,
            bytes_accessed=4 * KEYS * HEAD_DIM + 4 * rows * HEAD_DIM,
            transcendentals=rows * KEYS // 2,
        ),
    )(info, own_q, their_q, ends, *sources)


def pack_first_kernel(head, queries_ref, keys_ref, values_ref, ids_ref, out_ref):
    groups = out_ref.shape[0]
    heads = keys_ref.shape[1] // HEAD_DIM // groups
    ids = jnp.broadcast_to(ids_ref[...].astype(jnp.float32), (HEAD_DIM, HEAD_DIM)).T
    lane = lax.broadcasted_iota(jnp.int32, (HEAD_DIM, HEAD_DIM), 1)
    counts = jnp.sum(jnp.where(ids <= lane.astype(jnp.float32), 1.0, 0.0), axis=0, keepdims=True)
    ones = jnp.ones((HEAD_DIM, HEAD_DIM), jnp.bfloat16)
    lane = lane[:1]
    for g in range(groups):
        at = slice((g * heads + head) * HEAD_DIM, (g * heads + head + 1) * HEAD_DIM)
        out_ref[g, :HEAD_DIM] = keys_ref[:, at]
        out_ref[g, HEAD_DIM : 2 * HEAD_DIM] = values_ref[:, at].T
        note = counts
        for first, ref in ((K_NORM, keys_ref), (Q_NORM, queries_ref)):
            for h in range(heads):
                start = (g * heads + h) * HEAD_DIM
                rows = ref[:, start : start + HEAD_DIM].astype(jnp.float32)
                norm = jnp.max(dot((rows * rows).astype(jnp.bfloat16), ones), axis=0, keepdims=True)
                note = jnp.where(lane == first + h, norm * 1.02, note)
        out_ref[g, 2 * HEAD_DIM :] = jnp.broadcast_to(note, (NOTE, HEAD_DIM)).astype(jnp.bfloat16)


def pack_rest_kernel(others, queries_ref, keys_ref, values_ref, out_ref):
    groups = out_ref.shape[0]
    heads = keys_ref.shape[1] // HEAD_DIM // groups
    for g in range(groups):
        parts = [p for head in others for p in ((keys_ref, head, False), (values_ref, head, True))]
        parts += [(queries_ref, head, True) for head in range(heads)]
        for j, (ref, head, turn) in enumerate(parts):
            at = slice((g * heads + head) * HEAD_DIM, (g * heads + head + 1) * HEAD_DIM)
            out_ref[g, j * HEAD_DIM : (j + 1) * HEAD_DIM] = ref[:, at].T if turn else ref[:, at]


def pack(kernel, rows, *args):
    return pl.pallas_call(
        kernel, out_shape=jax.ShapeDtypeStruct((ZONES, rows, HEAD_DIM), jnp.bfloat16)
    )(*args)


def merge_kernel(*refs):
    out = refs[-1]

    def level(ref, zone):
        note = ref[zone, HEAD_DIM:, :].astype(jnp.float32)
        return note[0:1] + note[1:2] + note[2:3]

    for head in range(len(refs) // 2):
        one, two = refs[2 * head], refs[2 * head + 1]
        at = slice(head * HEAD_DIM, (head + 1) * HEAD_DIM)
        for zone in range(ZONES):
            share = 1.0 / (1.0 + jnp.exp2(level(two, zone) - level(one, zone)))
            a, b = (ref[zone, :HEAD_DIM, :].astype(jnp.float32) for ref in (one, two))
            out[zone, at, :] = (b + (a - b) * share).astype(jnp.bfloat16)


def merge(parts):
    return pack(merge_kernel, len(parts) // 2 * HEAD_DIM, *parts)


def gate_kernel(gate_ref, mixed_ref, out_ref):
    groups, local, _ = mixed_ref.shape
    for g in range(groups):
        for h in range(0, local, HEAD_DIM):
            at = slice(g * local + h, g * local + h + HEAD_DIM)
            attended = mixed_ref[g, h : h + HEAD_DIM, :].T.astype(jnp.float32)
            out_ref[:, at] = (gate_ref[:, at] * attended).astype(jnp.bfloat16)


def gate_rows(span_ids, timesteps, time_weight):
    half = time_weight.shape[0] // 2
    freqs = jnp.exp(-math.log(10000.0) * jnp.arange(half, dtype=jnp.float32) / half)
    angles = timesteps.astype(jnp.float32)[:, None] * freqs[None, :]
    embed = jnp.concatenate([jnp.cos(angles), jnp.sin(angles)], axis=1).astype(jnp.bfloat16)
    gate_table = jnp.dot(embed, time_weight, preferred_element_type=jnp.float32)
    onehot = (span_ids[:, None] == jnp.arange(timesteps.shape[0], dtype=jnp.int32)[None, :]).astype(
        jnp.float32
    )
    return jnp.dot(onehot, gate_table, precision=lax.Precision.HIGHEST)


def per_device(queries, keys, values, span_ids, timesteps, time_weight):
    runs, groups = lax.axis_size("span"), lax.axis_size("head")
    run, rank = lax.axis_index("span"), lax.axis_index("head")
    spans = timesteps.shape[0]
    chunk, width = queries.shape
    local = width // groups
    heads = local // HEAD_DIM

    def device(zone, core, y, x):
        return (2 * zone + core) * groups + 2 * y + x

    across = [
        [device(zone, core, y, x) for zone in range(ZONES)]
        for core in range(2)
        for y in range(4)
        for x in range(2)
    ]
    along_y = [
        [device(zone, core, y, x) for y in range(4) for core in range(2)]
        for zone in range(ZONES)
        for x in range(2)
    ]
    up = [(h, (h + 2) % groups) for h in range(groups)]
    down = [(h, (h - 2) % groups) for h in range(groups)]
    core_swap = [(s, s ^ 1) for s in range(runs)]
    partner = [(h, h ^ 1) for h in range(groups)]

    def exchange(parts):
        return lax.all_to_all(
            parts, BOTH, split_axis=0, concat_axis=0, axis_index_groups=across, tiled=True
        )

    def gather(block):
        block = lax.all_gather(block, BOTH, axis_index_groups=along_y, axis=0, tiled=True)
        return block.reshape(4, 2, ZONES, -1, HEAD_DIM)

    def after(*values):
        return lax.optimization_barrier(values)

    def swapped(block):
        return block, lax.ppermute(block, "span", core_swap)

    pair = 2 * HEAD_DIM
    note_rows = span_ids.reshape(1, -1)
    first = pack(
        functools.partial(pack_first_kernel, 1), pair + NOTE, queries, keys, values, note_rows
    )
    first = exchange(first)
    queries, first = after(queries, first)
    rest = pack(
        functools.partial(pack_rest_kernel, (0, 2)), 2 * pair + local, queries, keys, values
    )
    rest = exchange(rest)
    gathered = gather(first)
    block = rest[:, :pair]
    half = ZONES // 2
    below, above = lax.ppermute(block, "head", up), lax.ppermute(block, "head", down)
    their_q = [None] * heads
    for head in (1, 0, 2):
        start = 2 * pair + head * HEAD_DIM
        their_q[head] = lax.ppermute(rest[:, start : start + HEAD_DIM], "head", partner)

    def combined(notes):
        is_count = jnp.arange(HEAD_DIM) < K_NORM
        return jnp.where(is_count, jnp.sum(notes, axis=0), jnp.max(notes, axis=0))

    note = combined(gathered[:, :, :, pair].reshape(-1, HEAD_DIM).astype(jnp.float32))[None]
    note = combined(jnp.concatenate([note, lax.ppermute(note, "head", partner)]))
    squares = note[K_NORM : K_NORM + heads] * note[Q_NORM : Q_NORM + heads]
    plain = (squares * (1.05 * SCALE**2) < PLAIN_LIMIT**2).astype(jnp.int32)
    ends = note[:spans].astype(jnp.int32)

    core, y, side = run % 2, rank // 2, rank % 2
    sides = jnp.stack([side, 1 - side])[None, :, None] * HEAD_DIM
    position = jnp.arange(ZONES)[:, None, None] * 2048 + sides + jnp.arange(HEAD_DIM)[None, None, :]
    position = (position + (core * 1024 + y * SEGMENT)).reshape(ZONES, SEGMENT)
    reach = jnp.min(
        jnp.where(ends > position[..., None], ends, runs * groups * chunk), axis=2
    )
    reach = jnp.maximum(reach - side * HEAD_DIM, 0)
    seen = (reach // SEGMENT) * HEAD_DIM + jnp.minimum(reach % SEGMENT, HEAD_DIM)
    seen = seen.astype(jnp.int32)
    counts = jnp.maximum((jnp.max(seen, axis=1) + WIDTH - 1) // WIDTH, 1)
    info = jnp.concatenate([jnp.stack([core, y]), counts, plain]).astype(jnp.int32)
    seen = seen.reshape(ZONES, 1, SEGMENT)

    parts = [None] * (2 * heads)

    def attended(info, head, sources):
        parts[2 * head], theirs = attend(info, rest, their_q[head], seen, sources, head)
        info, theirs = after(info, theirs)
        parts[2 * head + 1] = lax.ppermute(theirs, "head", partner)
        return info

    info, below, above = after(info, below, above)
    pieces = [lax.ppermute(below[:half], "head", up), lax.ppermute(above[half:], "head", down)]
    near, far = swapped(jnp.stack([block, above, below]))
    info = attended(info, 1, (gathered,))
    info, *pieces = after(info, *pieces)
    near_last, far_last = swapped(jnp.concatenate(pieces)[None])
    info = attended(info, 0, (near, near_last, far, far_last))
    info = attended(info, 2, (gather(rest[:, pair : 2 * pair]),))
    mixed = exchange(merge(parts))
    gates = gate_rows(span_ids, timesteps, time_weight)
    return pl.pallas_call(
        gate_kernel, out_shape=jax.ShapeDtypeStruct((chunk, width), jnp.bfloat16)
    )(gates, mixed)


def solution(mesh):
    return jax.shard_map(
        per_device,
        mesh=mesh,
        in_specs=(
            P(("span", "head"), None),
            P(("span", "head"), None),
            P(("span", "head"), None),
            P(("span", "head")),
            P(),
            P(),
        ),
        out_specs=P(("span", "head"), None),
        check_vma=False,
    )
```

time: 300 us -> 276 us (0.920)
  blocking collectives: 58.6 us -> 41 us
  waiting for transfers between devices: 31.8 us -> 20.9 us
  local copies, waits for them, and re-layouts: 3.91 us -> 7.4 us
    all_to_all x4 -> x2, blocking collectives: 58.6 us -> 41 us  [exchange(): lax.all_to_all(parts, BOTH, split_axis=0, concat_axis=0, axis_index_group...]
    ppermute x13, waiting for transfers between devices: 23.8 us -> 13.8 us  [the longest x3 5.46 us: attended(): parts[2 * head + 1] = lax.ppermute(theirs, 'head', partner)]
    slice x2 -> x4, local copies, waits for them, and re-layouts: 0.04 us -> 3.49 us  [the longest x1 1.49 us: per_device(): info = attended(info, 2, (gather(rest[:, pair:2 * pair]),))]
  transfers between devices with their start and end apart: 16 -> 16, of which waited for: 5 -> 7; matrix products, arithmetic and copies ran while one was open for 2% -> 4% of each run, Pallas kernels for 52% -> 56%
where the time goes in v2:
time: 276 us; the launch traced here: 274 us
  Pallas kernels  162 us (59%)
  blocking collectives  41 us (15%)
  starting transfers between devices  21.3 us (8%)
  waiting for transfers between devices  20.9 us (8%)
  between operations  13.7 us (5%)
  local copies, waits for them, and re-layouts  7.4 us (3%)
  other arithmetic  5.5 us (2%)
    pallas_call x3, Pallas kernels, attend(): pl.pallas_call(functools.partial(attend_kernel, head, len(sources) > 1),...  150 us
    all_to_all x2, blocking collectives, exchange(): lax.all_to_all(parts, BOTH, split_axis=0, concat_axis=0, axis_index_group...  41 us
    pallas_call x3, Pallas kernels, pack(): pl.pallas_call(kernel, out_shape=jax.ShapeDtypeStruct((ZONES, rows, HEAD_...  9.11 us
    all_to_all x1, waiting for transfers between devices, exchange(): lax.all_to_all(parts, BOTH, split_axis=0, concat_axis=0, axis_index_group...  6.82 us
  transfers between devices with their start and end apart: 16, of which 7 were waited for; matrix products, arithmetic and copies ran while one was open for 4% of the time, Pallas kernels for 56%

profile of v2, /device:TPU:25, one launch (start us, length us, event | category | flops | bytes accessed | tf_op | source)
XLA Modules:
  0.0 274.1 jit_solution(4284707507313890852)
XLA Ops:
  6.5 3.1 %shard_map.64 = bf16[8,272,128]{2,1,0:T(8,128)(2,1)} custom-call(bf16[128,3072]{1,0:T(8,128)(2,1)} %queries_ref.2, bf16[128,3072]{1,0:T(8,128)(2,1)} %keys_ref.3, bf16[128,3072]{1,0:T(8,128)(2,1)} %values_ref.3, s32[1,128]{1,0:T(1,128)} %bitcast.46), custom_call_target="tpu_custom_call" | custom-call | tf_op jit(solution)/shard_map/pallas_call | solution.py:226
  9.7 15.4 %all_to_all.15 = bf16[8,272,128]{2,1,0:T(8,128)(2,1)} all-to-all(bf16[8,272,128]{2,1,0:T(8,128)(2,1)} %shard_map.64), channel_id=1, replica_groups={{0,16,32,48,64,80,96,112},{1,17,33,49,65,81,97,113},{2,18,34,50,66,82,9..., dimensions={0} | all-to-all | bytes 1114112 | tf_op jit(solution)/shard_map/all_to_all | solution.py:300
  25.1 0.0 all-gather.3.cloned.1.call-update
  25.1 0.0 all-gather.5.cloned.1.call-start
  25.2 3.3 %shard_map.65 = bf16[8,896,128]{2,1,0:T(8,128)(2,1)} custom-call(bf16[128,3072]{1,0:T(8,128)(2,1)} %queries_ref.2, bf16[128,3072]{1,0:T(8,128)(2,1)} %keys_ref.3, bf16[128,3072]{1,0:T(8,128)(2,1)} %values_ref.3), custom_call_target="tpu_custom_call" | custom-call | tf_op jit(solution)/shard_map/pallas_call | solution.py:226
  28.5 25.6 %all_to_all.16.own_q = bf16[8,896,128]{2,1,0:T(8,128)(2,1)S(1)} all-to-all(bf16[8,896,128]{2,1,0:T(8,128)(2,1)} %shard_map.65), channel_id=1, replica_groups={{0,16,32,48,64,80,96,112},{1,17,33,49,65,81,97,113},{2,18,34,50,66,82,9..., dimensions={0} | all-to-all | bytes 3670016 | tf_op jit(solution)/shard_map/all_to_all | solution.py:300
  54.0 1.5 fusion.18
  55.5 0.0 all-gather.5.cloned.1.call-update
  55.6 0.1 add_multiply_fusion
  55.7 0.1 broadcast_add_fusion
  55.8 0.1 fusion.12
  55.8 0.0 collective-permute-start.1
  55.8 1.5 collective-permute-start.2
  57.3 0.3 all-gather.3.cloned.1.call-done
  57.6 1.0 convert_reduce_fusion
  58.7 1.0 slice_reduce_fusion
  59.7 2.8 %collective-permute-start = (f32[1,128]{1,0:T(1,128)S(1)}, f32[1,128]{1,0:T(1,128)S(1)}, u32[]{:S(2)}, u32[]{:S(2)}) collective-permute-start(f32[1,128]{1,0:T(1,128)S(1)} %compare_select_fusion), channel_id=1, source_target_pairs={{0,1},{1,0},{2,3},{3,2},{4,5},{5,4},{6,7},{7,6},{8,9},{9,8},{10,11... | collective-permute-start | bytes 1544 | tf_op jit(solution)/shard_map/ppermute | solution.py:339
  62.4 0.1 fusion.19
  62.5 0.4 collective-permute-start.3
  62.9 0.8 collective-permute-done
  63.6 0.1 select_reduce_fusion
  63.8 0.1 fusion.15
  63.9 0.1 compare_convert_fusion
  64.0 0.6 pad_add_fusion.info_ref
  64.6 1.7 collective-permute-done.1
  66.3 1.0 collective-permute-done.2
  67.3 1.0 slice.39
  68.3 0.3 collective-permute-start.4
  68.6 1.0 slice.40
  69.6 1.3 collective-permute-start.5
  70.9 1.4 pad_maximum_fusion.refs_0_
  72.4 5.1 %collective-permute-start.7 = (bf16[3,8,256,128]{3,2,1,0:T(8,128)(2,1)S(1)}, bf16[3,8,256,128]{3,2,1,0:T(8,128)(2,1)}, u32[]{:S(2)}, u32[]{:S(2)}) collective-permute-start(bf16[3,8,256,128]{3,2,1,0:T(8,128)(2,1)S(1)} %pad_maximum_fusion.refs_0_), channel_id=1, source_target_pairs={{0,8},{8,0},{16,24},{24,16},{32,40},{40,32},{48,56},{56,48},{64,72... | collective-permute-start | bytes 4718600 | tf_op jit(solution)/shard_map/ppermute | solution.py:312
  77.4 0.6 fusion.13.end_ref
  78.1 0.0 collective-permute-done.3.their_q
  78.1 0.7 copy-done.10
  78.8 50.1 %shard_map.66 = (bf16[8,144,128]{2,1,0:T(8,128)(2,1)}, bf16[8,144,128]{2,1,0:T(8,128)(2,1)}) custom-call(s32[13]{0:T(128)} %pad_add_fusion.info_ref, bf16[8,896,128]{2,1,0:T(8,128)(2,1)} %copy-done.1, bf16[8,128,128]{2,1,0:T(8,128)(2,1)} %copy-done.10, s32[8,1,256]{2,1,0:T(1,128)} %fusion.13.end_ref, bf16[4,2,8,272,128]{4,3,2,1,0:T(8,128)(2,1)} %bitcast.49), custom_call_target="tpu_custom_call" | custom-call | flops 8589934592 | bytes 5242880 | tf_op jit(solution)/shard_map/pallas_call | solution.py:165
  128.9 0.0 collective-permute-done.4
  128.9 0.0 collective-permute-done.5
  128.9 0.1 collective-permute-start.8
  129.0 1.3 collective-permute-start.6
  130.3 1.8 collective-permute-start.11
  132.1 1.2 collective-permute-start.10
  133.3 4.8 %collective-permute-done.6.their_q = bf16[8,128,128]{2,1,0:T(8,128)(2,1)S(1)} collective-permute-done((bf16[8,128,128]{2,1,0:T(8,128)(2,1)S(1)}, bf16[8,128,128]{2,1,0:T(8,128)(2,1)S(1)}, u32[]{:S(2)}, u32[]{:S(2)}) %collective-permute-start.6) | collective-permute-done | bytes 262176 | tf_op jit(solution)/shard_map/ppermute | solution.py:332
  138.1 0.0 collective-permute-done.8.refs_3_
  138.1 0.0 collective-permute-done.7.refs_2_
  138.1 0.7 copy-done.12
  138.8 0.2 copy-done.9
  139.0 50.0 %shard_map.67 = (bf16[8,144,128]{2,1,0:T(8,128)(2,1)}, bf16[8,144,128]{2,1,0:T(8,128)(2,1)}) custom-call(s32[13]{0:T(128)} %pad_add_fusion.info_ref, bf16[8,896,128]{2,1,0:T(8,128)(2,1)} %copy-done.1, bf16[8,128,128]{2,1,0:T(8,128)(2,1)} %copy-done.12, s32[8,1,256]{2,1,0:T(1,128)} %fusion.13.end_ref, bf16[3,8,256,128]{3,2,1,0:T(8,128)(2,1)} %copy-done.4, ...), custom_call_target="tpu_custom_call" | custom-call | flops 8589934592 | bytes 5242880 | tf_op jit(solution)/shard_map/pallas_call | solution.py:165
  189.0 0.1 collective-permute-start.9
  189.1 0.0 collective-permute-done.11.their_q
  189.1 0.7 copy-done.11
  189.8 50.1 %shard_map.68 = (bf16[8,144,128]{2,1,0:T(8,128)(2,1)}, bf16[8,144,128]{2,1,0:T(8,128)(2,1)}) custom-call(s32[13]{0:T(128)} %pad_add_fusion.info_ref, bf16[8,896,128]{2,1,0:T(8,128)(2,1)} %copy-done.1, bf16[8,128,128]{2,1,0:T(8,128)(2,1)} %copy-done.11, s32[8,1,256]{2,1,0:T(1,128)} %fusion.13.end_ref, bf16[4,2,8,256,128]{4,3,2,1,0:T(8,128)(2,1)} %bitcast.50), custom_call_target="tpu_custom_call" | custom-call | flops 8589934592 | bytes 5242880 | tf_op jit(solution)/shard_map/pallas_call | solution.py:165
  239.9 1.9 collective-permute-start.12
  241.8 0.0 collective-permute-done.9.refs_1_
  241.8 5.5 %collective-permute-done.12.refs_5_ = bf16[8,144,128]{2,1,0:T(8,128)(2,1)S(1)} collective-permute-done((bf16[8,144,128]{2,1,0:T(8,128)(2,1)}, bf16[8,144,128]{2,1,0:T(8,128)(2,1)S(1)}, u32[]{:S(2)}, u32[]{:S(2)}) %collective-permute-start.12) | collective-permute-done | bytes 294944 | tf_op jit(solution)/shard_map/ppermute | solution.py:363
  247.3 0.7 copy-done.7
  248.0 2.6 shard_map.69
  250.7 3.7 %all-to-all-start.2 = ((bf16[8,384,128]{2,1,0:T(8,128)(2,1)}), bf16[8,384,128]{2,1,0:T(8,128)(2,1)S(1)}, u32[]{:S(2)}, u32[]{:S(2)}) async-start(bf16[8,384,128]{2,1,0:T(8,128)(2,1)} %shard_map.69), calls=%async_computation.2 | async-start | bytes 1572864 | tf_op jit(solution)/shard_map/all_to_all | solution.py:300
  254.3 0.1 fusion.2
  254.5 0.3 fusion.4
  254.8 2.0 fusion.gate_ref
  256.8 6.8 %all-to-all-done.2.mixed_ref = bf16[8,384,128]{2,1,0:T(8,128)(2,1)S(1)} async-done(((bf16[8,384,128]{2,1,0:T(8,128)(2,1)}), bf16[8,384,128]{2,1,0:T(8,128)(2,1)S(1)}, u32[]{:S(2)}, u32[]{:S(2)}) %all-to-all-start.2) | async-done | bytes 786464 | tf_op jit(solution)/shard_map/all_to_all | solution.py:300
  263.7 0.9 copy-done.2
  264.5 2.7 %shard_map.70 = bf16[128,3072]{1,0:T(8,128)(2,1)} custom-call(f32[128,3072]{1,0:T(8,128)} %fusion.gate_ref, bf16[8,384,128]{2,1,0:T(8,128)(2,1)} %copy-done.2), custom_call_target="tpu_custom_call" | custom-call | tf_op jit(solution)/shard_map/pallas_call | solution.py:376
  (36 shorter events, 0.2 us)
Async XLA Ops:
  6.5 247.9 %copy-start = (bf16[256,3072]{1,0:T(8,128)(2,1)S(1)}, bf16[256,3072]{1,0:T(8,128)(2,1)}, u32[]{:S(2)}) copy-start(bf16[256,3072]{1,0:T(8,128)(2,1)} %param.11) | copy-start | bytes 4718596
  6.5 51.1 %all-gather.3.cloned.1.call-start = ((), (), s32[]{:S(2)}) async-start(), calls=%async_computation.3 | async-start | bytes 5013504 | tf_op jit(solution)/shard_map/all_gather | solution.py:305
  25.1 164.0 %all-gather.5.cloned.1.call-start = ((), (), s32[]{:S(2)}) async-start(), calls=%async_computation.4 | async-start | bytes 4718592 | tf_op jit(solution)/shard_map/all_gather | solution.py:305
  54.0 8.4 %copy-start.1 = (bf16[8,896,128]{2,1,0:T(8,128)(2,1)}, bf16[8,896,128]{2,1,0:T(8,128)(2,1)S(1)}, u32[]{:S(2)}) copy-start(bf16[8,896,128]{2,1,0:T(8,128)(2,1)S(1)} %all_to_all.16.own_q) | copy-start | bytes 5505028
  55.8 10.5 %collective-permute-start.1 = (bf16[8,256,128]{2,1,0:T(8,128)(2,1)}, bf16[8,256,128]{2,1,0:T(8,128)(2,1)}, u32[]{:S(2)}, u32[]{:S(2)}) collective-permute-start(bf16[8,256,128]{2,1,0:T(8,128)(2,1)} %get-tuple-element.45), channel_id=1, source_target_pairs={{0,2},{1,3},{2,4},{3,5},{4,6},{5,7},{6,0},{7,1},{8,10},{9,11},{10,... | collective-permute-start | bytes 1572872 | tf_op jit(solution)/shard_map/ppermute | solution.py:328
  55.8 11.5 %collective-permute-start.2 = (bf16[8,256,128]{2,1,0:T(8,128)(2,1)}, bf16[8,256,128]{2,1,0:T(8,128)(2,1)}, u32[]{:S(2)}, u32[]{:S(2)}) collective-permute-start(bf16[8,256,128]{2,1,0:T(8,128)(2,1)} %get-tuple-element.45), channel_id=1, source_target_pairs={{0,6},{1,7},{2,0},{3,1},{4,2},{5,3},{6,4},{7,5},{8,14},{9,15},{10,... | collective-permute-start | bytes 1572872 | tf_op jit(solution)/shard_map/ppermute | solution.py:328
  57.6 13.3 %copy-start.3 = (bf16[1,8,256,128]{3,2,1,0:T(8,128)(2,1)S(1)}, bf16[1,8,256,128]{3,2,1,0:T(8,128)(2,1)}, u32[]{:S(2)}) copy-start(bf16[1,8,256,128]{3,2,1,0:T(8,128)(2,1)} %get-tuple-element.44) | copy-start | bytes 1572868
  59.7 4.0 %collective-permute-start = (f32[1,128]{1,0:T(1,128)S(1)}, f32[1,128]{1,0:T(1,128)S(1)}, u32[]{:S(2)}, u32[]{:S(2)}) collective-permute-start(f32[1,128]{1,0:T(1,128)S(1)} %compare_select_fusion), channel_id=1, source_target_pairs={{0,1},{1,0},{2,3},{3,2},{4,5},{5,4},{6,7},{7,6},{8,9},{9,8},{10,11... | collective-permute-start | bytes 1544 | tf_op jit(solution)/shard_map/ppermute | solution.py:339
  62.5 15.6 %collective-permute-start.3 = (bf16[8,128,128]{2,1,0:T(8,128)(2,1)S(1)}, bf16[8,128,128]{2,1,0:T(8,128)(2,1)S(1)}, u32[]{:S(2)}, u32[]{:S(2)}) collective-permute-start(bf16[8,128,128]{2,1,0:T(8,128)(2,1)S(1)} %get-tuple-element.48), channel_id=1, source_target_pairs={{0,1},{1,0},{2,3},{3,2},{4,5},{5,4},{6,7},{7,6},{8,9},{9,8},{10,11... | collective-permute-start | bytes 786440 | tf_op jit(solution)/shard_map/ppermute | solution.py:332
  68.3 60.5 %collective-permute-start.4 = (bf16[4,256,128]{2,1,0:T(8,128)(2,1)S(1)}, bf16[4,256,128]{2,1,0:T(8,128)(2,1)S(1)}, u32[]{:S(2)}, u32[]{:S(2)}) collective-permute-start(bf16[4,256,128]{2,1,0:T(8,128)(2,1)S(1)} %slice.39), channel_id=1, source_target_pairs={{0,2},{1,3},{2,4},{3,5},{4,6},{5,7},{6,0},{7,1},{8,10},{9,11},{10,... | collective-permute-start | bytes 786440 | tf_op jit(solution)/shard_map/ppermute | solution.py:367
  69.6 59.3 %collective-permute-start.5 = (bf16[4,256,128]{2,1,0:T(8,128)(2,1)S(1)}, bf16[4,256,128]{2,1,0:T(8,128)(2,1)S(1)}, u32[]{:S(2)}, u32[]{:S(2)}) collective-permute-start(bf16[4,256,128]{2,1,0:T(8,128)(2,1)S(1)} %slice.40), channel_id=1, source_target_pairs={{0,6},{1,7},{2,0},{3,1},{4,2},{5,3},{6,4},{7,5},{8,14},{9,15},{10,... | collective-permute-start | bytes 786440 | tf_op jit(solution)/shard_map/ppermute | solution.py:367
  72.4 56.5 %copy-start.4 = (bf16[3,8,256,128]{3,2,1,0:T(8,128)(2,1)}, bf16[3,8,256,128]{3,2,1,0:T(8,128)(2,1)S(1)}, u32[]{:S(2)}) copy-start(bf16[3,8,256,128]{3,2,1,0:T(8,128)(2,1)S(1)} %pad_maximum_fusion.refs_0_) | copy-start | bytes 4718596
  72.4 65.7 %collective-permute-start.7 = (bf16[3,8,256,128]{3,2,1,0:T(8,128)(2,1)S(1)}, bf16[3,8,256,128]{3,2,1,0:T(8,128)(2,1)}, u32[]{:S(2)}, u32[]{:S(2)}) collective-permute-start(bf16[3,8,256,128]{3,2,1,0:T(8,128)(2,1)S(1)} %pad_maximum_fusion.refs_0_), channel_id=1, source_target_pairs={{0,8},{8,0},{16,24},{24,16},{32,40},{40,32},{48,56},{56,48},{64,72... | collective-permute-start | bytes 4718600 | tf_op jit(solution)/shard_map/ppermute | solution.py:312
  78.1 0.7 copy-start.10
  128.9 9.2 %copy-start.5 = (bf16[1,8,256,128]{3,2,1,0:T(8,128)(2,1)}, bf16[1,8,256,128]{3,2,1,0:T(8,128)(2,1)S(1)}, u32[]{:S(2)}) copy-start(bf16[1,8,256,128]{3,2,1,0:T(8,128)(2,1)S(1)} %maximum_bitcast_fusion.refs_1_) | copy-start | bytes 1572868
  128.9 9.2 %collective-permute-start.8 = (bf16[1,8,256,128]{3,2,1,0:T(8,128)(2,1)S(1)}, bf16[1,8,256,128]{3,2,1,0:T(8,128)(2,1)S(1)}, u32[]{:S(2)}, u32[]{:S(2)}) collective-permute-start(bf16[1,8,256,128]{3,2,1,0:T(8,128)(2,1)S(1)} %maximum_bitcast_fusion.refs_1_), channel_id=1, source_target_pairs={{0,8},{8,0},{16,24},{24,16},{32,40},{40,32},{48,56},{56,48},{64,72... | collective-permute-start | bytes 1572872 | tf_op jit(solution)/shard_map/ppermute | solution.py:312
  129.0 9.1 %collective-permute-start.6 = (bf16[8,128,128]{2,1,0:T(8,128)(2,1)S(1)}, bf16[8,128,128]{2,1,0:T(8,128)(2,1)S(1)}, u32[]{:S(2)}, u32[]{:S(2)}) collective-permute-start(bf16[8,128,128]{2,1,0:T(8,128)(2,1)S(1)} %get-tuple-element.47), channel_id=1, source_target_pairs={{0,1},{1,0},{2,3},{3,2},{4,5},{5,4},{6,7},{7,6},{8,9},{9,8},{10,11... | collective-permute-start | bytes 786440 | tf_op jit(solution)/shard_map/ppermute | solution.py:332
  130.3 58.8 %collective-permute-start.11 = (bf16[8,128,128]{2,1,0:T(8,128)(2,1)S(1)}, bf16[8,128,128]{2,1,0:T(8,128)(2,1)S(1)}, u32[]{:S(2)}, u32[]{:S(2)}) collective-permute-start(bf16[8,128,128]{2,1,0:T(8,128)(2,1)S(1)} %get-tuple-element.46), channel_id=1, source_target_pairs={{0,1},{1,0},{2,3},{3,2},{4,5},{5,4},{6,7},{7,6},{8,9},{9,8},{10,11... | collective-permute-start | bytes 786440 | tf_op jit(solution)/shard_map/ppermute | solution.py:332
  132.1 109.7 %collective-permute-start.10 = (bf16[8,144,128]{2,1,0:T(8,128)(2,1)}, bf16[8,144,128]{2,1,0:T(8,128)(2,1)}, u32[]{:S(2)}, u32[]{:S(2)}) collective-permute-start(bf16[8,144,128]{2,1,0:T(8,128)(2,1)} %get-tuple-element.38), channel_id=1, source_target_pairs={{0,1},{1,0},{2,3},{3,2},{4,5},{5,4},{6,7},{7,6},{8,9},{9,8},{10,11... | collective-permute-start | bytes 884744 | tf_op jit(solution)/shard_map/ppermute | solution.py:363
  138.1 0.7 copy-start.12
  138.1 0.9 copy-start.9
  189.0 52.8 %collective-permute-start.9 = (bf16[8,144,128]{2,1,0:T(8,128)(2,1)}, bf16[8,144,128]{2,1,0:T(8,128)(2,1)S(1)}, u32[]{:S(2)}, u32[]{:S(2)}) collective-permute-start(bf16[8,144,128]{2,1,0:T(8,128)(2,1)} %get-tuple-element.36), channel_id=1, source_target_pairs={{0,1},{1,0},{2,3},{3,2},{4,5},{5,4},{6,7},{7,6},{8,9},{9,8},{10,11... | collective-permute-start | bytes 884744 | tf_op jit(solution)/shard_map/ppermute | solution.py:363
  189.1 0.7 copy-start.11
  189.8 52.0 %copy-start.13 = (s32[24]{0:T(128)S(1)}, s32[24]{0:T(128)}, u32[]{:S(2)}) copy-start(s32[24]{0:T(128)} %param.10) | copy-start | bytes 292
  239.9 7.4 %collective-permute-start.12 = (bf16[8,144,128]{2,1,0:T(8,128)(2,1)}, bf16[8,144,128]{2,1,0:T(8,128)(2,1)S(1)}, u32[]{:S(2)}, u32[]{:S(2)}) collective-permute-start(bf16[8,144,128]{2,1,0:T(8,128)(2,1)} %get-tuple-element.42), channel_id=1, source_target_pairs={{0,1},{1,0},{2,3},{3,2},{4,5},{5,4},{6,7},{7,6},{8,9},{9,8},{10,11... | collective-permute-start | bytes 884744 | tf_op jit(solution)/shard_map/ppermute | solution.py:363
  241.8 5.5 %copy-start.6 = (bf16[8,144,128]{2,1,0:T(8,128)(2,1)}, bf16[8,144,128]{2,1,0:T(8,128)(2,1)S(1)}, u32[]{:S(2)}) copy-start(bf16[8,144,128]{2,1,0:T(8,128)(2,1)S(1)} %collective-permute-done.9.refs_1_) | copy-start | bytes 884740
  247.3 0.7 copy-start.7
  250.7 4.1 %copy-start.8 = (s32[128]{0:T(128)S(1)}, s32[128]{0:T(128)}, u32[]{:S(2)}) copy-start(s32[128]{0:T(128)} %param.9) | copy-start | bytes 1540
  250.7 13.0 %all-to-all-start.2 = ((bf16[8,384,128]{2,1,0:T(8,128)(2,1)}), bf16[8,384,128]{2,1,0:T(8,128)(2,1)S(1)}, u32[]{:S(2)}, u32[]{:S(2)}) async-start(bf16[8,384,128]{2,1,0:T(8,128)(2,1)} %shard_map.69), calls=%async_computation.2 | async-start | bytes 1572864 | tf_op jit(solution)/shard_map/all_to_all | solution.py:300
  263.6 0.9 copy-start.2
Sparse Core Ops, SparseCore 0:
  25.2 32.3 all-gather.2
  59.3 37.3 all-gather.4

commit v3 on v2

--- a/solution.py
+++ b/solution.py
@@ -16,6 +16,7 @@
 SEGMENT = 2 * HEAD_DIM
 KEYS = 8192
 WIDTH = 512
+SUB = 256
 ITEMS = 4
 K_NORM, Q_NORM = 32, 40
 NOTE = 16
@@ -73,14 +74,23 @@
         row = lax.broadcasted_iota(jnp.int32, (WIDTH, SEGMENT), 0)
         return row < end_ref[r] - i * WIDTH
 
-    def weigh(slot, r, i):
-        r = jnp.minimum(r, blocks - 1)
-        weights = jnp.exp2(dot(keys_at(i), qt_ref[r]) * SCALE_LOG2)
-        weights = jnp.where(visible_at(r, i), weights, 0.0)
-        weight_ref[slot] = weights.astype(jnp.bfloat16)
-
-    def absorb(slot, r, i):
-        acc_ref[r] += dot(values_at(i), weight_ref[slot])
+    def score(item, half):
+        r, i = item
+        keys = kv_ref[2 * half : 2 * half + 2, i % 2, i // 2, :HEAD_DIM].reshape(SUB, HEAD_DIM)
+        return dot(keys, qt_ref[jnp.minimum(r, blocks - 1)])
+
+    def weigh(slot, item, half, scores):
+        r, i = item
+        row = lax.broadcasted_iota(jnp.int32, (SUB, SEGMENT), 0)
+        visible = row < end_ref[jnp.minimum(r, blocks - 1)] - (i * WIDTH + half * SUB)
+        weights = jnp.where(visible, jnp.exp2(scores * SCALE_LOG2), 0.0)
+        weight_ref[slot, half * SUB : (half + 1) * SUB] = weights.astype(jnp.bfloat16)
+
+    def absorb(slot, item, half):
+        r, i = item
+        block = kv_ref[2 * half : 2 * half + 2, i % 2, i // 2, HEAD_DIM:]
+        values = jnp.concatenate([jnp.concatenate([block[0], block[1]], axis=1), ones[:, :SUB]], axis=0)
+        acc_ref[r] += dot(values, weight_ref[slot, half * SUB : (half + 1) * SUB])
 
     def careful(r, i):
         scores = dot(keys_at(i), qt_ref[r]) * SCALE_LOG2
@@ -95,6 +105,7 @@
     def count(r):
         return info_ref[2 + r]
 
+    parts = [(slot, half) for slot in range(ITEMS) for half in range(2)]
     plain = info_ref[2 + blocks + head] == 1
 
     @pl.when(plain)
@@ -113,18 +124,22 @@
 
         def step(_, items):
             later = run(following(items[-1]))
-            for slot in range(ITEMS):
-                absorb(slot, *items[slot])
-                weigh(slot, *later[slot])
+            scores = score(later[0], 0)
+            for slot, half in parts:
+                now = scores
+                if (slot, half) != parts[-1]:
+                    scores = score(later[slot + half], 1 - half)
+                absorb(slot, items[slot], half)
+                weigh(slot, later[slot], half, now)
             return later
 
         items = run((jnp.int32(0), jnp.int32(0)))
-        for slot in range(ITEMS):
-            weigh(slot, *items[slot])
+        for slot, half in parts:
+            weigh(slot, items[slot], half, score(items[slot], half))
         total = sum(count(r) for r in range(blocks))
         items = lax.fori_loop(0, (total + ITEMS - 1) // ITEMS - 1, step, items)
-        for slot in range(ITEMS):
-            absorb(slot, *items[slot])
+        for slot, half in parts:
+            absorb(slot, items[slot], half)
 
     @pl.when(jnp.logical_not(plain))
     def _():
@@ -326,17 +341,19 @@
     block = rest[:, :pair]
     half = ZONES // 2
     below, above = lax.ppermute(block, "head", up), lax.ppermute(block, "head", down)
-    their_q = [None] * heads
-    for head in (1, 0, 2):
-        start = 2 * pair + head * HEAD_DIM
-        their_q[head] = lax.ppermute(rest[:, start : start + HEAD_DIM], "head", partner)
+    own_q = [rest[:, start : start + HEAD_DIM] for start in range(2 * pair, rest.shape[1], HEAD_DIM)]
+    their_q = [None, lax.ppermute(own_q[1], "head", partner), None]
 
     def combined(notes):
         is_count = jnp.arange(HEAD_DIM) < K_NORM
         return jnp.where(is_count, jnp.sum(notes, axis=0), jnp.max(notes, axis=0))
 
     note = combined(gathered[:, :, :, pair].reshape(-1, HEAD_DIM).astype(jnp.float32))[None]
-    note = combined(jnp.concatenate([note, lax.ppermute(note, "head", partner)]))
+    note, their_q[1] = after(note, their_q[1])
+    note_other = lax.ppermute(note, "head", partner)
+    own_q[0], note_other = after(own_q[0], note_other)
+    their_q[0] = lax.ppermute(own_q[0], "head", partner)
+    note = combined(jnp.concatenate([note, note_other]))
     squares = note[K_NORM : K_NORM + heads] * note[Q_NORM : Q_NORM + heads]
     plain = (squares * (1.05 * SCALE**2) < PLAIN_LIMIT**2).astype(jnp.int32)
     ends = note[:spans].astype(jnp.int32)
@@ -363,12 +380,13 @@
         parts[2 * head + 1] = lax.ppermute(theirs, "head", partner)
         return info
 
-    info, below, above = after(info, below, above)
     pieces = [lax.ppermute(below[:half], "head", up), lax.ppermute(above[half:], "head", down)]
     near, far = swapped(jnp.stack([block, above, below]))
+    info, their_q[0], *pieces = after(info, their_q[0], *pieces)
+    near_last, far_last = swapped(jnp.concatenate(pieces)[None])
     info = attended(info, 1, (gathered,))
-    info, *pieces = after(info, *pieces)
-    near_last, far_last = swapped(jnp.concatenate(pieces)[None])
+    own_q[2], info = after(own_q[2], info)
+    their_q[2] = lax.ppermute(own_q[2], "head", partner)
     info = attended(info, 0, (near, near_last, far, far_last))
     info = attended(info, 2, (gather(rest[:, pair : 2 * pair]),))
     mixed = exchange(merge(parts))

time: 276 us -> 283 us (1.025); the launches traced: 274 us -> 285 us
  waiting for transfers between devices: 20.9 us -> 26.1 us
  starting transfers between devices: 21.3 us -> 25.1 us
    ppermute x1, waiting for transfers between devices: 1.7 us -> 5.57 us  [per_device(): lax.ppermute(block, 'head', up)]
  transfers between devices with their start and end apart: 16 -> 16, of which waited for: 7 -> 4; matrix products, arithmetic and copies ran while one was open for 4% -> 4% of each run, Pallas kernels for 56% -> 54%
where the time goes in v3:
time: 283 us; the launch traced here: 285 us
  Pallas kernels  164 us (58%)
  blocking collectives  41 us (14%)
  waiting for transfers between devices  26.1 us (9%)
  starting transfers between devices  25.1 us (9%)
  between operations  13.6 us (5%)
  local copies, waits for them, and re-layouts  7.56 us (3%)
  other arithmetic  5.7 us (2%)
    pallas_call x3, Pallas kernels, attend(): pl.pallas_call(functools.partial(attend_kernel, head, len(sources) > 1),...  152 us
    all_to_all x2, blocking collectives, exchange(): lax.all_to_all(parts, BOTH, split_axis=0, concat_axis=0, axis_index_group...  41 us
    pallas_call x3, Pallas kernels, pack(): pl.pallas_call(kernel, out_shape=jax.ShapeDtypeStruct((ZONES, rows, HEAD_...  9.12 us
    ppermute x3, waiting for transfers between devices, attended(): parts[2 * head + 1] = lax.ppermute(theirs, 'head', partner)  7.09 us
    ppermute x1, waiting for transfers between devices, per_device(): their_q[0] = lax.ppermute(own_q[0], 'head', partner)  6.96 us
    ppermute x2, starting transfers between devices, swapped(): return (block, lax.ppermute(block, 'span', core_swap))  6.6 us
    all_to_all x1, waiting for transfers between devices, exchange(): lax.all_to_all(parts, BOTH, split_axis=0, concat_axis=0, axis_index_group...  6.44 us
  transfers between devices with their start and end apart: 16, of which 4 were waited for; matrix products, arithmetic and copies ran while one was open for 4% of the time, Pallas kernels for 54%

profile of v3, /device:TPU:25, one launch (start us, length us, event | category | flops | bytes accessed | tf_op | source)
XLA Modules:
  0.0 285.1 jit_solution(10926577566909714223)
XLA Ops:
  6.5 3.1 %shard_map.64 = bf16[8,272,128]{2,1,0:T(8,128)(2,1)} custom-call(bf16[128,3072]{1,0:T(8,128)(2,1)} %queries_ref.2, bf16[128,3072]{1,0:T(8,128)(2,1)} %keys_ref.3, bf16[128,3072]{1,0:T(8,128)(2,1)} %values_ref.3, s32[1,128]{1,0:T(1,128)} %bitcast.44), custom_call_target="tpu_custom_call" | custom-call | tf_op jit(solution)/shard_map/pallas_call | solution.py:241
  9.7 15.4 %all_to_all.15 = bf16[8,272,128]{2,1,0:T(8,128)(2,1)} all-to-all(bf16[8,272,128]{2,1,0:T(8,128)(2,1)} %shard_map.64), channel_id=1, replica_groups={{0,16,32,48,64,80,96,112},{1,17,33,49,65,81,97,113},{2,18,34,50,66,82,9..., dimensions={0} | all-to-all | bytes 1114112 | tf_op jit(solution)/shard_map/all_to_all | solution.py:315
  25.1 0.0 all-gather.3.cloned.1.call-update
  25.1 0.0 all-gather.5.cloned.1.call-start
  25.2 3.3 %shard_map.65 = bf16[8,896,128]{2,1,0:T(8,128)(2,1)} custom-call(bf16[128,3072]{1,0:T(8,128)(2,1)} %queries_ref.2, bf16[128,3072]{1,0:T(8,128)(2,1)} %keys_ref.3, bf16[128,3072]{1,0:T(8,128)(2,1)} %values_ref.3), custom_call_target="tpu_custom_call" | custom-call | tf_op jit(solution)/shard_map/pallas_call | solution.py:241
  28.5 25.6 %all_to_all.16.own_q = bf16[8,896,128]{2,1,0:T(8,128)(2,1)S(1)} all-to-all(bf16[8,896,128]{2,1,0:T(8,128)(2,1)} %shard_map.65), channel_id=1, replica_groups={{0,16,32,48,64,80,96,112},{1,17,33,49,65,81,97,113},{2,18,34,50,66,82,9..., dimensions={0} | all-to-all | bytes 3670016 | tf_op jit(solution)/shard_map/all_to_all | solution.py:315
  54.1 1.5 fusion.18
  55.6 0.0 all-gather.5.cloned.1.call-update
  55.6 0.1 add_multiply_fusion
  55.7 0.1 broadcast_add_fusion
  55.8 0.0 collective-permute-start.3
  55.8 1.5 collective-permute-start.5
  57.2 0.1 fusion.12
  57.3 0.9 fusion.19
  58.2 2.4 collective-permute-start
  60.7 5.6 %collective-permute-done.3 = bf16[8,256,128]{2,1,0:T(8,128)(2,1)} collective-permute-done((bf16[8,256,128]{2,1,0:T(8,128)(2,1)}, bf16[8,256,128]{2,1,0:T(8,128)(2,1)}, u32[]{:S(2)}, u32[]{:S(2)}) %collective-permute-start.3) | collective-permute-done | bytes 524320 | tf_op jit(solution)/shard_map/ppermute | solution.py:343
  66.3 1.0 slice.49
  67.2 1.3 collective-permute-start.4
  68.5 0.0 collective-permute-done.5
  68.5 1.0 slice.50
  69.5 0.3 collective-permute-start.6
  69.8 1.0 convert_reduce_fusion
  70.8 1.0 slice_reduce_fusion
  71.8 0.0 collective-permute-done.their_q
  71.8 2.5 collective-permute-start.1
  74.4 1.6 pad_maximum_fusion.refs_0_
  76.0 0.0 copy-done.12
  76.0 0.0 copy-start.3
  76.0 5.1 %collective-permute-start.7 = (bf16[3,8,256,128]{3,2,1,0:T(8,128)(2,1)S(1)}, bf16[3,8,256,128]{3,2,1,0:T(8,128)(2,1)}, u32[]{:S(2)}, u32[]{:S(2)}) collective-permute-start(bf16[3,8,256,128]{3,2,1,0:T(8,128)(2,1)S(1)} %pad_maximum_fusion.refs_0_), channel_id=1, source_target_pairs={{0,8},{8,0},{16,24},{24,16},{32,40},{40,32},{48,56},{56,48},{64,72... | collective-permute-start | bytes 4718600 | tf_op jit(solution)/shard_map/ppermute | solution.py:327
  81.1 0.0 collective-permute-done.1
  81.1 0.1 select_reduce_fusion
  81.2 0.1 compare_convert_fusion
  81.3 0.1 fusion.15
  81.5 0.6 collective-permute-start.2
  82.1 0.7 pad_add_fusion.info_ref
  82.7 0.6 fusion.13.end_ref
  83.3 0.0 collective-permute-done.4
  83.3 0.0 collective-permute-done.6
  83.3 7.0 %collective-permute-done.2.their_q = bf16[8,128,128]{2,1,0:T(8,128)(2,1)S(1)} collective-permute-done((bf16[8,128,128]{2,1,0:T(8,128)(2,1)S(1)}, bf16[8,128,128]{2,1,0:T(8,128)(2,1)S(1)}, u32[]{:S(2)}, u32[]{:S(2)}) %collective-permute-start.2) | collective-permute-done | bytes 262176 | tf_op jit(solution)/shard_map/ppermute | solution.py:355
  90.4 1.5 collective-permute-start.8
  91.9 50.6 %shard_map.66 = (bf16[8,144,128]{2,1,0:T(8,128)(2,1)}, bf16[8,144,128]{2,1,0:T(8,128)(2,1)}) custom-call(s32[13]{0:T(128)} %pad_add_fusion.info_ref, bf16[8,896,128]{2,1,0:T(8,128)(2,1)} %copy-done.1, bf16[8,128,128]{2,1,0:T(8,128)(2,1)} %copy-done.12, s32[8,1,256]{2,1,0:T(1,128)} %fusion.13.end_ref, bf16[4,2,8,272,128]{4,3,2,1,0:T(8,128)(2,1)} %bitcast.47), custom_call_target="tpu_custom_call" | custom-call | flops 8589934592 | bytes 5242880 | tf_op jit(solution)/shard_map/pallas_call | solution.py:180
  142.5 0.8 collective-permute-start.11
  143.4 2.2 collective-permute-start.10
  145.6 0.0 collective-permute-done.7.refs_2_
  145.6 0.0 collective-permute-done.8.refs_3_
  145.6 0.8 copy-done.11
  146.4 50.5 %shard_map.67 = (bf16[8,144,128]{2,1,0:T(8,128)(2,1)}, bf16[8,144,128]{2,1,0:T(8,128)(2,1)}) custom-call(s32[13]{0:T(128)} %pad_add_fusion.info_ref, bf16[8,896,128]{2,1,0:T(8,128)(2,1)} %copy-done.1, bf16[8,128,128]{2,1,0:T(8,128)(2,1)} %copy-done.13, s32[8,1,256]{2,1,0:T(1,128)} %fusion.13.end_ref, bf16[3,8,256,128]{3,2,1,0:T(8,128)(2,1)} %copy-done.3, ...), custom_call_target="tpu_custom_call" | custom-call | flops 8589934592 | bytes 5242880 | tf_op jit(solution)/shard_map/pallas_call | solution.py:180
  196.9 0.8 collective-permute-start.9
  197.8 0.0 collective-permute-done.11.their_q
  197.8 0.7 copy-done.14
  198.5 50.7 %shard_map.68 = (bf16[8,144,128]{2,1,0:T(8,128)(2,1)}, bf16[8,144,128]{2,1,0:T(8,128)(2,1)}) custom-call(s32[13]{0:T(128)} %pad_add_fusion.info_ref, bf16[8,896,128]{2,1,0:T(8,128)(2,1)} %copy-done.1, bf16[8,128,128]{2,1,0:T(8,128)(2,1)} %copy-done.14, s32[8,1,256]{2,1,0:T(1,128)} %fusion.13.end_ref, bf16[4,2,8,256,128]{4,3,2,1,0:T(8,128)(2,1)} %bitcast.48), custom_call_target="tpu_custom_call" | custom-call | flops 8589934592 | bytes 5242880 | tf_op jit(solution)/shard_map/pallas_call | solution.py:180
  249.1 2.3 collective-permute-start.12
  251.5 0.0 collective-permute-done.10.refs_3_
  251.5 0.0 collective-permute-done.9.refs_1_
  251.5 7.1 %collective-permute-done.12.refs_5_ = bf16[8,144,128]{2,1,0:T(8,128)(2,1)S(1)} collective-permute-done((bf16[8,144,128]{2,1,0:T(8,128)(2,1)}, bf16[8,144,128]{2,1,0:T(8,128)(2,1)S(1)}, u32[]{:S(2)}, u32[]{:S(2)}) %collective-permute-start.12) | collective-permute-done | bytes 294944 | tf_op jit(solution)/shard_map/ppermute | solution.py:380
  258.6 0.7 copy-done.7
  259.3 2.6 shard_map.69
  262.0 3.7 %all-to-all-start.2 = ((bf16[8,384,128]{2,1,0:T(8,128)(2,1)}), bf16[8,384,128]{2,1,0:T(8,128)(2,1)S(1)}, u32[]{:S(2)}, u32[]{:S(2)}) async-start(bf16[8,384,128]{2,1,0:T(8,128)(2,1)} %shard_map.69), calls=%async_computation.2 | async-start | bytes 1572864 | tf_op jit(solution)/shard_map/all_to_all | solution.py:315
  265.7 0.1 fusion.2
  265.8 0.3 fusion.4
  266.1 2.0 fusion.gate_ref
  268.1 6.4 %all-to-all-done.2.mixed_ref = bf16[8,384,128]{2,1,0:T(8,128)(2,1)S(1)} async-done(((bf16[8,384,128]{2,1,0:T(8,128)(2,1)}), bf16[8,384,128]{2,1,0:T(8,128)(2,1)S(1)}, u32[]{:S(2)}, u32[]{:S(2)}) %all-to-all-start.2) | async-done | bytes 786464 | tf_op jit(solution)/shard_map/all_to_all | solution.py:315
  274.6 0.9 copy-done.2
  275.5 2.7 shard_map.70
  (40 shorter events, 0.2 us)
Async XLA Ops:
  6.5 259.3 %copy-start = (bf16[256,3072]{1,0:T(8,128)(2,1)S(1)}, bf16[256,3072]{1,0:T(8,128)(2,1)}, u32[]{:S(2)}) copy-start(bf16[256,3072]{1,0:T(8,128)(2,1)} %param.11) | copy-start | bytes 4718596
  6.5 63.3 %all-gather.3.cloned.1.call-start = ((), (), s32[]{:S(2)}) async-start(), calls=%async_computation.3 | async-start | bytes 5013504 | tf_op jit(solution)/shard_map/all_gather | solution.py:320
  25.1 172.7 %all-gather.5.cloned.1.call-start = ((), (), s32[]{:S(2)}) async-start(), calls=%async_computation.4 | async-start | bytes 4718592 | tf_op jit(solution)/shard_map/all_gather | solution.py:320
  54.1 3.3 %copy-start.1 = (bf16[8,896,128]{2,1,0:T(8,128)(2,1)}, bf16[8,896,128]{2,1,0:T(8,128)(2,1)S(1)}, u32[]{:S(2)}) copy-start(bf16[8,896,128]{2,1,0:T(8,128)(2,1)S(1)} %all_to_all.16.own_q) | copy-start | bytes 5505028
  55.8 10.5 %collective-permute-start.3 = (bf16[8,256,128]{2,1,0:T(8,128)(2,1)}, bf16[8,256,128]{2,1,0:T(8,128)(2,1)}, u32[]{:S(2)}, u32[]{:S(2)}) collective-permute-start(bf16[8,256,128]{2,1,0:T(8,128)(2,1)} %get-tuple-element.53), channel_id=1, source_target_pairs={{0,2},{1,3},{2,4},{3,5},{4,6},{5,7},{6,0},{7,1},{8,10},{9,11},{10,... | collective-permute-start | bytes 1572872 | tf_op jit(solution)/shard_map/ppermute | solution.py:343
  55.8 12.8 %collective-permute-start.5 = (bf16[8,256,128]{2,1,0:T(8,128)(2,1)}, bf16[8,256,128]{2,1,0:T(8,128)(2,1)}, u32[]{:S(2)}, u32[]{:S(2)}) collective-permute-start(bf16[8,256,128]{2,1,0:T(8,128)(2,1)} %get-tuple-element.53), channel_id=1, source_target_pairs={{0,6},{1,7},{2,0},{3,1},{4,2},{5,3},{6,4},{7,5},{8,14},{9,15},{10,... | collective-permute-start | bytes 1572872 | tf_op jit(solution)/shard_map/ppermute | solution.py:343
  58.2 13.6 %collective-permute-start = (bf16[8,128,128]{2,1,0:T(8,128)(2,1)}, bf16[8,128,128]{2,1,0:T(8,128)(2,1)S(1)}, u32[]{:S(2)}, u32[]{:S(2)}) collective-permute-start(bf16[8,128,128]{2,1,0:T(8,128)(2,1)} %get-tuple-element.55), channel_id=1, source_target_pairs={{0,1},{1,0},{2,3},{3,2},{4,5},{5,4},{6,7},{7,6},{8,9},{9,8},{10,11... | collective-permute-start | bytes 786440 | tf_op jit(solution)/shard_map/ppermute | solution.py:345
  67.2 16.1 %collective-permute-start.4 = (bf16[4,256,128]{2,1,0:T(8,128)(2,1)S(1)}, bf16[4,256,128]{2,1,0:T(8,128)(2,1)S(1)}, u32[]{:S(2)}, u32[]{:S(2)}) collective-permute-start(bf16[4,256,128]{2,1,0:T(8,128)(2,1)S(1)} %slice.49), channel_id=1, source_target_pairs={{0,2},{1,3},{2,4},{3,5},{4,6},{5,7},{6,0},{7,1},{8,10},{9,11},{10,... | collective-permute-start | bytes 786440 | tf_op jit(solution)/shard_map/ppermute | solution.py:383
  69.5 13.8 %collective-permute-start.6 = (bf16[4,256,128]{2,1,0:T(8,128)(2,1)S(1)}, bf16[4,256,128]{2,1,0:T(8,128)(2,1)S(1)}, u32[]{:S(2)}, u32[]{:S(2)}) collective-permute-start(bf16[4,256,128]{2,1,0:T(8,128)(2,1)S(1)} %slice.50), channel_id=1, source_target_pairs={{0,6},{1,7},{2,0},{3,1},{4,2},{5,3},{6,4},{7,5},{8,14},{9,15},{10,... | collective-permute-start | bytes 786440 | tf_op jit(solution)/shard_map/ppermute | solution.py:383
  71.8 4.2 %copy-start.12 = (bf16[8,128,128]{2,1,0:T(8,128)(2,1)}, bf16[8,128,128]{2,1,0:T(8,128)(2,1)S(1)}, u32[]{:S(2)}) copy-start(bf16[8,128,128]{2,1,0:T(8,128)(2,1)S(1)} %collective-permute-done.their_q) | copy-start | bytes 786436
  71.8 9.3 %collective-permute-start.1 = (f32[1,128]{1,0:T(1,128)S(1)}, f32[1,128]{1,0:T(1,128)S(1)}, u32[]{:S(2)}, u32[]{:S(2)}) collective-permute-start(f32[1,128]{1,0:T(1,128)S(1)} %compare_select_fusion), channel_id=1, source_target_pairs={{0,1},{1,0},{2,3},{3,2},{4,5},{5,4},{6,7},{7,6},{8,9},{9,8},{10,11... | collective-permute-start | bytes 1544 | tf_op jit(solution)/shard_map/ppermute | solution.py:353
  74.4 7.1 %copy-start.9 = (bf16[8,128,128]{2,1,0:T(8,128)(2,1)S(1)}, bf16[8,128,128]{2,1,0:T(8,128)(2,1)}, u32[]{:S(2)}) copy-start(bf16[8,128,128]{2,1,0:T(8,128)(2,1)} %get-tuple-element.32) | copy-start | bytes 786436
  76.0 66.5 %copy-start.3 = (bf16[3,8,256,128]{3,2,1,0:T(8,128)(2,1)}, bf16[3,8,256,128]{3,2,1,0:T(8,128)(2,1)S(1)}, u32[]{:S(2)}) copy-start(bf16[3,8,256,128]{3,2,1,0:T(8,128)(2,1)S(1)} %pad_maximum_fusion.refs_0_) | copy-start | bytes 4718596
  76.0 69.6 %collective-permute-start.7 = (bf16[3,8,256,128]{3,2,1,0:T(8,128)(2,1)S(1)}, bf16[3,8,256,128]{3,2,1,0:T(8,128)(2,1)}, u32[]{:S(2)}, u32[]{:S(2)}) collective-permute-start(bf16[3,8,256,128]{3,2,1,0:T(8,128)(2,1)S(1)} %pad_maximum_fusion.refs_0_), channel_id=1, source_target_pairs={{0,8},{8,0},{16,24},{24,16},{32,40},{40,32},{48,56},{56,48},{64,72... | collective-permute-start | bytes 4718600 | tf_op jit(solution)/shard_map/ppermute | solution.py:327
  81.5 8.8 %collective-permute-start.2 = (bf16[8,128,128]{2,1,0:T(8,128)(2,1)S(1)}, bf16[8,128,128]{2,1,0:T(8,128)(2,1)S(1)}, u32[]{:S(2)}, u32[]{:S(2)}) collective-permute-start(bf16[8,128,128]{2,1,0:T(8,128)(2,1)S(1)} %copy-done.9), channel_id=1, source_target_pairs={{0,1},{1,0},{2,3},{3,2},{4,5},{5,4},{6,7},{7,6},{8,9},{9,8},{10,11... | collective-permute-start | bytes 786440 | tf_op jit(solution)/shard_map/ppermute | solution.py:355
  90.3 52.2 %copy-start.13 = (bf16[8,128,128]{2,1,0:T(8,128)(2,1)}, bf16[8,128,128]{2,1,0:T(8,128)(2,1)S(1)}, u32[]{:S(2)}) copy-start(bf16[8,128,128]{2,1,0:T(8,128)(2,1)S(1)} %collective-permute-done.2.their_q) | copy-start | bytes 786436
  90.4 52.2 %copy-start.4 = (bf16[1,8,256,128]{3,2,1,0:T(8,128)(2,1)}, bf16[1,8,256,128]{3,2,1,0:T(8,128)(2,1)S(1)}, u32[]{:S(2)}) copy-start(bf16[1,8,256,128]{3,2,1,0:T(8,128)(2,1)S(1)} %maximum_bitcast_fusion.refs_1_) | copy-start | bytes 1572868
  90.4 52.2 %copy-start.8 = (bf16[8,128,128]{2,1,0:T(8,128)(2,1)S(1)}, bf16[8,128,128]{2,1,0:T(8,128)(2,1)}, u32[]{:S(2)}) copy-start(bf16[8,128,128]{2,1,0:T(8,128)(2,1)} %get-tuple-element.47) | copy-start | bytes 786436
  90.4 55.2 %collective-permute-start.8 = (bf16[1,8,256,128]{3,2,1,0:T(8,128)(2,1)S(1)}, bf16[1,8,256,128]{3,2,1,0:T(8,128)(2,1)S(1)}, u32[]{:S(2)}, u32[]{:S(2)}) collective-permute-start(bf16[1,8,256,128]{3,2,1,0:T(8,128)(2,1)S(1)} %maximum_bitcast_fusion.refs_1_), channel_id=1, source_target_pairs={{0,8},{8,0},{16,24},{24,16},{32,40},{40,32},{48,56},{56,48},{64,72... | collective-permute-start | bytes 1572872 | tf_op jit(solution)/shard_map/ppermute | solution.py:327
  142.5 55.2 %collective-permute-start.11 = (bf16[8,128,128]{2,1,0:T(8,128)(2,1)S(1)}, bf16[8,128,128]{2,1,0:T(8,128)(2,1)S(1)}, u32[]{:S(2)}, u32[]{:S(2)}) collective-permute-start(bf16[8,128,128]{2,1,0:T(8,128)(2,1)S(1)} %copy-done.8), channel_id=1, source_target_pairs={{0,1},{1,0},{2,3},{3,2},{4,5},{5,4},{6,7},{7,6},{8,9},{9,8},{10,11... | collective-permute-start | bytes 786440 | tf_op jit(solution)/shard_map/ppermute | solution.py:389
  143.4 108.1 %collective-permute-start.10 = (bf16[8,144,128]{2,1,0:T(8,128)(2,1)}, bf16[8,144,128]{2,1,0:T(8,128)(2,1)S(1)}, u32[]{:S(2)}, u32[]{:S(2)}) collective-permute-start(bf16[8,144,128]{2,1,0:T(8,128)(2,1)} %get-tuple-element.45), channel_id=1, source_target_pairs={{0,1},{1,0},{2,3},{3,2},{4,5},{5,4},{6,7},{7,6},{8,9},{9,8},{10,11... | collective-permute-start | bytes 884744 | tf_op jit(solution)/shard_map/ppermute | solution.py:380
  145.6 0.8 copy-start.11
  196.9 54.5 %collective-permute-start.9 = (bf16[8,144,128]{2,1,0:T(8,128)(2,1)}, bf16[8,144,128]{2,1,0:T(8,128)(2,1)S(1)}, u32[]{:S(2)}, u32[]{:S(2)}) collective-permute-start(bf16[8,144,128]{2,1,0:T(8,128)(2,1)} %get-tuple-element.43), channel_id=1, source_target_pairs={{0,1},{1,0},{2,3},{3,2},{4,5},{5,4},{6,7},{7,6},{8,9},{9,8},{10,11... | collective-permute-start | bytes 884744 | tf_op jit(solution)/shard_map/ppermute | solution.py:380
  197.8 0.7 copy-start.14
  198.5 53.0 %copy-start.15 = (s32[24]{0:T(128)S(1)}, s32[24]{0:T(128)}, u32[]{:S(2)}) copy-start(s32[24]{0:T(128)} %param.10) | copy-start | bytes 292
  249.1 9.5 %collective-permute-start.12 = (bf16[8,144,128]{2,1,0:T(8,128)(2,1)}, bf16[8,144,128]{2,1,0:T(8,128)(2,1)S(1)}, u32[]{:S(2)}, u32[]{:S(2)}) collective-permute-start(bf16[8,144,128]{2,1,0:T(8,128)(2,1)} %get-tuple-element.50), channel_id=1, source_target_pairs={{0,1},{1,0},{2,3},{3,2},{4,5},{5,4},{6,7},{7,6},{8,9},{9,8},{10,11... | collective-permute-start | bytes 884744 | tf_op jit(solution)/shard_map/ppermute | solution.py:380
  251.5 7.1 %copy-start.5 = (bf16[8,144,128]{2,1,0:T(8,128)(2,1)}, bf16[8,144,128]{2,1,0:T(8,128)(2,1)S(1)}, u32[]{:S(2)}) copy-start(bf16[8,144,128]{2,1,0:T(8,128)(2,1)S(1)} %collective-permute-done.10.refs_3_) | copy-start | bytes 884740
  251.5 7.1 %copy-start.6 = (bf16[8,144,128]{2,1,0:T(8,128)(2,1)}, bf16[8,144,128]{2,1,0:T(8,128)(2,1)S(1)}, u32[]{:S(2)}) copy-start(bf16[8,144,128]{2,1,0:T(8,128)(2,1)S(1)} %collective-permute-done.9.refs_1_) | copy-start | bytes 884740
  258.6 0.7 copy-start.7
  262.0 4.1 %copy-start.10 = (s32[128]{0:T(128)S(1)}, s32[128]{0:T(128)}, u32[]{:S(2)}) copy-start(s32[128]{0:T(128)} %param.9) | copy-start | bytes 1540
  262.0 12.6 %all-to-all-start.2 = ((bf16[8,384,128]{2,1,0:T(8,128)(2,1)}), bf16[8,384,128]{2,1,0:T(8,128)(2,1)S(1)}, u32[]{:S(2)}, u32[]{:S(2)}) async-start(bf16[8,384,128]{2,1,0:T(8,128)(2,1)} %shard_map.69), calls=%async_computation.2 | async-start | bytes 1572864 | tf_op jit(solution)/shard_map/all_to_all | solution.py:315
  274.6 0.9 copy-start.2
Sparse Core Ops, SparseCore 0:
  25.2 32.3 all-gather.2
  59.3 37.3 all-gather.4

commit v4 on v3

--- a/solution.py
+++ b/solution.py
@@ -28,26 +28,28 @@
     return jnp.dot(a, b, preferred_element_type=jnp.float32)
 
 
-def attend_kernel(head, ringed, info_ref, own_q, their_q, end_ref, *refs):
-    sources, refs = refs[: 4 if ringed else 1], refs[4 if ringed else 1 :]
+def attend_kernel(head, info_ref, own_q, their_q, end_ref, *refs):
+    sources, refs = refs[:-8], refs[-8:]
     own_out, their_out, kv_ref, qt_ref, weight_ref, acc_ref, top_ref, sems = refs
     core, rank = info_ref[0], info_ref[1]
     blocks = ZONES
 
     copies = []
-    if ringed:
-        near, near_last, far, far_last = sources
-        for j, (src, last, c) in enumerate(((near, near_last, core), (far, far_last, 1 - core))):
-            pieces = [(src.at[0], 0), (src.at[1], 1), (last.at[0], 2), (src.at[2], 3)]
-            for piece, step in pieces:
-                copies.append(
-                    pltpu.make_async_copy(
-                        piece, kv_ref.at[(rank + step) % 4, c], sems.at[4 * j + step]
-                    )
-                )
-    else:
+    if len(sources) == 1:
         whole = sources[0].at[:, :, :, pl.ds(0, 2 * HEAD_DIM)]
         copies.append(pltpu.make_async_copy(whole, kv_ref, sems.at[0]))
+        sources = ()
+    half = len(sources) // 2
+    for j, (group, c) in enumerate(((sources[:half], core), (sources[half:], 1 - core))):
+        pieces = [src.at[k] for src in group for k in range(src.shape[0])]
+        for k, (piece, step) in enumerate(zip(pieces, (0, 1, 3, 2))):
+            copies.append(
+                pltpu.make_async_copy(
+                    piece.at[:, pl.ds(0, 2 * HEAD_DIM)],
+                    kv_ref.at[(rank + step) % 4, c],
+                    sems.at[4 * j + k],
+                )
+            )
     for copy in copies:
         copy.start()
 
@@ -171,18 +173,19 @@
             out[r, HEAD_DIM:, :] = note[:, at]
 
 
-def attend(info, own_q, their_q, ends, sources, head):
+def attend(info, own_q, their_q, at, ends, sources, head):
     rows = ZONES * SEGMENT
     out = jax.ShapeDtypeStruct((ZONES, HEAD_DIM + NOTE, HEAD_DIM), jnp.bfloat16)
     first = own_q.shape[1] // HEAD_DIM - 3
     own_spec = pl.BlockSpec((ZONES, HEAD_DIM, HEAD_DIM), lambda i, *_: (0, first + head, 0))
+    their_spec = pl.BlockSpec((ZONES, HEAD_DIM, HEAD_DIM), lambda i, *_: (0, at, 0))
     whole = pl.BlockSpec(memory_space=pltpu.VMEM)
     return pl.pallas_call(
-        functools.partial(attend_kernel, head, len(sources) > 1),
+        functools.partial(attend_kernel, head),
         grid_spec=pltpu.PrefetchScalarGridSpec(
             num_scalar_prefetch=1,
             grid=(1,),
-            in_specs=[own_spec, whole, whole]
+            in_specs=[own_spec, their_spec, whole]
             + [pl.BlockSpec(memory_space=pl.ANY)] * len(sources),
             out_specs=[whole, whole],
             scratch_shapes=[
@@ -339,28 +342,24 @@
     rest = exchange(rest)
     gathered = gather(first)
     block = rest[:, :pair]
-    half = ZONES // 2
-    below, above = lax.ppermute(block, "head", up), lax.ppermute(block, "head", down)
     own_q = [rest[:, start : start + HEAD_DIM] for start in range(2 * pair, rest.shape[1], HEAD_DIM)]
     their_q = [None, lax.ppermute(own_q[1], "head", partner), None]
+    above, below = lax.ppermute(block, "head", down), lax.ppermute(block, "head", up)
 
     def combined(notes):
         is_count = jnp.arange(HEAD_DIM) < K_NORM
         return jnp.where(is_count, jnp.sum(notes, axis=0), jnp.max(notes, axis=0))
 
     note = combined(gathered[:, :, :, pair].reshape(-1, HEAD_DIM).astype(jnp.float32))[None]
-    note, their_q[1] = after(note, their_q[1])
     note_other = lax.ppermute(note, "head", partner)
-    own_q[0], note_other = after(own_q[0], note_other)
-    their_q[0] = lax.ppermute(own_q[0], "head", partner)
     note = combined(jnp.concatenate([note, note_other]))
     squares = note[K_NORM : K_NORM + heads] * note[Q_NORM : Q_NORM + heads]
     plain = (squares * (1.05 * SCALE**2) < PLAIN_LIMIT**2).astype(jnp.int32)
     ends = note[:spans].astype(jnp.int32)
 
     core, y, side = run % 2, rank // 2, rank % 2
-    sides = jnp.stack([side, 1 - side])[None, :, None] * HEAD_DIM
-    position = jnp.arange(ZONES)[:, None, None] * 2048 + sides + jnp.arange(HEAD_DIM)[None, None, :]
+    offsets = jnp.stack([side, 1 - side])[None, :, None] * HEAD_DIM
+    position = jnp.arange(ZONES)[:, None, None] * 2048 + offsets + jnp.arange(HEAD_DIM)[None, None, :]
     position = (position + (core * 1024 + y * SEGMENT)).reshape(ZONES, SEGMENT)
     reach = jnp.min(
         jnp.where(ends > position[..., None], ends, runs * groups * chunk), axis=2
@@ -374,21 +373,23 @@
 
     parts = [None] * (2 * heads)
 
-    def attended(info, head, sources):
-        parts[2 * head], theirs = attend(info, rest, their_q[head], seen, sources, head)
+    def attended(info, head, their_q, at, sources):
+        parts[2 * head], theirs = attend(info, rest, their_q, at, seen, sources, head)
         info, theirs = after(info, theirs)
         parts[2 * head + 1] = lax.ppermute(theirs, "head", partner)
         return info
 
-    pieces = [lax.ppermute(below[:half], "head", up), lax.ppermute(above[half:], "head", down)]
-    near, far = swapped(jnp.stack([block, above, below]))
-    info, their_q[0], *pieces = after(info, their_q[0], *pieces)
-    near_last, far_last = swapped(jnp.concatenate(pieces)[None])
-    info = attended(info, 1, (gathered,))
-    own_q[2], info = after(own_q[2], info)
+    info, above, below = after(info, above, below)
+    opposite = lax.ppermute(below, "head", up)
+    own_q[0], own_q[2], info = after(own_q[0], own_q[2], info)
     their_q[2] = lax.ppermute(own_q[2], "head", partner)
-    info = attended(info, 0, (near, near_last, far, far_last))
-    info = attended(info, 2, (gather(rest[:, pair : 2 * pair]),))
+    info = attended(info, 1, their_q[1], 0, (gathered,))
+    info, opposite, their_q[2] = after(info, opposite, their_q[2])
+    near, far = swapped(jnp.stack([block, above, below, opposite]))
+    their_q[0] = lax.ppermute(own_q[0], "head", partner)
+    info = attended(info, 2, their_q[2], 0, (gather(rest[:, pair : 2 * pair]),))
+    info, parts[3] = after(info, parts[3])
+    info = attended(info, 0, their_q[0], 0, (near, far))
     mixed = exchange(merge(parts))
     gates = gate_rows(span_ids, timesteps, time_weight)
     return pl.pallas_call(

time: 283 us -> 267 us (0.943); the launches traced: 285 us -> 266 us
  waiting for transfers between devices: 26.1 us -> 14.8 us
  starting transfers between devices: 25.1 us -> 20.2 us
    ppermute x1, waiting for transfers between devices: 6.96 us -> 0.01 us  [per_device(): their_q[0] = lax.ppermute(own_q[0], 'head', partner)]
    ppermute x1, waiting for transfers between devices: 5.57 us -> 0.01 us  [per_device(): lax.ppermute(block, 'head', up)]
    ppermute x2 -> x1, starting transfers between devices: 6.6 us -> 1.52 us  [swapped(): return (block, lax.ppermute(block, 'span', core_swap))]
    ppermute x3, starting transfers between devices: 5.37 us -> 1.41 us  [attended(): parts[2 * head + 1] = lax.ppermute(theirs, 'head', partner)]
    slice x3 -> x0, local copies, waits for them, and re-layouts: 3.44 us -> none  [the longest x1 1.5 us: per_device(): info = attended(info, 2, (gather(rest[:, pair:2 * pair]),))]
  transfers between devices with their start and end apart: 16 -> 14, of which waited for: 4 -> 4; matrix products, arithmetic and copies ran while one was open for 4% -> 4% of each run, Pallas kernels for 54% -> 58%
where the time goes in v4:
time: 267 us; the launch traced here: 266 us
  Pallas kernels  162 us (61%)
  blocking collectives  41 us (15%)
  starting transfers between devices  20.2 us (8%)
  waiting for transfers between devices  14.8 us (6%)
  between operations  13.6 us (5%)
  other arithmetic  6.81 us (3%)
  local copies, waits for them, and re-layouts  5.3 us (2%)
    pallas_call x3, Pallas kernels, attend(): pl.pallas_call(functools.partial(attend_kernel, head), grid_spec=pltpu.Pr...  150 us
    all_to_all x2, blocking collectives, exchange(): lax.all_to_all(parts, BOTH, split_axis=0, concat_axis=0, axis_index_group...  41 us
    pallas_call x3, Pallas kernels, pack(): pl.pallas_call(kernel, out_shape=jax.ShapeDtypeStruct((ZONES, rows, HEAD_...  9.1 us
    all_to_all x1, waiting for transfers between devices, exchange(): lax.all_to_all(parts, BOTH, split_axis=0, concat_axis=0, axis_index_group...  6.45 us
    ppermute x3, waiting for transfers between devices, attended(): parts[2 * head + 1] = lax.ppermute(theirs, 'head', partner)  6.02 us
  transfers between devices with their start and end apart: 14, of which 4 were waited for; matrix products, arithmetic and copies ran while one was open for 4% of the time, Pallas kernels for 58%

profile of v4, /device:TPU:25, one launch (start us, length us, event | category | flops | bytes accessed | tf_op | source)
XLA Modules:
  0.0 265.8 jit_solution(17487156585980916079)
XLA Ops:
  6.5 0.0 copy-start
  6.5 0.0 all-gather.3.cloned.1.call-start
  6.5 3.1 %shard_map.64 = bf16[8,272,128]{2,1,0:T(8,128)(2,1)} custom-call(bf16[128,3072]{1,0:T(8,128)(2,1)} %queries_ref.2, bf16[128,3072]{1,0:T(8,128)(2,1)} %keys_ref.3, bf16[128,3072]{1,0:T(8,128)(2,1)} %values_ref.3, s32[1,128]{1,0:T(1,128)} %bitcast.46), custom_call_target="tpu_custom_call" | custom-call | tf_op jit(solution)/shard_map/pallas_call | solution.py:244
  9.7 15.4 %all_to_all.15 = bf16[8,272,128]{2,1,0:T(8,128)(2,1)} all-to-all(bf16[8,272,128]{2,1,0:T(8,128)(2,1)} %shard_map.64), channel_id=1, replica_groups={{0,16,32,48,64,80,96,112},{1,17,33,49,65,81,97,113},{2,18,34,50,66,82,9..., dimensions={0} | all-to-all | bytes 1114112 | tf_op jit(solution)/shard_map/all_to_all | solution.py:318
  25.1 0.0 all-gather.3.cloned.1.call-update
  25.1 0.0 all-gather.5.cloned.1.call-start
  25.2 3.3 %shard_map.65 = bf16[8,896,128]{2,1,0:T(8,128)(2,1)} custom-call(bf16[128,3072]{1,0:T(8,128)(2,1)} %queries_ref.2, bf16[128,3072]{1,0:T(8,128)(2,1)} %keys_ref.3, bf16[128,3072]{1,0:T(8,128)(2,1)} %values_ref.3), custom_call_target="tpu_custom_call" | custom-call | tf_op jit(solution)/shard_map/pallas_call | solution.py:244
  28.5 25.6 %all_to_all.16.own_q = bf16[8,896,128]{2,1,0:T(8,128)(2,1)S(1)} all-to-all(bf16[8,896,128]{2,1,0:T(8,128)(2,1)} %shard_map.65), channel_id=1, replica_groups={{0,16,32,48,64,80,96,112},{1,17,33,49,65,81,97,113},{2,18,34,50,66,82,9..., dimensions={0} | all-to-all | bytes 3670016 | tf_op jit(solution)/shard_map/all_to_all | solution.py:318
  54.1 1.5 slice_bitcast_fusion
  55.6 0.0 all-gather.5.cloned.1.call-update
  55.6 0.1 add_multiply_fusion
  55.7 0.1 broadcast_add_fusion
  55.8 0.1 fusion.12
  55.9 0.5 collective-permute-start.1
  56.3 2.2 collective-permute-start.2
  58.5 1.0 convert_reduce_fusion
  59.5 1.0 slice_reduce_fusion
  60.5 2.5 collective-permute-start
  63.0 0.8 fusion.18
  63.8 0.0 copy-done.1
  63.8 0.5 collective-permute-start.3
  64.3 0.2 collective-permute-done
  64.5 0.1 select_reduce_fusion
  64.6 0.1 compare_convert_fusion
  64.7 0.1 fusion.15
  64.9 0.6 pad_add_fusion.info_ref
  65.5 2.1 collective-permute-done.1
  67.6 0.0 collective-permute-done.2
  67.6 2.4 collective-permute-start.4
  70.0 2.4 collective-permute-start.5
  72.4 0.6 fusion.13.end_ref
  73.0 0.0 collective-permute-done.3.their_q
  73.0 0.7 copy-done.9
  73.7 50.1 %shard_map.66 = (bf16[8,144,128]{2,1,0:T(8,128)(2,1)}, bf16[8,144,128]{2,1,0:T(8,128)(2,1)}) custom-call(s32[13]{0:T(128)} %pad_add_fusion.info_ref, bf16[8,896,128]{2,1,0:T(8,128)(2,1)} %copy-done.1, bf16[8,128,128]{2,1,0:T(8,128)(2,1)} %copy-done.9, s32[8,1,256]{2,1,0:T(1,128)} %fusion.13.end_ref, bf16[4,2,8,272,128]{4,3,2,1,0:T(8,128)(2,1)} %bitcast.49), custom_call_target="tpu_custom_call" | custom-call | flops 8589934592 | bytes 5242880 | tf_op jit(solution)/shard_map/pallas_call | solution.py:183
  123.8 0.0 collective-permute-done.5.their_q
  123.8 0.0 copy-start.10
  123.8 0.0 collective-permute-done.4
  123.8 0.0 copy-done.3
  123.8 2.9 %pad_maximum_fusion.refs_0_ = bf16[4,8,256,128]{3,2,1,0:T(8,128)(2,1)} fusion(bf16[1,8,256,128]{3,2,1,0:T(8,128)(2,1)S(1)} %bitcast.45, bf16[1,8,256,128]{3,2,1,0:T(8,128)(2,1)} %bitcast.16, bf16[1,8,256,128]{3,2,1,0:T(8,128)(2,1)} %bitcast.15, bf16[1,8,256,128]{3,2,1,0:T(8,128)(2,1)S(1)} %copy-done.3), kind=kLoop, calls=%fused_computation | loop fusion | flops 3145728 | bytes 4194304 | tf_op jit(solution)/shard_map/stack | solution.py:388
  126.7 0.0 copy-done.10
  126.7 1.5 collective-permute-start.8
  128.2 0.0 copy-done.8
  128.2 0.0 collective-permute-start.6
  128.2 3.0 %collective-permute-start.7 = (bf16[8,128,128]{2,1,0:T(8,128)(2,1)}, bf16[8,128,128]{2,1,0:T(8,128)(2,1)S(1)}, u32[]{:S(2)}, u32[]{:S(2)}) collective-permute-start(bf16[8,128,128]{2,1,0:T(8,128)(2,1)} %get-tuple-element.43), channel_id=1, source_target_pairs={{0,1},{1,0},{2,3},{3,2},{4,5},{5,4},{6,7},{7,6},{8,9},{9,8},{10,11... | collective-permute-start | bytes 786440 | tf_op jit(solution)/shard_map/ppermute | solution.py:389
  131.2 50.0 %shard_map.67 = (bf16[8,144,128]{2,1,0:T(8,128)(2,1)}, bf16[8,144,128]{2,1,0:T(8,128)(2,1)}) custom-call(s32[13]{0:T(128)} %pad_add_fusion.info_ref, bf16[8,896,128]{2,1,0:T(8,128)(2,1)} %copy-done.1, bf16[8,128,128]{2,1,0:T(8,128)(2,1)} %copy-done.10, s32[8,1,256]{2,1,0:T(1,128)} %fusion.13.end_ref, bf16[4,2,8,256,128]{4,3,2,1,0:T(8,128)(2,1)} %bitcast.50), custom_call_target="tpu_custom_call" | custom-call | flops 8589934592 | bytes 5242880 | tf_op jit(solution)/shard_map/pallas_call | solution.py:183
  181.2 0.0 copy-start.12
  181.2 0.0 collective-permute-done.6.refs_3_
  181.2 0.1 collective-permute-start.10
  181.3 0.0 collective-permute-done.7.their_q
  181.3 0.0 collective-permute-done.8.refs_1_
  181.4 0.7 copy-done.11
  182.0 49.9 %shard_map.68 = (bf16[8,144,128]{2,1,0:T(8,128)(2,1)}, bf16[8,144,128]{2,1,0:T(8,128)(2,1)}) custom-call(s32[13]{0:T(128)} %pad_add_fusion.info_ref, bf16[8,896,128]{2,1,0:T(8,128)(2,1)} %copy-done.1, bf16[8,128,128]{2,1,0:T(8,128)(2,1)} %copy-done.11, s32[8,1,256]{2,1,0:T(1,128)} %fusion.13.end_ref, bf16[4,8,256,128]{3,2,1,0:T(8,128)(2,1)} %pad_maximum_fusion.refs_0_, ...), custom_call_target="tpu_custom_call" | custom-call | flops 8589934592 | bytes 5242880 | tf_op jit(solution)/shard_map/pallas_call | solution.py:183
  232.0 1.3 collective-permute-start.9
  233.3 0.0 collective-permute-done.10.refs_5_
  233.4 6.0 %collective-permute-done.9.refs_1_ = bf16[8,144,128]{2,1,0:T(8,128)(2,1)S(1)} collective-permute-done((bf16[8,144,128]{2,1,0:T(8,128)(2,1)}, bf16[8,144,128]{2,1,0:T(8,128)(2,1)S(1)}, u32[]{:S(2)}, u32[]{:S(2)}) %collective-permute-start.9) | collective-permute-done | bytes 294944 | tf_op jit(solution)/shard_map/ppermute | solution.py:379
  239.4 0.7 copy-done.6
  240.1 2.6 shard_map.69
  242.7 3.7 %all-to-all-start.2 = ((bf16[8,384,128]{2,1,0:T(8,128)(2,1)}), bf16[8,384,128]{2,1,0:T(8,128)(2,1)S(1)}, u32[]{:S(2)}, u32[]{:S(2)}) async-start(bf16[8,384,128]{2,1,0:T(8,128)(2,1)} %shard_map.69), calls=%async_computation.2 | async-start | bytes 1572864 | tf_op jit(solution)/shard_map/all_to_all | solution.py:318
  246.4 0.1 fusion.2
  246.6 0.3 fusion.4
  246.9 2.0 fusion.gate_ref
  248.9 6.5 %all-to-all-done.2.mixed_ref = bf16[8,384,128]{2,1,0:T(8,128)(2,1)S(1)} async-done(((bf16[8,384,128]{2,1,0:T(8,128)(2,1)}), bf16[8,384,128]{2,1,0:T(8,128)(2,1)S(1)}, u32[]{:S(2)}, u32[]{:S(2)}) %all-to-all-start.2) | async-done | bytes 786464 | tf_op jit(solution)/shard_map/all_to_all | solution.py:318
  255.3 0.9 copy-done.2
  256.2 2.7 %shard_map.70 = bf16[128,3072]{1,0:T(8,128)(2,1)} custom-call(f32[128,3072]{1,0:T(8,128)} %fusion.gate_ref, bf16[8,384,128]{2,1,0:T(8,128)(2,1)} %copy-done.2), custom_call_target="tpu_custom_call" | custom-call | tf_op jit(solution)/shard_map/pallas_call | solution.py:395
  (27 shorter events, 0.1 us)
Async XLA Ops:
  6.5 240.0 %copy-start = (bf16[256,3072]{1,0:T(8,128)(2,1)S(1)}, bf16[256,3072]{1,0:T(8,128)(2,1)}, u32[]{:S(2)}) copy-start(bf16[256,3072]{1,0:T(8,128)(2,1)} %param.11) | copy-start | bytes 4718596
  6.5 52.0 %all-gather.3.cloned.1.call-start = ((), (), s32[]{:S(2)}) async-start(), calls=%async_computation.3 | async-start | bytes 5013504 | tf_op jit(solution)/shard_map/all_gather | solution.py:323
  25.1 106.1 %all-gather.5.cloned.1.call-start = ((), (), s32[]{:S(2)}) async-start(), calls=%async_computation.4 | async-start | bytes 4718592 | tf_op jit(solution)/shard_map/all_gather | solution.py:323
  54.1 9.7 %copy-start.1 = (bf16[8,896,128]{2,1,0:T(8,128)(2,1)}, bf16[8,896,128]{2,1,0:T(8,128)(2,1)S(1)}, u32[]{:S(2)}) copy-start(bf16[8,896,128]{2,1,0:T(8,128)(2,1)S(1)} %all_to_all.16.own_q) | copy-start | bytes 5505028
  55.9 11.7 %collective-permute-start.1 = (bf16[8,256,128]{2,1,0:T(8,128)(2,1)}, bf16[8,256,128]{2,1,0:T(8,128)(2,1)}, u32[]{:S(2)}, u32[]{:S(2)}) collective-permute-start(bf16[8,256,128]{2,1,0:T(8,128)(2,1)} %get-tuple-element.55), channel_id=1, source_target_pairs={{0,6},{1,7},{2,0},{3,1},{4,2},{5,3},{6,4},{7,5},{8,14},{9,15},{10,... | collective-permute-start | bytes 1572872 | tf_op jit(solution)/shard_map/ppermute | solution.py:347
  56.3 11.2 %collective-permute-start.2 = (bf16[8,256,128]{2,1,0:T(8,128)(2,1)}, bf16[8,256,128]{2,1,0:T(8,128)(2,1)}, u32[]{:S(2)}, u32[]{:S(2)}) collective-permute-start(bf16[8,256,128]{2,1,0:T(8,128)(2,1)} %get-tuple-element.55), channel_id=1, source_target_pairs={{0,2},{1,3},{2,4},{3,5},{4,6},{5,7},{6,0},{7,1},{8,10},{9,11},{10,... | collective-permute-start | bytes 1572872 | tf_op jit(solution)/shard_map/ppermute | solution.py:347
  60.5 4.0 %collective-permute-start = (f32[1,128]{1,0:T(1,128)S(1)}, f32[1,128]{1,0:T(1,128)S(1)}, u32[]{:S(2)}, u32[]{:S(2)}) collective-permute-start(f32[1,128]{1,0:T(1,128)S(1)} %compare_select_fusion), channel_id=1, source_target_pairs={{0,1},{1,0},{2,3},{3,2},{4,5},{5,4},{6,7},{7,6},{8,9},{9,8},{10,11... | collective-permute-start | bytes 1544 | tf_op jit(solution)/shard_map/ppermute | solution.py:354
  63.8 9.2 %collective-permute-start.3 = (bf16[8,128,128]{2,1,0:T(8,128)(2,1)S(1)}, bf16[8,128,128]{2,1,0:T(8,128)(2,1)S(1)}, u32[]{:S(2)}, u32[]{:S(2)}) collective-permute-start(bf16[8,128,128]{2,1,0:T(8,128)(2,1)S(1)} %get-tuple-element.56), channel_id=1, source_target_pairs={{0,1},{1,0},{2,3},{3,2},{4,5},{5,4},{6,7},{7,6},{8,9},{9,8},{10,11... | collective-permute-start | bytes 786440 | tf_op jit(solution)/shard_map/ppermute | solution.py:346
  67.6 56.2 %collective-permute-start.4 = (bf16[8,256,128]{2,1,0:T(8,128)(2,1)}, bf16[8,256,128]{2,1,0:T(8,128)(2,1)S(1)}, u32[]{:S(2)}, u32[]{:S(2)}) collective-permute-start(bf16[8,256,128]{2,1,0:T(8,128)(2,1)} %collective-permute-done.2), channel_id=1, source_target_pairs={{0,2},{1,3},{2,4},{3,5},{4,6},{5,7},{6,0},{7,1},{8,10},{9,11},{10,... | collective-permute-start | bytes 1572872 | tf_op jit(solution)/shard_map/ppermute | solution.py:383
  70.0 53.8 %collective-permute-start.5 = (bf16[8,128,128]{2,1,0:T(8,128)(2,1)S(1)}, bf16[8,128,128]{2,1,0:T(8,128)(2,1)S(1)}, u32[]{:S(2)}, u32[]{:S(2)}) collective-permute-start(bf16[8,128,128]{2,1,0:T(8,128)(2,1)S(1)} %get-tuple-element.36), channel_id=1, source_target_pairs={{0,1},{1,0},{2,3},{3,2},{4,5},{5,4},{6,7},{7,6},{8,9},{9,8},{10,11... | collective-permute-start | bytes 786440 | tf_op jit(solution)/shard_map/ppermute | solution.py:385
  73.0 50.8 %copy-start.3 = (bf16[1,8,256,128]{3,2,1,0:T(8,128)(2,1)S(1)}, bf16[1,8,256,128]{3,2,1,0:T(8,128)(2,1)}, u32[]{:S(2)}) copy-start(bf16[1,8,256,128]{3,2,1,0:T(8,128)(2,1)} %get-tuple-element.53) | copy-start | bytes 1572868
  73.0 0.7 copy-start.9
  123.8 2.9 %copy-start.10 = (bf16[8,128,128]{2,1,0:T(8,128)(2,1)}, bf16[8,128,128]{2,1,0:T(8,128)(2,1)S(1)}, u32[]{:S(2)}) copy-start(bf16[8,128,128]{2,1,0:T(8,128)(2,1)S(1)} %collective-permute-done.5.their_q) | copy-start | bytes 786436
  123.8 4.4 %copy-start.8 = (bf16[8,144,128]{2,1,0:T(8,128)(2,1)S(1)}, bf16[8,144,128]{2,1,0:T(8,128)(2,1)}, u32[]{:S(2)}) copy-start(bf16[8,144,128]{2,1,0:T(8,128)(2,1)} %get-tuple-element.41) | copy-start | bytes 884740
  126.7 54.6 %collective-permute-start.8 = (bf16[4,8,256,128]{3,2,1,0:T(8,128)(2,1)}, bf16[4,8,256,128]{3,2,1,0:T(8,128)(2,1)}, u32[]{:S(2)}, u32[]{:S(2)}) collective-permute-start(bf16[4,8,256,128]{3,2,1,0:T(8,128)(2,1)} %pad_maximum_fusion.refs_0_), channel_id=1, source_target_pairs={{0,8},{8,0},{16,24},{24,16},{32,40},{40,32},{48,56},{56,48},{64,72... | collective-permute-start | bytes 6291464 | tf_op jit(solution)/shard_map/ppermute | solution.py:330
  128.2 53.0 %collective-permute-start.6 = (bf16[8,144,128]{2,1,0:T(8,128)(2,1)S(1)}, bf16[8,144,128]{2,1,0:T(8,128)(2,1)S(1)}, u32[]{:S(2)}, u32[]{:S(2)}) collective-permute-start(bf16[8,144,128]{2,1,0:T(8,128)(2,1)S(1)} %copy-done.8), channel_id=1, source_target_pairs={{0,1},{1,0},{2,3},{3,2},{4,5},{5,4},{6,7},{7,6},{8,9},{9,8},{10,11... | collective-permute-start | bytes 884744 | tf_op jit(solution)/shard_map/ppermute | solution.py:379
  128.2 53.1 %collective-permute-start.7 = (bf16[8,128,128]{2,1,0:T(8,128)(2,1)}, bf16[8,128,128]{2,1,0:T(8,128)(2,1)S(1)}, u32[]{:S(2)}, u32[]{:S(2)}) collective-permute-start(bf16[8,128,128]{2,1,0:T(8,128)(2,1)} %get-tuple-element.43), channel_id=1, source_target_pairs={{0,1},{1,0},{2,3},{3,2},{4,5},{5,4},{6,7},{7,6},{8,9},{9,8},{10,11... | collective-permute-start | bytes 786440 | tf_op jit(solution)/shard_map/ppermute | solution.py:389
  181.2 52.1 %copy-start.12 = (s32[24]{0:T(128)S(1)}, s32[24]{0:T(128)}, u32[]{:S(2)}) copy-start(s32[24]{0:T(128)} %param.10) | copy-start | bytes 292
  181.2 50.8 %copy-start.4 = (bf16[8,144,128]{2,1,0:T(8,128)(2,1)}, bf16[8,144,128]{2,1,0:T(8,128)(2,1)S(1)}, u32[]{:S(2)}) copy-start(bf16[8,144,128]{2,1,0:T(8,128)(2,1)S(1)} %collective-permute-done.6.refs_3_) | copy-start | bytes 884740
  181.2 52.1 %collective-permute-start.10 = (bf16[8,144,128]{2,1,0:T(8,128)(2,1)}, bf16[8,144,128]{2,1,0:T(8,128)(2,1)S(1)}, u32[]{:S(2)}, u32[]{:S(2)}) collective-permute-start(bf16[8,144,128]{2,1,0:T(8,128)(2,1)} %get-tuple-element.52), channel_id=1, source_target_pairs={{0,1},{1,0},{2,3},{3,2},{4,5},{5,4},{6,7},{7,6},{8,9},{9,8},{10,11... | collective-permute-start | bytes 884744 | tf_op jit(solution)/shard_map/ppermute | solution.py:379
  181.3 0.7 copy-start.11
  232.0 7.4 %collective-permute-start.9 = (bf16[8,144,128]{2,1,0:T(8,128)(2,1)}, bf16[8,144,128]{2,1,0:T(8,128)(2,1)S(1)}, u32[]{:S(2)}, u32[]{:S(2)}) collective-permute-start(bf16[8,144,128]{2,1,0:T(8,128)(2,1)} %get-tuple-element.48), channel_id=1, source_target_pairs={{0,1},{1,0},{2,3},{3,2},{4,5},{5,4},{6,7},{7,6},{8,9},{9,8},{10,11... | collective-permute-start | bytes 884744 | tf_op jit(solution)/shard_map/ppermute | solution.py:379
  233.3 6.0 %copy-start.5 = (bf16[8,144,128]{2,1,0:T(8,128)(2,1)}, bf16[8,144,128]{2,1,0:T(8,128)(2,1)S(1)}, u32[]{:S(2)}) copy-start(bf16[8,144,128]{2,1,0:T(8,128)(2,1)S(1)} %collective-permute-done.10.refs_5_) | copy-start | bytes 884740
  239.4 0.7 copy-start.6
  242.7 4.1 %copy-start.7 = (s32[128]{0:T(128)S(1)}, s32[128]{0:T(128)}, u32[]{:S(2)}) copy-start(s32[128]{0:T(128)} %param.9) | copy-start | bytes 1540
  242.7 12.6 %all-to-all-start.2 = ((bf16[8,384,128]{2,1,0:T(8,128)(2,1)}), bf16[8,384,128]{2,1,0:T(8,128)(2,1)S(1)}, u32[]{:S(2)}, u32[]{:S(2)}) async-start(bf16[8,384,128]{2,1,0:T(8,128)(2,1)} %shard_map.69), calls=%async_computation.2 | async-start | bytes 1572864 | tf_op jit(solution)/shard_map/all_to_all | solution.py:318
  255.3 0.9 copy-start.2
Sparse Core Ops, SparseCore 0:
  25.2 32.3 all-gather.2
  59.3 41.0 all-gather.4

commit v5 on v4

--- a/solution.py
+++ b/solution.py
@@ -213,19 +213,20 @@
     ids = jnp.broadcast_to(ids_ref[...].astype(jnp.float32), (HEAD_DIM, HEAD_DIM)).T
     lane = lax.broadcasted_iota(jnp.int32, (HEAD_DIM, HEAD_DIM), 1)
     counts = jnp.sum(jnp.where(ids <= lane.astype(jnp.float32), 1.0, 0.0), axis=0, keepdims=True)
-    ones = jnp.ones((HEAD_DIM, HEAD_DIM), jnp.bfloat16)
-    lane = lane[:1]
+    local = heads * HEAD_DIM
+    row = lax.broadcasted_iota(jnp.int32, (2 * local, HEAD_DIM), 0) // HEAD_DIM
+    column = lax.broadcasted_iota(jnp.int32, (2 * local, HEAD_DIM), 1)
+    wanted = jnp.where(row < heads, row + K_NORM, row - heads + Q_NORM)
+    pick = jnp.where(column == wanted, 1.0, 0.0).astype(jnp.bfloat16)
+    is_count = lane[:1] < K_NORM
     for g in range(groups):
         at = slice((g * heads + head) * HEAD_DIM, (g * heads + head + 1) * HEAD_DIM)
         out_ref[g, :HEAD_DIM] = keys_ref[:, at]
         out_ref[g, HEAD_DIM : 2 * HEAD_DIM] = values_ref[:, at].T
-        note = counts
-        for first, ref in ((K_NORM, keys_ref), (Q_NORM, queries_ref)):
-            for h in range(heads):
-                start = (g * heads + h) * HEAD_DIM
-                rows = ref[:, start : start + HEAD_DIM].astype(jnp.float32)
-                norm = jnp.max(dot((rows * rows).astype(jnp.bfloat16), ones), axis=0, keepdims=True)
-                note = jnp.where(lane == first + h, norm * 1.02, note)
+        rows = [ref[:, g * local : (g + 1) * local].astype(jnp.float32) for ref in (keys_ref, queries_ref)]
+        squares = jnp.concatenate([(x * x).astype(jnp.bfloat16) for x in rows], axis=1)
+        norms = jnp.max(dot(squares, pick), axis=0, keepdims=True) * 1.02
+        note = jnp.where(is_count, counts, norms)
         out_ref[g, 2 * HEAD_DIM :] = jnp.broadcast_to(note, (NOTE, HEAD_DIM)).astype(jnp.bfloat16)
 
 
@@ -253,7 +254,7 @@
         note = ref[zone, HEAD_DIM:, :].astype(jnp.float32)
         return note[0:1] + note[1:2] + note[2:3]
 
-    for head in range(len(refs) // 2):
+    for head in range(out.shape[1] // HEAD_DIM):
         one, two = refs[2 * head], refs[2 * head + 1]
         at = slice(head * HEAD_DIM, (head + 1) * HEAD_DIM)
         for zone in range(ZONES):
@@ -262,16 +263,23 @@
             out[zone, at, :] = (b + (a - b) * share).astype(jnp.bfloat16)
 
 
-def merge(parts):
-    return pack(merge_kernel, len(parts) // 2 * HEAD_DIM, *parts)
-
-
-def gate_kernel(gate_ref, mixed_ref, out_ref):
-    groups, local, _ = mixed_ref.shape
+def merge(parts, follows=None):
+    heads = len(parts) // 2
+    rest = [] if follows is None else [follows]
+    specs = [pl.BlockSpec(memory_space=pltpu.VMEM)] * len(parts)
+    specs += [pl.BlockSpec(memory_space=pl.ANY)] * len(rest)
+    shape = jax.ShapeDtypeStruct((ZONES, heads * HEAD_DIM, HEAD_DIM), jnp.bfloat16)
+    return pl.pallas_call(merge_kernel, in_specs=specs, out_shape=shape)(*parts, *rest)
+
+
+def gate_kernel(gate_ref, early_ref, late_ref, out_ref):
+    groups = early_ref.shape[0]
+    heads = [(late_ref, 0), (early_ref, 0), (early_ref, HEAD_DIM)]
     for g in range(groups):
-        for h in range(0, local, HEAD_DIM):
-            at = slice(g * local + h, g * local + h + HEAD_DIM)
-            attended = mixed_ref[g, h : h + HEAD_DIM, :].T.astype(jnp.float32)
+        for head, (ref, h) in enumerate(heads):
+            start = (g * len(heads) + head) * HEAD_DIM
+            at = slice(start, start + HEAD_DIM)
+            attended = ref[g, h : h + HEAD_DIM, :].T.astype(jnp.float32)
             out_ref[:, at] = (gate_ref[:, at] * attended).astype(jnp.bfloat16)
 
 
@@ -341,8 +349,8 @@
     )
     rest = exchange(rest)
     gathered = gather(first)
-    block = rest[:, :pair]
     own_q = [rest[:, start : start + HEAD_DIM] for start in range(2 * pair, rest.shape[1], HEAD_DIM)]
+    own_q[1], block, second = after(own_q[1], rest[:, :pair], rest[:, pair : 2 * pair])
     their_q = [None, lax.ppermute(own_q[1], "head", partner), None]
     above, below = lax.ppermute(block, "head", down), lax.ppermute(block, "head", up)
 
@@ -351,6 +359,7 @@
         return jnp.where(is_count, jnp.sum(notes, axis=0), jnp.max(notes, axis=0))
 
     note = combined(gathered[:, :, :, pair].reshape(-1, HEAD_DIM).astype(jnp.float32))[None]
+    note, their_q[1] = after(note, their_q[1])
     note_other = lax.ppermute(note, "head", partner)
     note = combined(jnp.concatenate([note, note_other]))
     squares = note[K_NORM : K_NORM + heads] * note[Q_NORM : Q_NORM + heads]
@@ -380,21 +389,21 @@
         return info
 
     info, above, below = after(info, above, below)
-    opposite = lax.ppermute(below, "head", up)
+    opposite = lax.ppermute(above, "head", down)
     own_q[0], own_q[2], info = after(own_q[0], own_q[2], info)
     their_q[2] = lax.ppermute(own_q[2], "head", partner)
     info = attended(info, 1, their_q[1], 0, (gathered,))
     info, opposite, their_q[2] = after(info, opposite, their_q[2])
     near, far = swapped(jnp.stack([block, above, below, opposite]))
     their_q[0] = lax.ppermute(own_q[0], "head", partner)
-    info = attended(info, 2, their_q[2], 0, (gather(rest[:, pair : 2 * pair]),))
+    info = attended(info, 2, their_q[2], 0, (gather(second),))
     info, parts[3] = after(info, parts[3])
     info = attended(info, 0, their_q[0], 0, (near, far))
-    mixed = exchange(merge(parts))
+    mixed = [exchange(merge(parts[2:], parts[0])), exchange(merge(parts[:2]))]
     gates = gate_rows(span_ids, timesteps, time_weight)
     return pl.pallas_call(
         gate_kernel, out_shape=jax.ShapeDtypeStruct((chunk, width), jnp.bfloat16)
-    )(gates, mixed)
+    )(gates, *mixed)
 
 
 def solution(mesh):

time: 267 us -> 291 us (1.090)
  waiting for transfers between devices: 14.8 us -> 28.2 us
  starting transfers between devices: 20.2 us -> 30.8 us
    ppermute x1, waiting for transfers between devices: 2.08 us -> 14.1 us  [per_device(): lax.ppermute(block, 'head', down)]
    ppermute x1, starting transfers between devices: 1.52 us -> 9.77 us  [swapped(): return (block, lax.ppermute(block, 'span', core_swap))]
    all_to_all x1 -> x2, starting transfers between devices: 3.68 us -> 8.33 us  [exchange(): lax.all_to_all(parts, BOTH, split_axis=0, concat_axis=0, axis_index_group...]
    pallas_call x0 -> x2, Pallas kernels: none -> 4.15 us  [merge(): pl.pallas_call(merge_kernel, in_specs=specs, out_shape=shape)(*parts, *rest)]
    pallas_call x3 -> x2, Pallas kernels: 9.1 us -> 6.51 us  [pack(): pl.pallas_call(kernel, out_shape=jax.ShapeDtypeStruct((ZONES, rows, HEAD_...]
    all_to_all x1 -> x2, waiting for transfers between devices: 6.45 us -> 4.12 us  [exchange(): lax.all_to_all(parts, BOTH, split_axis=0, concat_axis=0, axis_index_group...]
  transfers between devices with their start and end apart: 14 -> 15, of which waited for: 4 -> 4; matrix products, arithmetic and copies ran while one was open for 4% -> 3% of each run, Pallas kernels for 58% -> 54%
where the time goes in v5:
time: 291 us; the launch traced here: 290 us
  Pallas kernels  164 us (56%)
  blocking collectives  41 us (14%)
  starting transfers between devices  30.8 us (11%)
  waiting for transfers between devices  28.2 us (10%)
  between operations  13.7 us (5%)
  other arithmetic  5.55 us (2%)
  local copies, waits for them, and re-layouts  4.91 us (2%)
    pallas_call x3, Pallas kernels, attend(): pl.pallas_call(functools.partial(attend_kernel, head), grid_spec=pltpu.Pr...  150 us
    all_to_all x2, blocking collectives, exchange(): lax.all_to_all(parts, BOTH, split_axis=0, concat_axis=0, axis_index_group...  41 us
    ppermute x1, waiting for transfers between devices, per_device(): lax.ppermute(block, 'head', down)  14.1 us
    ppermute x1, starting transfers between devices, swapped(): return (block, lax.ppermute(block, 'span', core_swap))  9.77 us
    all_to_all x2, starting transfers between devices, exchange(): lax.all_to_all(parts, BOTH, split_axis=0, concat_axis=0, axis_index_group...  8.33 us
    ppermute x3, waiting for transfers between devices, attended(): parts[2 * head + 1] = lax.ppermute(theirs, 'head', partner)  7.36 us
    pallas_call x2, Pallas kernels, pack(): pl.pallas_call(kernel, out_shape=jax.ShapeDtypeStruct((ZONES, rows, HEAD_...  6.51 us
  transfers between devices with their start and end apart: 15, of which 4 were waited for; matrix products, arithmetic and copies ran while one was open for 3% of the time, Pallas kernels for 54%

profile of v5, /device:TPU:25, one launch (start us, length us, event | category | flops | bytes accessed | tf_op | source)
XLA Modules:
  0.0 290.0 jit_solution(14538268895489002594)
XLA Ops:
  6.5 3.2 %shard_map.64 = bf16[8,272,128]{2,1,0:T(8,128)(2,1)} custom-call(bf16[128,3072]{1,0:T(8,128)(2,1)} %queries_ref.2, bf16[128,3072]{1,0:T(8,128)(2,1)} %keys_ref.3, bf16[128,3072]{1,0:T(8,128)(2,1)} %values_ref.3, s32[1,128]{1,0:T(1,128)} %bitcast.46), custom_call_target="tpu_custom_call" | custom-call | tf_op jit(solution)/shard_map/pallas_call | solution.py:245
  9.7 15.4 %all_to_all.20 = bf16[8,272,128]{2,1,0:T(8,128)(2,1)} all-to-all(bf16[8,272,128]{2,1,0:T(8,128)(2,1)} %shard_map.64), channel_id=1, replica_groups={{0,16,32,48,64,80,96,112},{1,17,33,49,65,81,97,113},{2,18,34,50,66,82,9..., dimensions={0} | all-to-all | bytes 1114112 | tf_op jit(solution)/shard_map/all_to_all | solution.py:326
  25.1 0.0 all-gather.3.cloned.1.call-update
  25.2 0.0 all-gather.5.cloned.1.call-start
  25.2 3.3 %shard_map.65 = bf16[8,896,128]{2,1,0:T(8,128)(2,1)} custom-call(bf16[128,3072]{1,0:T(8,128)(2,1)} %queries_ref.2, bf16[128,3072]{1,0:T(8,128)(2,1)} %keys_ref.3, bf16[128,3072]{1,0:T(8,128)(2,1)} %values_ref.3), custom_call_target="tpu_custom_call" | custom-call | tf_op jit(solution)/shard_map/pallas_call | solution.py:245
  28.5 25.6 %all_to_all.21.own_q = bf16[8,896,128]{2,1,0:T(8,128)(2,1)S(1)} all-to-all(bf16[8,896,128]{2,1,0:T(8,128)(2,1)} %shard_map.65), channel_id=1, replica_groups={{0,16,32,48,64,80,96,112},{1,17,33,49,65,81,97,113},{2,18,34,50,66,82,9..., dimensions={0} | all-to-all | bytes 3670016 | tf_op jit(solution)/shard_map/all_to_all | solution.py:326
  54.1 1.0 fusion.19
  55.0 1.1 fusion.18
  56.1 0.0 all-gather.5.cloned.1.call-update
  56.2 0.1 add_multiply_fusion
  56.3 0.1 broadcast_add_fusion
  56.4 2.5 collective-permute-start
  58.8 1.0 slice_reduce_fusion
  59.8 1.0 convert_reduce_fusion
  60.8 2.5 collective-permute-done.their_q
  63.3 2.5 collective-permute-start.1
  65.8 0.1 fusion.12
  65.8 0.5 collective-permute-start.2
  66.3 2.2 collective-permute-start.3
  68.5 0.0 collective-permute-done.1
  68.5 0.1 select_reduce_fusion
  68.6 0.1 fusion.15
  68.8 0.1 compare_convert_fusion
  68.9 0.6 pad_add_fusion.info_ref
  69.5 14.1 %collective-permute-done.2 = bf16[8,256,128]{2,1,0:T(8,128)(2,1)S(1)} collective-permute-done((bf16[8,256,128]{2,1,0:T(8,128)(2,1)}, bf16[8,256,128]{2,1,0:T(8,128)(2,1)S(1)}, u32[]{:S(2)}, u32[]{:S(2)}) %collective-permute-start.2) | collective-permute-done | bytes 524320 | tf_op jit(solution)/shard_map/ppermute | solution.py:355
  83.6 0.0 collective-permute-done.3
  83.6 0.0 collective-permute-start.4
  83.6 0.0 collective-permute-start.5
  83.7 0.6 fusion.13.end_ref
  84.3 50.2 %shard_map.66 = (bf16[8,144,128]{2,1,0:T(8,128)(2,1)}, bf16[8,144,128]{2,1,0:T(8,128)(2,1)}) custom-call(s32[13]{0:T(128)} %pad_add_fusion.info_ref, bf16[8,896,128]{2,1,0:T(8,128)(2,1)} %copy-done.1, bf16[8,128,128]{2,1,0:T(8,128)(2,1)} %copy-done.12, s32[8,1,256]{2,1,0:T(1,128)} %fusion.13.end_ref, bf16[4,2,8,272,128]{4,3,2,1,0:T(8,128)(2,1)} %bitcast.49), custom_call_target="tpu_custom_call" | custom-call | flops 8589934592 | bytes 5242880 | tf_op jit(solution)/shard_map/pallas_call | solution.py:183
  134.5 0.0 collective-permute-done.5.their_q
  134.5 0.0 collective-permute-done.4
  134.5 0.0 copy-done.3
  134.5 0.0 copy-start.15
  134.5 1.6 pad_maximum_fusion.refs_0_
  136.2 9.8 %collective-permute-start.9 = (bf16[4,8,256,128]{3,2,1,0:T(8,128)(2,1)}, bf16[4,8,256,128]{3,2,1,0:T(8,128)(2,1)}, u32[]{:S(2)}, u32[]{:S(2)}) collective-permute-start(bf16[4,8,256,128]{3,2,1,0:T(8,128)(2,1)} %pad_maximum_fusion.refs_0_), channel_id=1, source_target_pairs={{0,8},{8,0},{16,24},{24,16},{32,40},{40,32},{48,56},{56,48},{64,72... | collective-permute-start | bytes 6291464 | tf_op jit(solution)/shard_map/ppermute | solution.py:338
  145.9 0.0 copy-done.15
  146.0 2.2 collective-permute-start.6
  148.2 0.9 collective-permute-start.8
  149.0 50.0 %shard_map.67 = (bf16[8,144,128]{2,1,0:T(8,128)(2,1)}, bf16[8,144,128]{2,1,0:T(8,128)(2,1)}) custom-call(s32[13]{0:T(128)} %pad_add_fusion.info_ref, bf16[8,896,128]{2,1,0:T(8,128)(2,1)} %copy-done.1, bf16[8,128,128]{2,1,0:T(8,128)(2,1)} %copy-done.13, s32[8,1,256]{2,1,0:T(1,128)} %fusion.13.end_ref, bf16[4,2,8,256,128]{4,3,2,1,0:T(8,128)(2,1)} %bitcast.50), custom_call_target="tpu_custom_call" | custom-call | flops 8589934592 | bytes 5242880 | tf_op jit(solution)/shard_map/pallas_call | solution.py:183
  199.0 0.0 collective-permute-done.6.refs_1_
  199.0 0.0 copy-start.6
  199.0 1.1 collective-permute-start.7
  200.1 0.0 collective-permute-done.8.their_q
  200.1 0.0 collective-permute-done.9.refs_1_
  200.1 0.7 copy-done.14
  200.8 50.1 %shard_map.68 = (bf16[8,144,128]{2,1,0:T(8,128)(2,1)}, bf16[8,144,128]{2,1,0:T(8,128)(2,1)}) custom-call(s32[13]{0:T(128)} %pad_add_fusion.info_ref, bf16[8,896,128]{2,1,0:T(8,128)(2,1)} %copy-done.1, bf16[8,128,128]{2,1,0:T(8,128)(2,1)} %copy-done.14, s32[8,1,256]{2,1,0:T(1,128)} %fusion.13.end_ref, bf16[4,8,256,128]{3,2,1,0:T(8,128)(2,1)} %pad_maximum_fusion.refs_0_, ...), custom_call_target="tpu_custom_call" | custom-call | flops 8589934592 | bytes 5242880 | tf_op jit(solution)/shard_map/pallas_call | solution.py:183
  250.9 0.0 collective-permute-done.7.refs_3_
  250.9 0.0 copy-start.7
  250.9 0.7 copy-done.7
  251.6 2.3 shard_map.69
  253.9 3.6 %all-to-all-start.2 = ((bf16[8,256,128]{2,1,0:T(8,128)(2,1)}), bf16[8,256,128]{2,1,0:T(8,128)(2,1)S(1)}, u32[]{:S(2)}, u32[]{:S(2)}) async-start(bf16[8,256,128]{2,1,0:T(8,128)(2,1)} %shard_map.69), calls=%async_computation.2 | async-start | bytes 1048576 | tf_op jit(solution)/shard_map/all_to_all | solution.py:326
  257.5 0.9 collective-permute-start.10
  258.5 0.1 fusion.2
  258.6 0.3 fusion.4
  258.9 7.4 %collective-permute-done.10.refs_1_ = bf16[8,144,128]{2,1,0:T(8,128)(2,1)S(1)} collective-permute-done((bf16[8,144,128]{2,1,0:T(8,128)(2,1)S(1)}, bf16[8,144,128]{2,1,0:T(8,128)(2,1)S(1)}, u32[]{:S(2)}, u32[]{:S(2)}) %collective-permute-start.10) | collective-permute-done | bytes 294944 | tf_op jit(solution)/shard_map/ppermute | solution.py:388
  266.3 0.7 copy-done.5
  267.0 1.9 shard_map.70
  268.9 0.0 all-to-all-done.2.early_ref
  268.9 4.7 %all-to-all-start.3 = ((bf16[8,128,128]{2,1,0:T(8,128)(2,1)}), bf16[8,128,128]{2,1,0:T(8,128)(2,1)S(1)}, u32[]{:S(2)}, u32[]{:S(2)}) async-start(bf16[8,128,128]{2,1,0:T(8,128)(2,1)} %shard_map.70), calls=%async_computation.3 | async-start | bytes 524288 | tf_op jit(solution)/shard_map/all_to_all | solution.py:326
  273.6 2.0 fusion.gate_ref
  275.6 4.1 %all-to-all-done.3.late_ref = bf16[8,128,128]{2,1,0:T(8,128)(2,1)S(1)} async-done(((bf16[8,128,128]{2,1,0:T(8,128)(2,1)}), bf16[8,128,128]{2,1,0:T(8,128)(2,1)S(1)}, u32[]{:S(2)}, u32[]{:S(2)}) %all-to-all-start.3) | async-done | bytes 262176 | tf_op jit(solution)/shard_map/all_to_all | solution.py:326
  279.7 0.7 copy-done.4
  280.4 2.7 shard_map.71
  (36 shorter events, 0.1 us)
Async XLA Ops:
  6.5 252.1 %copy-start = (bf16[256,3072]{1,0:T(8,128)(2,1)S(1)}, bf16[256,3072]{1,0:T(8,128)(2,1)}, u32[]{:S(2)}) copy-start(bf16[256,3072]{1,0:T(8,128)(2,1)} %param.11) | copy-start | bytes 4718596
  6.5 52.3 %all-gather.3.cloned.1.call-start = ((), (), s32[]{:S(2)}) async-start(), calls=%async_computation.4 | async-start | bytes 5013504 | tf_op jit(solution)/shard_map/all_gather | solution.py:331
  25.2 123.9 %all-gather.5.cloned.1.call-start = ((), (), s32[]{:S(2)}) async-start(), calls=%async_computation.5 | async-start | bytes 4718592 | tf_op jit(solution)/shard_map/all_gather | solution.py:331
  54.1 2.1 copy-start.1
  56.4 6.9 %collective-permute-start = (bf16[8,128,128]{2,1,0:T(8,128)(2,1)}, bf16[8,128,128]{2,1,0:T(8,128)(2,1)S(1)}, u32[]{:S(2)}, u32[]{:S(2)}) collective-permute-start(bf16[8,128,128]{2,1,0:T(8,128)(2,1)} %get-tuple-element.36), channel_id=1, source_target_pairs={{0,1},{1,0},{2,3},{3,2},{4,5},{5,4},{6,7},{7,6},{8,9},{9,8},{10,11... | collective-permute-start | bytes 786440 | tf_op jit(solution)/shard_map/ppermute | solution.py:354
  63.3 21.0 %copy-start.12 = (bf16[8,128,128]{2,1,0:T(8,128)(2,1)}, bf16[8,128,128]{2,1,0:T(8,128)(2,1)S(1)}, u32[]{:S(2)}) copy-start(bf16[8,128,128]{2,1,0:T(8,128)(2,1)S(1)} %collective-permute-done.their_q) | copy-start | bytes 786436
  63.3 5.2 %collective-permute-start.1 = (f32[1,128]{1,0:T(1,128)S(1)}, f32[1,128]{1,0:T(1,128)S(1)}, u32[]{:S(2)}, u32[]{:S(2)}) collective-permute-start(f32[1,128]{1,0:T(1,128)S(1)} %compare_select_fusion), channel_id=1, source_target_pairs={{0,1},{1,0},{2,3},{3,2},{4,5},{5,4},{6,7},{7,6},{8,9},{9,8},{10,11... | collective-permute-start | bytes 1544 | tf_op jit(solution)/shard_map/ppermute | solution.py:363
  65.8 17.8 %collective-permute-start.2 = (bf16[8,256,128]{2,1,0:T(8,128)(2,1)}, bf16[8,256,128]{2,1,0:T(8,128)(2,1)S(1)}, u32[]{:S(2)}, u32[]{:S(2)}) collective-permute-start(bf16[8,256,128]{2,1,0:T(8,128)(2,1)} %get-tuple-element.38), channel_id=1, source_target_pairs={{0,6},{1,7},{2,0},{3,1},{4,2},{5,3},{6,4},{7,5},{8,14},{9,15},{10,... | collective-permute-start | bytes 1572872 | tf_op jit(solution)/shard_map/ppermute | solution.py:355
  66.3 17.4 %collective-permute-start.3 = (bf16[8,256,128]{2,1,0:T(8,128)(2,1)}, bf16[8,256,128]{2,1,0:T(8,128)(2,1)S(1)}, u32[]{:S(2)}, u32[]{:S(2)}) collective-permute-start(bf16[8,256,128]{2,1,0:T(8,128)(2,1)} %get-tuple-element.38), channel_id=1, source_target_pairs={{0,2},{1,3},{2,4},{3,5},{4,6},{5,7},{6,0},{7,1},{8,10},{9,11},{10,... | collective-permute-start | bytes 1572872 | tf_op jit(solution)/shard_map/ppermute | solution.py:355
  83.6 50.8 %collective-permute-start.4 = (bf16[8,256,128]{2,1,0:T(8,128)(2,1)S(1)}, bf16[8,256,128]{2,1,0:T(8,128)(2,1)S(1)}, u32[]{:S(2)}, u32[]{:S(2)}) collective-permute-start(bf16[8,256,128]{2,1,0:T(8,128)(2,1)S(1)} %collective-permute-done.2), channel_id=1, source_target_pairs={{0,6},{1,7},{2,0},{3,1},{4,2},{5,3},{6,4},{7,5},{8,14},{9,15},{10,... | collective-permute-start | bytes 1572872 | tf_op jit(solution)/shard_map/ppermute | solution.py:392
  83.6 50.8 %collective-permute-start.5 = (bf16[8,128,128]{2,1,0:T(8,128)(2,1)}, bf16[8,128,128]{2,1,0:T(8,128)(2,1)S(1)}, u32[]{:S(2)}, u32[]{:S(2)}) collective-permute-start(bf16[8,128,128]{2,1,0:T(8,128)(2,1)} %get-tuple-element.46), channel_id=1, source_target_pairs={{0,1},{1,0},{2,3},{3,2},{4,5},{5,4},{6,7},{7,6},{8,9},{9,8},{10,11... | collective-permute-start | bytes 786440 | tf_op jit(solution)/shard_map/ppermute | solution.py:394
  84.3 50.2 %copy-start.3 = (bf16[8,256,128]{2,1,0:T(8,128)(2,1)S(1)}, bf16[8,256,128]{2,1,0:T(8,128)(2,1)}, u32[]{:S(2)}) copy-start(bf16[8,256,128]{2,1,0:T(8,128)(2,1)} %get-tuple-element.38) | copy-start | bytes 1572868
  134.5 1.7 copy-start.13
  134.5 11.4 %copy-start.15 = (s32[24]{0:T(128)S(1)}, s32[24]{0:T(128)}, u32[]{:S(2)}) copy-start(s32[24]{0:T(128)} %param.10) | copy-start | bytes 292
  134.5 11.4 %copy-start.10 = (bf16[8,144,128]{2,1,0:T(8,128)(2,1)S(1)}, bf16[8,144,128]{2,1,0:T(8,128)(2,1)}, u32[]{:S(2)}) copy-start(bf16[8,144,128]{2,1,0:T(8,128)(2,1)} %get-tuple-element.52) | copy-start | bytes 884740
  134.5 13.6 %copy-start.8 = (bf16[8,128,128]{2,1,0:T(8,128)(2,1)S(1)}, bf16[8,128,128]{2,1,0:T(8,128)(2,1)}, u32[]{:S(2)}) copy-start(bf16[8,128,128]{2,1,0:T(8,128)(2,1)} %get-tuple-element.57) | copy-start | bytes 786436
  136.2 63.9 %collective-permute-start.9 = (bf16[4,8,256,128]{3,2,1,0:T(8,128)(2,1)}, bf16[4,8,256,128]{3,2,1,0:T(8,128)(2,1)}, u32[]{:S(2)}, u32[]{:S(2)}) collective-permute-start(bf16[4,8,256,128]{3,2,1,0:T(8,128)(2,1)} %pad_maximum_fusion.refs_0_), channel_id=1, source_target_pairs={{0,8},{8,0},{16,24},{24,16},{32,40},{40,32},{48,56},{56,48},{64,72... | collective-permute-start | bytes 6291464 | tf_op jit(solution)/shard_map/ppermute | solution.py:338
  146.0 53.0 %collective-permute-start.6 = (bf16[8,144,128]{2,1,0:T(8,128)(2,1)S(1)}, bf16[8,144,128]{2,1,0:T(8,128)(2,1)S(1)}, u32[]{:S(2)}, u32[]{:S(2)}) collective-permute-start(bf16[8,144,128]{2,1,0:T(8,128)(2,1)S(1)} %copy-done.10), channel_id=1, source_target_pairs={{0,1},{1,0},{2,3},{3,2},{4,5},{5,4},{6,7},{7,6},{8,9},{9,8},{10,11... | collective-permute-start | bytes 884744 | tf_op jit(solution)/shard_map/ppermute | solution.py:388
  148.2 51.9 %collective-permute-start.8 = (bf16[8,128,128]{2,1,0:T(8,128)(2,1)S(1)}, bf16[8,128,128]{2,1,0:T(8,128)(2,1)S(1)}, u32[]{:S(2)}, u32[]{:S(2)}) collective-permute-start(bf16[8,128,128]{2,1,0:T(8,128)(2,1)S(1)} %copy-done.8), channel_id=1, source_target_pairs={{0,1},{1,0},{2,3},{3,2},{4,5},{5,4},{6,7},{7,6},{8,9},{9,8},{10,11... | collective-permute-start | bytes 786440 | tf_op jit(solution)/shard_map/ppermute | solution.py:398
  199.0 51.9 %copy-start.6 = (bf16[8,144,128]{2,1,0:T(8,128)(2,1)}, bf16[8,144,128]{2,1,0:T(8,128)(2,1)S(1)}, u32[]{:S(2)}) copy-start(bf16[8,144,128]{2,1,0:T(8,128)(2,1)S(1)} %collective-permute-done.6.refs_1_) | copy-start | bytes 884740
  199.0 51.9 %collective-permute-start.7 = (bf16[8,144,128]{2,1,0:T(8,128)(2,1)}, bf16[8,144,128]{2,1,0:T(8,128)(2,1)S(1)}, u32[]{:S(2)}, u32[]{:S(2)}) collective-permute-start(bf16[8,144,128]{2,1,0:T(8,128)(2,1)} %get-tuple-element.55), channel_id=1, source_target_pairs={{0,1},{1,0},{2,3},{3,2},{4,5},{5,4},{6,7},{7,6},{8,9},{9,8},{10,11... | collective-permute-start | bytes 884744 | tf_op jit(solution)/shard_map/ppermute | solution.py:388
  200.1 0.7 copy-start.14
  250.9 6.6 %copy-start.11 = (bf16[8,144,128]{2,1,0:T(8,128)(2,1)S(1)}, bf16[8,144,128]{2,1,0:T(8,128)(2,1)}, u32[]{:S(2)}) copy-start(bf16[8,144,128]{2,1,0:T(8,128)(2,1)} %get-tuple-element.62) | copy-start | bytes 884740
  250.9 0.7 copy-start.7
  253.9 19.7 %copy-start.9 = (s32[128]{0:T(128)S(1)}, s32[128]{0:T(128)}, u32[]{:S(2)}) copy-start(s32[128]{0:T(128)} %param.9) | copy-start | bytes 1540
  253.9 15.0 %all-to-all-start.2 = ((bf16[8,256,128]{2,1,0:T(8,128)(2,1)}), bf16[8,256,128]{2,1,0:T(8,128)(2,1)S(1)}, u32[]{:S(2)}, u32[]{:S(2)}) async-start(bf16[8,256,128]{2,1,0:T(8,128)(2,1)} %shard_map.69), calls=%async_computation.2 | async-start | bytes 1048576 | tf_op jit(solution)/shard_map/all_to_all | solution.py:326
  257.5 8.7 %collective-permute-start.10 = (bf16[8,144,128]{2,1,0:T(8,128)(2,1)S(1)}, bf16[8,144,128]{2,1,0:T(8,128)(2,1)S(1)}, u32[]{:S(2)}, u32[]{:S(2)}) collective-permute-start(bf16[8,144,128]{2,1,0:T(8,128)(2,1)S(1)} %copy-done.11), channel_id=1, source_target_pairs={{0,1},{1,0},{2,3},{3,2},{4,5},{5,4},{6,7},{7,6},{8,9},{9,8},{10,11... | collective-permute-start | bytes 884744 | tf_op jit(solution)/shard_map/ppermute | solution.py:388
  266.3 0.7 copy-start.5
  268.9 10.8 %copy-start.2 = (bf16[8,256,128]{2,1,0:T(8,128)(2,1)}, bf16[8,256,128]{2,1,0:T(8,128)(2,1)S(1)}, u32[]{:S(2)}) copy-start(bf16[8,256,128]{2,1,0:T(8,128)(2,1)S(1)} %all-to-all-done.2.early_ref) | copy-start | bytes 1572868
  268.9 10.8 %all-to-all-start.3 = ((bf16[8,128,128]{2,1,0:T(8,128)(2,1)}), bf16[8,128,128]{2,1,0:T(8,128)(2,1)S(1)}, u32[]{:S(2)}, u32[]{:S(2)}) async-start(bf16[8,128,128]{2,1,0:T(8,128)(2,1)} %shard_map.70), calls=%async_computation.3 | async-start | bytes 524288 | tf_op jit(solution)/shard_map/all_to_all | solution.py:326
  279.7 0.7 copy-start.4
Sparse Core Ops, SparseCore 0:
  25.3 32.3 all-gather.2
  59.4 44.7 all-gather.4

commit v6 on v4

--- a/solution.py
+++ b/solution.py
@@ -304,14 +304,10 @@
         for y in range(4)
         for x in range(2)
     ]
-    along_y = [
-        [device(zone, core, y, x) for y in range(4) for core in range(2)]
-        for zone in range(ZONES)
-        for x in range(2)
-    ]
     up = [(h, (h + 2) % groups) for h in range(groups)]
     down = [(h, (h - 2) % groups) for h in range(groups)]
     core_swap = [(s, s ^ 1) for s in range(runs)]
+    other = [((s * groups + h), ((s ^ 1) * groups + (h ^ 1))) for s in range(runs) for h in range(groups)]
     partner = [(h, h ^ 1) for h in range(groups)]
 
     def exchange(parts):
@@ -319,40 +315,47 @@
             parts, BOTH, split_axis=0, concat_axis=0, axis_index_groups=across, tiled=True
         )
 
-    def gather(block):
-        block = lax.all_gather(block, BOTH, axis_index_groups=along_y, axis=0, tiled=True)
-        return block.reshape(4, 2, ZONES, -1, HEAD_DIM)
-
     def after(*values):
         return lax.optimization_barrier(values)
 
     def swapped(block):
         return block, lax.ppermute(block, "span", core_swap)
+
+    def sides(block):
+        return lax.ppermute(block, "head", down), lax.ppermute(block, "head", up)
 
     pair = 2 * HEAD_DIM
     note_rows = span_ids.reshape(1, -1)
     first = pack(
-        functools.partial(pack_first_kernel, 1), pair + NOTE, queries, keys, values, note_rows
+        functools.partial(pack_first_kernel, 0), pair + NOTE, queries, keys, values, note_rows
     )
     first = exchange(first)
+    above, below = sides(first)
     queries, first = after(queries, first)
     rest = pack(
-        functools.partial(pack_rest_kernel, (0, 2)), 2 * pair + local, queries, keys, values
+        functools.partial(pack_rest_kernel, (1, 2)), 2 * pair + local, queries, keys, values
     )
     rest = exchange(rest)
-    gathered = gather(first)
-    block = rest[:, :pair]
-    own_q = [rest[:, start : start + HEAD_DIM] for start in range(2 * pair, rest.shape[1], HEAD_DIM)]
-    their_q = [None, lax.ppermute(own_q[1], "head", partner), None]
-    above, below = lax.ppermute(block, "head", down), lax.ppermute(block, "head", up)
+    near = jnp.stack([first, above, below, lax.ppermute(above, "head", down)])
 
     def combined(notes):
         is_count = jnp.arange(HEAD_DIM) < K_NORM
         return jnp.where(is_count, jnp.sum(notes, axis=0), jnp.max(notes, axis=0))
 
-    note = combined(gathered[:, :, :, pair].reshape(-1, HEAD_DIM).astype(jnp.float32))[None]
-    note_other = lax.ppermute(note, "head", partner)
-    note = combined(jnp.concatenate([note, note_other]))
+    note = combined(near[:, :, pair].reshape(-1, HEAD_DIM).astype(jnp.float32))[None]
+    rest, near, note = after(rest, near, note)
+    notes = [
+        note,
+        lax.ppermute(note, "span", core_swap),
+        lax.ppermute(note, "head", partner),
+        lax.ppermute(note, BOTH, other),
+    ]
+    near, far = swapped(near)
+    own_q = [rest[:, start : start + HEAD_DIM] for start in range(2 * pair, rest.shape[1], HEAD_DIM)]
+    own_q[0], block_one, block_two = after(own_q[0], rest[:, :pair], rest[:, pair : 2 * pair])
+    their_q = [lax.ppermute(own_q[0], "head", partner), None, None]
+    above, below = sides(block_one)
+    note = combined(jnp.concatenate(notes))
     squares = note[K_NORM : K_NORM + heads] * note[Q_NORM : Q_NORM + heads]
     plain = (squares * (1.05 * SCALE**2) < PLAIN_LIMIT**2).astype(jnp.int32)
     ends = note[:spans].astype(jnp.int32)
@@ -379,17 +382,23 @@
         parts[2 * head + 1] = lax.ppermute(theirs, "head", partner)
         return info
 
-    info, above, below = after(info, above, below)
+    info, block_two, above, below = after(info, block_two, above, below)
     opposite = lax.ppermute(below, "head", up)
-    own_q[0], own_q[2], info = after(own_q[0], own_q[2], info)
+    above_two, below_two = sides(block_two)
+    own_q[1], own_q[2], info = after(own_q[1], own_q[2], info)
+    their_q[1] = lax.ppermute(own_q[1], "head", partner)
+    info = attended(info, 0, their_q[0], 0, (near, far))
+    info, opposite, above_two, below_two, their_q[1] = after(
+        info, opposite, above_two, below_two, their_q[1]
+    )
+    near, far = swapped(jnp.stack([block_one, above, below, opposite]))
+    opposite = lax.ppermute(above_two, "head", down)
+    near_two, far_two = swapped(jnp.stack([block_two, above_two, below_two]))
     their_q[2] = lax.ppermute(own_q[2], "head", partner)
-    info = attended(info, 1, their_q[1], 0, (gathered,))
+    info = attended(info, 1, their_q[1], 0, (near, far))
     info, opposite, their_q[2] = after(info, opposite, their_q[2])
-    near, far = swapped(jnp.stack([block, above, below, opposite]))
-    their_q[0] = lax.ppermute(own_q[0], "head", partner)
-    info = attended(info, 2, their_q[2], 0, (gather(rest[:, pair : 2 * pair]),))
-    info, parts[3] = after(info, parts[3])
-    info = attended(info, 0, their_q[0], 0, (near, far))
+    last, far_last = swapped(opposite[None])
+    info = attended(info, 2, their_q[2], 0, (near_two, last, far_two, far_last))
     mixed = exchange(merge(parts))
     gates = gate_rows(span_ids, timesteps, time_weight)
     return pl.pallas_call(

time: 267 us -> 270 us (1.011)
  waiting for transfers between devices: 14.8 us -> 43 us
  blocking collectives: 41 us -> 15.4 us
  between operations: 13.6 us -> 0.45 us
  starting transfers between devices: 20.2 us -> 32.6 us
    all_to_all x2 -> x1, blocking collectives: 41 us -> 15.4 us  [exchange(): lax.all_to_all(parts, BOTH, split_axis=0, concat_axis=0, axis_index_group...]
    ppermute x5 -> x13, waiting for transfers between devices: 2.26 us -> 23.8 us  [the longest x6 17.4 us: sides(): return (lax.ppermute(block, 'head', down), lax.ppermute(block, 'head', up))]
    ppermute x5 -> x13, starting transfers between devices: 8.7 us -> 20.2 us  [the longest x6 8.16 us: sides(): return (lax.ppermute(block, 'head', down), lax.ppermute(block, 'head', up))]
    all_to_all x1 -> x2, starting transfers between devices: 3.68 us -> 7.27 us  [exchange(): lax.all_to_all(parts, BOTH, split_axis=0, concat_axis=0, axis_index_group...]
    all_to_all x1 -> x2, waiting for transfers between devices: 6.45 us -> 9.14 us  [exchange(): lax.all_to_all(parts, BOTH, split_axis=0, concat_axis=0, axis_index_group...]
  transfers between devices with their start and end apart: 14 -> 24, of which waited for: 4 -> 7; matrix products, arithmetic and copies ran while one was open for 4% -> 3% of each run, Pallas kernels for 58% -> 57%
where the time goes in v6:
time: 270 us; the launch traced here: 271 us
  Pallas kernels  163 us (60%)
  waiting for transfers between devices  43 us (16%)
  starting transfers between devices  32.6 us (12%)
  blocking collectives  15.4 us (6%)
  other arithmetic  7.18 us (3%)
  local copies, waits for them, and re-layouts  6.2 us (2%)
    pallas_call x3, Pallas kernels, attend(): pl.pallas_call(functools.partial(attend_kernel, head), grid_spec=pltpu.Pr...  152 us
    ppermute x6, waiting for transfers between devices, sides(): return (lax.ppermute(block, 'head', down), lax.ppermute(block, 'head', up))  17.4 us
    all_to_all x1, blocking collectives, exchange(): lax.all_to_all(parts, BOTH, split_axis=0, concat_axis=0, axis_index_group...  15.4 us
    all_to_all x2, waiting for transfers between devices, exchange(): lax.all_to_all(parts, BOTH, split_axis=0, concat_axis=0, axis_index_group...  9.14 us
    pallas_call x3, Pallas kernels, pack(): pl.pallas_call(kernel, out_shape=jax.ShapeDtypeStruct((ZONES, rows, HEAD_...  9.05 us
    ppermute x6, starting transfers between devices, sides(): return (lax.ppermute(block, 'head', down), lax.ppermute(block, 'head', up))  8.16 us
    ppermute x3, waiting for transfers between devices, attended(): parts[2 * head + 1] = lax.ppermute(theirs, 'head', partner)  7.84 us
    all_to_all x2, starting transfers between devices, exchange(): lax.all_to_all(parts, BOTH, split_axis=0, concat_axis=0, axis_index_group...  7.27 us
  transfers between devices with their start and end apart: 24, of which 7 were waited for; matrix products, arithmetic and copies ran while one was open for 3% of the time, Pallas kernels for 57%

profile of v6, /device:TPU:25, one launch (start us, length us, event | category | flops | bytes accessed | tf_op | source)
XLA Modules:
  0.0 270.6 jit_solution(797010315855028665)
XLA Ops:
  0.0 3.1 %shard_map.64 = bf16[8,272,128]{2,1,0:T(8,128)(2,1)} custom-call(bf16[128,3072]{1,0:T(8,128)(2,1)} %queries_ref.2, bf16[128,3072]{1,0:T(8,128)(2,1)} %keys_ref.3, bf16[128,3072]{1,0:T(8,128)(2,1)} %values_ref.3, s32[1,128]{1,0:T(1,128)} %bitcast.55), custom_call_target="tpu_custom_call" | custom-call | tf_op jit(solution)/shard_map/pallas_call | solution.py:244
  3.1 15.4 %all_to_all.15 = bf16[8,272,128]{2,1,0:T(8,128)(2,1)} all-to-all(bf16[8,272,128]{2,1,0:T(8,128)(2,1)} %shard_map.64), channel_id=1, replica_groups={{0,16,32,48,64,80,96,112},{1,17,33,49,65,81,97,113},{2,18,34,50,66,82,9..., dimensions={0} | all-to-all | bytes 1114112 | tf_op jit(solution)/shard_map/all_to_all | solution.py:314
  18.6 0.5 collective-permute-start
  19.0 3.3 %shard_map.65 = bf16[8,896,128]{2,1,0:T(8,128)(2,1)} custom-call(bf16[128,3072]{1,0:T(8,128)(2,1)} %queries_ref.2, bf16[128,3072]{1,0:T(8,128)(2,1)} %keys_ref.3, bf16[128,3072]{1,0:T(8,128)(2,1)} %values_ref.3), custom_call_target="tpu_custom_call" | custom-call | tf_op jit(solution)/shard_map/pallas_call | solution.py:244
  22.3 3.6 %all-to-all-start.1 = ((bf16[8,896,128]{2,1,0:T(8,128)(2,1)}), bf16[8,896,128]{2,1,0:T(8,128)(2,1)S(1)}, u32[]{:S(2)}, u32[]{:S(2)}) async-start(bf16[8,896,128]{2,1,0:T(8,128)(2,1)} %shard_map.65), calls=%async_computation.1 | async-start | bytes 3670016 | tf_op jit(solution)/shard_map/all_to_all | solution.py:314
  26.0 2.3 collective-permute-start.1
  28.2 3.7 %collective-permute-done = bf16[8,272,128]{2,1,0:T(8,128)(2,1)} collective-permute-done((bf16[8,272,128]{2,1,0:T(8,128)(2,1)}, bf16[8,272,128]{2,1,0:T(8,128)(2,1)}, u32[]{:S(2)}, u32[]{:S(2)}) %collective-permute-start) | collective-permute-done | bytes 557088 | tf_op jit(solution)/shard_map/ppermute | solution.py:325
  32.0 0.0 collective-permute-start.2
  32.0 0.1 add_multiply_fusion
  32.0 0.1 broadcast_add_fusion
  32.1 0.1 fusion.12
  32.2 5.8 %collective-permute-done.1 = bf16[8,272,128]{2,1,0:T(8,128)(2,1)S(1)} collective-permute-done((bf16[8,272,128]{2,1,0:T(8,128)(2,1)}, bf16[8,272,128]{2,1,0:T(8,128)(2,1)S(1)}, u32[]{:S(2)}, u32[]{:S(2)}) %collective-permute-start.1) | collective-permute-done | bytes 557088 | tf_op jit(solution)/shard_map/ppermute | solution.py:325
  37.9 6.4 %collective-permute-done.2 = bf16[8,272,128]{2,1,0:T(8,128)(2,1)S(1)} collective-permute-done((bf16[8,272,128]{2,1,0:T(8,128)(2,1)}, bf16[8,272,128]{2,1,0:T(8,128)(2,1)S(1)}, u32[]{:S(2)}, u32[]{:S(2)}) %collective-permute-start.2) | collective-permute-done | bytes 557088 | tf_op jit(solution)/shard_map/ppermute | solution.py:339
  44.3 1.5 pad_maximum_fusion.refs_0_
  45.9 0.1 slice_reduce_fusion
  45.9 0.1 convert_reduce_fusion
  46.0 1.3 copy-done.3
  47.2 6.5 %collective-permute-start.5 = (f32[1,128]{1,0:T(1,128)S(1)}, f32[1,128]{1,0:T(1,128)S(1)}, u32[]{:S(2)}, u32[]{:S(2)}) collective-permute-start(f32[1,128]{1,0:T(1,128)S(1)} %compare_select_fusion.1), channel_id=1, source_target_pairs={{0,9},{1,8},{2,11},{3,10},{4,13},{5,12},{6,15},{7,14},{8,1},{9,0},... | collective-permute-start | bytes 1544 | tf_op jit(solution)/shard_map/ppermute | solution.py:351
  53.8 0.5 collective-permute-start.4
  54.3 0.1 fusion.18
  54.4 0.6 collective-permute-start.9
  55.0 0.9 fusion.19
  55.8 0.0 collective-permute-start.6
  55.8 2.7 collective-permute-start.7
  58.5 2.5 collective-permute-start.8
  61.0 0.1 select_reduce_fusion
  61.1 0.1 compare_convert_fusion
  61.2 0.1 fusion.15
  61.4 0.7 pad_add_fusion.info_ref
  62.0 0.6 fusion.13.end_ref
  62.6 7.9 %collective-permute-done.6 = bf16[8,256,128]{2,1,0:T(8,128)(2,1)S(1)} collective-permute-done((bf16[8,256,128]{2,1,0:T(8,128)(2,1)S(1)}, bf16[8,256,128]{2,1,0:T(8,128)(2,1)S(1)}, u32[]{:S(2)}, u32[]{:S(2)}) %collective-permute-start.6) | collective-permute-done | bytes 524320 | tf_op jit(solution)/shard_map/ppermute | solution.py:325
  70.5 0.1 collective-permute-start.12
  70.6 2.7 collective-permute-start.13
  73.3 1.1 collective-permute-start.11
  74.4 0.7 copy-done.16
  75.1 2.5 collective-permute-start.14
  77.6 50.5 %shard_map.66 = (bf16[8,144,128]{2,1,0:T(8,128)(2,1)}, bf16[8,144,128]{2,1,0:T(8,128)(2,1)}) custom-call(s32[13]{0:T(128)} %pad_add_fusion.info_ref, bf16[8,896,128]{2,1,0:T(8,128)(2,1)} %copy-done.1, bf16[8,128,128]{2,1,0:T(8,128)(2,1)} %copy-done.16, s32[8,1,256]{2,1,0:T(1,128)} %fusion.13.end_ref, bf16[4,8,272,128]{3,2,1,0:T(8,128)(2,1)} %copy-done.3, ...), custom_call_target="tpu_custom_call" | custom-call | flops 8589934592 | bytes 5242880 | tf_op jit(solution)/shard_map/pallas_call | solution.py:183
  128.2 0.8 copy-done.7
  129.0 1.8 pad_maximum_fusion.1.refs_0_
  130.9 0.1 collective-permute-start.15
  131.0 1.7 pad_maximum_fusion.2.refs_0_
  132.7 0.1 collective-permute-start.19
  132.8 0.1 collective-permute-start.18
  132.9 0.1 collective-permute-start.17
  133.0 2.2 collective-permute-done.15.refs_1_
  135.2 50.5 %shard_map.67 = (bf16[8,144,128]{2,1,0:T(8,128)(2,1)}, bf16[8,144,128]{2,1,0:T(8,128)(2,1)}) custom-call(s32[13]{0:T(128)} %pad_add_fusion.info_ref, bf16[8,896,128]{2,1,0:T(8,128)(2,1)} %copy-done.1, bf16[8,128,128]{2,1,0:T(8,128)(2,1)} %collective-permute-done.14.their_q, s32[8,1,256]{2,1,0:T(1,128)} %fusion.13.end_ref, ...), custom_call_target="tpu_custom_call" | custom-call | flops 8589934592 | bytes 5242880 | tf_op jit(solution)/shard_map/pallas_call | solution.py:183
  185.8 0.0 copy-start.14
  185.8 0.0 copy-start.17
  185.8 0.1 collective-permute-start.20
  185.9 0.1 collective-permute-start.10
  186.0 3.0 %collective-permute-start.16 = (bf16[8,144,128]{2,1,0:T(8,128)(2,1)}, bf16[8,144,128]{2,1,0:T(8,128)(2,1)}, u32[]{:S(2)}, u32[]{:S(2)}) collective-permute-start(bf16[8,144,128]{2,1,0:T(8,128)(2,1)} %get-tuple-element.62), channel_id=1, source_target_pairs={{0,1},{1,0},{2,3},{3,2},{4,5},{5,4},{6,7},{7,6},{8,9},{9,8},{10,11... | collective-permute-start | bytes 884744 | tf_op jit(solution)/shard_map/ppermute | solution.py:382
  189.0 0.8 copy-done.15
  189.8 50.5 %shard_map.68 = (bf16[8,144,128]{2,1,0:T(8,128)(2,1)}, bf16[8,144,128]{2,1,0:T(8,128)(2,1)}) custom-call(s32[13]{0:T(128)} %pad_add_fusion.info_ref, bf16[8,896,128]{2,1,0:T(8,128)(2,1)} %copy-done.1, bf16[8,128,128]{2,1,0:T(8,128)(2,1)} %collective-permute-done.18.their_q, s32[8,1,256]{2,1,0:T(1,128)} %fusion.13.end_ref, ...), custom_call_target="tpu_custom_call" | custom-call | flops 8589934592 | bytes 5242880 | tf_op jit(solution)/shard_map/pallas_call | solution.py:183
  240.3 0.1 collective-permute-start.21
  240.5 7.8 %collective-permute-done.21.refs_5_ = bf16[8,144,128]{2,1,0:T(8,128)(2,1)S(1)} collective-permute-done((bf16[8,144,128]{2,1,0:T(8,128)(2,1)}, bf16[8,144,128]{2,1,0:T(8,128)(2,1)S(1)}, u32[]{:S(2)}, u32[]{:S(2)}) %collective-permute-start.21) | collective-permute-done | bytes 294944 | tf_op jit(solution)/shard_map/ppermute | solution.py:382
  248.3 0.7 copy-done.11
  249.0 2.6 shard_map.69
  251.7 3.7 %all-to-all-start.2 = ((bf16[8,384,128]{2,1,0:T(8,128)(2,1)}), bf16[8,384,128]{2,1,0:T(8,128)(2,1)S(1)}, u32[]{:S(2)}, u32[]{:S(2)}) async-start(bf16[8,384,128]{2,1,0:T(8,128)(2,1)} %shard_map.69), calls=%async_computation.2 | async-start | bytes 1572864 | tf_op jit(solution)/shard_map/all_to_all | solution.py:314
  255.4 0.1 fusion.2
  255.5 0.3 fusion.4
  255.8 2.0 fusion.gate_ref
  257.8 9.1 %all-to-all-done.2.mixed_ref = bf16[8,384,128]{2,1,0:T(8,128)(2,1)S(1)} async-done(((bf16[8,384,128]{2,1,0:T(8,128)(2,1)}), bf16[8,384,128]{2,1,0:T(8,128)(2,1)S(1)}, u32[]{:S(2)}, u32[]{:S(2)}) %all-to-all-start.2) | async-done | bytes 786464 | tf_op jit(solution)/shard_map/all_to_all | solution.py:314
  267.0 0.9 copy-done.2
  267.9 2.7 %shard_map.70 = bf16[128,3072]{1,0:T(8,128)(2,1)} custom-call(f32[128,3072]{1,0:T(8,128)} %fusion.gate_ref, bf16[8,384,128]{2,1,0:T(8,128)(2,1)} %copy-done.2), custom_call_target="tpu_custom_call" | custom-call | tf_op jit(solution)/shard_map/pallas_call | solution.py:404
  (56 shorter events, 0.2 us)
Async XLA Ops:
  0.0 255.5 %copy-start = (bf16[256,3072]{1,0:T(8,128)(2,1)S(1)}, bf16[256,3072]{1,0:T(8,128)(2,1)}, u32[]{:S(2)}) copy-start(bf16[256,3072]{1,0:T(8,128)(2,1)} %param.11) | copy-start | bytes 4718596
  18.6 13.4 %collective-permute-start = (bf16[8,272,128]{2,1,0:T(8,128)(2,1)}, bf16[8,272,128]{2,1,0:T(8,128)(2,1)}, u32[]{:S(2)}, u32[]{:S(2)}) collective-permute-start(bf16[8,272,128]{2,1,0:T(8,128)(2,1)} %all_to_all.15), channel_id=1, source_target_pairs={{0,6},{1,7},{2,0},{3,1},{4,2},{5,3},{6,4},{7,5},{8,14},{9,15},{10,... | collective-permute-start | bytes 1671176 | tf_op jit(solution)/shard_map/ppermute | solution.py:325
  22.3 24.9 %all-to-all-start.1 = ((bf16[8,896,128]{2,1,0:T(8,128)(2,1)}), bf16[8,896,128]{2,1,0:T(8,128)(2,1)S(1)}, u32[]{:S(2)}, u32[]{:S(2)}) async-start(bf16[8,896,128]{2,1,0:T(8,128)(2,1)} %shard_map.65), calls=%async_computation.1 | async-start | bytes 3670016 | tf_op jit(solution)/shard_map/all_to_all | solution.py:314
  26.0 12.0 %collective-permute-start.1 = (bf16[8,272,128]{2,1,0:T(8,128)(2,1)}, bf16[8,272,128]{2,1,0:T(8,128)(2,1)S(1)}, u32[]{:S(2)}, u32[]{:S(2)}) collective-permute-start(bf16[8,272,128]{2,1,0:T(8,128)(2,1)} %all_to_all.15), channel_id=1, source_target_pairs={{0,2},{1,3},{2,4},{3,5},{4,6},{5,7},{6,0},{7,1},{8,10},{9,11},{10,... | collective-permute-start | bytes 1671176 | tf_op jit(solution)/shard_map/ppermute | solution.py:325
  32.0 12.4 %collective-permute-start.2 = (bf16[8,272,128]{2,1,0:T(8,128)(2,1)}, bf16[8,272,128]{2,1,0:T(8,128)(2,1)S(1)}, u32[]{:S(2)}, u32[]{:S(2)}) collective-permute-start(bf16[8,272,128]{2,1,0:T(8,128)(2,1)} %collective-permute-done), channel_id=1, source_target_pairs={{0,6},{1,7},{2,0},{3,1},{4,2},{5,3},{6,4},{7,5},{8,14},{9,15},{10,... | collective-permute-start | bytes 1671176 | tf_op jit(solution)/shard_map/ppermute | solution.py:339
  45.8 1.4 copy-start.3
  47.2 30.3 %copy-start.1 = (bf16[8,896,128]{2,1,0:T(8,128)(2,1)}, bf16[8,896,128]{2,1,0:T(8,128)(2,1)S(1)}, u32[]{:S(2)}) copy-start(bf16[8,896,128]{2,1,0:T(8,128)(2,1)S(1)} %all-to-all-done.1.own_q) | copy-start | bytes 5505028
  47.2 8.6 %collective-permute-start.5 = (f32[1,128]{1,0:T(1,128)S(1)}, f32[1,128]{1,0:T(1,128)S(1)}, u32[]{:S(2)}, u32[]{:S(2)}) collective-permute-start(f32[1,128]{1,0:T(1,128)S(1)} %compare_select_fusion.1), channel_id=1, source_target_pairs={{0,9},{1,8},{2,11},{3,10},{4,13},{5,12},{6,15},{7,14},{8,1},{9,0},... | collective-permute-start | bytes 1544 | tf_op jit(solution)/shard_map/ppermute | solution.py:351
  53.8 4.7 %collective-permute-start.4 = (f32[1,128]{1,0:T(1,128)S(1)}, f32[1,128]{1,0:T(1,128)S(1)}, u32[]{:S(2)}, u32[]{:S(2)}) collective-permute-start(f32[1,128]{1,0:T(1,128)S(1)} %compare_select_fusion.1), channel_id=1, source_target_pairs={{0,1},{1,0},{2,3},{3,2},{4,5},{5,4},{6,7},{7,6},{8,9},{9,8},{10,11... | collective-permute-start | bytes 1544 | tf_op jit(solution)/shard_map/ppermute | solution.py:350
  54.3 6.7 %collective-permute-start.3 = (f32[1,128]{1,0:T(1,128)S(1)}, f32[1,128]{1,0:T(1,128)S(1)}, u32[]{:S(2)}, u32[]{:S(2)}) collective-permute-start(f32[1,128]{1,0:T(1,128)S(1)} %compare_select_fusion.1), channel_id=1, source_target_pairs={{0,8},{8,0},{16,24},{24,16},{32,40},{40,32},{48,56},{56,48},{64,72... | collective-permute-start | bytes 1544 | tf_op jit(solution)/shard_map/ppermute | solution.py:349
  54.4 73.7 %copy-start.5 = (bf16[8,256,128]{2,1,0:T(8,128)(2,1)}, bf16[8,256,128]{2,1,0:T(8,128)(2,1)S(1)}, u32[]{:S(2)}) copy-start(bf16[8,256,128]{2,1,0:T(8,128)(2,1)S(1)} %get-tuple-element.44) | copy-start | bytes 1572868
  54.4 23.2 %collective-permute-start.9 = (bf16[4,8,272,128]{3,2,1,0:T(8,128)(2,1)}, bf16[4,8,272,128]{3,2,1,0:T(8,128)(2,1)}, u32[]{:S(2)}, u32[]{:S(2)}) collective-permute-start(bf16[4,8,272,128]{3,2,1,0:T(8,128)(2,1)} %copy-done.3), channel_id=1, source_target_pairs={{0,8},{8,0},{16,24},{24,16},{32,40},{40,32},{48,56},{56,48},{64,72... | collective-permute-start | bytes 6684680 | tf_op jit(solution)/shard_map/ppermute | solution.py:322
  55.8 14.7 %collective-permute-start.6 = (bf16[8,256,128]{2,1,0:T(8,128)(2,1)S(1)}, bf16[8,256,128]{2,1,0:T(8,128)(2,1)S(1)}, u32[]{:S(2)}, u32[]{:S(2)}) collective-permute-start(bf16[8,256,128]{2,1,0:T(8,128)(2,1)S(1)} %get-tuple-element.44), channel_id=1, source_target_pairs={{0,6},{1,7},{2,0},{3,1},{4,2},{5,3},{6,4},{7,5},{8,14},{9,15},{10,... | collective-permute-start | bytes 1572872 | tf_op jit(solution)/shard_map/ppermute | solution.py:325
  55.8 14.7 %collective-permute-start.7 = (bf16[8,256,128]{2,1,0:T(8,128)(2,1)S(1)}, bf16[8,256,128]{2,1,0:T(8,128)(2,1)S(1)}, u32[]{:S(2)}, u32[]{:S(2)}) collective-permute-start(bf16[8,256,128]{2,1,0:T(8,128)(2,1)S(1)} %get-tuple-element.44), channel_id=1, source_target_pairs={{0,2},{1,3},{2,4},{3,5},{4,6},{5,7},{6,0},{7,1},{8,10},{9,11},{10,... | collective-permute-start | bytes 1572872 | tf_op jit(solution)/shard_map/ppermute | solution.py:325
  58.5 15.9 %collective-permute-start.8 = (bf16[8,128,128]{2,1,0:T(8,128)(2,1)S(1)}, bf16[8,128,128]{2,1,0:T(8,128)(2,1)S(1)}, u32[]{:S(2)}, u32[]{:S(2)}) collective-permute-start(bf16[8,128,128]{2,1,0:T(8,128)(2,1)S(1)} %get-tuple-element.47), channel_id=1, source_target_pairs={{0,1},{1,0},{2,3},{3,2},{4,5},{5,4},{6,7},{7,6},{8,9},{9,8},{10,11... | collective-permute-start | bytes 786440 | tf_op jit(solution)/shard_map/ppermute | solution.py:356
  70.5 57.6 %copy-start.9 = (bf16[8,256,128]{2,1,0:T(8,128)(2,1)}, bf16[8,256,128]{2,1,0:T(8,128)(2,1)S(1)}, u32[]{:S(2)}) copy-start(bf16[8,256,128]{2,1,0:T(8,128)(2,1)S(1)} %collective-permute-done.6) | copy-start | bytes 1572868
  70.5 57.6 %copy-start.10 = (bf16[8,256,128]{2,1,0:T(8,128)(2,1)}, bf16[8,256,128]{2,1,0:T(8,128)(2,1)S(1)}, u32[]{:S(2)}) copy-start(bf16[8,256,128]{2,1,0:T(8,128)(2,1)S(1)} %collective-permute-done.7) | copy-start | bytes 1572868
  70.5 57.6 %collective-permute-start.12 = (bf16[8,256,128]{2,1,0:T(8,128)(2,1)S(1)}, bf16[8,256,128]{2,1,0:T(8,128)(2,1)}, u32[]{:S(2)}, u32[]{:S(2)}) collective-permute-start(bf16[8,256,128]{2,1,0:T(8,128)(2,1)S(1)} %get-tuple-element.54), channel_id=1, source_target_pairs={{0,6},{1,7},{2,0},{3,1},{4,2},{5,3},{6,4},{7,5},{8,14},{9,15},{10,... | collective-permute-start | bytes 1572872 | tf_op jit(solution)/shard_map/ppermute | solution.py:325
  70.6 57.6 %collective-permute-start.13 = (bf16[8,256,128]{2,1,0:T(8,128)(2,1)S(1)}, bf16[8,256,128]{2,1,0:T(8,128)(2,1)S(1)}, u32[]{:S(2)}, u32[]{:S(2)}) collective-permute-start(bf16[8,256,128]{2,1,0:T(8,128)(2,1)S(1)} %get-tuple-element.54), channel_id=1, source_target_pairs={{0,2},{1,3},{2,4},{3,5},{4,6},{5,7},{6,0},{7,1},{8,10},{9,11},{10,... | collective-permute-start | bytes 1572872 | tf_op jit(solution)/shard_map/ppermute | solution.py:325
  73.3 54.9 %collective-permute-start.11 = (bf16[8,256,128]{2,1,0:T(8,128)(2,1)S(1)}, bf16[8,256,128]{2,1,0:T(8,128)(2,1)}, u32[]{:S(2)}, u32[]{:S(2)}) collective-permute-start(bf16[8,256,128]{2,1,0:T(8,128)(2,1)S(1)} %collective-permute-done.7), channel_id=1, source_target_pairs={{0,2},{1,3},{2,4},{3,5},{4,6},{5,7},{6,0},{7,1},{8,10},{9,11},{10,... | collective-permute-start | bytes 1572872 | tf_op jit(solution)/shard_map/ppermute | solution.py:386
  74.4 0.7 copy-start.16
  75.1 53.1 %collective-permute-start.14 = (bf16[8,128,128]{2,1,0:T(8,128)(2,1)}, bf16[8,128,128]{2,1,0:T(8,128)(2,1)}, u32[]{:S(2)}, u32[]{:S(2)}) collective-permute-start(bf16[8,128,128]{2,1,0:T(8,128)(2,1)} %get-tuple-element.55), channel_id=1, source_target_pairs={{0,1},{1,0},{2,3},{3,2},{4,5},{5,4},{6,7},{7,6},{8,9},{9,8},{10,11... | collective-permute-start | bytes 786440 | tf_op jit(solution)/shard_map/ppermute | solution.py:389
  128.2 0.8 copy-start.7
  129.0 2.0 copy-start.8
  130.9 4.4 %copy-start.4 = (bf16[4,8,256,128]{3,2,1,0:T(8,128)(2,1)}, bf16[4,8,256,128]{3,2,1,0:T(8,128)(2,1)S(1)}, u32[]{:S(2)}) copy-start(bf16[4,8,256,128]{3,2,1,0:T(8,128)(2,1)S(1)} %pad_maximum_fusion.1.refs_0_) | copy-start | bytes 6291460
  130.9 2.0 copy-start.12
  130.9 4.4 %collective-permute-start.15 = (bf16[4,8,256,128]{3,2,1,0:T(8,128)(2,1)S(1)}, bf16[4,8,256,128]{3,2,1,0:T(8,128)(2,1)}, u32[]{:S(2)}, u32[]{:S(2)}) collective-permute-start(bf16[4,8,256,128]{3,2,1,0:T(8,128)(2,1)S(1)} %pad_maximum_fusion.1.refs_0_), channel_id=1, source_target_pairs={{0,8},{8,0},{16,24},{24,16},{32,40},{40,32},{48,56},{56,48},{64,72... | collective-permute-start | bytes 6291464 | tf_op jit(solution)/shard_map/ppermute | solution.py:322
  132.7 53.0 %copy-start.6 = (bf16[3,8,256,128]{3,2,1,0:T(8,128)(2,1)}, bf16[3,8,256,128]{3,2,1,0:T(8,128)(2,1)S(1)}, u32[]{:S(2)}) copy-start(bf16[3,8,256,128]{3,2,1,0:T(8,128)(2,1)S(1)} %pad_maximum_fusion.2.refs_0_) | copy-start | bytes 4718596
  132.7 56.2 %collective-permute-start.19 = (bf16[3,8,256,128]{3,2,1,0:T(8,128)(2,1)S(1)}, bf16[3,8,256,128]{3,2,1,0:T(8,128)(2,1)}, u32[]{:S(2)}, u32[]{:S(2)}) collective-permute-start(bf16[3,8,256,128]{3,2,1,0:T(8,128)(2,1)S(1)} %pad_maximum_fusion.2.refs_0_), channel_id=1, source_target_pairs={{0,8},{8,0},{16,24},{24,16},{32,40},{40,32},{48,56},{56,48},{64,72... | collective-permute-start | bytes 4718600 | tf_op jit(solution)/shard_map/ppermute | solution.py:322
  132.8 52.9 %collective-permute-start.18 = (bf16[8,128,128]{2,1,0:T(8,128)(2,1)S(1)}, bf16[8,128,128]{2,1,0:T(8,128)(2,1)}, u32[]{:S(2)}, u32[]{:S(2)}) collective-permute-start(bf16[8,128,128]{2,1,0:T(8,128)(2,1)S(1)} %copy-done.12), channel_id=1, source_target_pairs={{0,1},{1,0},{2,3},{3,2},{4,5},{5,4},{6,7},{7,6},{8,9},{9,8},{10,11... | collective-permute-start | bytes 786440 | tf_op jit(solution)/shard_map/ppermute | solution.py:397
  132.9 52.9 %collective-permute-start.17 = (bf16[8,256,128]{2,1,0:T(8,128)(2,1)}, bf16[8,256,128]{2,1,0:T(8,128)(2,1)S(1)}, u32[]{:S(2)}, u32[]{:S(2)}) collective-permute-start(bf16[8,256,128]{2,1,0:T(8,128)(2,1)} %collective-permute-done.12), channel_id=1, source_target_pairs={{0,6},{1,7},{2,0},{3,1},{4,2},{5,3},{6,4},{7,5},{8,14},{9,15},{10,... | collective-permute-start | bytes 1572872 | tf_op jit(solution)/shard_map/ppermute | solution.py:395
  185.8 3.2 %copy-start.14 = (bf16[8,256,128]{2,1,0:T(8,128)(2,1)}, bf16[8,256,128]{2,1,0:T(8,128)(2,1)S(1)}, u32[]{:S(2)}) copy-start(bf16[8,256,128]{2,1,0:T(8,128)(2,1)S(1)} %collective-permute-done.17) | copy-start | bytes 1572868
  185.8 54.6 %copy-start.17 = (s32[24]{0:T(128)S(1)}, s32[24]{0:T(128)}, u32[]{:S(2)}) copy-start(s32[24]{0:T(128)} %param.10) | copy-start | bytes 292
  185.8 3.1 %collective-permute-start.20 = (bf16[1,8,256,128]{3,2,1,0:T(8,128)(2,1)S(1)}, bf16[1,8,256,128]{3,2,1,0:T(8,128)(2,1)S(1)}, u32[]{:S(2)}, u32[]{:S(2)}) collective-permute-start(bf16[1,8,256,128]{3,2,1,0:T(8,128)(2,1)S(1)} %bitcast.56), channel_id=1, source_target_pairs={{0,8},{8,0},{16,24},{24,16},{32,40},{40,32},{48,56},{56,48},{64,72... | collective-permute-start | bytes 1572872 | tf_op jit(solution)/shard_map/ppermute | solution.py:322
  185.9 54.5 %collective-permute-start.10 = (bf16[8,144,128]{2,1,0:T(8,128)(2,1)}, bf16[8,144,128]{2,1,0:T(8,128)(2,1)}, u32[]{:S(2)}, u32[]{:S(2)}) collective-permute-start(bf16[8,144,128]{2,1,0:T(8,128)(2,1)} %get-tuple-element.51), channel_id=1, source_target_pairs={{0,1},{1,0},{2,3},{3,2},{4,5},{5,4},{6,7},{7,6},{8,9},{9,8},{10,11... | collective-permute-start | bytes 884744 | tf_op jit(solution)/shard_map/ppermute | solution.py:382
  186.0 54.4 %collective-permute-start.16 = (bf16[8,144,128]{2,1,0:T(8,128)(2,1)}, bf16[8,144,128]{2,1,0:T(8,128)(2,1)}, u32[]{:S(2)}, u32[]{:S(2)}) collective-permute-start(bf16[8,144,128]{2,1,0:T(8,128)(2,1)} %get-tuple-element.62), channel_id=1, source_target_pairs={{0,1},{1,0},{2,3},{3,2},{4,5},{5,4},{6,7},{7,6},{8,9},{9,8},{10,11... | collective-permute-start | bytes 884744 | tf_op jit(solution)/shard_map/ppermute | solution.py:382
  189.0 0.8 copy-start.15
  240.3 8.0 %collective-permute-start.21 = (bf16[8,144,128]{2,1,0:T(8,128)(2,1)}, bf16[8,144,128]{2,1,0:T(8,128)(2,1)S(1)}, u32[]{:S(2)}, u32[]{:S(2)}) collective-permute-start(bf16[8,144,128]{2,1,0:T(8,128)(2,1)} %get-tuple-element.72), channel_id=1, source_target_pairs={{0,1},{1,0},{2,3},{3,2},{4,5},{5,4},{6,7},{7,6},{8,9},{9,8},{10,11... | collective-permute-start | bytes 884744 | tf_op jit(solution)/shard_map/ppermute | solution.py:382
  248.3 0.7 copy-start.11
  251.7 4.1 %copy-start.13 = (s32[128]{0:T(128)S(1)}, s32[128]{0:T(128)}, u32[]{:S(2)}) copy-start(s32[128]{0:T(128)} %param.9) | copy-start | bytes 1540
  251.7 15.3 %all-to-all-start.2 = ((bf16[8,384,128]{2,1,0:T(8,128)(2,1)}), bf16[8,384,128]{2,1,0:T(8,128)(2,1)S(1)}, u32[]{:S(2)}, u32[]{:S(2)}) async-start(bf16[8,384,128]{2,1,0:T(8,128)(2,1)} %shard_map.69), calls=%async_computation.2 | async-start | bytes 1572864 | tf_op jit(solution)/shard_map/all_to_all | solution.py:314
  267.0 0.9 copy-start.2

commit v7 on v6

--- a/solution.py
+++ b/solution.py
@@ -15,9 +15,9 @@
 ZONES = 8
 SEGMENT = 2 * HEAD_DIM
 KEYS = 8192
-WIDTH = 512
-SUB = 256
-ITEMS = 4
+WIDTH = 256
+ITEMS = 8
+FIRST_ZONES = 2
 K_NORM, Q_NORM = 32, 40
 NOTE = 16
 PLAIN_LIMIT = 70.0
@@ -35,21 +35,18 @@
     blocks = ZONES
 
     copies = []
-    if len(sources) == 1:
-        whole = sources[0].at[:, :, :, pl.ds(0, 2 * HEAD_DIM)]
-        copies.append(pltpu.make_async_copy(whole, kv_ref, sems.at[0]))
-        sources = ()
     half = len(sources) // 2
-    for j, (group, c) in enumerate(((sources[:half], core), (sources[half:], 1 - core))):
-        pieces = [src.at[k] for src in group for k in range(src.shape[0])]
-        for k, (piece, step) in enumerate(zip(pieces, (0, 1, 3, 2))):
-            copies.append(
-                pltpu.make_async_copy(
-                    piece.at[:, pl.ds(0, 2 * HEAD_DIM)],
-                    kv_ref.at[(rank + step) % 4, c],
-                    sems.at[4 * j + k],
+    for j, zones in enumerate((pl.ds(0, FIRST_ZONES), pl.ds(FIRST_ZONES, ZONES - FIRST_ZONES))):
+        for group, c in ((sources[:half], core), (sources[half:], 1 - core)):
+            pieces = [src.at[k] for src in group for k in range(src.shape[0])]
+            for piece, step in zip(pieces, (0, 1, 3, 2)):
+                copies.append(
+                    pltpu.make_async_copy(
+                        piece.at[zones, pl.ds(0, 2 * HEAD_DIM)],
+                        kv_ref.at[(rank + step) % 4, c, zones],
+                        sems.at[len(copies)],
+                    )
                 )
-            )
     for copy in copies:
         copy.start()
 
@@ -58,41 +55,36 @@
     acc_ref[...] = jnp.zeros_like(acc_ref)
     top_ref[...] = jnp.zeros_like(top_ref)
     ones = jnp.ones((NOTE, WIDTH), jnp.bfloat16)
-    for copy in copies:
+    for copy in copies[: len(copies) // 2]:
         copy.wait()
 
     def part(i, rows):
-        return kv_ref[:, i % 2, i // 2, rows]
+        return kv_ref[pl.ds((i % 2) * 2, 2), (i // 2) % 2, i // 4, rows]
 
     def keys_at(i):
         return part(i, slice(0, HEAD_DIM)).reshape(WIDTH, HEAD_DIM)
 
     def values_at(i):
         block = part(i, slice(HEAD_DIM, 2 * HEAD_DIM))
-        block = jnp.concatenate([block[y] for y in range(4)], axis=1)
-        return jnp.concatenate([block, ones], axis=0)
+        return jnp.concatenate([jnp.concatenate([block[0], block[1]], axis=1), ones], axis=0)
 
     def visible_at(r, i):
         row = lax.broadcasted_iota(jnp.int32, (WIDTH, SEGMENT), 0)
         return row < end_ref[r] - i * WIDTH
 
-    def score(item, half):
+    def score(item):
         r, i = item
-        keys = kv_ref[2 * half : 2 * half + 2, i % 2, i // 2, :HEAD_DIM].reshape(SUB, HEAD_DIM)
-        return dot(keys, qt_ref[jnp.minimum(r, blocks - 1)])
-
-    def weigh(slot, item, half, scores):
+        return dot(keys_at(i), qt_ref[jnp.minimum(r, blocks - 1)])
+
+    def weigh(slot, item, scores):
         r, i = item
-        row = lax.broadcasted_iota(jnp.int32, (SUB, SEGMENT), 0)
-        visible = row < end_ref[jnp.minimum(r, blocks - 1)] - (i * WIDTH + half * SUB)
-        weights = jnp.where(visible, jnp.exp2(scores * SCALE_LOG2), 0.0)
-        weight_ref[slot, half * SUB : (half + 1) * SUB] = weights.astype(jnp.bfloat16)
-
-    def absorb(slot, item, half):
+        weights = jnp.exp2(scores * SCALE_LOG2)
+        weights = jnp.where(visible_at(jnp.minimum(r, blocks - 1), i), weights, 0.0)
+        weight_ref[slot] = weights.astype(jnp.bfloat16)
+
+    def absorb(slot, item):
         r, i = item
-        block = kv_ref[2 * half : 2 * half + 2, i % 2, i // 2, HEAD_DIM:]
-        values = jnp.concatenate([jnp.concatenate([block[0], block[1]], axis=1), ones[:, :SUB]], axis=0)
-        acc_ref[r] += dot(values, weight_ref[slot, half * SUB : (half + 1) * SUB])
+        acc_ref[r] += dot(values_at(i), weight_ref[slot])
 
     def careful(r, i):
         scores = dot(keys_at(i), qt_ref[r]) * SCALE_LOG2
@@ -107,7 +99,6 @@
     def count(r):
         return info_ref[2 + r]
 
-    parts = [(slot, half) for slot in range(ITEMS) for half in range(2)]
     plain = info_ref[2 + blocks + head] == 1
 
     @pl.when(plain)
@@ -126,26 +117,30 @@
 
         def step(_, items):
             later = run(following(items[-1]))
-            scores = score(later[0], 0)
-            for slot, half in parts:
+            scores = score(later[0])
+            for slot in range(ITEMS):
                 now = scores
-                if (slot, half) != parts[-1]:
-                    scores = score(later[slot + half], 1 - half)
-                absorb(slot, items[slot], half)
-                weigh(slot, later[slot], half, now)
+                if slot + 1 < ITEMS:
+                    scores = score(later[slot + 1])
+                absorb(slot, items[slot])
+                weigh(slot, later[slot], now)
             return later
 
         items = run((jnp.int32(0), jnp.int32(0)))
-        for slot, half in parts:
-            weigh(slot, items[slot], half, score(items[slot], half))
+        for slot in range(ITEMS):
+            weigh(slot, items[slot], score(items[slot]))
+        for copy in copies[len(copies) // 2 :]:
+            copy.wait()
         total = sum(count(r) for r in range(blocks))
         items = lax.fori_loop(0, (total + ITEMS - 1) // ITEMS - 1, step, items)
-        for slot, half in parts:
-            absorb(slot, items[slot], half)
+        for slot in range(ITEMS):
+            absorb(slot, items[slot])
 
     @pl.when(jnp.logical_not(plain))
     def _():
         top_ref[...] = jnp.full_like(top_ref, LOW)
+        for copy in copies[len(copies) // 2 :]:
+            copy.wait()
 
         def over_block(r, carry):
             def over_chunk(i, carry):
@@ -194,7 +189,7 @@
                 pltpu.VMEM((ITEMS, WIDTH, SEGMENT), jnp.bfloat16),
                 pltpu.VMEM((ZONES + 1, HEAD_DIM + NOTE, SEGMENT), jnp.float32),
                 pltpu.VMEM((ZONES, 8, SEGMENT), jnp.float32),
-                pltpu.SemaphoreType.DMA((8,)),
+                pltpu.SemaphoreType.DMA((16,)),
             ],
         ),
         out_shape=[out, out],
@@ -344,17 +339,18 @@
 
     note = combined(near[:, :, pair].reshape(-1, HEAD_DIM).astype(jnp.float32))[None]
     rest, near, note = after(rest, near, note)
+    own_q = [rest[:, start : start + HEAD_DIM] for start in range(2 * pair, rest.shape[1], HEAD_DIM)]
+    own_q[0], block_one, block_two = after(own_q[0], rest[:, :pair], rest[:, pair : 2 * pair])
+    above, below = sides(block_one)
+    their_q = [lax.ppermute(own_q[0], "head", partner), None, None]
+    near, far = swapped(near)
+    note, their_q[0] = after(note, their_q[0])
     notes = [
         note,
         lax.ppermute(note, "span", core_swap),
         lax.ppermute(note, "head", partner),
         lax.ppermute(note, BOTH, other),
     ]
-    near, far = swapped(near)
-    own_q = [rest[:, start : start + HEAD_DIM] for start in range(2 * pair, rest.shape[1], HEAD_DIM)]
-    own_q[0], block_one, block_two = after(own_q[0], rest[:, :pair], rest[:, pair : 2 * pair])
-    their_q = [lax.ppermute(own_q[0], "head", partner), None, None]
-    above, below = sides(block_one)
     note = combined(jnp.concatenate(notes))
     squares = note[K_NORM : K_NORM + heads] * note[Q_NORM : Q_NORM + heads]
     plain = (squares * (1.05 * SCALE**2) < PLAIN_LIMIT**2).astype(jnp.int32)

time: 270 us -> 337 us (1.25)
  Pallas kernels: 163 us -> 226 us
  starting transfers between devices: 32.6 us -> 36.9 us
    pallas_call x3, Pallas kernels: 152 us -> 214 us  [attend(): pl.pallas_call(functools.partial(attend_kernel, head), grid_spec=pltpu.Pr...]
    ppermute x4, starting transfers between devices: 0.84 us -> 4.8 us  [swapped(): return (block, lax.ppermute(block, 'span', core_swap))]
  transfers between devices with their start and end apart: 24 -> 24, of which waited for: 7 -> 9; matrix products, arithmetic and copies ran while one was open for 3% -> 2% of each run, Pallas kernels for 57% -> 64%
where the time goes in v7:
time: 337 us; the launch traced here: 338 us
  Pallas kernels  226 us (67%)
  waiting for transfers between devices  43.2 us (13%)
  starting transfers between devices  36.9 us (11%)
  blocking collectives  15.4 us (5%)
  other arithmetic  7.14 us (2%)
  local copies, waits for them, and re-layouts  6.74 us (2%)
    pallas_call x3, Pallas kernels, attend(): pl.pallas_call(functools.partial(attend_kernel, head), grid_spec=pltpu.Pr...  214 us
    ppermute x6, waiting for transfers between devices, sides(): return (lax.ppermute(block, 'head', down), lax.ppermute(block, 'head', up))  19.2 us
    all_to_all x1, blocking collectives, exchange(): lax.all_to_all(parts, BOTH, split_axis=0, concat_axis=0, axis_index_group...  15.4 us
    pallas_call x3, Pallas kernels, pack(): pl.pallas_call(kernel, out_shape=jax.ShapeDtypeStruct((ZONES, rows, HEAD_...  9.06 us
    ppermute x1, starting transfers between devices, per_device(): lax.ppermute(note, BOTH, other)  7.6 us
    ppermute x6, starting transfers between devices, sides(): return (lax.ppermute(block, 'head', down), lax.ppermute(block, 'head', up))  7.53 us
    all_to_all x2, starting transfers between devices, exchange(): lax.all_to_all(parts, BOTH, split_axis=0, concat_axis=0, axis_index_group...  7.27 us
    ppermute x3, waiting for transfers between devices, attended(): parts[2 * head + 1] = lax.ppermute(theirs, 'head', partner)  7.2 us
  transfers between devices with their start and end apart: 24, of which 9 were waited for; matrix products, arithmetic and copies ran while one was open for 2% of the time, Pallas kernels for 64%

profile of v7, /device:TPU:25, one launch (start us, length us, event | category | flops | bytes accessed | tf_op | source)
XLA Modules:
  0.0 338.0 jit_solution(15110839085395418135)
XLA Ops:
  0.0 3.1 shard_map.64
  3.1 15.4 %all_to_all.15 = bf16[8,272,128]{2,1,0:T(8,128)(2,1)} all-to-all(bf16[8,272,128]{2,1,0:T(8,128)(2,1)} %shard_map.64), channel_id=1, replica_groups={{0,16,32,48,64,80,96,112},{1,17,33,49,65,81,97,113},{2,18,34,50,66,82,9..., dimensions={0} | all-to-all | bytes 1114112 | tf_op jit(solution)/shard_map/all_to_all | solution.py:309
  18.6 0.5 collective-permute-start
  19.0 3.3 shard_map.65
  22.3 3.6 %all-to-all-start.1 = ((bf16[8,896,128]{2,1,0:T(8,128)(2,1)}), bf16[8,896,128]{2,1,0:T(8,128)(2,1)S(1)}, u32[]{:S(2)}, u32[]{:S(2)}) async-start(bf16[8,896,128]{2,1,0:T(8,128)(2,1)} %shard_map.65), calls=%async_computation.1 | async-start | bytes 3670016 | tf_op jit(solution)/shard_map/all_to_all | solution.py:309
  25.9 2.3 collective-permute-start.1
  28.2 3.8 %collective-permute-done = bf16[8,272,128]{2,1,0:T(8,128)(2,1)} collective-permute-done((bf16[8,272,128]{2,1,0:T(8,128)(2,1)}, bf16[8,272,128]{2,1,0:T(8,128)(2,1)}, u32[]{:S(2)}, u32[]{:S(2)}) %collective-permute-start) | collective-permute-done | bytes 557088 | tf_op jit(solution)/shard_map/ppermute | solution.py:320
  32.0 5.9 %collective-permute-done.1 = bf16[8,272,128]{2,1,0:T(8,128)(2,1)} collective-permute-done((bf16[8,272,128]{2,1,0:T(8,128)(2,1)}, bf16[8,272,128]{2,1,0:T(8,128)(2,1)}, u32[]{:S(2)}, u32[]{:S(2)}) %collective-permute-start.1) | collective-permute-done | bytes 557088 | tf_op jit(solution)/shard_map/ppermute | solution.py:320
  37.9 6.5 %collective-permute-done.2 = bf16[8,272,128]{2,1,0:T(8,128)(2,1)} collective-permute-done((bf16[8,272,128]{2,1,0:T(8,128)(2,1)}, bf16[8,272,128]{2,1,0:T(8,128)(2,1)}, u32[]{:S(2)}, u32[]{:S(2)}) %collective-permute-start.2) | collective-permute-done | bytes 557088 | tf_op jit(solution)/shard_map/ppermute | solution.py:334
  44.4 1.8 pad_maximum_fusion.refs_0_
  46.3 0.1 slice_reduce_fusion
  46.3 0.1 convert_reduce_fusion
  46.4 1.3 copy-done.3
  47.7 1.0 fusion.19
  48.6 1.1 fusion.18
  49.7 2.5 collective-permute-start.3
  52.2 0.1 add_multiply_fusion
  52.3 0.1 broadcast_add_fusion
  52.4 4.4 %collective-permute-start.9 = (bf16[4,8,272,128]{3,2,1,0:T(8,128)(2,1)}, bf16[4,8,272,128]{3,2,1,0:T(8,128)(2,1)}, u32[]{:S(2)}, u32[]{:S(2)}) collective-permute-start(bf16[4,8,272,128]{3,2,1,0:T(8,128)(2,1)} %copy-done.3), channel_id=1, source_target_pairs={{0,8},{8,0},{16,24},{24,16},{32,40},{40,32},{48,56},{56,48},{64,72... | collective-permute-start | bytes 6684680 | tf_op jit(solution)/shard_map/ppermute | solution.py:317
  56.7 0.0 collective-permute-done.3.their_q
  56.8 7.6 %collective-permute-start.6 = (f32[1,128]{1,0:T(1,128)S(1)}, f32[1,128]{1,0:T(1,128)S(1)}, u32[]{:S(2)}, u32[]{:S(2)}) collective-permute-start(f32[1,128]{1,0:T(1,128)S(1)} %compare_select_fusion.1), channel_id=1, source_target_pairs={{0,9},{1,8},{2,11},{3,10},{4,13},{5,12},{6,15},{7,14},{8,1},{9,0},... | collective-permute-start | bytes 1544 | tf_op jit(solution)/shard_map/ppermute | solution.py:352
  64.4 0.5 collective-permute-start.5
  64.8 0.1 fusion.12
  64.9 0.0 collective-permute-start.7
  64.9 0.6 collective-permute-done.6
  65.6 2.0 collective-permute-start.8
  67.6 0.6 collective-permute-done.5
  68.3 0.1 select_reduce_fusion
  68.4 0.1 compare_convert_fusion
  68.5 0.1 fusion.15
  68.6 0.6 pad_add_fusion.info_ref
  69.2 0.6 fusion.13.end_ref
  69.8 9.5 %collective-permute-done.7 = bf16[8,256,128]{2,1,0:T(8,128)(2,1)S(1)} collective-permute-done((bf16[8,256,128]{2,1,0:T(8,128)(2,1)}, bf16[8,256,128]{2,1,0:T(8,128)(2,1)S(1)}, u32[]{:S(2)}, u32[]{:S(2)}) %collective-permute-start.7) | collective-permute-done | bytes 524320 | tf_op jit(solution)/shard_map/ppermute | solution.py:320
  79.3 0.1 collective-permute-start.12
  79.4 2.7 collective-permute-start.13
  82.1 1.1 collective-permute-start.11
  83.2 2.5 collective-permute-start.14
  85.7 71.4 %shard_map.66 = (bf16[8,144,128]{2,1,0:T(8,128)(2,1)}, bf16[8,144,128]{2,1,0:T(8,128)(2,1)}) custom-call(s32[13]{0:T(128)} %pad_add_fusion.info_ref, bf16[8,896,128]{2,1,0:T(8,128)(2,1)} %copy-done.1, bf16[8,128,128]{2,1,0:T(8,128)(2,1)} %collective-permute-done.3.their_q, s32[8,1,256]{2,1,0:T(1,128)} %fusion.13.end_ref, bf16[4,8,272,128]{3,2,1,0:T(8,128)(2,1)} %copy-done.3, ...), custom_call_target="tpu_custom_call" | custom-call | flops 8589934592 | bytes 5242880 | tf_op jit(solution)/shard_map/pallas_call | solution.py:178
  157.1 0.8 copy-done.7
  157.9 0.2 copy-done.9
  158.1 1.7 pad_maximum_fusion.1.refs_0_
  159.9 0.1 collective-permute-start.15
  160.0 1.6 pad_maximum_fusion.2.refs_0_
  161.6 0.3 collective-permute-start.19
  161.9 2.4 collective-permute-done.15.refs_1_
  164.3 71.4 %shard_map.67 = (bf16[8,144,128]{2,1,0:T(8,128)(2,1)}, bf16[8,144,128]{2,1,0:T(8,128)(2,1)}) custom-call(s32[13]{0:T(128)} %pad_add_fusion.info_ref, bf16[8,896,128]{2,1,0:T(8,128)(2,1)} %copy-done.1, bf16[8,128,128]{2,1,0:T(8,128)(2,1)} %collective-permute-done.14.their_q, s32[8,1,256]{2,1,0:T(1,128)} %fusion.13.end_ref, ...), custom_call_target="tpu_custom_call" | custom-call | flops 8589934592 | bytes 5242880 | tf_op jit(solution)/shard_map/pallas_call | solution.py:178
  235.7 0.0 copy-start.18
  235.7 0.0 copy-start.22
  235.7 0.1 collective-permute-start.20
  235.8 0.1 collective-permute-start.10
  235.9 3.0 collective-permute-start.16
  238.9 0.8 copy-done.19
  239.7 71.4 %shard_map.68 = (bf16[8,144,128]{2,1,0:T(8,128)(2,1)}, bf16[8,144,128]{2,1,0:T(8,128)(2,1)}) custom-call(s32[13]{0:T(128)} %pad_add_fusion.info_ref, bf16[8,896,128]{2,1,0:T(8,128)(2,1)} %copy-done.1, bf16[8,128,128]{2,1,0:T(8,128)(2,1)} %copy-done.21, s32[8,1,256]{2,1,0:T(1,128)} %fusion.13.end_ref, bf16[3,8,256,128]{3,2,1,0:T(8,128)(2,1)} %pad_maximum_fusion.2.refs_0_, ...), custom_call_target="tpu_custom_call" | custom-call | flops 8589934592 | bytes 5242880 | tf_op jit(solution)/shard_map/pallas_call | solution.py:178
  311.0 0.1 collective-permute-start.21
  311.2 7.2 %collective-permute-done.21.refs_5_ = bf16[8,144,128]{2,1,0:T(8,128)(2,1)S(1)} collective-permute-done((bf16[8,144,128]{2,1,0:T(8,128)(2,1)}, bf16[8,144,128]{2,1,0:T(8,128)(2,1)S(1)}, u32[]{:S(2)}, u32[]{:S(2)}) %collective-permute-start.21) | collective-permute-done | bytes 294944 | tf_op jit(solution)/shard_map/ppermute | solution.py:378
  318.4 0.7 copy-done.15
  319.1 2.6 shard_map.69
  321.8 3.7 %all-to-all-start.2 = ((bf16[8,384,128]{2,1,0:T(8,128)(2,1)}), bf16[8,384,128]{2,1,0:T(8,128)(2,1)S(1)}, u32[]{:S(2)}, u32[]{:S(2)}) async-start(bf16[8,384,128]{2,1,0:T(8,128)(2,1)} %shard_map.69), calls=%async_computation.2 | async-start | bytes 1572864 | tf_op jit(solution)/shard_map/all_to_all | solution.py:309
  325.5 0.1 fusion.2
  325.6 0.3 fusion.4
  325.9 2.0 fusion.gate_ref
  327.9 6.5 %all-to-all-done.2.mixed_ref = bf16[8,384,128]{2,1,0:T(8,128)(2,1)S(1)} async-done(((bf16[8,384,128]{2,1,0:T(8,128)(2,1)}), bf16[8,384,128]{2,1,0:T(8,128)(2,1)S(1)}, u32[]{:S(2)}, u32[]{:S(2)}) %all-to-all-start.2) | async-done | bytes 786464 | tf_op jit(solution)/shard_map/all_to_all | solution.py:309
  334.4 0.9 copy-done.2
  335.3 2.7 shard_map.70
  (66 shorter events, 0.2 us)
Async XLA Ops:
  0.0 325.6 %copy-start = (bf16[256,3072]{1,0:T(8,128)(2,1)S(1)}, bf16[256,3072]{1,0:T(8,128)(2,1)}, u32[]{:S(2)}) copy-start(bf16[256,3072]{1,0:T(8,128)(2,1)} %param.11) | copy-start | bytes 4718596
  18.6 13.4 %collective-permute-start = (bf16[8,272,128]{2,1,0:T(8,128)(2,1)}, bf16[8,272,128]{2,1,0:T(8,128)(2,1)}, u32[]{:S(2)}, u32[]{:S(2)}) collective-permute-start(bf16[8,272,128]{2,1,0:T(8,128)(2,1)} %all_to_all.15), channel_id=1, source_target_pairs={{0,6},{1,7},{2,0},{3,1},{4,2},{5,3},{6,4},{7,5},{8,14},{9,15},{10,... | collective-permute-start | bytes 1671176 | tf_op jit(solution)/shard_map/ppermute | solution.py:320
  22.3 25.4 %all-to-all-start.1 = ((bf16[8,896,128]{2,1,0:T(8,128)(2,1)}), bf16[8,896,128]{2,1,0:T(8,128)(2,1)S(1)}, u32[]{:S(2)}, u32[]{:S(2)}) async-start(bf16[8,896,128]{2,1,0:T(8,128)(2,1)} %shard_map.65), calls=%async_computation.1 | async-start | bytes 3670016 | tf_op jit(solution)/shard_map/all_to_all | solution.py:309
  25.9 12.0 %collective-permute-start.1 = (bf16[8,272,128]{2,1,0:T(8,128)(2,1)}, bf16[8,272,128]{2,1,0:T(8,128)(2,1)}, u32[]{:S(2)}, u32[]{:S(2)}) collective-permute-start(bf16[8,272,128]{2,1,0:T(8,128)(2,1)} %all_to_all.15), channel_id=1, source_target_pairs={{0,2},{1,3},{2,4},{3,5},{4,6},{5,7},{6,0},{7,1},{8,10},{9,11},{10,... | collective-permute-start | bytes 1671176 | tf_op jit(solution)/shard_map/ppermute | solution.py:320
  32.0 12.5 %collective-permute-start.2 = (bf16[8,272,128]{2,1,0:T(8,128)(2,1)}, bf16[8,272,128]{2,1,0:T(8,128)(2,1)}, u32[]{:S(2)}, u32[]{:S(2)}) collective-permute-start(bf16[8,272,128]{2,1,0:T(8,128)(2,1)} %collective-permute-done), channel_id=1, source_target_pairs={{0,6},{1,7},{2,0},{3,1},{4,2},{5,3},{6,4},{7,5},{8,14},{9,15},{10,... | collective-permute-start | bytes 1671176 | tf_op jit(solution)/shard_map/ppermute | solution.py:334
  46.3 1.4 copy-start.3
  47.7 38.0 %copy-start.1 = (bf16[8,896,128]{2,1,0:T(8,128)(2,1)}, bf16[8,896,128]{2,1,0:T(8,128)(2,1)S(1)}, u32[]{:S(2)}) copy-start(bf16[8,896,128]{2,1,0:T(8,128)(2,1)S(1)} %all-to-all-done.1.own_q) | copy-start | bytes 5505028
  49.7 7.0 %collective-permute-start.3 = (bf16[8,128,128]{2,1,0:T(8,128)(2,1)}, bf16[8,128,128]{2,1,0:T(8,128)(2,1)}, u32[]{:S(2)}, u32[]{:S(2)}) collective-permute-start(bf16[8,128,128]{2,1,0:T(8,128)(2,1)} %get-tuple-element.45), channel_id=1, source_target_pairs={{0,1},{1,0},{2,3},{3,2},{4,5},{5,4},{6,7},{7,6},{8,9},{9,8},{10,11... | collective-permute-start | bytes 786440 | tf_op jit(solution)/shard_map/ppermute | solution.py:345
  52.4 33.3 %collective-permute-start.9 = (bf16[4,8,272,128]{3,2,1,0:T(8,128)(2,1)}, bf16[4,8,272,128]{3,2,1,0:T(8,128)(2,1)}, u32[]{:S(2)}, u32[]{:S(2)}) collective-permute-start(bf16[4,8,272,128]{3,2,1,0:T(8,128)(2,1)} %copy-done.3), channel_id=1, source_target_pairs={{0,8},{8,0},{16,24},{24,16},{32,40},{40,32},{48,56},{56,48},{64,72... | collective-permute-start | bytes 6684680 | tf_op jit(solution)/shard_map/ppermute | solution.py:317
  56.8 8.8 %collective-permute-start.6 = (f32[1,128]{1,0:T(1,128)S(1)}, f32[1,128]{1,0:T(1,128)S(1)}, u32[]{:S(2)}, u32[]{:S(2)}) collective-permute-start(f32[1,128]{1,0:T(1,128)S(1)} %compare_select_fusion.1), channel_id=1, source_target_pairs={{0,9},{1,8},{2,11},{3,10},{4,13},{5,12},{6,15},{7,14},{8,1},{9,0},... | collective-permute-start | bytes 1544 | tf_op jit(solution)/shard_map/ppermute | solution.py:352
  64.4 3.9 %collective-permute-start.5 = (f32[1,128]{1,0:T(1,128)S(1)}, f32[1,128]{1,0:T(1,128)S(1)}, u32[]{:S(2)}, u32[]{:S(2)}) collective-permute-start(f32[1,128]{1,0:T(1,128)S(1)} %compare_select_fusion.1), channel_id=1, source_target_pairs={{0,1},{1,0},{2,3},{3,2},{4,5},{5,4},{6,7},{7,6},{8,9},{9,8},{10,11... | collective-permute-start | bytes 1544 | tf_op jit(solution)/shard_map/ppermute | solution.py:351
  64.8 3.4 %collective-permute-start.4 = (f32[1,128]{1,0:T(1,128)S(1)}, f32[1,128]{1,0:T(1,128)S(1)}, u32[]{:S(2)}, u32[]{:S(2)}) collective-permute-start(f32[1,128]{1,0:T(1,128)S(1)} %compare_select_fusion.1), channel_id=1, source_target_pairs={{0,8},{8,0},{16,24},{24,16},{32,40},{40,32},{48,56},{56,48},{64,72... | collective-permute-start | bytes 1544 | tf_op jit(solution)/shard_map/ppermute | solution.py:350
  64.9 14.4 %collective-permute-start.7 = (bf16[8,256,128]{2,1,0:T(8,128)(2,1)}, bf16[8,256,128]{2,1,0:T(8,128)(2,1)S(1)}, u32[]{:S(2)}, u32[]{:S(2)}) collective-permute-start(bf16[8,256,128]{2,1,0:T(8,128)(2,1)} %get-tuple-element.48), channel_id=1, source_target_pairs={{0,6},{1,7},{2,0},{3,1},{4,2},{5,3},{6,4},{7,5},{8,14},{9,15},{10,... | collective-permute-start | bytes 1572872 | tf_op jit(solution)/shard_map/ppermute | solution.py:320
  65.6 13.8 %collective-permute-start.8 = (bf16[8,256,128]{2,1,0:T(8,128)(2,1)}, bf16[8,256,128]{2,1,0:T(8,128)(2,1)S(1)}, u32[]{:S(2)}, u32[]{:S(2)}) collective-permute-start(bf16[8,256,128]{2,1,0:T(8,128)(2,1)} %get-tuple-element.48), channel_id=1, source_target_pairs={{0,2},{1,3},{2,4},{3,5},{4,6},{5,7},{6,0},{7,1},{8,10},{9,11},{10,... | collective-permute-start | bytes 1572872 | tf_op jit(solution)/shard_map/ppermute | solution.py:320
  79.3 77.7 %copy-start.11 = (bf16[8,256,128]{2,1,0:T(8,128)(2,1)}, bf16[8,256,128]{2,1,0:T(8,128)(2,1)S(1)}, u32[]{:S(2)}) copy-start(bf16[8,256,128]{2,1,0:T(8,128)(2,1)S(1)} %collective-permute-done.7) | copy-start | bytes 1572868
  79.3 77.7 %copy-start.12 = (bf16[8,256,128]{2,1,0:T(8,128)(2,1)}, bf16[8,256,128]{2,1,0:T(8,128)(2,1)S(1)}, u32[]{:S(2)}) copy-start(bf16[8,256,128]{2,1,0:T(8,128)(2,1)S(1)} %collective-permute-done.8) | copy-start | bytes 1572868
  79.3 77.8 %collective-permute-start.12 = (bf16[8,256,128]{2,1,0:T(8,128)(2,1)}, bf16[8,256,128]{2,1,0:T(8,128)(2,1)S(1)}, u32[]{:S(2)}, u32[]{:S(2)}) collective-permute-start(bf16[8,256,128]{2,1,0:T(8,128)(2,1)} %get-tuple-element.58), channel_id=1, source_target_pairs={{0,6},{1,7},{2,0},{3,1},{4,2},{5,3},{6,4},{7,5},{8,14},{9,15},{10,... | collective-permute-start | bytes 1572872 | tf_op jit(solution)/shard_map/ppermute | solution.py:320
  79.4 77.7 %collective-permute-start.13 = (bf16[8,256,128]{2,1,0:T(8,128)(2,1)}, bf16[8,256,128]{2,1,0:T(8,128)(2,1)S(1)}, u32[]{:S(2)}, u32[]{:S(2)}) collective-permute-start(bf16[8,256,128]{2,1,0:T(8,128)(2,1)} %get-tuple-element.58), channel_id=1, source_target_pairs={{0,2},{1,3},{2,4},{3,5},{4,6},{5,7},{6,0},{7,1},{8,10},{9,11},{10,... | collective-permute-start | bytes 1572872 | tf_op jit(solution)/shard_map/ppermute | solution.py:320
  82.1 76.0 %copy-start.6 = (bf16[8,256,128]{2,1,0:T(8,128)(2,1)S(1)}, bf16[8,256,128]{2,1,0:T(8,128)(2,1)}, u32[]{:S(2)}) copy-start(bf16[8,256,128]{2,1,0:T(8,128)(2,1)} %get-tuple-element.48) | copy-start | bytes 1572868
  82.1 75.0 %collective-permute-start.11 = (bf16[8,256,128]{2,1,0:T(8,128)(2,1)S(1)}, bf16[8,256,128]{2,1,0:T(8,128)(2,1)}, u32[]{:S(2)}, u32[]{:S(2)}) collective-permute-start(bf16[8,256,128]{2,1,0:T(8,128)(2,1)S(1)} %collective-permute-done.8), channel_id=1, source_target_pairs={{0,2},{1,3},{2,4},{3,5},{4,6},{5,7},{6,0},{7,1},{8,10},{9,11},{10,... | collective-permute-start | bytes 1572872 | tf_op jit(solution)/shard_map/ppermute | solution.py:382
  83.2 73.9 %collective-permute-start.14 = (bf16[8,128,128]{2,1,0:T(8,128)(2,1)}, bf16[8,128,128]{2,1,0:T(8,128)(2,1)}, u32[]{:S(2)}, u32[]{:S(2)}) collective-permute-start(bf16[8,128,128]{2,1,0:T(8,128)(2,1)} %get-tuple-element.59), channel_id=1, source_target_pairs={{0,1},{1,0},{2,3},{3,2},{4,5},{5,4},{6,7},{7,6},{8,9},{9,8},{10,11... | collective-permute-start | bytes 786440 | tf_op jit(solution)/shard_map/ppermute | solution.py:385
  157.1 0.8 copy-start.7
  157.1 1.0 copy-start.9
  158.1 1.9 copy-start.5
  158.1 1.9 copy-start.8
  158.1 1.9 copy-start.10
  159.9 4.4 %copy-start.4 = (bf16[4,8,256,128]{3,2,1,0:T(8,128)(2,1)}, bf16[4,8,256,128]{3,2,1,0:T(8,128)(2,1)S(1)}, u32[]{:S(2)}) copy-start(bf16[4,8,256,128]{3,2,1,0:T(8,128)(2,1)S(1)} %pad_maximum_fusion.1.refs_0_) | copy-start | bytes 6291460
  159.9 2.0 copy-start.16
  159.9 4.4 %collective-permute-start.15 = (bf16[4,8,256,128]{3,2,1,0:T(8,128)(2,1)S(1)}, bf16[4,8,256,128]{3,2,1,0:T(8,128)(2,1)}, u32[]{:S(2)}, u32[]{:S(2)}) collective-permute-start(bf16[4,8,256,128]{3,2,1,0:T(8,128)(2,1)S(1)} %pad_maximum_fusion.1.refs_0_), channel_id=1, source_target_pairs={{0,8},{8,0},{16,24},{24,16},{32,40},{40,32},{48,56},{56,48},{64,72... | collective-permute-start | bytes 6291464 | tf_op jit(solution)/shard_map/ppermute | solution.py:317
  161.6 74.2 %copy-start.20 = (bf16[8,144,128]{2,1,0:T(8,128)(2,1)S(1)}, bf16[8,144,128]{2,1,0:T(8,128)(2,1)}, u32[]{:S(2)}) copy-start(bf16[8,144,128]{2,1,0:T(8,128)(2,1)} %get-tuple-element.55) | copy-start | bytes 884740
  161.6 77.3 %collective-permute-start.19 = (bf16[3,8,256,128]{3,2,1,0:T(8,128)(2,1)}, bf16[3,8,256,128]{3,2,1,0:T(8,128)(2,1)}, u32[]{:S(2)}, u32[]{:S(2)}) collective-permute-start(bf16[3,8,256,128]{3,2,1,0:T(8,128)(2,1)} %pad_maximum_fusion.2.refs_0_), channel_id=1, source_target_pairs={{0,8},{8,0},{16,24},{24,16},{32,40},{40,32},{48,56},{56,48},{64,72... | collective-permute-start | bytes 4718600 | tf_op jit(solution)/shard_map/ppermute | solution.py:317
  161.8 73.8 %collective-permute-start.18 = (bf16[8,128,128]{2,1,0:T(8,128)(2,1)S(1)}, bf16[8,128,128]{2,1,0:T(8,128)(2,1)S(1)}, u32[]{:S(2)}, u32[]{:S(2)}) collective-permute-start(bf16[8,128,128]{2,1,0:T(8,128)(2,1)S(1)} %copy-done.16), channel_id=1, source_target_pairs={{0,1},{1,0},{2,3},{3,2},{4,5},{5,4},{6,7},{7,6},{8,9},{9,8},{10,11... | collective-permute-start | bytes 786440 | tf_op jit(solution)/shard_map/ppermute | solution.py:393
  161.8 73.8 %collective-permute-start.17 = (bf16[8,256,128]{2,1,0:T(8,128)(2,1)S(1)}, bf16[8,256,128]{2,1,0:T(8,128)(2,1)S(1)}, u32[]{:S(2)}, u32[]{:S(2)}) collective-permute-start(bf16[8,256,128]{2,1,0:T(8,128)(2,1)S(1)} %copy-done.8), channel_id=1, source_target_pairs={{0,6},{1,7},{2,0},{3,1},{4,2},{5,3},{6,4},{7,5},{8,14},{9,15},{10,... | collective-permute-start | bytes 1572872 | tf_op jit(solution)/shard_map/ppermute | solution.py:391
  235.6 3.2 copy-start.21
  235.7 3.2 copy-start.18
  235.7 75.5 %copy-start.22 = (s32[24]{0:T(128)S(1)}, s32[24]{0:T(128)}, u32[]{:S(2)}) copy-start(s32[24]{0:T(128)} %param.10) | copy-start | bytes 292
  235.7 3.2 collective-permute-start.20
  235.8 75.4 %collective-permute-start.10 = (bf16[8,144,128]{2,1,0:T(8,128)(2,1)S(1)}, bf16[8,144,128]{2,1,0:T(8,128)(2,1)S(1)}, u32[]{:S(2)}, u32[]{:S(2)}) collective-permute-start(bf16[8,144,128]{2,1,0:T(8,128)(2,1)S(1)} %copy-done.20), channel_id=1, source_target_pairs={{0,1},{1,0},{2,3},{3,2},{4,5},{5,4},{6,7},{7,6},{8,9},{9,8},{10,11... | collective-permute-start | bytes 884744 | tf_op jit(solution)/shard_map/ppermute | solution.py:378
  235.9 75.3 %collective-permute-start.16 = (bf16[8,144,128]{2,1,0:T(8,128)(2,1)}, bf16[8,144,128]{2,1,0:T(8,128)(2,1)S(1)}, u32[]{:S(2)}, u32[]{:S(2)}) collective-permute-start(bf16[8,144,128]{2,1,0:T(8,128)(2,1)} %get-tuple-element.66), channel_id=1, source_target_pairs={{0,1},{1,0},{2,3},{3,2},{4,5},{5,4},{6,7},{7,6},{8,9},{9,8},{10,11... | collective-permute-start | bytes 884744 | tf_op jit(solution)/shard_map/ppermute | solution.py:378
  238.9 0.8 copy-start.19
  311.0 7.4 %collective-permute-start.21 = (bf16[8,144,128]{2,1,0:T(8,128)(2,1)}, bf16[8,144,128]{2,1,0:T(8,128)(2,1)S(1)}, u32[]{:S(2)}, u32[]{:S(2)}) collective-permute-start(bf16[8,144,128]{2,1,0:T(8,128)(2,1)} %get-tuple-element.76), channel_id=1, source_target_pairs={{0,1},{1,0},{2,3},{3,2},{4,5},{5,4},{6,7},{7,6},{8,9},{9,8},{10,11... | collective-permute-start | bytes 884744 | tf_op jit(solution)/shard_map/ppermute | solution.py:378
  311.2 7.2 %copy-start.13 = (bf16[8,144,128]{2,1,0:T(8,128)(2,1)}, bf16[8,144,128]{2,1,0:T(8,128)(2,1)S(1)}, u32[]{:S(2)}) copy-start(bf16[8,144,128]{2,1,0:T(8,128)(2,1)S(1)} %collective-permute-done.10.refs_1_) | copy-start | bytes 884740
  311.2 7.2 %copy-start.14 = (bf16[8,144,128]{2,1,0:T(8,128)(2,1)}, bf16[8,144,128]{2,1,0:T(8,128)(2,1)S(1)}, u32[]{:S(2)}) copy-start(bf16[8,144,128]{2,1,0:T(8,128)(2,1)S(1)} %collective-permute-done.16.refs_3_) | copy-start | bytes 884740
  318.4 0.7 copy-start.15
  321.8 4.1 %copy-start.17 = (s32[128]{0:T(128)S(1)}, s32[128]{0:T(128)}, u32[]{:S(2)}) copy-start(s32[128]{0:T(128)} %param.9) | copy-start | bytes 1540
  321.8 12.6 %all-to-all-start.2 = ((bf16[8,384,128]{2,1,0:T(8,128)(2,1)}), bf16[8,384,128]{2,1,0:T(8,128)(2,1)S(1)}, u32[]{:S(2)}, u32[]{:S(2)}) async-start(bf16[8,384,128]{2,1,0:T(8,128)(2,1)} %shard_map.69), calls=%async_computation.2 | async-start | bytes 1572864 | tf_op jit(solution)/shard_map/all_to_all | solution.py:309
  334.4 0.9 copy-start.2

commit v8 on v7

--- a/solution.py
+++ b/solution.py
@@ -168,19 +168,17 @@
             out[r, HEAD_DIM:, :] = note[:, at]
 
 
-def attend(info, own_q, their_q, at, ends, sources, head):
+def attend(info, own_q, at, their_q, ends, sources, head):
     rows = ZONES * SEGMENT
     out = jax.ShapeDtypeStruct((ZONES, HEAD_DIM + NOTE, HEAD_DIM), jnp.bfloat16)
-    first = own_q.shape[1] // HEAD_DIM - 3
-    own_spec = pl.BlockSpec((ZONES, HEAD_DIM, HEAD_DIM), lambda i, *_: (0, first + head, 0))
-    their_spec = pl.BlockSpec((ZONES, HEAD_DIM, HEAD_DIM), lambda i, *_: (0, at, 0))
+    own_spec = pl.BlockSpec((ZONES, HEAD_DIM, HEAD_DIM), lambda i, *_: (0, at, 0))
     whole = pl.BlockSpec(memory_space=pltpu.VMEM)
     return pl.pallas_call(
         functools.partial(attend_kernel, head),
         grid_spec=pltpu.PrefetchScalarGridSpec(
             num_scalar_prefetch=1,
             grid=(1,),
-            in_specs=[own_spec, their_spec, whole]
+            in_specs=[own_spec, whole, whole]
             + [pl.BlockSpec(memory_space=pl.ANY)] * len(sources),
             out_specs=[whole, whole],
             scratch_shapes=[
@@ -193,7 +191,7 @@
             ],
         ),
         out_shape=[out, out],
-        compiler_params=pltpu.CompilerParams(vmem_limit_bytes=58 << 20),
+        compiler_params=pltpu.CompilerParams(vmem_limit_bytes=24 << 20),
         cost_estimate=pl.CostEstimate(
             flops=4 * rows * KEYS * HEAD_DIM,
             bytes_accessed=4 * KEYS * HEAD_DIM + 4 * rows * HEAD_DIM,
@@ -202,43 +200,37 @@
     )(info, own_q, their_q, ends, *sources)
 
 
-def pack_first_kernel(head, queries_ref, keys_ref, values_ref, ids_ref, out_ref):
-    groups = out_ref.shape[0]
+def pack_kernel(queries_ref, keys_ref, values_ref, ids_ref, first_ref, rest_ref):
+    groups = first_ref.shape[0]
     heads = keys_ref.shape[1] // HEAD_DIM // groups
     ids = jnp.broadcast_to(ids_ref[...].astype(jnp.float32), (HEAD_DIM, HEAD_DIM)).T
     lane = lax.broadcasted_iota(jnp.int32, (HEAD_DIM, HEAD_DIM), 1)
     counts = jnp.sum(jnp.where(ids <= lane.astype(jnp.float32), 1.0, 0.0), axis=0, keepdims=True)
-    ones = jnp.ones((HEAD_DIM, HEAD_DIM), jnp.bfloat16)
-    lane = lane[:1]
+    local = heads * HEAD_DIM
+    row = lax.broadcasted_iota(jnp.int32, (2 * local, HEAD_DIM), 0) // HEAD_DIM
+    column = lax.broadcasted_iota(jnp.int32, (2 * local, HEAD_DIM), 1)
+    wanted = jnp.where(row < heads, row + K_NORM, row - heads + Q_NORM)
+    pick = jnp.where(column == wanted, 1.0, 0.0).astype(jnp.bfloat16)
+    is_count = lane[:1] < K_NORM
+    queries, keys, values = (queries_ref, True), (keys_ref, False), (values_ref, True)
+    first = [(queries, 0, 0), (keys, 0, 128), (values, 0, 256), (keys, 1, 400), (values, 1, 528)]
+    rest = [(keys, 2, 0), (values, 2, 128), (queries, 1, 256), (queries, 2, 384)]
     for g in range(groups):
-        at = slice((g * heads + head) * HEAD_DIM, (g * heads + head + 1) * HEAD_DIM)
-        out_ref[g, :HEAD_DIM] = keys_ref[:, at]
-        out_ref[g, HEAD_DIM : 2 * HEAD_DIM] = values_ref[:, at].T
-        note = counts
-        for first, ref in ((K_NORM, keys_ref), (Q_NORM, queries_ref)):
-            for h in range(heads):
-                start = (g * heads + h) * HEAD_DIM
-                rows = ref[:, start : start + HEAD_DIM].astype(jnp.float32)
-                norm = jnp.max(dot((rows * rows).astype(jnp.bfloat16), ones), axis=0, keepdims=True)
-                note = jnp.where(lane == first + h, norm * 1.02, note)
-        out_ref[g, 2 * HEAD_DIM :] = jnp.broadcast_to(note, (NOTE, HEAD_DIM)).astype(jnp.bfloat16)
-
-
-def pack_rest_kernel(others, queries_ref, keys_ref, values_ref, out_ref):
-    groups = out_ref.shape[0]
-    heads = keys_ref.shape[1] // HEAD_DIM // groups
-    for g in range(groups):
-        parts = [p for head in others for p in ((keys_ref, head, False), (values_ref, head, True))]
-        parts += [(queries_ref, head, True) for head in range(heads)]
-        for j, (ref, head, turn) in enumerate(parts):
-            at = slice((g * heads + head) * HEAD_DIM, (g * heads + head + 1) * HEAD_DIM)
-            out_ref[g, j * HEAD_DIM : (j + 1) * HEAD_DIM] = ref[:, at].T if turn else ref[:, at]
-
-
-def pack(kernel, rows, *args):
-    return pl.pallas_call(
-        kernel, out_shape=jax.ShapeDtypeStruct((ZONES, rows, HEAD_DIM), jnp.bfloat16)
-    )(*args)
+        for out_ref, parts in ((first_ref, first), (rest_ref, rest)):
+            for (ref, turn), head, at in parts:
+                start = g * local + head * HEAD_DIM
+                block = ref[:, start : start + HEAD_DIM]
+                out_ref[g, at : at + HEAD_DIM] = block.T if turn else block
+        rows = [ref[:, g * local : (g + 1) * local].astype(jnp.float32) for ref in (keys_ref, queries_ref)]
+        squares = jnp.concatenate([(x * x).astype(jnp.bfloat16) for x in rows], axis=1)
+        norms = jnp.max(dot(squares, pick), axis=0, keepdims=True) * 1.02
+        note = jnp.where(is_count, counts, norms)
+        note = jnp.broadcast_to(note, (NOTE, HEAD_DIM)).astype(jnp.bfloat16)
+        first_ref[g, 3 * HEAD_DIM : 3 * HEAD_DIM + NOTE] = note
+
+
+def packed(rows):
+    return jax.ShapeDtypeStruct((ZONES, rows, HEAD_DIM), jnp.bfloat16)
 
 
 def merge_kernel(*refs):
@@ -258,7 +250,7 @@
 
 
 def merge(parts):
-    return pack(merge_kernel, len(parts) // 2 * HEAD_DIM, *parts)
+    return pl.pallas_call(merge_kernel, out_shape=packed(len(parts) // 2 * HEAD_DIM))(*parts)
 
 
 def gate_kernel(gate_ref, mixed_ref, out_ref):
@@ -320,37 +312,36 @@
         return lax.ppermute(block, "head", down), lax.ppermute(block, "head", up)
 
     pair = 2 * HEAD_DIM
-    note_rows = span_ids.reshape(1, -1)
-    first = pack(
-        functools.partial(pack_first_kernel, 0), pair + NOTE, queries, keys, values, note_rows
+    first, rest = pl.pallas_call(
+        pack_kernel, out_shape=[packed(5 * HEAD_DIM + NOTE), packed(4 * HEAD_DIM)]
+    )(queries, keys, values, span_ids.reshape(1, -1))
+    first = exchange(first)
+    rest, first = after(rest, first)
+    rest = exchange(rest)
+    one_from = 3 * HEAD_DIM + NOTE
+    own_q, block, block_one = after(
+        first[:, :HEAD_DIM], first[:, HEAD_DIM:one_from], first[:, one_from:]
     )
-    first = exchange(first)
-    above, below = sides(first)
-    queries, first = after(queries, first)
-    rest = pack(
-        functools.partial(pack_rest_kernel, (1, 2)), 2 * pair + local, queries, keys, values
-    )
-    rest = exchange(rest)
-    near = jnp.stack([first, above, below, lax.ppermute(above, "head", down)])
+    their_q = [lax.ppermute(own_q, "head", partner), None, None]
+    above, below = sides(block)
+    block_one, above, below = after(block_one, above, below)
+    above_one, below_one = sides(block_one)
+    near = jnp.stack([block, above, below, lax.ppermute(above, "head", down)])
 
     def combined(notes):
         is_count = jnp.arange(HEAD_DIM) < K_NORM
         return jnp.where(is_count, jnp.sum(notes, axis=0), jnp.max(notes, axis=0))
 
     note = combined(near[:, :, pair].reshape(-1, HEAD_DIM).astype(jnp.float32))[None]
-    rest, near, note = after(rest, near, note)
-    own_q = [rest[:, start : start + HEAD_DIM] for start in range(2 * pair, rest.shape[1], HEAD_DIM)]
-    own_q[0], block_one, block_two = after(own_q[0], rest[:, :pair], rest[:, pair : 2 * pair])
-    above, below = sides(block_one)
-    their_q = [lax.ppermute(own_q[0], "head", partner), None, None]
-    near, far = swapped(near)
-    note, their_q[0] = after(note, their_q[0])
+    note, above_one, below_one = after(note, above_one, below_one)
     notes = [
         note,
         lax.ppermute(note, "span", core_swap),
         lax.ppermute(note, "head", partner),
         lax.ppermute(note, BOTH, other),
     ]
+    near, far = swapped(near)
+    block_two, *own_q = after(rest[:, :pair], rest[:, pair:-HEAD_DIM], rest[:, -HEAD_DIM:])
     note = combined(jnp.concatenate(notes))
     squares = note[K_NORM : K_NORM + heads] * note[Q_NORM : Q_NORM + heads]
     plain = (squares * (1.05 * SCALE**2) < PLAIN_LIMIT**2).astype(jnp.int32)
@@ -372,29 +363,30 @@
 
     parts = [None] * (2 * heads)
 
-    def attended(info, head, their_q, at, sources):
-        parts[2 * head], theirs = attend(info, rest, their_q, at, seen, sources, head)
+    def attended(info, head, sources):
+        own, at = (first, 0) if head == 0 else (rest, 1 + head)
+        parts[2 * head], theirs = attend(info, own, at, their_q[head], seen, sources, head)
         info, theirs = after(info, theirs)
         parts[2 * head + 1] = lax.ppermute(theirs, "head", partner)
         return info
 
-    info, block_two, above, below = after(info, block_two, above, below)
+    info, block_two, above, below = after(info, block_two, above_one, below_one)
     opposite = lax.ppermute(below, "head", up)
     above_two, below_two = sides(block_two)
-    own_q[1], own_q[2], info = after(own_q[1], own_q[2], info)
-    their_q[1] = lax.ppermute(own_q[1], "head", partner)
-    info = attended(info, 0, their_q[0], 0, (near, far))
+    own_q[0], own_q[1], info = after(own_q[0], own_q[1], info)
+    their_q[1] = lax.ppermute(own_q[0], "head", partner)
+    info = attended(info, 0, (near, far))
     info, opposite, above_two, below_two, their_q[1] = after(
         info, opposite, above_two, below_two, their_q[1]
     )
     near, far = swapped(jnp.stack([block_one, above, below, opposite]))
     opposite = lax.ppermute(above_two, "head", down)
     near_two, far_two = swapped(jnp.stack([block_two, above_two, below_two]))
-    their_q[2] = lax.ppermute(own_q[2], "head", partner)
-    info = attended(info, 1, their_q[1], 0, (near, far))
+    their_q[2] = lax.ppermute(own_q[1], "head", partner)
+    info = attended(info, 1, (near, far))
     info, opposite, their_q[2] = after(info, opposite, their_q[2])
     last, far_last = swapped(opposite[None])
-    info = attended(info, 2, their_q[2], 0, (near_two, last, far_two, far_last))
+    info = attended(info, 2, (near_two, last, far_two, far_last))
     mixed = exchange(merge(parts))
     gates = gate_rows(span_ids, timesteps, time_weight)
     return pl.pallas_call(

time: 337 us -> 326 us (0.967)
  Pallas kernels: 226 us -> 214 us
  blocking collectives: 15.4 us -> 23.9 us
  waiting for transfers between devices: 43.2 us -> 36.8 us
  starting transfers between devices: 36.9 us -> 33 us
    pallas_call x3, Pallas kernels: 214 us -> 204 us  [attend(): pl.pallas_call(functools.partial(attend_kernel, head), grid_spec=pltpu.Pr...]
    all_to_all x1, blocking collectives: 15.4 us -> 23.9 us  [exchange(): lax.all_to_all(parts, BOTH, split_axis=0, concat_axis=0, axis_index_group...]
    ppermute x1, starting transfers between devices: 7.6 us -> 0.69 us  [per_device(): lax.ppermute(note, BOTH, other)]
    ppermute x1, starting transfers between devices: 0.01 us -> 3.97 us  [per_device(): lax.ppermute(note, 'span', core_swap)]
    ppermute x4, starting transfers between devices: 4.8 us -> 0.97 us  [swapped(): return (block, lax.ppermute(block, 'span', core_swap))]
    ppermute x4, waiting for transfers between devices: 6.59 us -> 3.01 us  [the longest x1 3 us: per_device(): near = jnp.stack([block, above, below, lax.ppermute(above, 'head', down)])]
    pallas_call x3 -> x2, Pallas kernels: 9.06 us -> 6.64 us  [the longest x1 4 us: per_device(): pl.pallas_call(pack_kernel, out_shape=[packed(5 * HEAD_DIM + NOTE), packe...]
  transfers between devices with their start and end apart: 24 -> 24, of which waited for: 9 -> 7; matrix products, arithmetic and copies ran while one was open for 2% -> 3% of each run, Pallas kernels for 64% -> 63%
where the time goes in v8:
time: 326 us; the launch traced here: 325 us
  Pallas kernels  214 us (66%)
  waiting for transfers between devices  36.8 us (11%)
  starting transfers between devices  33 us (10%)
  blocking collectives  23.9 us (7%)
  local copies, waits for them, and re-layouts  7.57 us (2%)
  other arithmetic  7.48 us (2%)
    pallas_call x3, Pallas kernels, attend(): pl.pallas_call(functools.partial(attend_kernel, head), grid_spec=pltpu.Pr...  204 us
    all_to_all x1, blocking collectives, exchange(): lax.all_to_all(parts, BOTH, split_axis=0, concat_axis=0, axis_index_group...  23.9 us
    ppermute x6, waiting for transfers between devices, sides(): return (lax.ppermute(block, 'head', down), lax.ppermute(block, 'head', up))  16.8 us
    ppermute x6, starting transfers between devices, sides(): return (lax.ppermute(block, 'head', down), lax.ppermute(block, 'head', up))  8.03 us
    all_to_all x2, starting transfers between devices, exchange(): lax.all_to_all(parts, BOTH, split_axis=0, concat_axis=0, axis_index_group...  7.92 us
    all_to_all x2, waiting for transfers between devices, exchange(): lax.all_to_all(parts, BOTH, split_axis=0, concat_axis=0, axis_index_group...  7.46 us
  transfers between devices with their start and end apart: 24, of which 7 were waited for; matrix products, arithmetic and copies ran while one was open for 3% of the time, Pallas kernels for 63%

profile of v8, /device:TPU:25, one launch (start us, length us, event | category | flops | bytes accessed | tf_op | source)
XLA Modules:
  0.0 325.0 jit_solution(12914597677247792479)
XLA Ops:
  0.0 4.0 %shard_map.64 = (bf16[8,656,128]{2,1,0:T(8,128)(2,1)}, bf16[8,512,128]{2,1,0:T(8,128)(2,1)}) custom-call(bf16[128,3072]{1,0:T(8,128)(2,1)} %queries_ref.1, bf16[128,3072]{1,0:T(8,128)(2,1)} %keys_ref.1, bf16[128,3072]{1,0:T(8,128)(2,1)} %values_ref.1, s32[1,128]{1,0:T(1,128)} %bitcast.56), custom_call_target="tpu_custom_call" | custom-call | tf_op jit(solution)/shard_map/pallas_call | solution.py:315
  4.0 23.9 %all_to_all.15.own_q = bf16[8,656,128]{2,1,0:T(8,128)(2,1)S(1)} all-to-all(bf16[8,656,128]{2,1,0:T(8,128)(2,1)} %get-tuple-element.48), channel_id=1, replica_groups={{0,16,32,48,64,80,96,112},{1,17,33,49,65,81,97,113},{2,18,34,50,66,82,9..., dimensions={0} | all-to-all | bytes 2686976 | tf_op jit(solution)/shard_map/all_to_all | solution.py:301
  27.9 0.0 copy-start.5
  27.9 0.9 slice.35
  28.8 0.7 slice.33
  29.5 0.5 collective-permute-start
  30.0 2.2 collective-permute-start.1
  32.2 0.1 add_multiply_fusion
  32.3 10.5 %collective-permute-done = bf16[8,272,128]{2,1,0:T(8,128)(2,1)} collective-permute-done((bf16[8,272,128]{2,1,0:T(8,128)(2,1)S(1)}, bf16[8,272,128]{2,1,0:T(8,128)(2,1)}, u32[]{:S(2)}, u32[]{:S(2)}) %collective-permute-start) | collective-permute-done | bytes 557088 | tf_op jit(solution)/shard_map/ppermute | solution.py:312
  42.8 0.0 collective-permute-done.1
  42.8 0.0 collective-permute-start.2
  42.8 0.1 broadcast_add_fusion
  42.9 4.2 %all-to-all-start.1 = ((bf16[8,512,128]{2,1,0:T(8,128)(2,1)}), bf16[8,512,128]{2,1,0:T(8,128)(2,1)}, u32[]{:S(2)}, u32[]{:S(2)}) async-start(bf16[8,512,128]{2,1,0:T(8,128)(2,1)} %get-tuple-element.49), calls=%async_computation.1 | async-start | bytes 2097152 | tf_op jit(solution)/shard_map/all_to_all | solution.py:301
  47.2 0.1 fusion.12
  47.3 2.5 collective-permute-start.8
  49.8 0.9 collective-permute-start.3
  50.6 1.8 collective-permute-start.4
  52.4 3.0 collective-permute-done.2
  55.4 3.2 pad_maximum_fusion.refs_0_
  58.7 0.9 convert_reduce_fusion
  59.6 0.9 slice_reduce_fusion
  60.5 6.2 %collective-permute-done.3 = bf16[8,256,128]{2,1,0:T(8,128)(2,1)} collective-permute-done((bf16[8,256,128]{2,1,0:T(8,128)(2,1)}, bf16[8,256,128]{2,1,0:T(8,128)(2,1)}, u32[]{:S(2)}, u32[]{:S(2)}) %collective-permute-start.3) | collective-permute-done | bytes 524320 | tf_op jit(solution)/shard_map/ppermute | solution.py:312
  66.7 4.0 %collective-permute-start.5 = (f32[1,128]{1,0:T(1,128)S(1)}, f32[1,128]{1,0:T(1,128)S(1)}, u32[]{:S(2)}, u32[]{:S(2)}) collective-permute-start(f32[1,128]{1,0:T(1,128)S(1)} %compare_select_fusion), channel_id=1, source_target_pairs={{0,8},{8,0},{16,24},{24,16},{32,40},{40,32},{48,56},{56,48},{64,72... | collective-permute-start | bytes 1544 | tf_op jit(solution)/shard_map/ppermute | solution.py:339
  70.7 2.4 collective-permute-start.6
  73.1 0.7 collective-permute-start.7
  73.8 0.2 collective-permute-start.9
  74.0 1.1 fusion.18
  75.1 1.1 slice.40
  76.2 1.4 collective-permute-done.7
  77.6 0.1 select_reduce_fusion
  77.7 0.1 compare_convert_fusion
  77.8 0.1 fusion.15
  78.0 0.1 pad_add_fusion.info_ref
  78.0 0.0 collective-permute-start.12
  78.1 2.7 collective-permute-start.13
  80.7 0.0 collective-permute-start.11
  80.8 1.2 collective-permute-start.14
  82.0 66.9 %shard_map.65 = (bf16[8,144,128]{2,1,0:T(8,128)(2,1)S(1)}, bf16[8,144,128]{2,1,0:T(8,128)(2,1)S(1)}) custom-call(s32[13]{0:T(128)S(1)} %pad_add_fusion.info_ref, bf16[8,656,128]{2,1,0:T(8,128)(2,1)S(1)} %all_to_all.15.own_q, bf16[8,128,128]{2,1,0:T(8,128)(2,1)S(1)} %collective-permute-done.8.their_q, s32[8,1,256]{2,1,0:T(1,128)S(1)} %fusion.13.end_ref, ...), custom_call_target="tpu_custom_call" | custom-call | flops 8589934592 | bytes 5242880 | tf_op jit(solution)/shard_map/pallas_call | solution.py:176
  148.9 0.7 copy-done.1
  149.6 1.5 pad_maximum_fusion.1.refs_0_
  151.1 0.1 collective-permute-start.15
  151.2 0.2 pad_maximum_fusion.2.refs_0_
  151.4 0.6 collective-permute-start.19
  152.0 1.5 collective-permute-start.18
  153.4 0.2 collective-permute-start.17
  153.6 1.7 collective-permute-done.15.refs_1_
  155.3 68.8 %shard_map.66 = (bf16[8,144,128]{2,1,0:T(8,128)(2,1)S(1)}, bf16[8,144,128]{2,1,0:T(8,128)(2,1)S(1)}) custom-call(s32[13]{0:T(128)S(1)} %pad_add_fusion.info_ref, bf16[8,512,128]{2,1,0:T(8,128)(2,1)} %all-to-all-done.1.own_q, bf16[8,128,128]{2,1,0:T(8,128)(2,1)S(1)} %collective-permute-done.14.their_q, s32[8,1,256]{2,1,0:T(1,128)S(1)} %fusion.13.end_ref, ...), custom_call_target="tpu_custom_call" | custom-call | flops 8589934592 | bytes 5242880 | tf_op jit(solution)/shard_map/pallas_call | solution.py:176
  224.1 0.7 copy-done.2
  224.8 0.1 collective-permute-start.20
  224.9 1.1 collective-permute-start.10
  226.0 1.9 collective-permute-start.16
  228.0 68.6 %shard_map.67 = (bf16[8,144,128]{2,1,0:T(8,128)(2,1)S(1)}, bf16[8,144,128]{2,1,0:T(8,128)(2,1)S(1)}) custom-call(s32[13]{0:T(128)S(1)} %pad_add_fusion.info_ref, bf16[8,512,128]{2,1,0:T(8,128)(2,1)} %all-to-all-done.1.own_q, bf16[8,128,128]{2,1,0:T(8,128)(2,1)S(1)} %collective-permute-done.18.their_q, s32[8,1,256]{2,1,0:T(1,128)S(1)} %fusion.13.end_ref, ...), custom_call_target="tpu_custom_call" | custom-call | flops 8589934592 | bytes 5242880 | tf_op jit(solution)/shard_map/pallas_call | solution.py:176
  296.6 0.7 copy-done.3
  297.3 0.6 collective-permute-start.21
  298.0 6.4 %collective-permute-done.21.refs_5_ = bf16[8,144,128]{2,1,0:T(8,128)(2,1)S(1)} collective-permute-done((bf16[8,144,128]{2,1,0:T(8,128)(2,1)S(1)}, bf16[8,144,128]{2,1,0:T(8,128)(2,1)S(1)}, u32[]{:S(2)}, u32[]{:S(2)}) %collective-permute-start.21) | collective-permute-done | bytes 294944 | tf_op jit(solution)/shard_map/ppermute | solution.py:370
  304.4 0.7 copy-done.9
  305.1 2.6 shard_map.68
  307.7 3.7 %all-to-all-start.2 = ((bf16[8,384,128]{2,1,0:T(8,128)(2,1)}), bf16[8,384,128]{2,1,0:T(8,128)(2,1)S(1)}, u32[]{:S(2)}, u32[]{:S(2)}) async-start(bf16[8,384,128]{2,1,0:T(8,128)(2,1)} %shard_map.68), calls=%async_computation.2 | async-start | bytes 1572864 | tf_op jit(solution)/shard_map/all_to_all | solution.py:301
  311.4 0.1 fusion.2
  311.6 0.3 fusion.4
  311.9 2.0 fusion.gate_ref
  313.9 7.5 %all-to-all-done.2.mixed_ref = bf16[8,384,128]{2,1,0:T(8,128)(2,1)S(1)} async-done(((bf16[8,384,128]{2,1,0:T(8,128)(2,1)}), bf16[8,384,128]{2,1,0:T(8,128)(2,1)S(1)}, u32[]{:S(2)}, u32[]{:S(2)}) %all-to-all-start.2) | async-done | bytes 786464 | tf_op jit(solution)/shard_map/all_to_all | solution.py:301
  321.4 0.9 copy-done.4
  322.3 2.7 shard_map.69
  (46 shorter events, 0.2 us)
Async XLA Ops:
  0.0 311.6 %copy-start = (bf16[256,3072]{1,0:T(8,128)(2,1)S(1)}, bf16[256,3072]{1,0:T(8,128)(2,1)}, u32[]{:S(2)}) copy-start(bf16[256,3072]{1,0:T(8,128)(2,1)} %param.11) | copy-start | bytes 4718596
  27.9 19.3 %copy-start.5 = (bf16[8,272,128]{2,1,0:T(8,128)(2,1)}, bf16[8,272,128]{2,1,0:T(8,128)(2,1)S(1)}, u32[]{:S(2)}) copy-start(bf16[8,272,128]{2,1,0:T(8,128)(2,1)S(1)} %slice.34) | copy-start | bytes 1671172
  29.5 13.3 %collective-permute-start = (bf16[8,272,128]{2,1,0:T(8,128)(2,1)S(1)}, bf16[8,272,128]{2,1,0:T(8,128)(2,1)}, u32[]{:S(2)}, u32[]{:S(2)}) collective-permute-start(bf16[8,272,128]{2,1,0:T(8,128)(2,1)S(1)} %slice.34), channel_id=1, source_target_pairs={{0,6},{1,7},{2,0},{3,1},{4,2},{5,3},{6,4},{7,5},{8,14},{9,15},{10,... | collective-permute-start | bytes 1671176 | tf_op jit(solution)/shard_map/ppermute | solution.py:312
  30.0 12.8 %collective-permute-start.1 = (bf16[8,272,128]{2,1,0:T(8,128)(2,1)S(1)}, bf16[8,272,128]{2,1,0:T(8,128)(2,1)}, u32[]{:S(2)}, u32[]{:S(2)}) collective-permute-start(bf16[8,272,128]{2,1,0:T(8,128)(2,1)S(1)} %slice.34), channel_id=1, source_target_pairs={{0,2},{1,3},{2,4},{3,5},{4,6},{5,7},{6,0},{7,1},{8,10},{9,11},{10,... | collective-permute-start | bytes 1671176 | tf_op jit(solution)/shard_map/ppermute | solution.py:312
  42.8 12.6 %collective-permute-start.2 = (bf16[8,272,128]{2,1,0:T(8,128)(2,1)}, bf16[8,272,128]{2,1,0:T(8,128)(2,1)}, u32[]{:S(2)}, u32[]{:S(2)}) collective-permute-start(bf16[8,272,128]{2,1,0:T(8,128)(2,1)} %collective-permute-done), channel_id=1, source_target_pairs={{0,6},{1,7},{2,0},{3,1},{4,2},{5,3},{6,4},{7,5},{8,14},{9,15},{10,... | collective-permute-start | bytes 1671176 | tf_op jit(solution)/shard_map/ppermute | solution.py:329
  42.9 31.1 %all-to-all-start.1 = ((bf16[8,512,128]{2,1,0:T(8,128)(2,1)}), bf16[8,512,128]{2,1,0:T(8,128)(2,1)}, u32[]{:S(2)}, u32[]{:S(2)}) async-start(bf16[8,512,128]{2,1,0:T(8,128)(2,1)} %get-tuple-element.49), calls=%async_computation.1 | async-start | bytes 2097152 | tf_op jit(solution)/shard_map/all_to_all | solution.py:301
  47.3 33.5 %collective-permute-start.8 = (bf16[8,128,128]{2,1,0:T(8,128)(2,1)}, bf16[8,128,128]{2,1,0:T(8,128)(2,1)S(1)}, u32[]{:S(2)}, u32[]{:S(2)}) collective-permute-start(bf16[8,128,128]{2,1,0:T(8,128)(2,1)} %slice.33), channel_id=1, source_target_pairs={{0,1},{1,0},{2,3},{3,2},{4,5},{5,4},{6,7},{7,6},{8,9},{9,8},{10,11... | collective-permute-start | bytes 786440 | tf_op jit(solution)/shard_map/ppermute | solution.py:325
  49.8 16.9 %collective-permute-start.3 = (bf16[8,256,128]{2,1,0:T(8,128)(2,1)}, bf16[8,256,128]{2,1,0:T(8,128)(2,1)}, u32[]{:S(2)}, u32[]{:S(2)}) collective-permute-start(bf16[8,256,128]{2,1,0:T(8,128)(2,1)} %slice.35), channel_id=1, source_target_pairs={{0,6},{1,7},{2,0},{3,1},{4,2},{5,3},{6,4},{7,5},{8,14},{9,15},{10,... | collective-permute-start | bytes 1572872 | tf_op jit(solution)/shard_map/ppermute | solution.py:312
  50.6 16.1 %collective-permute-start.4 = (bf16[8,256,128]{2,1,0:T(8,128)(2,1)}, bf16[8,256,128]{2,1,0:T(8,128)(2,1)}, u32[]{:S(2)}, u32[]{:S(2)}) collective-permute-start(bf16[8,256,128]{2,1,0:T(8,128)(2,1)} %slice.35), channel_id=1, source_target_pairs={{0,2},{1,3},{2,4},{3,5},{4,6},{5,7},{6,0},{7,1},{8,10},{9,11},{10,... | collective-permute-start | bytes 1572872 | tf_op jit(solution)/shard_map/ppermute | solution.py:312
  66.7 9.5 %collective-permute-start.5 = (f32[1,128]{1,0:T(1,128)S(1)}, f32[1,128]{1,0:T(1,128)S(1)}, u32[]{:S(2)}, u32[]{:S(2)}) collective-permute-start(f32[1,128]{1,0:T(1,128)S(1)} %compare_select_fusion), channel_id=1, source_target_pairs={{0,8},{8,0},{16,24},{24,16},{32,40},{40,32},{48,56},{56,48},{64,72... | collective-permute-start | bytes 1544 | tf_op jit(solution)/shard_map/ppermute | solution.py:339
  70.7 5.5 %collective-permute-start.6 = (f32[1,128]{1,0:T(1,128)S(1)}, f32[1,128]{1,0:T(1,128)S(1)}, u32[]{:S(2)}, u32[]{:S(2)}) collective-permute-start(f32[1,128]{1,0:T(1,128)S(1)} %compare_select_fusion), channel_id=1, source_target_pairs={{0,1},{1,0},{2,3},{3,2},{4,5},{5,4},{6,7},{7,6},{8,9},{9,8},{10,11... | collective-permute-start | bytes 1544 | tf_op jit(solution)/shard_map/ppermute | solution.py:340
  73.1 4.5 %collective-permute-start.7 = (f32[1,128]{1,0:T(1,128)S(1)}, f32[1,128]{1,0:T(1,128)S(1)}, u32[]{:S(2)}, u32[]{:S(2)}) collective-permute-start(f32[1,128]{1,0:T(1,128)S(1)} %compare_select_fusion), channel_id=1, source_target_pairs={{0,9},{1,8},{2,11},{3,10},{4,13},{5,12},{6,15},{7,14},{8,1},{9,0},... | collective-permute-start | bytes 1544 | tf_op jit(solution)/shard_map/ppermute | solution.py:341
  73.8 8.2 %collective-permute-start.9 = (bf16[4,8,272,128]{3,2,1,0:T(8,128)(2,1)}, bf16[4,8,272,128]{3,2,1,0:T(8,128)(2,1)}, u32[]{:S(2)}, u32[]{:S(2)}) collective-permute-start(bf16[4,8,272,128]{3,2,1,0:T(8,128)(2,1)} %pad_maximum_fusion.refs_0_), channel_id=1, source_target_pairs={{0,8},{8,0},{16,24},{24,16},{32,40},{40,32},{48,56},{56,48},{64,72... | collective-permute-start | bytes 6684680 | tf_op jit(solution)/shard_map/ppermute | solution.py:309
  78.0 71.6 %collective-permute-start.12 = (bf16[8,256,128]{2,1,0:T(8,128)(2,1)S(1)}, bf16[8,256,128]{2,1,0:T(8,128)(2,1)S(1)}, u32[]{:S(2)}, u32[]{:S(2)}) collective-permute-start(bf16[8,256,128]{2,1,0:T(8,128)(2,1)S(1)} %slice.40), channel_id=1, source_target_pairs={{0,6},{1,7},{2,0},{3,1},{4,2},{5,3},{6,4},{7,5},{8,14},{9,15},{10,... | collective-permute-start | bytes 1572872 | tf_op jit(solution)/shard_map/ppermute | solution.py:312
  78.1 71.6 %collective-permute-start.13 = (bf16[8,256,128]{2,1,0:T(8,128)(2,1)S(1)}, bf16[8,256,128]{2,1,0:T(8,128)(2,1)S(1)}, u32[]{:S(2)}, u32[]{:S(2)}) collective-permute-start(bf16[8,256,128]{2,1,0:T(8,128)(2,1)S(1)} %slice.40), channel_id=1, source_target_pairs={{0,2},{1,3},{2,4},{3,5},{4,6},{5,7},{6,0},{7,1},{8,10},{9,11},{10,... | collective-permute-start | bytes 1572872 | tf_op jit(solution)/shard_map/ppermute | solution.py:312
  80.7 68.9 %collective-permute-start.11 = (bf16[8,256,128]{2,1,0:T(8,128)(2,1)}, bf16[8,256,128]{2,1,0:T(8,128)(2,1)S(1)}, u32[]{:S(2)}, u32[]{:S(2)}) collective-permute-start(bf16[8,256,128]{2,1,0:T(8,128)(2,1)} %collective-permute-done.4), channel_id=1, source_target_pairs={{0,2},{1,3},{2,4},{3,5},{4,6},{5,7},{6,0},{7,1},{8,10},{9,11},{10,... | collective-permute-start | bytes 1572872 | tf_op jit(solution)/shard_map/ppermute | solution.py:374
  80.8 68.8 %copy-start.6 = (bf16[8,256,128]{2,1,0:T(8,128)(2,1)S(1)}, bf16[8,256,128]{2,1,0:T(8,128)(2,1)}, u32[]{:S(2)}) copy-start(bf16[8,256,128]{2,1,0:T(8,128)(2,1)} %slice.35) | copy-start | bytes 1572868
  80.8 68.8 %collective-permute-start.14 = (bf16[8,128,128]{2,1,0:T(8,128)(2,1)S(1)}, bf16[8,128,128]{2,1,0:T(8,128)(2,1)S(1)}, u32[]{:S(2)}, u32[]{:S(2)}) collective-permute-start(bf16[8,128,128]{2,1,0:T(8,128)(2,1)S(1)} %get-tuple-element.71), channel_id=1, source_target_pairs={{0,1},{1,0},{2,3},{3,2},{4,5},{5,4},{6,7},{7,6},{8,9},{9,8},{10,11... | collective-permute-start | bytes 786440 | tf_op jit(solution)/shard_map/ppermute | solution.py:377
  148.9 0.7 copy-start.1
  151.1 4.2 %collective-permute-start.15 = (bf16[4,8,256,128]{3,2,1,0:T(8,128)(2,1)S(1)}, bf16[4,8,256,128]{3,2,1,0:T(8,128)(2,1)S(1)}, u32[]{:S(2)}, u32[]{:S(2)}) collective-permute-start(bf16[4,8,256,128]{3,2,1,0:T(8,128)(2,1)S(1)} %pad_maximum_fusion.1.refs_0_), channel_id=1, source_target_pairs={{0,8},{8,0},{16,24},{24,16},{32,40},{40,32},{48,56},{56,48},{64,72... | collective-permute-start | bytes 6291464 | tf_op jit(solution)/shard_map/ppermute | solution.py:309
  151.4 76.6 %collective-permute-start.19 = (bf16[3,8,256,128]{3,2,1,0:T(8,128)(2,1)S(1)}, bf16[3,8,256,128]{3,2,1,0:T(8,128)(2,1)S(1)}, u32[]{:S(2)}, u32[]{:S(2)}) collective-permute-start(bf16[3,8,256,128]{3,2,1,0:T(8,128)(2,1)S(1)} %pad_maximum_fusion.2.refs_0_), channel_id=1, source_target_pairs={{0,8},{8,0},{16,24},{24,16},{32,40},{40,32},{48,56},{56,48},{64,72... | collective-permute-start | bytes 4718600 | tf_op jit(solution)/shard_map/ppermute | solution.py:309
  152.0 72.9 %collective-permute-start.18 = (bf16[8,128,128]{2,1,0:T(8,128)(2,1)S(1)}, bf16[8,128,128]{2,1,0:T(8,128)(2,1)S(1)}, u32[]{:S(2)}, u32[]{:S(2)}) collective-permute-start(bf16[8,128,128]{2,1,0:T(8,128)(2,1)S(1)} %get-tuple-element.81), channel_id=1, source_target_pairs={{0,1},{1,0},{2,3},{3,2},{4,5},{5,4},{6,7},{7,6},{8,9},{9,8},{10,11... | collective-permute-start | bytes 786440 | tf_op jit(solution)/shard_map/ppermute | solution.py:385
  153.4 71.4 %collective-permute-start.17 = (bf16[8,256,128]{2,1,0:T(8,128)(2,1)S(1)}, bf16[8,256,128]{2,1,0:T(8,128)(2,1)S(1)}, u32[]{:S(2)}, u32[]{:S(2)}) collective-permute-start(bf16[8,256,128]{2,1,0:T(8,128)(2,1)S(1)} %collective-permute-done.12), channel_id=1, source_target_pairs={{0,6},{1,7},{2,0},{3,1},{4,2},{5,3},{6,4},{7,5},{8,14},{9,15},{10,... | collective-permute-start | bytes 1572872 | tf_op jit(solution)/shard_map/ppermute | solution.py:383
  224.1 0.7 copy-start.2
  224.8 73.1 %copy-start.11 = (s32[24]{0:T(128)S(1)}, s32[24]{0:T(128)}, u32[]{:S(2)}) copy-start(s32[24]{0:T(128)} %param.10) | copy-start | bytes 292
  224.8 3.1 collective-permute-start.20
  224.9 73.0 %collective-permute-start.10 = (bf16[8,144,128]{2,1,0:T(8,128)(2,1)S(1)}, bf16[8,144,128]{2,1,0:T(8,128)(2,1)S(1)}, u32[]{:S(2)}, u32[]{:S(2)}) collective-permute-start(bf16[8,144,128]{2,1,0:T(8,128)(2,1)S(1)} %get-tuple-element.67), channel_id=1, source_target_pairs={{0,1},{1,0},{2,3},{3,2},{4,5},{5,4},{6,7},{7,6},{8,9},{9,8},{10,11... | collective-permute-start | bytes 884744 | tf_op jit(solution)/shard_map/ppermute | solution.py:370
  226.0 71.9 %collective-permute-start.16 = (bf16[8,144,128]{2,1,0:T(8,128)(2,1)S(1)}, bf16[8,144,128]{2,1,0:T(8,128)(2,1)S(1)}, u32[]{:S(2)}, u32[]{:S(2)}) collective-permute-start(bf16[8,144,128]{2,1,0:T(8,128)(2,1)S(1)} %get-tuple-element.78), channel_id=1, source_target_pairs={{0,1},{1,0},{2,3},{3,2},{4,5},{5,4},{6,7},{7,6},{8,9},{9,8},{10,11... | collective-permute-start | bytes 884744 | tf_op jit(solution)/shard_map/ppermute | solution.py:370
  296.6 0.7 copy-start.3
  297.3 7.1 %collective-permute-start.21 = (bf16[8,144,128]{2,1,0:T(8,128)(2,1)S(1)}, bf16[8,144,128]{2,1,0:T(8,128)(2,1)S(1)}, u32[]{:S(2)}, u32[]{:S(2)}) collective-permute-start(bf16[8,144,128]{2,1,0:T(8,128)(2,1)S(1)} %get-tuple-element.88), channel_id=1, source_target_pairs={{0,1},{1,0},{2,3},{3,2},{4,5},{5,4},{6,7},{7,6},{8,9},{9,8},{10,11... | collective-permute-start | bytes 884744 | tf_op jit(solution)/shard_map/ppermute | solution.py:370
  297.9 6.4 %copy-start.7 = (bf16[8,144,128]{2,1,0:T(8,128)(2,1)}, bf16[8,144,128]{2,1,0:T(8,128)(2,1)S(1)}, u32[]{:S(2)}) copy-start(bf16[8,144,128]{2,1,0:T(8,128)(2,1)S(1)} %collective-permute-done.10.refs_1_) | copy-start | bytes 884740
  298.0 6.4 %copy-start.8 = (bf16[8,144,128]{2,1,0:T(8,128)(2,1)}, bf16[8,144,128]{2,1,0:T(8,128)(2,1)S(1)}, u32[]{:S(2)}) copy-start(bf16[8,144,128]{2,1,0:T(8,128)(2,1)S(1)} %collective-permute-done.16.refs_3_) | copy-start | bytes 884740
  304.4 0.7 copy-start.9
  307.7 4.1 %copy-start.10 = (s32[128]{0:T(128)S(1)}, s32[128]{0:T(128)}, u32[]{:S(2)}) copy-start(s32[128]{0:T(128)} %param.9) | copy-start | bytes 1540
  307.7 13.6 %all-to-all-start.2 = ((bf16[8,384,128]{2,1,0:T(8,128)(2,1)}), bf16[8,384,128]{2,1,0:T(8,128)(2,1)S(1)}, u32[]{:S(2)}, u32[]{:S(2)}) async-start(bf16[8,384,128]{2,1,0:T(8,128)(2,1)} %shard_map.68), calls=%async_computation.2 | async-start | bytes 1572864 | tf_op jit(solution)/shard_map/all_to_all | solution.py:301
  321.4 0.9 copy-start.4

commit v9 on v8

--- a/solution.py
+++ b/solution.py
@@ -22,6 +22,7 @@
 NOTE = 16
 PLAIN_LIMIT = 70.0
 LOW = -1e30
+ROOMY = pltpu.CompilerParams(vmem_limit_bytes=24 << 20)
 
 
 def dot(a, b):
@@ -179,7 +180,7 @@
             num_scalar_prefetch=1,
             grid=(1,),
             in_specs=[own_spec, whole, whole]
-            + [pl.BlockSpec(memory_space=pl.ANY)] * len(sources),
+            + [pl.BlockSpec(memory_space=pltpu.HBM)] * len(sources),
             out_specs=[whole, whole],
             scratch_shapes=[
                 pltpu.VMEM((4, 2, ZONES, 2 * HEAD_DIM, HEAD_DIM), jnp.bfloat16),
@@ -191,7 +192,7 @@
             ],
         ),
         out_shape=[out, out],
-        compiler_params=pltpu.CompilerParams(vmem_limit_bytes=24 << 20),
+        compiler_params=ROOMY,
         cost_estimate=pl.CostEstimate(
             flops=4 * rows * KEYS * HEAD_DIM,
             bytes_accessed=4 * KEYS * HEAD_DIM + 4 * rows * HEAD_DIM,
@@ -213,20 +214,21 @@
     pick = jnp.where(column == wanted, 1.0, 0.0).astype(jnp.bfloat16)
     is_count = lane[:1] < K_NORM
     queries, keys, values = (queries_ref, True), (keys_ref, False), (values_ref, True)
-    first = [(queries, 0, 0), (keys, 0, 128), (values, 0, 256), (keys, 1, 400), (values, 1, 528)]
-    rest = [(keys, 2, 0), (values, 2, 128), (queries, 1, 256), (queries, 2, 384)]
+    first = [(keys, 0), (values, 0)]
+    rest = [(part, head) for head in range(1, heads) for part in (keys, values)]
+    rest += [(queries, head) for head in range(heads)]
     for g in range(groups):
         for out_ref, parts in ((first_ref, first), (rest_ref, rest)):
-            for (ref, turn), head, at in parts:
+            for j, ((ref, turn), head) in enumerate(parts):
                 start = g * local + head * HEAD_DIM
                 block = ref[:, start : start + HEAD_DIM]
-                out_ref[g, at : at + HEAD_DIM] = block.T if turn else block
+                out_ref[g, j * HEAD_DIM : (j + 1) * HEAD_DIM] = block.T if turn else block
         rows = [ref[:, g * local : (g + 1) * local].astype(jnp.float32) for ref in (keys_ref, queries_ref)]
         squares = jnp.concatenate([(x * x).astype(jnp.bfloat16) for x in rows], axis=1)
         norms = jnp.max(dot(squares, pick), axis=0, keepdims=True) * 1.02
         note = jnp.where(is_count, counts, norms)
         note = jnp.broadcast_to(note, (NOTE, HEAD_DIM)).astype(jnp.bfloat16)
-        first_ref[g, 3 * HEAD_DIM : 3 * HEAD_DIM + NOTE] = note
+        first_ref[g, len(first) * HEAD_DIM :] = note
 
 
 def packed(rows):
@@ -250,7 +252,7 @@
 
 
 def merge(parts):
-    return pl.pallas_call(merge_kernel, out_shape=packed(len(parts) // 2 * HEAD_DIM))(*parts)
+    return pl.pallas_call(merge_kernel, out_shape=packed(len(parts) // 2 * HEAD_DIM), compiler_params=ROOMY)(*parts)
 
 
 def gate_kernel(gate_ref, mixed_ref, out_ref):
@@ -313,35 +315,32 @@
 
     pair = 2 * HEAD_DIM
     first, rest = pl.pallas_call(
-        pack_kernel, out_shape=[packed(5 * HEAD_DIM + NOTE), packed(4 * HEAD_DIM)]
+        pack_kernel, out_shape=[packed(pair + NOTE), packed((3 * heads - 2) * HEAD_DIM)], compiler_params=ROOMY
     )(queries, keys, values, span_ids.reshape(1, -1))
     first = exchange(first)
     rest, first = after(rest, first)
     rest = exchange(rest)
-    one_from = 3 * HEAD_DIM + NOTE
-    own_q, block, block_one = after(
-        first[:, :HEAD_DIM], first[:, HEAD_DIM:one_from], first[:, one_from:]
-    )
-    their_q = [lax.ppermute(own_q, "head", partner), None, None]
-    above, below = sides(block)
-    block_one, above, below = after(block_one, above, below)
-    above_one, below_one = sides(block_one)
-    near = jnp.stack([block, above, below, lax.ppermute(above, "head", down)])
+    above, below = sides(first)
+    near = jnp.stack([first, above, below, lax.ppermute(above, "head", down)])
 
     def combined(notes):
         is_count = jnp.arange(HEAD_DIM) < K_NORM
         return jnp.where(is_count, jnp.sum(notes, axis=0), jnp.max(notes, axis=0))
 
     note = combined(near[:, :, pair].reshape(-1, HEAD_DIM).astype(jnp.float32))[None]
-    note, above_one, below_one = after(note, above_one, below_one)
+    rest, near, note = after(rest, near, note)
+    own_q = [rest[:, start : start + HEAD_DIM] for start in range(2 * pair, rest.shape[1], HEAD_DIM)]
+    own_q[0], block_one, block_two = after(own_q[0], rest[:, :pair], rest[:, pair : 2 * pair])
+    above, below = sides(block_one)
+    their_q = [lax.ppermute(own_q[0], "head", partner), None, None]
+    near, far = swapped(near)
+    note, above, below = after(note, above, below)
     notes = [
         note,
         lax.ppermute(note, "span", core_swap),
         lax.ppermute(note, "head", partner),
         lax.ppermute(note, BOTH, other),
     ]
-    near, far = swapped(near)
-    block_two, *own_q = after(rest[:, :pair], rest[:, pair:-HEAD_DIM], rest[:, -HEAD_DIM:])
     note = combined(jnp.concatenate(notes))
     squares = note[K_NORM : K_NORM + heads] * note[Q_NORM : Q_NORM + heads]
     plain = (squares * (1.05 * SCALE**2) < PLAIN_LIMIT**2).astype(jnp.int32)
@@ -364,17 +363,16 @@
     parts = [None] * (2 * heads)
 
     def attended(info, head, sources):
-        own, at = (first, 0) if head == 0 else (rest, 1 + head)
-        parts[2 * head], theirs = attend(info, own, at, their_q[head], seen, sources, head)
+        parts[2 * head], theirs = attend(info, rest, 4 + head, their_q[head], seen, sources, head)
         info, theirs = after(info, theirs)
         parts[2 * head + 1] = lax.ppermute(theirs, "head", partner)
         return info
 
-    info, block_two, above, below = after(info, block_two, above_one, below_one)
+    info, block_two, above, below = after(info, block_two, above, below)
     opposite = lax.ppermute(below, "head", up)
     above_two, below_two = sides(block_two)
-    own_q[0], own_q[1], info = after(own_q[0], own_q[1], info)
-    their_q[1] = lax.ppermute(own_q[0], "head", partner)
+    own_q[1], own_q[2], info = after(own_q[1], own_q[2], info)
+    their_q[1] = lax.ppermute(own_q[1], "head", partner)
     info = attended(info, 0, (near, far))
     info, opposite, above_two, below_two, their_q[1] = after(
         info, opposite, above_two, below_two, their_q[1]
@@ -382,7 +380,7 @@
     near, far = swapped(jnp.stack([block_one, above, below, opposite]))
     opposite = lax.ppermute(above_two, "head", down)
     near_two, far_two = swapped(jnp.stack([block_two, above_two, below_two]))
-    their_q[2] = lax.ppermute(own_q[1], "head", partner)
+    their_q[2] = lax.ppermute(own_q[2], "head", partner)
     info = attended(info, 1, (near, far))
     info, opposite, their_q[2] = after(info, opposite, their_q[2])
     last, far_last = swapped(opposite[None])
@@ -390,7 +388,7 @@
     mixed = exchange(merge(parts))
     gates = gate_rows(span_ids, timesteps, time_weight)
     return pl.pallas_call(
-        gate_kernel, out_shape=jax.ShapeDtypeStruct((chunk, width), jnp.bfloat16)
+        gate_kernel, out_shape=jax.ShapeDtypeStruct((chunk, width), jnp.bfloat16), compiler_params=ROOMY
     )(gates, mixed)
 
 

time: 326 us -> 321 us (0.985)
  blocking collectives: 23.9 us -> 15.2 us
  waiting for transfers between devices: 36.8 us -> 44.1 us
  Pallas kernels: 214 us -> 208 us
  starting transfers between devices: 33 us -> 37.4 us
    ppermute x4, waiting for transfers between devices: 3.01 us -> 12.9 us  [the longest x1 9.82 us: per_device(): near = jnp.stack([first, above, below, lax.ppermute(above, 'head', down)])]
    all_to_all x1, blocking collectives: 23.9 us -> 15.2 us  [exchange(): lax.all_to_all(parts, BOTH, split_axis=0, concat_axis=0, axis_index_group...]
    ppermute x1, starting transfers between devices: 0.69 us -> 7.35 us  [per_device(): lax.ppermute(note, BOTH, other)]
    pallas_call x2, Pallas kernels: 6.64 us -> 2.17 us  [the longest x1 1.25 us: merge(): pl.pallas_call(merge_kernel, out_shape=packed(len(parts) // 2 * HEAD_DIM)...]
    ppermute x6, waiting for transfers between devices: 16.8 us -> 12.8 us  [sides(): return (lax.ppermute(block, 'head', down), lax.ppermute(block, 'head', up))]
    ppermute x4, starting transfers between devices: 0.97 us -> 4.91 us  [swapped(): return (block, lax.ppermute(block, 'span', core_swap))]
    unnamed x24 -> x32, local copies, waits for them, and re-layouts: 3.76 us -> 7.7 us
    ppermute x1, starting transfers between devices: 3.97 us -> 0.67 us  [per_device(): lax.ppermute(note, 'span', core_swap)]
  transfers between devices with their start and end apart: 24 -> 24, of which waited for: 7 -> 9; matrix products, arithmetic and copies ran while one was open for 3% -> 2% of each run, Pallas kernels for 63% -> 63%
where the time goes in v9:
time: 321 us; the launch traced here: 322 us
  Pallas kernels  208 us (65%)
  waiting for transfers between devices  44.1 us (14%)
  starting transfers between devices  37.4 us (12%)
  blocking collectives  15.2 us (5%)
  local copies, waits for them, and re-layouts  9.5 us (3%)
  other arithmetic  6.27 us (2%)
    pallas_call x3, Pallas kernels, attend(): pl.pallas_call(functools.partial(attend_kernel, head), grid_spec=pltpu.Pr...  204 us
    all_to_all x1, blocking collectives, exchange(): lax.all_to_all(parts, BOTH, split_axis=0, concat_axis=0, axis_index_group...  15.2 us
    ppermute x6, waiting for transfers between devices, sides(): return (lax.ppermute(block, 'head', down), lax.ppermute(block, 'head', up))  12.8 us
    ppermute x1, waiting for transfers between devices, per_device(): near = jnp.stack([first, above, below, lax.ppermute(above, 'head', down)])  9.82 us
    all_to_all x2, waiting for transfers between devices, exchange(): lax.all_to_all(parts, BOTH, split_axis=0, concat_axis=0, axis_index_group...  9.13 us
    all_to_all x2, starting transfers between devices, exchange(): lax.all_to_all(parts, BOTH, split_axis=0, concat_axis=0, axis_index_group...  7.93 us
    unnamed x32, local copies, waits for them, and re-layouts  7.7 us
    ppermute x1, starting transfers between devices, per_device(): lax.ppermute(note, BOTH, other)  7.35 us
  transfers between devices with their start and end apart: 24, of which 9 were waited for; matrix products, arithmetic and copies ran while one was open for 2% of the time, Pallas kernels for 63%

profile of v9, /device:TPU:25, one launch (start us, length us, event | category | flops | bytes accessed | tf_op | source)
XLA Modules:
  0.0 322.1 jit_solution(306126867640698734)
XLA Ops:
  0.0 1.3 copy-done.2
  1.3 1.1 copy-done.3
  2.4 1.1 copy-done.4
  3.5 0.7 copy-done.5
  4.2 0.9 shard_map.64
  5.1 1.2 copy-done.1
  6.3 15.2 %all_to_all.15 = bf16[8,272,128]{2,1,0:T(8,128)(2,1)} all-to-all(bf16[8,272,128]{2,1,0:T(8,128)(2,1)S(1)} %get-tuple-element.45), channel_id=1, replica_groups={{0,16,32,48,64,80,96,112},{1,17,33,49,65,81,97,113},{2,18,34,50,66,82,9..., dimensions={0} | all-to-all | bytes 1114112 | tf_op jit(solution)/shard_map/all_to_all | solution.py:303
  21.5 0.5 collective-permute-start
  22.0 3.6 %all-to-all-start.1 = ((bf16[8,896,128]{2,1,0:T(8,128)(2,1)}), bf16[8,896,128]{2,1,0:T(8,128)(2,1)S(1)}, u32[]{:S(2)}, u32[]{:S(2)}) async-start(bf16[8,896,128]{2,1,0:T(8,128)(2,1)} %copy-done.1), calls=%async_computation.1 | async-start | bytes 3670016 | tf_op jit(solution)/shard_map/all_to_all | solution.py:303
  25.6 2.3 collective-permute-start.1
  27.9 7.1 %collective-permute-done = bf16[8,272,128]{2,1,0:T(8,128)(2,1)} collective-permute-done((bf16[8,272,128]{2,1,0:T(8,128)(2,1)}, bf16[8,272,128]{2,1,0:T(8,128)(2,1)}, u32[]{:S(2)}, u32[]{:S(2)}) %collective-permute-start) | collective-permute-done | bytes 557088 | tf_op jit(solution)/shard_map/ppermute | solution.py:314
  34.9 2.7 collective-permute-done.1
  37.6 9.8 %collective-permute-done.2 = bf16[8,272,128]{2,1,0:T(8,128)(2,1)} collective-permute-done((bf16[8,272,128]{2,1,0:T(8,128)(2,1)}, bf16[8,272,128]{2,1,0:T(8,128)(2,1)}, u32[]{:S(2)}, u32[]{:S(2)}) %collective-permute-start.2) | collective-permute-done | bytes 557088 | tf_op jit(solution)/shard_map/ppermute | solution.py:324
  47.4 3.2 pad_maximum_fusion.refs_0_
  50.6 0.9 slice_reduce_fusion
  51.5 0.9 convert_reduce_fusion
  52.4 0.9 fusion.19
  53.3 0.9 fusion.18
  54.2 0.8 copy-done.8
  55.0 1.9 collective-permute-start.4
  56.9 0.1 add_multiply_fusion
  57.0 0.1 broadcast_add_fusion
  57.1 4.7 %collective-permute-start.9 = (bf16[4,8,272,128]{3,2,1,0:T(8,128)(2,1)}, bf16[4,8,272,128]{3,2,1,0:T(8,128)(2,1)}, u32[]{:S(2)}, u32[]{:S(2)}) collective-permute-start(bf16[4,8,272,128]{3,2,1,0:T(8,128)(2,1)} %pad_maximum_fusion.refs_0_), channel_id=1, source_target_pairs={{0,8},{8,0},{16,24},{24,16},{32,40},{40,32},{48,56},{56,48},{64,72... | collective-permute-start | bytes 6684680 | tf_op jit(solution)/shard_map/ppermute | solution.py:311
  61.7 3.0 collective-permute-done.3
  64.8 0.8 copy-done.10
  65.6 7.4 %collective-permute-start.7 = (f32[1,128]{1,0:T(1,128)S(1)}, f32[1,128]{1,0:T(1,128)S(1)}, u32[]{:S(2)}, u32[]{:S(2)}) collective-permute-start(f32[1,128]{1,0:T(1,128)S(1)} %compare_select_fusion.1), channel_id=1, source_target_pairs={{0,9},{1,8},{2,11},{3,10},{4,13},{5,12},{6,15},{7,14},{8,1},{9,0},... | collective-permute-start | bytes 1544 | tf_op jit(solution)/shard_map/ppermute | solution.py:342
  72.9 0.5 collective-permute-start.6
  73.4 0.7 collective-permute-start.5
  74.1 0.1 fusion.12
  74.2 1.8 collective-permute-start.8
  76.0 0.8 collective-permute-done.6
  76.8 0.1 select_reduce_fusion
  77.0 0.1 compare_convert_fusion
  77.0 0.1 fusion.15
  77.2 0.1 pad_add_fusion.info_ref
  77.3 0.0 collective-permute-start.12
  77.3 2.7 collective-permute-start.13
  80.0 0.7 collective-permute-start.11
  80.7 3.1 collective-permute-done.8.their_q
  83.8 1.3 collective-permute-start.14
  85.1 67.3 %shard_map.65 = (bf16[8,144,128]{2,1,0:T(8,128)(2,1)S(1)}, bf16[8,144,128]{2,1,0:T(8,128)(2,1)S(1)}) custom-call(s32[13]{0:T(128)S(1)} %pad_add_fusion.info_ref, bf16[8,896,128]{2,1,0:T(8,128)(2,1)S(1)} %all-to-all-done.1.own_q, bf16[8,128,128]{2,1,0:T(8,128)(2,1)S(1)} %collective-permute-done.8.their_q, s32[8,1,256]{2,1,0:T(1,128)S(1)} %fusion.13.end_ref, ...), custom_call_target="tpu_custom_call" | custom-call | flops 8589934592 | bytes 5242880 | tf_op jit(solution)/shard_map/pallas_call | solution.py:177
  152.5 0.0 copy-start.7
  152.5 0.3 pad_maximum_fusion.1.refs_0_
  152.8 0.1 collective-permute-start.15
  152.9 0.7 copy-done.7
  153.5 0.2 pad_maximum_fusion.2.refs_0_
  153.7 0.1 collective-permute-start.19
  153.8 1.4 collective-permute-start.18
  155.2 1.8 collective-permute-done.15.refs_1_
  157.0 68.3 %shard_map.66 = (bf16[8,144,128]{2,1,0:T(8,128)(2,1)S(1)}, bf16[8,144,128]{2,1,0:T(8,128)(2,1)S(1)}) custom-call(s32[13]{0:T(128)S(1)} %pad_add_fusion.info_ref, bf16[8,896,128]{2,1,0:T(8,128)(2,1)S(1)} %all-to-all-done.1.own_q, bf16[8,128,128]{2,1,0:T(8,128)(2,1)S(1)} %collective-permute-done.14.their_q, s32[8,1,256]{2,1,0:T(1,128)S(1)} %fusion.13.end_ref, ...), custom_call_target="tpu_custom_call" | custom-call | flops 8589934592 | bytes 5242880 | tf_op jit(solution)/shard_map/pallas_call | solution.py:177
  225.3 0.0 copy-start.15
  225.4 0.1 collective-permute-start.20
  225.4 0.9 collective-permute-start.10
  226.4 2.1 collective-permute-start.16
  228.5 68.1 %shard_map.67 = (bf16[8,144,128]{2,1,0:T(8,128)(2,1)S(1)}, bf16[8,144,128]{2,1,0:T(8,128)(2,1)S(1)}) custom-call(s32[13]{0:T(128)S(1)} %pad_add_fusion.info_ref, bf16[8,896,128]{2,1,0:T(8,128)(2,1)S(1)} %all-to-all-done.1.own_q, bf16[8,128,128]{2,1,0:T(8,128)(2,1)S(1)} %collective-permute-done.18.their_q, s32[8,1,256]{2,1,0:T(1,128)S(1)} %fusion.13.end_ref, ...), custom_call_target="tpu_custom_call" | custom-call | flops 8589934592 | bytes 5242880 | tf_op jit(solution)/shard_map/pallas_call | solution.py:177
  296.6 0.5 collective-permute-start.21
  297.2 6.6 %collective-permute-done.21.refs_5_ = bf16[8,144,128]{2,1,0:T(8,128)(2,1)S(1)} collective-permute-done((bf16[8,144,128]{2,1,0:T(8,128)(2,1)S(1)}, bf16[8,144,128]{2,1,0:T(8,128)(2,1)S(1)}, u32[]{:S(2)}, u32[]{:S(2)}) %collective-permute-start.21) | collective-permute-done | bytes 294944 | tf_op jit(solution)/shard_map/ppermute | solution.py:368
  303.8 1.3 shard_map.68
  305.0 4.3 %all-to-all-start.2 = ((bf16[8,384,128]{2,1,0:T(8,128)(2,1)}), bf16[8,384,128]{2,1,0:T(8,128)(2,1)}, u32[]{:S(2)}, u32[]{:S(2)}) async-start(bf16[8,384,128]{2,1,0:T(8,128)(2,1)} %shard_map.68), calls=%async_computation.2 | async-start | bytes 1572864 | tf_op jit(solution)/shard_map/all_to_all | solution.py:303
  309.4 0.1 fusion.2
  309.5 0.3 fusion.4
  309.8 0.8 fusion.gate_ref
  310.7 9.1 %all-to-all-done.2.mixed_ref = bf16[8,384,128]{2,1,0:T(8,128)(2,1)} async-done(((bf16[8,384,128]{2,1,0:T(8,128)(2,1)}), bf16[8,384,128]{2,1,0:T(8,128)(2,1)}, u32[]{:S(2)}, u32[]{:S(2)}) %all-to-all-start.2) | async-done | bytes 786464 | tf_op jit(solution)/shard_map/all_to_all | solution.py:303
  319.8 2.3 shard_map.69
  (51 shorter events, 0.2 us)
Async XLA Ops:
  0.0 309.5 %copy-start = (bf16[256,3072]{1,0:T(8,128)(2,1)S(1)}, bf16[256,3072]{1,0:T(8,128)(2,1)}, u32[]{:S(2)}) copy-start(bf16[256,3072]{1,0:T(8,128)(2,1)} %param.11) | copy-start | bytes 4718596
  0.0 1.3 copy-start.2
  1.3 1.1 copy-start.3
  2.4 1.1 copy-start.4
  3.5 0.7 copy-start.5
  5.1 1.2 copy-start.1
  21.5 13.4 %collective-permute-start = (bf16[8,272,128]{2,1,0:T(8,128)(2,1)}, bf16[8,272,128]{2,1,0:T(8,128)(2,1)}, u32[]{:S(2)}, u32[]{:S(2)}) collective-permute-start(bf16[8,272,128]{2,1,0:T(8,128)(2,1)} %all_to_all.15), channel_id=1, source_target_pairs={{0,6},{1,7},{2,0},{3,1},{4,2},{5,3},{6,4},{7,5},{8,14},{9,15},{10,... | collective-permute-start | bytes 1671176 | tf_op jit(solution)/shard_map/ppermute | solution.py:314
  22.0 30.4 %all-to-all-start.1 = ((bf16[8,896,128]{2,1,0:T(8,128)(2,1)}), bf16[8,896,128]{2,1,0:T(8,128)(2,1)S(1)}, u32[]{:S(2)}, u32[]{:S(2)}) async-start(bf16[8,896,128]{2,1,0:T(8,128)(2,1)} %copy-done.1), calls=%async_computation.1 | async-start | bytes 3670016 | tf_op jit(solution)/shard_map/all_to_all | solution.py:303
  25.6 12.0 %collective-permute-start.1 = (bf16[8,272,128]{2,1,0:T(8,128)(2,1)}, bf16[8,272,128]{2,1,0:T(8,128)(2,1)}, u32[]{:S(2)}, u32[]{:S(2)}) collective-permute-start(bf16[8,272,128]{2,1,0:T(8,128)(2,1)} %all_to_all.15), channel_id=1, source_target_pairs={{0,2},{1,3},{2,4},{3,5},{4,6},{5,7},{6,0},{7,1},{8,10},{9,11},{10,... | collective-permute-start | bytes 1671176 | tf_op jit(solution)/shard_map/ppermute | solution.py:314
  34.9 12.5 %collective-permute-start.2 = (bf16[8,272,128]{2,1,0:T(8,128)(2,1)}, bf16[8,272,128]{2,1,0:T(8,128)(2,1)}, u32[]{:S(2)}, u32[]{:S(2)}) collective-permute-start(bf16[8,272,128]{2,1,0:T(8,128)(2,1)} %collective-permute-done), channel_id=1, source_target_pairs={{0,6},{1,7},{2,0},{3,1},{4,2},{5,3},{6,4},{7,5},{8,14},{9,15},{10,... | collective-permute-start | bytes 1671176 | tf_op jit(solution)/shard_map/ppermute | solution.py:324
  54.2 0.8 copy-start.8
  54.2 10.5 %collective-permute-start.3 = (bf16[8,256,128]{2,1,0:T(8,128)(2,1)S(1)}, bf16[8,256,128]{2,1,0:T(8,128)(2,1)S(1)}, u32[]{:S(2)}, u32[]{:S(2)}) collective-permute-start(bf16[8,256,128]{2,1,0:T(8,128)(2,1)S(1)} %get-tuple-element.50), channel_id=1, source_target_pairs={{0,6},{1,7},{2,0},{3,1},{4,2},{5,3},{6,4},{7,5},{8,14},{9,15},{10,... | collective-permute-start | bytes 1572872 | tf_op jit(solution)/shard_map/ppermute | solution.py:314
  55.0 9.8 %collective-permute-start.4 = (bf16[8,256,128]{2,1,0:T(8,128)(2,1)S(1)}, bf16[8,256,128]{2,1,0:T(8,128)(2,1)S(1)}, u32[]{:S(2)}, u32[]{:S(2)}) collective-permute-start(bf16[8,256,128]{2,1,0:T(8,128)(2,1)S(1)} %get-tuple-element.50), channel_id=1, source_target_pairs={{0,2},{1,3},{2,4},{3,5},{4,6},{5,7},{6,0},{7,1},{8,10},{9,11},{10,... | collective-permute-start | bytes 1572872 | tf_op jit(solution)/shard_map/ppermute | solution.py:314
  57.1 28.0 %collective-permute-start.9 = (bf16[4,8,272,128]{3,2,1,0:T(8,128)(2,1)}, bf16[4,8,272,128]{3,2,1,0:T(8,128)(2,1)}, u32[]{:S(2)}, u32[]{:S(2)}) collective-permute-start(bf16[4,8,272,128]{3,2,1,0:T(8,128)(2,1)} %pad_maximum_fusion.refs_0_), channel_id=1, source_target_pairs={{0,8},{8,0},{16,24},{24,16},{32,40},{40,32},{48,56},{56,48},{64,72... | collective-permute-start | bytes 6684680 | tf_op jit(solution)/shard_map/ppermute | solution.py:311
  64.8 0.8 copy-start.10
  65.6 7.4 %copy-start.12 = (bf16[8,256,128]{2,1,0:T(8,128)(2,1)}, bf16[8,256,128]{2,1,0:T(8,128)(2,1)S(1)}, u32[]{:S(2)}) copy-start(bf16[8,256,128]{2,1,0:T(8,128)(2,1)S(1)} %collective-permute-done.4) | copy-start | bytes 1572868
  65.6 10.4 %collective-permute-start.7 = (f32[1,128]{1,0:T(1,128)S(1)}, f32[1,128]{1,0:T(1,128)S(1)}, u32[]{:S(2)}, u32[]{:S(2)}) collective-permute-start(f32[1,128]{1,0:T(1,128)S(1)} %compare_select_fusion.1), channel_id=1, source_target_pairs={{0,9},{1,8},{2,11},{3,10},{4,13},{5,12},{6,15},{7,14},{8,1},{9,0},... | collective-permute-start | bytes 1544 | tf_op jit(solution)/shard_map/ppermute | solution.py:342
  72.9 3.9 %collective-permute-start.6 = (f32[1,128]{1,0:T(1,128)S(1)}, f32[1,128]{1,0:T(1,128)S(1)}, u32[]{:S(2)}, u32[]{:S(2)}) collective-permute-start(f32[1,128]{1,0:T(1,128)S(1)} %compare_select_fusion.1), channel_id=1, source_target_pairs={{0,1},{1,0},{2,3},{3,2},{4,5},{5,4},{6,7},{7,6},{8,9},{9,8},{10,11... | collective-permute-start | bytes 1544 | tf_op jit(solution)/shard_map/ppermute | solution.py:341
  73.4 3.4 %collective-permute-start.5 = (f32[1,128]{1,0:T(1,128)S(1)}, f32[1,128]{1,0:T(1,128)S(1)}, u32[]{:S(2)}, u32[]{:S(2)}) collective-permute-start(f32[1,128]{1,0:T(1,128)S(1)} %compare_select_fusion.1), channel_id=1, source_target_pairs={{0,8},{8,0},{16,24},{24,16},{32,40},{40,32},{48,56},{56,48},{64,72... | collective-permute-start | bytes 1544 | tf_op jit(solution)/shard_map/ppermute | solution.py:340
  74.2 9.6 %collective-permute-start.8 = (bf16[8,128,128]{2,1,0:T(8,128)(2,1)}, bf16[8,128,128]{2,1,0:T(8,128)(2,1)S(1)}, u32[]{:S(2)}, u32[]{:S(2)}) collective-permute-start(bf16[8,128,128]{2,1,0:T(8,128)(2,1)} %get-tuple-element.57), channel_id=1, source_target_pairs={{0,1},{1,0},{2,3},{3,2},{4,5},{5,4},{6,7},{7,6},{8,9},{9,8},{10,11... | collective-permute-start | bytes 786440 | tf_op jit(solution)/shard_map/ppermute | solution.py:335
  77.3 75.1 %collective-permute-start.12 = (bf16[8,256,128]{2,1,0:T(8,128)(2,1)}, bf16[8,256,128]{2,1,0:T(8,128)(2,1)S(1)}, u32[]{:S(2)}, u32[]{:S(2)}) collective-permute-start(bf16[8,256,128]{2,1,0:T(8,128)(2,1)} %get-tuple-element.64), channel_id=1, source_target_pairs={{0,6},{1,7},{2,0},{3,1},{4,2},{5,3},{6,4},{7,5},{8,14},{9,15},{10,... | collective-permute-start | bytes 1572872 | tf_op jit(solution)/shard_map/ppermute | solution.py:314
  77.3 75.1 %collective-permute-start.13 = (bf16[8,256,128]{2,1,0:T(8,128)(2,1)}, bf16[8,256,128]{2,1,0:T(8,128)(2,1)S(1)}, u32[]{:S(2)}, u32[]{:S(2)}) collective-permute-start(bf16[8,256,128]{2,1,0:T(8,128)(2,1)} %get-tuple-element.64), channel_id=1, source_target_pairs={{0,2},{1,3},{2,4},{3,5},{4,6},{5,7},{6,0},{7,1},{8,10},{9,11},{10,... | collective-permute-start | bytes 1572872 | tf_op jit(solution)/shard_map/ppermute | solution.py:314
  80.0 72.4 %collective-permute-start.11 = (bf16[8,256,128]{2,1,0:T(8,128)(2,1)}, bf16[8,256,128]{2,1,0:T(8,128)(2,1)S(1)}, u32[]{:S(2)}, u32[]{:S(2)}) collective-permute-start(bf16[8,256,128]{2,1,0:T(8,128)(2,1)} %copy-done.12), channel_id=1, source_target_pairs={{0,2},{1,3},{2,4},{3,5},{4,6},{5,7},{6,0},{7,1},{8,10},{9,11},{10,... | collective-permute-start | bytes 1572872 | tf_op jit(solution)/shard_map/ppermute | solution.py:372
  80.7 71.8 %copy-start.9 = (bf16[8,256,128]{2,1,0:T(8,128)(2,1)S(1)}, bf16[8,256,128]{2,1,0:T(8,128)(2,1)}, u32[]{:S(2)}) copy-start(bf16[8,256,128]{2,1,0:T(8,128)(2,1)} %copy-done.8) | copy-start | bytes 1572868
  80.7 71.8 %copy-start.11 = (bf16[8,256,128]{2,1,0:T(8,128)(2,1)S(1)}, bf16[8,256,128]{2,1,0:T(8,128)(2,1)}, u32[]{:S(2)}) copy-start(bf16[8,256,128]{2,1,0:T(8,128)(2,1)} %copy-done.10) | copy-start | bytes 1572868
  80.7 71.8 %copy-start.13 = (bf16[8,256,128]{2,1,0:T(8,128)(2,1)S(1)}, bf16[8,256,128]{2,1,0:T(8,128)(2,1)}, u32[]{:S(2)}) copy-start(bf16[8,256,128]{2,1,0:T(8,128)(2,1)} %copy-done.12) | copy-start | bytes 1572868
  83.8 68.6 %collective-permute-start.14 = (bf16[8,128,128]{2,1,0:T(8,128)(2,1)}, bf16[8,128,128]{2,1,0:T(8,128)(2,1)S(1)}, u32[]{:S(2)}, u32[]{:S(2)}) collective-permute-start(bf16[8,128,128]{2,1,0:T(8,128)(2,1)} %get-tuple-element.65), channel_id=1, source_target_pairs={{0,1},{1,0},{2,3},{3,2},{4,5},{5,4},{6,7},{7,6},{8,9},{9,8},{10,11... | collective-permute-start | bytes 786440 | tf_op jit(solution)/shard_map/ppermute | solution.py:375
  152.5 1.0 copy-start.7
  152.8 1.0 copy-start.14
  152.8 4.2 %collective-permute-start.15 = (bf16[4,8,256,128]{3,2,1,0:T(8,128)(2,1)S(1)}, bf16[4,8,256,128]{3,2,1,0:T(8,128)(2,1)S(1)}, u32[]{:S(2)}, u32[]{:S(2)}) collective-permute-start(bf16[4,8,256,128]{3,2,1,0:T(8,128)(2,1)S(1)} %pad_maximum_fusion.1.refs_0_), channel_id=1, source_target_pairs={{0,8},{8,0},{16,24},{24,16},{32,40},{40,32},{48,56},{56,48},{64,72... | collective-permute-start | bytes 6291464 | tf_op jit(solution)/shard_map/ppermute | solution.py:311
  153.7 74.8 %collective-permute-start.19 = (bf16[3,8,256,128]{3,2,1,0:T(8,128)(2,1)S(1)}, bf16[3,8,256,128]{3,2,1,0:T(8,128)(2,1)S(1)}, u32[]{:S(2)}, u32[]{:S(2)}) collective-permute-start(bf16[3,8,256,128]{3,2,1,0:T(8,128)(2,1)S(1)} %pad_maximum_fusion.2.refs_0_), channel_id=1, source_target_pairs={{0,8},{8,0},{16,24},{24,16},{32,40},{40,32},{48,56},{56,48},{64,72... | collective-permute-start | bytes 4718600 | tf_op jit(solution)/shard_map/ppermute | solution.py:311
  153.8 71.5 %collective-permute-start.18 = (bf16[8,128,128]{2,1,0:T(8,128)(2,1)S(1)}, bf16[8,128,128]{2,1,0:T(8,128)(2,1)S(1)}, u32[]{:S(2)}, u32[]{:S(2)}) collective-permute-start(bf16[8,128,128]{2,1,0:T(8,128)(2,1)S(1)} %copy-done.14), channel_id=1, source_target_pairs={{0,1},{1,0},{2,3},{3,2},{4,5},{5,4},{6,7},{7,6},{8,9},{9,8},{10,11... | collective-permute-start | bytes 786440 | tf_op jit(solution)/shard_map/ppermute | solution.py:383
  155.2 70.2 %collective-permute-start.17 = (bf16[8,256,128]{2,1,0:T(8,128)(2,1)S(1)}, bf16[8,256,128]{2,1,0:T(8,128)(2,1)S(1)}, u32[]{:S(2)}, u32[]{:S(2)}) collective-permute-start(bf16[8,256,128]{2,1,0:T(8,128)(2,1)S(1)} %collective-permute-done.12), channel_id=1, source_target_pairs={{0,6},{1,7},{2,0},{3,1},{4,2},{5,3},{6,4},{7,5},{8,14},{9,15},{10,... | collective-permute-start | bytes 1572872 | tf_op jit(solution)/shard_map/ppermute | solution.py:381
  225.3 71.8 %copy-start.15 = (s32[24]{0:T(128)S(1)}, s32[24]{0:T(128)}, u32[]{:S(2)}) copy-start(s32[24]{0:T(128)} %param.10) | copy-start | bytes 292
  225.4 3.1 collective-permute-start.20
  225.4 71.7 %collective-permute-start.10 = (bf16[8,144,128]{2,1,0:T(8,128)(2,1)S(1)}, bf16[8,144,128]{2,1,0:T(8,128)(2,1)S(1)}, u32[]{:S(2)}, u32[]{:S(2)}) collective-permute-start(bf16[8,144,128]{2,1,0:T(8,128)(2,1)S(1)} %get-tuple-element.61), channel_id=1, source_target_pairs={{0,1},{1,0},{2,3},{3,2},{4,5},{5,4},{6,7},{7,6},{8,9},{9,8},{10,11... | collective-permute-start | bytes 884744 | tf_op jit(solution)/shard_map/ppermute | solution.py:368
  226.4 70.8 %collective-permute-start.16 = (bf16[8,144,128]{2,1,0:T(8,128)(2,1)S(1)}, bf16[8,144,128]{2,1,0:T(8,128)(2,1)S(1)}, u32[]{:S(2)}, u32[]{:S(2)}) collective-permute-start(bf16[8,144,128]{2,1,0:T(8,128)(2,1)S(1)} %get-tuple-element.72), channel_id=1, source_target_pairs={{0,1},{1,0},{2,3},{3,2},{4,5},{5,4},{6,7},{7,6},{8,9},{9,8},{10,11... | collective-permute-start | bytes 884744 | tf_op jit(solution)/shard_map/ppermute | solution.py:368
  296.6 7.2 %collective-permute-start.21 = (bf16[8,144,128]{2,1,0:T(8,128)(2,1)S(1)}, bf16[8,144,128]{2,1,0:T(8,128)(2,1)S(1)}, u32[]{:S(2)}, u32[]{:S(2)}) collective-permute-start(bf16[8,144,128]{2,1,0:T(8,128)(2,1)S(1)} %get-tuple-element.82), channel_id=1, source_target_pairs={{0,1},{1,0},{2,3},{3,2},{4,5},{5,4},{6,7},{7,6},{8,9},{9,8},{10,11... | collective-permute-start | bytes 884744 | tf_op jit(solution)/shard_map/ppermute | solution.py:368
  305.0 4.8 %copy-start.6 = (s32[128]{0:T(128)S(1)}, s32[128]{0:T(128)}, u32[]{:S(2)}) copy-start(s32[128]{0:T(128)} %param.9) | copy-start | bytes 1540
  305.0 14.8 %all-to-all-start.2 = ((bf16[8,384,128]{2,1,0:T(8,128)(2,1)}), bf16[8,384,128]{2,1,0:T(8,128)(2,1)}, u32[]{:S(2)}, u32[]{:S(2)}) async-start(bf16[8,384,128]{2,1,0:T(8,128)(2,1)} %shard_map.68), calls=%async_computation.2 | async-start | bytes 1572864 | tf_op jit(solution)/shard_map/all_to_all | solution.py:303

commit v10 on v9

--- a/solution.py
+++ b/solution.py
@@ -296,7 +296,6 @@
     up = [(h, (h + 2) % groups) for h in range(groups)]
     down = [(h, (h - 2) % groups) for h in range(groups)]
     core_swap = [(s, s ^ 1) for s in range(runs)]
-    other = [((s * groups + h), ((s ^ 1) * groups + (h ^ 1))) for s in range(runs) for h in range(groups)]
     partner = [(h, h ^ 1) for h in range(groups)]
 
     def exchange(parts):
@@ -315,7 +314,7 @@
 
     pair = 2 * HEAD_DIM
     first, rest = pl.pallas_call(
-        pack_kernel, out_shape=[packed(pair + NOTE), packed((3 * heads - 2) * HEAD_DIM)], compiler_params=ROOMY
+        pack_kernel, out_shape=[packed(pair + NOTE), packed((3 * heads - 2) * HEAD_DIM)]
     )(queries, keys, values, span_ids.reshape(1, -1))
     first = exchange(first)
     rest, first = after(rest, first)
@@ -327,21 +326,19 @@
         is_count = jnp.arange(HEAD_DIM) < K_NORM
         return jnp.where(is_count, jnp.sum(notes, axis=0), jnp.max(notes, axis=0))
 
-    note = combined(near[:, :, pair].reshape(-1, HEAD_DIM).astype(jnp.float32))[None]
+    def noted(blocks):
+        return combined(blocks[:, :, pair].reshape(-1, HEAD_DIM).astype(jnp.float32))
+
+    note = noted(near)
     rest, near, note = after(rest, near, note)
     own_q = [rest[:, start : start + HEAD_DIM] for start in range(2 * pair, rest.shape[1], HEAD_DIM)]
     own_q[0], block_one, block_two = after(own_q[0], rest[:, :pair], rest[:, pair : 2 * pair])
     above, below = sides(block_one)
     their_q = [lax.ppermute(own_q[0], "head", partner), None, None]
     near, far = swapped(near)
-    note, above, below = after(note, above, below)
-    notes = [
-        note,
-        lax.ppermute(note, "span", core_swap),
-        lax.ppermute(note, "head", partner),
-        lax.ppermute(note, BOTH, other),
-    ]
-    note = combined(jnp.concatenate(notes))
+    note = combined(jnp.stack([note, noted(far)]))[None]
+    note, above, below, their_q[0] = after(note, above, below, their_q[0])
+    note = combined(jnp.concatenate([note, lax.ppermute(note, "head", partner)]))
     squares = note[K_NORM : K_NORM + heads] * note[Q_NORM : Q_NORM + heads]
     plain = (squares * (1.05 * SCALE**2) < PLAIN_LIMIT**2).astype(jnp.int32)
     ends = note[:spans].astype(jnp.int32)

time: 321 us -> 322 us (level)
  starting transfers between devices: 37.4 us -> 31.4 us
  Pallas kernels: 208 us -> 213 us
    ppermute x2 -> x0, starting transfers between devices: 8.02 us -> none  [the longest x1 7.35 us: per_device(): lax.ppermute(note, BOTH, other)]
    unnamed x32 -> x30, local copies, waits for them, and re-layouts: 7.7 us -> 6.05 us
  transfers between devices with their start and end apart: 24 -> 22, of which waited for: 9 -> 9; matrix products, arithmetic and copies ran while one was open for 2% -> 2% of each run, Pallas kernels for 63% -> 64%
where the time goes in v10:
time: 322 us; the launch traced here: 321 us
  Pallas kernels  213 us (66%)
  waiting for transfers between devices  47.1 us (15%)
  starting transfers between devices  31.4 us (10%)
  blocking collectives  15.4 us (5%)
  local copies, waits for them, and re-layouts  7.79 us (2%)
  other arithmetic  4.66 us (1%)
    pallas_call x3, Pallas kernels, attend(): pl.pallas_call(functools.partial(attend_kernel, head), grid_spec=pltpu.Pr...  206 us
    all_to_all x1, blocking collectives, exchange(): lax.all_to_all(parts, BOTH, split_axis=0, concat_axis=0, axis_index_group...  15.4 us
    ppermute x6, waiting for transfers between devices, sides(): return (lax.ppermute(block, 'head', down), lax.ppermute(block, 'head', up))  12.3 us
    ppermute x1, waiting for transfers between devices, per_device(): near = jnp.stack([first, above, below, lax.ppermute(above, 'head', down)])  9.72 us
    all_to_all x2, waiting for transfers between devices, exchange(): lax.all_to_all(parts, BOTH, split_axis=0, concat_axis=0, axis_index_group...  9.13 us
    ppermute x6, starting transfers between devices, sides(): return (lax.ppermute(block, 'head', down), lax.ppermute(block, 'head', up))  8.1 us
    all_to_all x2, starting transfers between devices, exchange(): lax.all_to_all(parts, BOTH, split_axis=0, concat_axis=0, axis_index_group...  7.93 us
    ppermute x3, waiting for transfers between devices, attended(): parts[2 * head + 1] = lax.ppermute(theirs, 'head', partner)  7.01 us
  transfers between devices with their start and end apart: 22, of which 9 were waited for; matrix products, arithmetic and copies ran while one was open for 2% of the time, Pallas kernels for 64%

profile of v10, /device:TPU:25, one launch (start us, length us, event | category | flops | bytes accessed | tf_op | source)
XLA Modules:
  0.0 321.2 jit_solution(3679699777880812811)
XLA Ops:
  0.0 4.0 %shard_map.64 = (bf16[8,272,128]{2,1,0:T(8,128)(2,1)}, bf16[8,896,128]{2,1,0:T(8,128)(2,1)}) custom-call(bf16[128,3072]{1,0:T(8,128)(2,1)} %queries_ref.1, bf16[128,3072]{1,0:T(8,128)(2,1)} %keys_ref.1, bf16[128,3072]{1,0:T(8,128)(2,1)} %values_ref.1, s32[1,128]{1,0:T(1,128)} %bitcast.56), custom_call_target="tpu_custom_call" | custom-call | tf_op jit(solution)/shard_map/pallas_call | solution.py:316
  4.0 15.4 %all_to_all.15 = bf16[8,272,128]{2,1,0:T(8,128)(2,1)} all-to-all(bf16[8,272,128]{2,1,0:T(8,128)(2,1)} %get-tuple-element.46), channel_id=1, replica_groups={{0,16,32,48,64,80,96,112},{1,17,33,49,65,81,97,113},{2,18,34,50,66,82,9..., dimensions={0} | all-to-all | bytes 1114112 | tf_op jit(solution)/shard_map/all_to_all | solution.py:302
  19.4 0.5 collective-permute-start
  19.8 3.6 %all-to-all-start.1 = ((bf16[8,896,128]{2,1,0:T(8,128)(2,1)}), bf16[8,896,128]{2,1,0:T(8,128)(2,1)S(1)}, u32[]{:S(2)}, u32[]{:S(2)}) async-start(bf16[8,896,128]{2,1,0:T(8,128)(2,1)} %get-tuple-element.47), calls=%async_computation.1 | async-start | bytes 3670016 | tf_op jit(solution)/shard_map/all_to_all | solution.py:302
  23.4 2.3 collective-permute-start.1
  25.7 7.1 %collective-permute-done = bf16[8,272,128]{2,1,0:T(8,128)(2,1)} collective-permute-done((bf16[8,272,128]{2,1,0:T(8,128)(2,1)}, bf16[8,272,128]{2,1,0:T(8,128)(2,1)}, u32[]{:S(2)}, u32[]{:S(2)}) %collective-permute-start) | collective-permute-done | bytes 557088 | tf_op jit(solution)/shard_map/ppermute | solution.py:313
  32.8 0.0 collective-permute-start.2
  32.8 2.7 collective-permute-done.1
  35.4 9.7 %collective-permute-done.2 = bf16[8,272,128]{2,1,0:T(8,128)(2,1)S(1)} collective-permute-done((bf16[8,272,128]{2,1,0:T(8,128)(2,1)}, bf16[8,272,128]{2,1,0:T(8,128)(2,1)S(1)}, u32[]{:S(2)}, u32[]{:S(2)}) %collective-permute-start.2) | collective-permute-done | bytes 557088 | tf_op jit(solution)/shard_map/ppermute | solution.py:323
  45.1 1.5 pad_maximum_fusion.refs_0_
  46.6 0.1 convert_reduce_fusion.1
  46.7 0.1 slice_reduce_fusion.1
  46.7 1.3 copy-done.1
  48.0 4.1 %collective-permute-start.3 = (bf16[4,8,272,128]{3,2,1,0:T(8,128)(2,1)}, bf16[4,8,272,128]{3,2,1,0:T(8,128)(2,1)}, u32[]{:S(2)}, u32[]{:S(2)}) collective-permute-start(bf16[4,8,272,128]{3,2,1,0:T(8,128)(2,1)} %copy-done.1), channel_id=1, source_target_pairs={{0,8},{8,0},{16,24},{24,16},{32,40},{40,32},{48,56},{56,48},{64,72... | collective-permute-start | bytes 6684680 | tf_op jit(solution)/shard_map/ppermute | solution.py:310
  52.1 0.1 add_multiply_fusion
  52.2 0.1 broadcast_add_fusion
  52.3 0.9 fusion.19
  53.1 0.9 fusion.18
  54.0 2.7 collective-permute-start.5
  56.7 2.5 collective-permute-start.6
  59.2 0.9 convert_reduce_fusion
  60.1 0.9 slice_reduce_fusion
  61.0 4.5 %collective-permute-done.6.their_q = bf16[8,128,128]{2,1,0:T(8,128)(2,1)S(1)} collective-permute-done((bf16[8,128,128]{2,1,0:T(8,128)(2,1)S(1)}, bf16[8,128,128]{2,1,0:T(8,128)(2,1)S(1)}, u32[]{:S(2)}, u32[]{:S(2)}) %collective-permute-start.6) | collective-permute-done | bytes 262176 | tf_op jit(solution)/shard_map/ppermute | solution.py:337
  65.5 0.7 copy-done.3
  66.2 2.6 collective-permute-done.4
  68.7 0.8 copy-done.8
  69.5 2.5 collective-permute-start.7
  72.0 0.1 fusion.12
  72.1 1.4 collective-permute-done.7
  73.4 0.1 compare_convert_fusion
  73.5 0.1 select_reduce_fusion
  73.6 0.1 fusion.15
  73.8 0.1 pad_add_fusion.info_ref
  73.9 0.0 collective-permute-start.10
  73.9 2.7 collective-permute-start.11
  76.6 0.3 collective-permute-start.9
  76.9 2.5 collective-permute-start.12
  79.4 1.6 copy-done.2
  81.0 0.9 copy-done.4
  82.0 67.9 %shard_map.65 = (bf16[8,144,128]{2,1,0:T(8,128)(2,1)S(1)}, bf16[8,144,128]{2,1,0:T(8,128)(2,1)S(1)}) custom-call(s32[13]{0:T(128)S(1)} %pad_add_fusion.info_ref, bf16[8,896,128]{2,1,0:T(8,128)(2,1)S(1)} %all-to-all-done.1.own_q, bf16[8,128,128]{2,1,0:T(8,128)(2,1)S(1)} %copy-done.4, s32[8,1,256]{2,1,0:T(1,128)S(1)} %fusion.13.end_ref, ...), custom_call_target="tpu_custom_call" | custom-call | flops 8589934592 | bytes 5242880 | tf_op jit(solution)/shard_map/pallas_call | solution.py:177
  150.0 0.0 copy-start.5
  150.0 0.3 pad_maximum_fusion.1.refs_0_
  150.3 0.1 collective-permute-start.13
  150.4 0.7 copy-done.5
  151.0 0.2 pad_maximum_fusion.2.refs_0_
  151.2 0.1 collective-permute-start.17
  151.3 0.1 collective-permute-start.16
  151.4 0.1 collective-permute-start.15
  151.5 3.0 collective-permute-done.13.refs_1_
  154.5 69.1 %shard_map.66 = (bf16[8,144,128]{2,1,0:T(8,128)(2,1)S(1)}, bf16[8,144,128]{2,1,0:T(8,128)(2,1)S(1)}) custom-call(s32[13]{0:T(128)S(1)} %pad_add_fusion.info_ref, bf16[8,896,128]{2,1,0:T(8,128)(2,1)S(1)} %all-to-all-done.1.own_q, bf16[8,128,128]{2,1,0:T(8,128)(2,1)S(1)} %collective-permute-done.12.their_q, s32[8,1,256]{2,1,0:T(1,128)S(1)} %fusion.13.end_ref, ...), custom_call_target="tpu_custom_call" | custom-call | flops 8589934592 | bytes 5242880 | tf_op jit(solution)/shard_map/pallas_call | solution.py:177
  223.7 0.0 copy-start.14
  223.7 0.1 collective-permute-start.18
  223.8 0.1 collective-permute-start.8
  223.9 3.0 collective-permute-start.14
  226.8 68.9 %shard_map.67 = (bf16[8,144,128]{2,1,0:T(8,128)(2,1)S(1)}, bf16[8,144,128]{2,1,0:T(8,128)(2,1)S(1)}) custom-call(s32[13]{0:T(128)S(1)} %pad_add_fusion.info_ref, bf16[8,896,128]{2,1,0:T(8,128)(2,1)S(1)} %all-to-all-done.1.own_q, bf16[8,128,128]{2,1,0:T(8,128)(2,1)S(1)} %collective-permute-done.16.their_q, s32[8,1,256]{2,1,0:T(1,128)S(1)} %fusion.13.end_ref, ...), custom_call_target="tpu_custom_call" | custom-call | flops 8589934592 | bytes 5242880 | tf_op jit(solution)/shard_map/pallas_call | solution.py:177
  295.8 0.1 collective-permute-start.19
  295.9 7.0 %collective-permute-done.19.refs_5_ = bf16[8,144,128]{2,1,0:T(8,128)(2,1)S(1)} collective-permute-done((bf16[8,144,128]{2,1,0:T(8,128)(2,1)S(1)}, bf16[8,144,128]{2,1,0:T(8,128)(2,1)S(1)}, u32[]{:S(2)}, u32[]{:S(2)}) %collective-permute-start.19) | collective-permute-done | bytes 294944 | tf_op jit(solution)/shard_map/ppermute | solution.py:365
  302.9 1.3 shard_map.68
  304.2 4.3 %all-to-all-start.2 = ((bf16[8,384,128]{2,1,0:T(8,128)(2,1)}), bf16[8,384,128]{2,1,0:T(8,128)(2,1)}, u32[]{:S(2)}, u32[]{:S(2)}) async-start(bf16[8,384,128]{2,1,0:T(8,128)(2,1)} %shard_map.68), calls=%async_computation.2 | async-start | bytes 1572864 | tf_op jit(solution)/shard_map/all_to_all | solution.py:302
  308.5 0.1 fusion.2
  308.7 0.3 fusion.4
  309.0 0.8 fusion.gate_ref
  309.8 9.1 %all-to-all-done.2.mixed_ref = bf16[8,384,128]{2,1,0:T(8,128)(2,1)} async-done(((bf16[8,384,128]{2,1,0:T(8,128)(2,1)}), bf16[8,384,128]{2,1,0:T(8,128)(2,1)}, u32[]{:S(2)}, u32[]{:S(2)}) %all-to-all-start.2) | async-done | bytes 786464 | tf_op jit(solution)/shard_map/all_to_all | solution.py:302
  318.9 2.3 shard_map.69
  (48 shorter events, 0.2 us)
Async XLA Ops:
  0.0 308.7 %copy-start = (bf16[256,3072]{1,0:T(8,128)(2,1)S(1)}, bf16[256,3072]{1,0:T(8,128)(2,1)}, u32[]{:S(2)}) copy-start(bf16[256,3072]{1,0:T(8,128)(2,1)} %param.11) | copy-start | bytes 4718596
  19.4 13.4 %collective-permute-start = (bf16[8,272,128]{2,1,0:T(8,128)(2,1)}, bf16[8,272,128]{2,1,0:T(8,128)(2,1)}, u32[]{:S(2)}, u32[]{:S(2)}) collective-permute-start(bf16[8,272,128]{2,1,0:T(8,128)(2,1)} %all_to_all.15), channel_id=1, source_target_pairs={{0,6},{1,7},{2,0},{3,1},{4,2},{5,3},{6,4},{7,5},{8,14},{9,15},{10,... | collective-permute-start | bytes 1671176 | tf_op jit(solution)/shard_map/ppermute | solution.py:313
  19.8 28.2 %all-to-all-start.1 = ((bf16[8,896,128]{2,1,0:T(8,128)(2,1)}), bf16[8,896,128]{2,1,0:T(8,128)(2,1)S(1)}, u32[]{:S(2)}, u32[]{:S(2)}) async-start(bf16[8,896,128]{2,1,0:T(8,128)(2,1)} %get-tuple-element.47), calls=%async_computation.1 | async-start | bytes 3670016 | tf_op jit(solution)/shard_map/all_to_all | solution.py:302
  23.4 12.0 %collective-permute-start.1 = (bf16[8,272,128]{2,1,0:T(8,128)(2,1)}, bf16[8,272,128]{2,1,0:T(8,128)(2,1)S(1)}, u32[]{:S(2)}, u32[]{:S(2)}) collective-permute-start(bf16[8,272,128]{2,1,0:T(8,128)(2,1)} %all_to_all.15), channel_id=1, source_target_pairs={{0,2},{1,3},{2,4},{3,5},{4,6},{5,7},{6,0},{7,1},{8,10},{9,11},{10,... | collective-permute-start | bytes 1671176 | tf_op jit(solution)/shard_map/ppermute | solution.py:313
  32.8 12.4 %collective-permute-start.2 = (bf16[8,272,128]{2,1,0:T(8,128)(2,1)}, bf16[8,272,128]{2,1,0:T(8,128)(2,1)S(1)}, u32[]{:S(2)}, u32[]{:S(2)}) collective-permute-start(bf16[8,272,128]{2,1,0:T(8,128)(2,1)} %collective-permute-done), channel_id=1, source_target_pairs={{0,6},{1,7},{2,0},{3,1},{4,2},{5,3},{6,4},{7,5},{8,14},{9,15},{10,... | collective-permute-start | bytes 1671176 | tf_op jit(solution)/shard_map/ppermute | solution.py:323
  46.6 1.4 copy-start.1
  48.0 11.1 %collective-permute-start.3 = (bf16[4,8,272,128]{3,2,1,0:T(8,128)(2,1)}, bf16[4,8,272,128]{3,2,1,0:T(8,128)(2,1)}, u32[]{:S(2)}, u32[]{:S(2)}) collective-permute-start(bf16[4,8,272,128]{3,2,1,0:T(8,128)(2,1)} %copy-done.1), channel_id=1, source_target_pairs={{0,8},{8,0},{16,24},{24,16},{32,40},{40,32},{48,56},{56,48},{64,72... | collective-permute-start | bytes 6684680 | tf_op jit(solution)/shard_map/ppermute | solution.py:310
  54.0 11.4 %copy-start.6 = (bf16[8,256,128]{2,1,0:T(8,128)(2,1)}, bf16[8,256,128]{2,1,0:T(8,128)(2,1)S(1)}, u32[]{:S(2)}) copy-start(bf16[8,256,128]{2,1,0:T(8,128)(2,1)S(1)} %get-tuple-element.52) | copy-start | bytes 1572868
  54.0 14.7 %collective-permute-start.4 = (bf16[8,256,128]{2,1,0:T(8,128)(2,1)S(1)}, bf16[8,256,128]{2,1,0:T(8,128)(2,1)S(1)}, u32[]{:S(2)}, u32[]{:S(2)}) collective-permute-start(bf16[8,256,128]{2,1,0:T(8,128)(2,1)S(1)} %get-tuple-element.52), channel_id=1, source_target_pairs={{0,6},{1,7},{2,0},{3,1},{4,2},{5,3},{6,4},{7,5},{8,14},{9,15},{10,... | collective-permute-start | bytes 1572872 | tf_op jit(solution)/shard_map/ppermute | solution.py:313
  54.0 14.7 %collective-permute-start.5 = (bf16[8,256,128]{2,1,0:T(8,128)(2,1)S(1)}, bf16[8,256,128]{2,1,0:T(8,128)(2,1)S(1)}, u32[]{:S(2)}, u32[]{:S(2)}) collective-permute-start(bf16[8,256,128]{2,1,0:T(8,128)(2,1)S(1)} %get-tuple-element.52), channel_id=1, source_target_pairs={{0,2},{1,3},{2,4},{3,5},{4,6},{5,7},{6,0},{7,1},{8,10},{9,11},{10,... | collective-permute-start | bytes 1572872 | tf_op jit(solution)/shard_map/ppermute | solution.py:313
  56.7 8.8 %collective-permute-start.6 = (bf16[8,128,128]{2,1,0:T(8,128)(2,1)S(1)}, bf16[8,128,128]{2,1,0:T(8,128)(2,1)S(1)}, u32[]{:S(2)}, u32[]{:S(2)}) collective-permute-start(bf16[8,128,128]{2,1,0:T(8,128)(2,1)S(1)} %get-tuple-element.53), channel_id=1, source_target_pairs={{0,1},{1,0},{2,3},{3,2},{4,5},{5,4},{6,7},{7,6},{8,9},{9,8},{10,11... | collective-permute-start | bytes 786440 | tf_op jit(solution)/shard_map/ppermute | solution.py:337
  65.5 0.7 copy-start.3
  68.7 0.8 copy-start.8
  69.5 2.5 copy-start.10
  69.5 3.9 %collective-permute-start.7 = (f32[1,128]{1,0:T(1,128)S(1)}, f32[1,128]{1,0:T(1,128)S(1)}, u32[]{:S(2)}, u32[]{:S(2)}) collective-permute-start(f32[1,128]{1,0:T(1,128)S(1)} %select_bitcast_fusion), channel_id=1, source_target_pairs={{0,1},{1,0},{2,3},{3,2},{4,5},{5,4},{6,7},{7,6},{8,9},{9,8},{10,11... | collective-permute-start | bytes 1544 | tf_op jit(solution)/shard_map/ppermute | solution.py:341
  73.9 76.0 %collective-permute-start.10 = (bf16[8,256,128]{2,1,0:T(8,128)(2,1)}, bf16[8,256,128]{2,1,0:T(8,128)(2,1)S(1)}, u32[]{:S(2)}, u32[]{:S(2)}) collective-permute-start(bf16[8,256,128]{2,1,0:T(8,128)(2,1)} %get-tuple-element.66), channel_id=1, source_target_pairs={{0,6},{1,7},{2,0},{3,1},{4,2},{5,3},{6,4},{7,5},{8,14},{9,15},{10,... | collective-permute-start | bytes 1572872 | tf_op jit(solution)/shard_map/ppermute | solution.py:313
  73.9 76.0 %collective-permute-start.11 = (bf16[8,256,128]{2,1,0:T(8,128)(2,1)}, bf16[8,256,128]{2,1,0:T(8,128)(2,1)S(1)}, u32[]{:S(2)}, u32[]{:S(2)}) collective-permute-start(bf16[8,256,128]{2,1,0:T(8,128)(2,1)} %get-tuple-element.66), channel_id=1, source_target_pairs={{0,2},{1,3},{2,4},{3,5},{4,6},{5,7},{6,0},{7,1},{8,10},{9,11},{10,... | collective-permute-start | bytes 1572872 | tf_op jit(solution)/shard_map/ppermute | solution.py:313
  76.6 73.3 %collective-permute-start.9 = (bf16[8,256,128]{2,1,0:T(8,128)(2,1)}, bf16[8,256,128]{2,1,0:T(8,128)(2,1)S(1)}, u32[]{:S(2)}, u32[]{:S(2)}) collective-permute-start(bf16[8,256,128]{2,1,0:T(8,128)(2,1)} %copy-done.10), channel_id=1, source_target_pairs={{0,2},{1,3},{2,4},{3,5},{4,6},{5,7},{6,0},{7,1},{8,10},{9,11},{10,... | collective-permute-start | bytes 1572872 | tf_op jit(solution)/shard_map/ppermute | solution.py:369
  76.9 73.0 %collective-permute-start.12 = (bf16[8,128,128]{2,1,0:T(8,128)(2,1)}, bf16[8,128,128]{2,1,0:T(8,128)(2,1)S(1)}, u32[]{:S(2)}, u32[]{:S(2)}) collective-permute-start(bf16[8,128,128]{2,1,0:T(8,128)(2,1)} %get-tuple-element.67), channel_id=1, source_target_pairs={{0,1},{1,0},{2,3},{3,2},{4,5},{5,4},{6,7},{7,6},{8,9},{9,8},{10,11... | collective-permute-start | bytes 786440 | tf_op jit(solution)/shard_map/ppermute | solution.py:372
  79.4 1.6 copy-start.2
  81.0 0.9 copy-start.4
  82.0 68.0 %copy-start.7 = (bf16[8,256,128]{2,1,0:T(8,128)(2,1)S(1)}, bf16[8,256,128]{2,1,0:T(8,128)(2,1)}, u32[]{:S(2)}) copy-start(bf16[8,256,128]{2,1,0:T(8,128)(2,1)} %copy-done.6) | copy-start | bytes 1572868
  82.0 68.0 %copy-start.9 = (bf16[8,256,128]{2,1,0:T(8,128)(2,1)S(1)}, bf16[8,256,128]{2,1,0:T(8,128)(2,1)}, u32[]{:S(2)}) copy-start(bf16[8,256,128]{2,1,0:T(8,128)(2,1)} %copy-done.8) | copy-start | bytes 1572868
  82.0 68.0 %copy-start.11 = (bf16[8,256,128]{2,1,0:T(8,128)(2,1)S(1)}, bf16[8,256,128]{2,1,0:T(8,128)(2,1)}, u32[]{:S(2)}) copy-start(bf16[8,256,128]{2,1,0:T(8,128)(2,1)} %copy-done.10) | copy-start | bytes 1572868
  150.0 1.0 copy-start.5
  150.3 1.0 copy-start.12
  150.3 4.2 %collective-permute-start.13 = (bf16[4,8,256,128]{3,2,1,0:T(8,128)(2,1)S(1)}, bf16[4,8,256,128]{3,2,1,0:T(8,128)(2,1)S(1)}, u32[]{:S(2)}, u32[]{:S(2)}) collective-permute-start(bf16[4,8,256,128]{3,2,1,0:T(8,128)(2,1)S(1)} %pad_maximum_fusion.1.refs_0_), channel_id=1, source_target_pairs={{0,8},{8,0},{16,24},{24,16},{32,40},{40,32},{48,56},{56,48},{64,72... | collective-permute-start | bytes 6291464 | tf_op jit(solution)/shard_map/ppermute | solution.py:310
  151.2 75.6 %collective-permute-start.17 = (bf16[3,8,256,128]{3,2,1,0:T(8,128)(2,1)S(1)}, bf16[3,8,256,128]{3,2,1,0:T(8,128)(2,1)S(1)}, u32[]{:S(2)}, u32[]{:S(2)}) collective-permute-start(bf16[3,8,256,128]{3,2,1,0:T(8,128)(2,1)S(1)} %pad_maximum_fusion.2.refs_0_), channel_id=1, source_target_pairs={{0,8},{8,0},{16,24},{24,16},{32,40},{40,32},{48,56},{56,48},{64,72... | collective-permute-start | bytes 4718600 | tf_op jit(solution)/shard_map/ppermute | solution.py:310
  151.3 72.3 %collective-permute-start.16 = (bf16[8,128,128]{2,1,0:T(8,128)(2,1)S(1)}, bf16[8,128,128]{2,1,0:T(8,128)(2,1)S(1)}, u32[]{:S(2)}, u32[]{:S(2)}) collective-permute-start(bf16[8,128,128]{2,1,0:T(8,128)(2,1)S(1)} %copy-done.12), channel_id=1, source_target_pairs={{0,1},{1,0},{2,3},{3,2},{4,5},{5,4},{6,7},{7,6},{8,9},{9,8},{10,11... | collective-permute-start | bytes 786440 | tf_op jit(solution)/shard_map/ppermute | solution.py:380
  151.4 72.3 %collective-permute-start.15 = (bf16[8,256,128]{2,1,0:T(8,128)(2,1)S(1)}, bf16[8,256,128]{2,1,0:T(8,128)(2,1)S(1)}, u32[]{:S(2)}, u32[]{:S(2)}) collective-permute-start(bf16[8,256,128]{2,1,0:T(8,128)(2,1)S(1)} %collective-permute-done.10), channel_id=1, source_target_pairs={{0,6},{1,7},{2,0},{3,1},{4,2},{5,3},{6,4},{7,5},{8,14},{9,15},{10,... | collective-permute-start | bytes 1572872 | tf_op jit(solution)/shard_map/ppermute | solution.py:378
  223.7 72.2 %copy-start.14 = (s32[24]{0:T(128)S(1)}, s32[24]{0:T(128)}, u32[]{:S(2)}) copy-start(s32[24]{0:T(128)} %param.10) | copy-start | bytes 292
  223.7 3.1 collective-permute-start.18
  223.8 72.1 %collective-permute-start.8 = (bf16[8,144,128]{2,1,0:T(8,128)(2,1)S(1)}, bf16[8,144,128]{2,1,0:T(8,128)(2,1)S(1)}, u32[]{:S(2)}, u32[]{:S(2)}) collective-permute-start(bf16[8,144,128]{2,1,0:T(8,128)(2,1)S(1)} %get-tuple-element.63), channel_id=1, source_target_pairs={{0,1},{1,0},{2,3},{3,2},{4,5},{5,4},{6,7},{7,6},{8,9},{9,8},{10,11... | collective-permute-start | bytes 884744 | tf_op jit(solution)/shard_map/ppermute | solution.py:365
  223.9 72.0 %collective-permute-start.14 = (bf16[8,144,128]{2,1,0:T(8,128)(2,1)S(1)}, bf16[8,144,128]{2,1,0:T(8,128)(2,1)S(1)}, u32[]{:S(2)}, u32[]{:S(2)}) collective-permute-start(bf16[8,144,128]{2,1,0:T(8,128)(2,1)S(1)} %get-tuple-element.74), channel_id=1, source_target_pairs={{0,1},{1,0},{2,3},{3,2},{4,5},{5,4},{6,7},{7,6},{8,9},{9,8},{10,11... | collective-permute-start | bytes 884744 | tf_op jit(solution)/shard_map/ppermute | solution.py:365
  295.8 7.2 %collective-permute-start.19 = (bf16[8,144,128]{2,1,0:T(8,128)(2,1)S(1)}, bf16[8,144,128]{2,1,0:T(8,128)(2,1)S(1)}, u32[]{:S(2)}, u32[]{:S(2)}) collective-permute-start(bf16[8,144,128]{2,1,0:T(8,128)(2,1)S(1)} %get-tuple-element.84), channel_id=1, source_target_pairs={{0,1},{1,0},{2,3},{3,2},{4,5},{5,4},{6,7},{7,6},{8,9},{9,8},{10,11... | collective-permute-start | bytes 884744 | tf_op jit(solution)/shard_map/ppermute | solution.py:365
  304.2 4.8 %copy-start.13 = (s32[128]{0:T(128)S(1)}, s32[128]{0:T(128)}, u32[]{:S(2)}) copy-start(s32[128]{0:T(128)} %param.9) | copy-start | bytes 1540
  304.2 14.8 %all-to-all-start.2 = ((bf16[8,384,128]{2,1,0:T(8,128)(2,1)}), bf16[8,384,128]{2,1,0:T(8,128)(2,1)}, u32[]{:S(2)}, u32[]{:S(2)}) async-start(bf16[8,384,128]{2,1,0:T(8,128)(2,1)} %shard_map.68), calls=%async_computation.2 | async-start | bytes 1572864 | tf_op jit(solution)/shard_map/all_to_all | solution.py:302

commit v11 on v10

--- a/solution.py
+++ b/solution.py
@@ -320,7 +320,9 @@
     rest, first = after(rest, first)
     rest = exchange(rest)
     above, below = sides(first)
-    near = jnp.stack([first, above, below, lax.ppermute(above, "head", down)])
+    half = ZONES // 2
+    opposite = [lax.ppermute(below[:half], "head", up), lax.ppermute(above[half:], "head", down)]
+    near = jnp.stack([first, above, below, jnp.concatenate(opposite)])
 
     def combined(notes):
         is_count = jnp.arange(HEAD_DIM) < K_NORM

time: 322 us -> 318 us (0.988)
  waiting for transfers between devices: 47.1 us -> 39.6 us
    ppermute x1 -> x2, waiting for transfers between devices: 9.72 us -> 3.49 us  [the longest x1 3.18 us: per_device(): lax.ppermute(above[half:], 'head', down)]
  transfers between devices with their start and end apart: 22 -> 23, of which waited for: 9 -> 10; matrix products, arithmetic and copies ran while one was open for 2% -> 3% of each run, Pallas kernels for 64% -> 65%
where the time goes in v11:
time: 318 us; the launch traced here: 317 us
  Pallas kernels  212 us (67%)
  waiting for transfers between devices  39.6 us (12%)
  starting transfers between devices  33.7 us (11%)
  blocking collectives  15.4 us (5%)
  local copies, waits for them, and re-layouts  9.79 us (3%)
  other arithmetic  4.88 us (2%)
    pallas_call x3, Pallas kernels, attend(): pl.pallas_call(functools.partial(attend_kernel, head), grid_spec=pltpu.Pr...  205 us
    all_to_all x1, blocking collectives, exchange(): lax.all_to_all(parts, BOTH, split_axis=0, concat_axis=0, axis_index_group...  15.4 us
    all_to_all x2, waiting for transfers between devices, exchange(): lax.all_to_all(parts, BOTH, split_axis=0, concat_axis=0, axis_index_group...  10.5 us
    ppermute x6, waiting for transfers between devices, sides(): return (lax.ppermute(block, 'head', down), lax.ppermute(block, 'head', up))  9.69 us
    ppermute x6, starting transfers between devices, sides(): return (lax.ppermute(block, 'head', down), lax.ppermute(block, 'head', up))  8.03 us
    all_to_all x2, starting transfers between devices, exchange(): lax.all_to_all(parts, BOTH, split_axis=0, concat_axis=0, axis_index_group...  7.95 us
    ppermute x3, waiting for transfers between devices, attended(): parts[2 * head + 1] = lax.ppermute(theirs, 'head', partner)  7.01 us
  transfers between devices with their start and end apart: 23, of which 10 were waited for; matrix products, arithmetic and copies ran while one was open for 3% of the time, Pallas kernels for 65%

profile of v11, /device:TPU:25, one launch (start us, length us, event | category | flops | bytes accessed | tf_op | source)
XLA Modules:
  0.0 317.2 jit_solution(5021823609066379265)
XLA Ops:
  0.0 4.0 %shard_map.64 = (bf16[8,272,128]{2,1,0:T(8,128)(2,1)}, bf16[8,896,128]{2,1,0:T(8,128)(2,1)}) custom-call(bf16[128,3072]{1,0:T(8,128)(2,1)} %queries_ref.1, bf16[128,3072]{1,0:T(8,128)(2,1)} %keys_ref.1, bf16[128,3072]{1,0:T(8,128)(2,1)} %values_ref.1, s32[1,128]{1,0:T(1,128)} %bitcast.55), custom_call_target="tpu_custom_call" | custom-call | tf_op jit(solution)/shard_map/pallas_call | solution.py:316
  4.0 15.4 %all_to_all.15 = bf16[8,272,128]{2,1,0:T(8,128)(2,1)} all-to-all(bf16[8,272,128]{2,1,0:T(8,128)(2,1)} %get-tuple-element.46), channel_id=1, replica_groups={{0,16,32,48,64,80,96,112},{1,17,33,49,65,81,97,113},{2,18,34,50,66,82,9..., dimensions={0} | all-to-all | bytes 1114112 | tf_op jit(solution)/shard_map/all_to_all | solution.py:302
  19.4 0.5 collective-permute-start
  19.8 2.2 collective-permute-start.1
  22.0 3.6 %all-to-all-start.1 = ((bf16[8,896,128]{2,1,0:T(8,128)(2,1)}), bf16[8,896,128]{2,1,0:T(8,128)(2,1)S(1)}, u32[]{:S(2)}, u32[]{:S(2)}) async-start(bf16[8,896,128]{2,1,0:T(8,128)(2,1)} %get-tuple-element.47), calls=%async_computation.1 | async-start | bytes 3670016 | tf_op jit(solution)/shard_map/all_to_all | solution.py:302
  25.6 7.1 %collective-permute-done = bf16[8,272,128]{2,1,0:T(8,128)(2,1)} collective-permute-done((bf16[8,272,128]{2,1,0:T(8,128)(2,1)}, bf16[8,272,128]{2,1,0:T(8,128)(2,1)}, u32[]{:S(2)}, u32[]{:S(2)}) %collective-permute-start) | collective-permute-done | bytes 557088 | tf_op jit(solution)/shard_map/ppermute | solution.py:313
  32.8 1.0 slice.49
  33.7 0.1 collective-permute-start.3
  33.8 1.0 slice.48
  34.8 2.7 collective-permute-start.2
  37.5 3.2 %collective-permute-done.3 = bf16[4,272,128]{2,1,0:T(8,128)(2,1)S(1)} collective-permute-done((bf16[4,272,128]{2,1,0:T(8,128)(2,1)S(1)}, bf16[4,272,128]{2,1,0:T(8,128)(2,1)S(1)}, u32[]{:S(2)}, u32[]{:S(2)}) %collective-permute-start.3) | collective-permute-done | bytes 278560 | tf_op jit(solution)/shard_map/ppermute | solution.py:324
  40.7 0.3 collective-permute-done.2
  41.1 1.7 pad_maximum_fusion.refs_0_
  42.8 0.1 slice_reduce_fusion.1
  42.9 1.3 copy-done.1
  44.2 2.8 all-to-all-done.1.own_q
  46.9 3.7 %collective-permute-start.4 = (bf16[4,8,272,128]{3,2,1,0:T(8,128)(2,1)}, bf16[4,8,272,128]{3,2,1,0:T(8,128)(2,1)}, u32[]{:S(2)}, u32[]{:S(2)}) collective-permute-start(bf16[4,8,272,128]{3,2,1,0:T(8,128)(2,1)} %copy-done.1), channel_id=1, source_target_pairs={{0,8},{8,0},{16,24},{24,16},{32,40},{40,32},{48,56},{56,48},{64,72... | collective-permute-start | bytes 6684680 | tf_op jit(solution)/shard_map/ppermute | solution.py:310
  50.7 0.1 add_multiply_fusion
  50.7 0.1 broadcast_add_fusion
  50.8 0.9 fusion.19
  51.7 0.9 fusion.18
  52.6 2.7 collective-permute-start.6
  55.2 2.5 collective-permute-start.7
  57.7 0.9 convert_reduce_fusion
  58.6 0.9 slice_reduce_fusion
  59.5 4.6 %collective-permute-done.7.their_q = bf16[8,128,128]{2,1,0:T(8,128)(2,1)S(1)} collective-permute-done((bf16[8,128,128]{2,1,0:T(8,128)(2,1)S(1)}, bf16[8,128,128]{2,1,0:T(8,128)(2,1)S(1)}, u32[]{:S(2)}, u32[]{:S(2)}) %collective-permute-start.7) | collective-permute-done | bytes 262176 | tf_op jit(solution)/shard_map/ppermute | solution.py:339
  64.1 0.7 copy-done.3
  64.8 2.6 collective-permute-done.5
  67.3 0.8 copy-done.8
  68.1 2.5 collective-permute-start.8
  70.6 0.1 fusion.12
  70.7 1.4 collective-permute-done.8
  72.0 0.1 compare_convert_fusion
  72.1 0.1 select_reduce_fusion
  72.2 0.1 fusion.15
  72.4 0.1 pad_add_fusion.info_ref
  72.5 2.7 collective-permute-start.12
  75.2 0.3 collective-permute-start.10
  75.5 2.5 collective-permute-start.13
  78.0 1.6 copy-done.2
  79.6 0.9 copy-done.4
  80.6 67.5 %shard_map.65 = (bf16[8,144,128]{2,1,0:T(8,128)(2,1)S(1)}, bf16[8,144,128]{2,1,0:T(8,128)(2,1)S(1)}) custom-call(s32[13]{0:T(128)S(1)} %pad_add_fusion.info_ref, bf16[8,896,128]{2,1,0:T(8,128)(2,1)S(1)} %all-to-all-done.1.own_q, bf16[8,128,128]{2,1,0:T(8,128)(2,1)S(1)} %copy-done.4, s32[8,1,256]{2,1,0:T(1,128)S(1)} %fusion.13.end_ref, ...), custom_call_target="tpu_custom_call" | custom-call | flops 8589934592 | bytes 5242880 | tf_op jit(solution)/shard_map/pallas_call | solution.py:177
  148.2 0.3 pad_maximum_fusion.1.refs_0_
  148.4 0.1 collective-permute-start.14
  148.5 0.7 copy-done.5
  149.2 0.2 pad_maximum_fusion.2.refs_0_
  149.4 0.1 collective-permute-start.18
  149.5 0.1 collective-permute-start.17
  149.6 0.1 collective-permute-start.16
  149.7 3.0 collective-permute-done.14.refs_1_
  152.7 68.7 %shard_map.66 = (bf16[8,144,128]{2,1,0:T(8,128)(2,1)S(1)}, bf16[8,144,128]{2,1,0:T(8,128)(2,1)S(1)}) custom-call(s32[13]{0:T(128)S(1)} %pad_add_fusion.info_ref, bf16[8,896,128]{2,1,0:T(8,128)(2,1)S(1)} %all-to-all-done.1.own_q, bf16[8,128,128]{2,1,0:T(8,128)(2,1)S(1)} %collective-permute-done.13.their_q, s32[8,1,256]{2,1,0:T(1,128)S(1)} %fusion.13.end_ref, ...), custom_call_target="tpu_custom_call" | custom-call | flops 8589934592 | bytes 5242880 | tf_op jit(solution)/shard_map/pallas_call | solution.py:177
  221.4 0.1 collective-permute-start.19
  221.5 0.1 collective-permute-start.9
  221.6 3.0 collective-permute-start.15
  224.6 68.5 %shard_map.67 = (bf16[8,144,128]{2,1,0:T(8,128)(2,1)S(1)}, bf16[8,144,128]{2,1,0:T(8,128)(2,1)S(1)}) custom-call(s32[13]{0:T(128)S(1)} %pad_add_fusion.info_ref, bf16[8,896,128]{2,1,0:T(8,128)(2,1)S(1)} %all-to-all-done.1.own_q, bf16[8,128,128]{2,1,0:T(8,128)(2,1)S(1)} %collective-permute-done.17.their_q, s32[8,1,256]{2,1,0:T(1,128)S(1)} %fusion.13.end_ref, ...), custom_call_target="tpu_custom_call" | custom-call | flops 8589934592 | bytes 5242880 | tf_op jit(solution)/shard_map/pallas_call | solution.py:177
  293.1 0.1 collective-permute-start.20
  293.3 7.0 %collective-permute-done.20.refs_5_ = bf16[8,144,128]{2,1,0:T(8,128)(2,1)S(1)} collective-permute-done((bf16[8,144,128]{2,1,0:T(8,128)(2,1)S(1)}, bf16[8,144,128]{2,1,0:T(8,128)(2,1)S(1)}, u32[]{:S(2)}, u32[]{:S(2)}) %collective-permute-start.20) | collective-permute-done | bytes 294944 | tf_op jit(solution)/shard_map/ppermute | solution.py:367
  300.3 1.3 shard_map.68
  301.5 4.4 %all-to-all-start.2 = ((bf16[8,384,128]{2,1,0:T(8,128)(2,1)}), bf16[8,384,128]{2,1,0:T(8,128)(2,1)}, u32[]{:S(2)}, u32[]{:S(2)}) async-start(bf16[8,384,128]{2,1,0:T(8,128)(2,1)} %shard_map.68), calls=%async_computation.2 | async-start | bytes 1572864 | tf_op jit(solution)/shard_map/all_to_all | solution.py:302
  305.9 0.1 fusion.2
  306.0 0.3 fusion.4
  306.3 0.8 fusion.gate_ref
  307.2 7.7 %all-to-all-done.2.mixed_ref = bf16[8,384,128]{2,1,0:T(8,128)(2,1)} async-done(((bf16[8,384,128]{2,1,0:T(8,128)(2,1)}), bf16[8,384,128]{2,1,0:T(8,128)(2,1)}, u32[]{:S(2)}, u32[]{:S(2)}) %all-to-all-start.2) | async-done | bytes 786464 | tf_op jit(solution)/shard_map/all_to_all | solution.py:302
  314.9 2.3 shard_map.69
  (53 shorter events, 0.3 us)
Async XLA Ops:
  0.0 306.0 %copy-start = (bf16[256,3072]{1,0:T(8,128)(2,1)S(1)}, bf16[256,3072]{1,0:T(8,128)(2,1)}, u32[]{:S(2)}) copy-start(bf16[256,3072]{1,0:T(8,128)(2,1)} %param.11) | copy-start | bytes 4718596
  19.4 13.4 %collective-permute-start = (bf16[8,272,128]{2,1,0:T(8,128)(2,1)}, bf16[8,272,128]{2,1,0:T(8,128)(2,1)}, u32[]{:S(2)}, u32[]{:S(2)}) collective-permute-start(bf16[8,272,128]{2,1,0:T(8,128)(2,1)} %all_to_all.15), channel_id=1, source_target_pairs={{0,6},{1,7},{2,0},{3,1},{4,2},{5,3},{6,4},{7,5},{8,14},{9,15},{10,... | collective-permute-start | bytes 1671176 | tf_op jit(solution)/shard_map/ppermute | solution.py:313
  19.8 14.0 %collective-permute-start.1 = (bf16[8,272,128]{2,1,0:T(8,128)(2,1)}, bf16[8,272,128]{2,1,0:T(8,128)(2,1)}, u32[]{:S(2)}, u32[]{:S(2)}) collective-permute-start(bf16[8,272,128]{2,1,0:T(8,128)(2,1)} %all_to_all.15), channel_id=1, source_target_pairs={{0,2},{1,3},{2,4},{3,5},{4,6},{5,7},{6,0},{7,1},{8,10},{9,11},{10,... | collective-permute-start | bytes 1671176 | tf_op jit(solution)/shard_map/ppermute | solution.py:313
  22.0 24.9 %all-to-all-start.1 = ((bf16[8,896,128]{2,1,0:T(8,128)(2,1)}), bf16[8,896,128]{2,1,0:T(8,128)(2,1)S(1)}, u32[]{:S(2)}, u32[]{:S(2)}) async-start(bf16[8,896,128]{2,1,0:T(8,128)(2,1)} %get-tuple-element.47), calls=%async_computation.1 | async-start | bytes 3670016 | tf_op jit(solution)/shard_map/all_to_all | solution.py:302
  33.7 7.0 %collective-permute-start.3 = (bf16[4,272,128]{2,1,0:T(8,128)(2,1)S(1)}, bf16[4,272,128]{2,1,0:T(8,128)(2,1)S(1)}, u32[]{:S(2)}, u32[]{:S(2)}) collective-permute-start(bf16[4,272,128]{2,1,0:T(8,128)(2,1)S(1)} %slice.49), channel_id=1, source_target_pairs={{0,6},{1,7},{2,0},{3,1},{4,2},{5,3},{6,4},{7,5},{8,14},{9,15},{10,... | collective-permute-start | bytes 835592 | tf_op jit(solution)/shard_map/ppermute | solution.py:324
  34.8 6.2 %collective-permute-start.2 = (bf16[4,272,128]{2,1,0:T(8,128)(2,1)S(1)}, bf16[4,272,128]{2,1,0:T(8,128)(2,1)S(1)}, u32[]{:S(2)}, u32[]{:S(2)}) collective-permute-start(bf16[4,272,128]{2,1,0:T(8,128)(2,1)S(1)} %slice.48), channel_id=1, source_target_pairs={{0,2},{1,3},{2,4},{3,5},{4,6},{5,7},{6,0},{7,1},{8,10},{9,11},{10,... | collective-permute-start | bytes 835592 | tf_op jit(solution)/shard_map/ppermute | solution.py:324
  42.8 1.4 copy-start.1
  46.9 10.8 %collective-permute-start.4 = (bf16[4,8,272,128]{3,2,1,0:T(8,128)(2,1)}, bf16[4,8,272,128]{3,2,1,0:T(8,128)(2,1)}, u32[]{:S(2)}, u32[]{:S(2)}) collective-permute-start(bf16[4,8,272,128]{3,2,1,0:T(8,128)(2,1)} %copy-done.1), channel_id=1, source_target_pairs={{0,8},{8,0},{16,24},{24,16},{32,40},{40,32},{48,56},{56,48},{64,72... | collective-permute-start | bytes 6684680 | tf_op jit(solution)/shard_map/ppermute | solution.py:310
  52.6 11.5 %copy-start.6 = (bf16[8,256,128]{2,1,0:T(8,128)(2,1)}, bf16[8,256,128]{2,1,0:T(8,128)(2,1)S(1)}, u32[]{:S(2)}) copy-start(bf16[8,256,128]{2,1,0:T(8,128)(2,1)S(1)} %get-tuple-element.52) | copy-start | bytes 1572868
  52.6 14.8 %collective-permute-start.5 = (bf16[8,256,128]{2,1,0:T(8,128)(2,1)S(1)}, bf16[8,256,128]{2,1,0:T(8,128)(2,1)S(1)}, u32[]{:S(2)}, u32[]{:S(2)}) collective-permute-start(bf16[8,256,128]{2,1,0:T(8,128)(2,1)S(1)} %get-tuple-element.52), channel_id=1, source_target_pairs={{0,6},{1,7},{2,0},{3,1},{4,2},{5,3},{6,4},{7,5},{8,14},{9,15},{10,... | collective-permute-start | bytes 1572872 | tf_op jit(solution)/shard_map/ppermute | solution.py:313
  52.6 14.8 %collective-permute-start.6 = (bf16[8,256,128]{2,1,0:T(8,128)(2,1)S(1)}, bf16[8,256,128]{2,1,0:T(8,128)(2,1)S(1)}, u32[]{:S(2)}, u32[]{:S(2)}) collective-permute-start(bf16[8,256,128]{2,1,0:T(8,128)(2,1)S(1)} %get-tuple-element.52), channel_id=1, source_target_pairs={{0,2},{1,3},{2,4},{3,5},{4,6},{5,7},{6,0},{7,1},{8,10},{9,11},{10,... | collective-permute-start | bytes 1572872 | tf_op jit(solution)/shard_map/ppermute | solution.py:313
  55.2 8.8 %collective-permute-start.7 = (bf16[8,128,128]{2,1,0:T(8,128)(2,1)S(1)}, bf16[8,128,128]{2,1,0:T(8,128)(2,1)S(1)}, u32[]{:S(2)}, u32[]{:S(2)}) collective-permute-start(bf16[8,128,128]{2,1,0:T(8,128)(2,1)S(1)} %get-tuple-element.53), channel_id=1, source_target_pairs={{0,1},{1,0},{2,3},{3,2},{4,5},{5,4},{6,7},{7,6},{8,9},{9,8},{10,11... | collective-permute-start | bytes 786440 | tf_op jit(solution)/shard_map/ppermute | solution.py:339
  64.0 0.7 copy-start.3
  67.3 0.8 copy-start.8
  68.1 2.5 copy-start.10
  68.1 3.9 %collective-permute-start.8 = (f32[1,128]{1,0:T(1,128)S(1)}, f32[1,128]{1,0:T(1,128)S(1)}, u32[]{:S(2)}, u32[]{:S(2)}) collective-permute-start(f32[1,128]{1,0:T(1,128)S(1)} %select_bitcast_fusion), channel_id=1, source_target_pairs={{0,1},{1,0},{2,3},{3,2},{4,5},{5,4},{6,7},{7,6},{8,9},{9,8},{10,11... | collective-permute-start | bytes 1544 | tf_op jit(solution)/shard_map/ppermute | solution.py:343
  72.5 75.6 %collective-permute-start.11 = (bf16[8,256,128]{2,1,0:T(8,128)(2,1)}, bf16[8,256,128]{2,1,0:T(8,128)(2,1)S(1)}, u32[]{:S(2)}, u32[]{:S(2)}) collective-permute-start(bf16[8,256,128]{2,1,0:T(8,128)(2,1)} %get-tuple-element.66), channel_id=1, source_target_pairs={{0,6},{1,7},{2,0},{3,1},{4,2},{5,3},{6,4},{7,5},{8,14},{9,15},{10,... | collective-permute-start | bytes 1572872 | tf_op jit(solution)/shard_map/ppermute | solution.py:313
  72.5 75.6 %collective-permute-start.12 = (bf16[8,256,128]{2,1,0:T(8,128)(2,1)}, bf16[8,256,128]{2,1,0:T(8,128)(2,1)S(1)}, u32[]{:S(2)}, u32[]{:S(2)}) collective-permute-start(bf16[8,256,128]{2,1,0:T(8,128)(2,1)} %get-tuple-element.66), channel_id=1, source_target_pairs={{0,2},{1,3},{2,4},{3,5},{4,6},{5,7},{6,0},{7,1},{8,10},{9,11},{10,... | collective-permute-start | bytes 1572872 | tf_op jit(solution)/shard_map/ppermute | solution.py:313
  75.2 72.9 %collective-permute-start.10 = (bf16[8,256,128]{2,1,0:T(8,128)(2,1)}, bf16[8,256,128]{2,1,0:T(8,128)(2,1)S(1)}, u32[]{:S(2)}, u32[]{:S(2)}) collective-permute-start(bf16[8,256,128]{2,1,0:T(8,128)(2,1)} %copy-done.10), channel_id=1, source_target_pairs={{0,2},{1,3},{2,4},{3,5},{4,6},{5,7},{6,0},{7,1},{8,10},{9,11},{10,... | collective-permute-start | bytes 1572872 | tf_op jit(solution)/shard_map/ppermute | solution.py:371
  75.5 72.6 %collective-permute-start.13 = (bf16[8,128,128]{2,1,0:T(8,128)(2,1)}, bf16[8,128,128]{2,1,0:T(8,128)(2,1)S(1)}, u32[]{:S(2)}, u32[]{:S(2)}) collective-permute-start(bf16[8,128,128]{2,1,0:T(8,128)(2,1)} %get-tuple-element.67), channel_id=1, source_target_pairs={{0,1},{1,0},{2,3},{3,2},{4,5},{5,4},{6,7},{7,6},{8,9},{9,8},{10,11... | collective-permute-start | bytes 786440 | tf_op jit(solution)/shard_map/ppermute | solution.py:374
  78.0 1.6 copy-start.2
  79.6 0.9 copy-start.4
  80.6 67.5 %copy-start.7 = (bf16[8,256,128]{2,1,0:T(8,128)(2,1)S(1)}, bf16[8,256,128]{2,1,0:T(8,128)(2,1)}, u32[]{:S(2)}) copy-start(bf16[8,256,128]{2,1,0:T(8,128)(2,1)} %copy-done.6) | copy-start | bytes 1572868
  80.6 67.5 %copy-start.9 = (bf16[8,256,128]{2,1,0:T(8,128)(2,1)S(1)}, bf16[8,256,128]{2,1,0:T(8,128)(2,1)}, u32[]{:S(2)}) copy-start(bf16[8,256,128]{2,1,0:T(8,128)(2,1)} %copy-done.8) | copy-start | bytes 1572868
  80.6 67.6 %copy-start.11 = (bf16[8,256,128]{2,1,0:T(8,128)(2,1)S(1)}, bf16[8,256,128]{2,1,0:T(8,128)(2,1)}, u32[]{:S(2)}) copy-start(bf16[8,256,128]{2,1,0:T(8,128)(2,1)} %copy-done.10) | copy-start | bytes 1572868
  148.2 1.0 copy-start.5
  148.4 1.0 copy-start.12
  148.4 4.2 %collective-permute-start.14 = (bf16[4,8,256,128]{3,2,1,0:T(8,128)(2,1)S(1)}, bf16[4,8,256,128]{3,2,1,0:T(8,128)(2,1)S(1)}, u32[]{:S(2)}, u32[]{:S(2)}) collective-permute-start(bf16[4,8,256,128]{3,2,1,0:T(8,128)(2,1)S(1)} %pad_maximum_fusion.1.refs_0_), channel_id=1, source_target_pairs={{0,8},{8,0},{16,24},{24,16},{32,40},{40,32},{48,56},{56,48},{64,72... | collective-permute-start | bytes 6291464 | tf_op jit(solution)/shard_map/ppermute | solution.py:310
  149.4 75.2 %collective-permute-start.18 = (bf16[3,8,256,128]{3,2,1,0:T(8,128)(2,1)S(1)}, bf16[3,8,256,128]{3,2,1,0:T(8,128)(2,1)S(1)}, u32[]{:S(2)}, u32[]{:S(2)}) collective-permute-start(bf16[3,8,256,128]{3,2,1,0:T(8,128)(2,1)S(1)} %pad_maximum_fusion.2.refs_0_), channel_id=1, source_target_pairs={{0,8},{8,0},{16,24},{24,16},{32,40},{40,32},{48,56},{56,48},{64,72... | collective-permute-start | bytes 4718600 | tf_op jit(solution)/shard_map/ppermute | solution.py:310
  149.5 71.9 %collective-permute-start.17 = (bf16[8,128,128]{2,1,0:T(8,128)(2,1)S(1)}, bf16[8,128,128]{2,1,0:T(8,128)(2,1)S(1)}, u32[]{:S(2)}, u32[]{:S(2)}) collective-permute-start(bf16[8,128,128]{2,1,0:T(8,128)(2,1)S(1)} %copy-done.12), channel_id=1, source_target_pairs={{0,1},{1,0},{2,3},{3,2},{4,5},{5,4},{6,7},{7,6},{8,9},{9,8},{10,11... | collective-permute-start | bytes 786440 | tf_op jit(solution)/shard_map/ppermute | solution.py:382
  149.6 71.8 %collective-permute-start.16 = (bf16[8,256,128]{2,1,0:T(8,128)(2,1)S(1)}, bf16[8,256,128]{2,1,0:T(8,128)(2,1)S(1)}, u32[]{:S(2)}, u32[]{:S(2)}) collective-permute-start(bf16[8,256,128]{2,1,0:T(8,128)(2,1)S(1)} %collective-permute-done.11), channel_id=1, source_target_pairs={{0,6},{1,7},{2,0},{3,1},{4,2},{5,3},{6,4},{7,5},{8,14},{9,15},{10,... | collective-permute-start | bytes 1572872 | tf_op jit(solution)/shard_map/ppermute | solution.py:380
  221.4 71.8 %copy-start.14 = (s32[24]{0:T(128)S(1)}, s32[24]{0:T(128)}, u32[]{:S(2)}) copy-start(s32[24]{0:T(128)} %param.10) | copy-start | bytes 292
  221.4 3.1 collective-permute-start.19
  221.5 71.7 %collective-permute-start.9 = (bf16[8,144,128]{2,1,0:T(8,128)(2,1)S(1)}, bf16[8,144,128]{2,1,0:T(8,128)(2,1)S(1)}, u32[]{:S(2)}, u32[]{:S(2)}) collective-permute-start(bf16[8,144,128]{2,1,0:T(8,128)(2,1)S(1)} %get-tuple-element.63), channel_id=1, source_target_pairs={{0,1},{1,0},{2,3},{3,2},{4,5},{5,4},{6,7},{7,6},{8,9},{9,8},{10,11... | collective-permute-start | bytes 884744 | tf_op jit(solution)/shard_map/ppermute | solution.py:367
  221.6 71.6 %collective-permute-start.15 = (bf16[8,144,128]{2,1,0:T(8,128)(2,1)S(1)}, bf16[8,144,128]{2,1,0:T(8,128)(2,1)S(1)}, u32[]{:S(2)}, u32[]{:S(2)}) collective-permute-start(bf16[8,144,128]{2,1,0:T(8,128)(2,1)S(1)} %get-tuple-element.74), channel_id=1, source_target_pairs={{0,1},{1,0},{2,3},{3,2},{4,5},{5,4},{6,7},{7,6},{8,9},{9,8},{10,11... | collective-permute-start | bytes 884744 | tf_op jit(solution)/shard_map/ppermute | solution.py:367
  293.1 7.2 %collective-permute-start.20 = (bf16[8,144,128]{2,1,0:T(8,128)(2,1)S(1)}, bf16[8,144,128]{2,1,0:T(8,128)(2,1)S(1)}, u32[]{:S(2)}, u32[]{:S(2)}) collective-permute-start(bf16[8,144,128]{2,1,0:T(8,128)(2,1)S(1)} %get-tuple-element.84), channel_id=1, source_target_pairs={{0,1},{1,0},{2,3},{3,2},{4,5},{5,4},{6,7},{7,6},{8,9},{9,8},{10,11... | collective-permute-start | bytes 884744 | tf_op jit(solution)/shard_map/ppermute | solution.py:367
  301.5 4.8 %copy-start.13 = (s32[128]{0:T(128)S(1)}, s32[128]{0:T(128)}, u32[]{:S(2)}) copy-start(s32[128]{0:T(128)} %param.9) | copy-start | bytes 1540
  301.5 13.4 %all-to-all-start.2 = ((bf16[8,384,128]{2,1,0:T(8,128)(2,1)}), bf16[8,384,128]{2,1,0:T(8,128)(2,1)}, u32[]{:S(2)}, u32[]{:S(2)}) async-start(bf16[8,384,128]{2,1,0:T(8,128)(2,1)} %shard_map.68), calls=%async_computation.2 | async-start | bytes 1572864 | tf_op jit(solution)/shard_map/all_to_all | solution.py:302

commit v12 on v11

--- a/solution.py
+++ b/solution.py
@@ -306,6 +306,9 @@
     def after(*values):
         return lax.optimization_barrier(values)
 
+    def when(value, *ended):
+        return value + sum(x[0, 0, 0].astype(value.dtype) for x in ended) * 0.0
+
     def swapped(block):
         return block, lax.ppermute(block, "span", core_swap)
 
@@ -332,14 +335,14 @@
         return combined(blocks[:, :, pair].reshape(-1, HEAD_DIM).astype(jnp.float32))
 
     note = noted(near)
-    rest, near, note = after(rest, near, note)
+    rest, note = after(rest, note)
     own_q = [rest[:, start : start + HEAD_DIM] for start in range(2 * pair, rest.shape[1], HEAD_DIM)]
     own_q[0], block_one, block_two = after(own_q[0], rest[:, :pair], rest[:, pair : 2 * pair])
     above, below = sides(block_one)
     their_q = [lax.ppermute(own_q[0], "head", partner), None, None]
     near, far = swapped(near)
     note = combined(jnp.stack([note, noted(far)]))[None]
-    note, above, below, their_q[0] = after(note, above, below, their_q[0])
+    note = when(note, above, below, their_q[0])
     note = combined(jnp.concatenate([note, lax.ppermute(note, "head", partner)]))
     squares = note[K_NORM : K_NORM + heads] * note[Q_NORM : Q_NORM + heads]
     plain = (squares * (1.05 * SCALE**2) < PLAIN_LIMIT**2).astype(jnp.int32)

time: 318 us -> 331 us (1.041)
  other arithmetic: 4.88 us -> 10.4 us
  waiting for transfers between devices: 39.6 us -> 44.3 us
  starting transfers between devices: 33.7 us -> 37.3 us
    all_to_all x2, waiting for transfers between devices: 10.5 us -> 18.7 us  [exchange(): lax.all_to_all(parts, BOTH, split_axis=0, concat_axis=0, axis_index_group...]
    unnamed x30 -> x16, local copies, waits for them, and re-layouts: 6.09 us -> 0.04 us
    slice x0 -> x3, local copies, waits for them, and re-layouts: none -> 3.62 us  [when(): return value + sum((x[0, 0, 0].astype(value.dtype) for x in ended)) * 0.0]
  transfers between devices with their start and end apart: 23 -> 23, of which waited for: 10 -> 8; matrix products, arithmetic and copies ran while one was open for 3% -> 5% of each run, Pallas kernels for 65% -> 62%
where the time goes in v12:
time: 331 us; the launch traced here: 329 us
  Pallas kernels  211 us (64%)
  waiting for transfers between devices  44.3 us (13%)
  starting transfers between devices  37.3 us (11%)
  blocking collectives  15.3 us (5%)
  other arithmetic  10.4 us (3%)
  local copies, waits for them, and re-layouts  7.21 us (2%)
    pallas_call x3, Pallas kernels, attend(): pl.pallas_call(functools.partial(attend_kernel, head), grid_spec=pltpu.Pr...  203 us
    all_to_all x2, waiting for transfers between devices, exchange(): lax.all_to_all(parts, BOTH, split_axis=0, concat_axis=0, axis_index_group...  18.7 us
    all_to_all x1, blocking collectives, exchange(): lax.all_to_all(parts, BOTH, split_axis=0, concat_axis=0, axis_index_group...  15.3 us
    ppermute x6, waiting for transfers between devices, sides(): return (lax.ppermute(block, 'head', down), lax.ppermute(block, 'head', up))  10.4 us
    all_to_all x2, starting transfers between devices, exchange(): lax.all_to_all(parts, BOTH, split_axis=0, concat_axis=0, axis_index_group...  8.07 us
    ppermute x6, starting transfers between devices, sides(): return (lax.ppermute(block, 'head', down), lax.ppermute(block, 'head', up))  8.03 us
    ppermute x3, waiting for transfers between devices, attended(): parts[2 * head + 1] = lax.ppermute(theirs, 'head', partner)  7.01 us
  transfers between devices with their start and end apart: 23, of which 8 were waited for; matrix products, arithmetic and copies ran while one was open for 5% of the time, Pallas kernels for 62%

profile of v12, /device:TPU:25, one launch (start us, length us, event | category | flops | bytes accessed | tf_op | source)
XLA Modules:
  0.0 328.7 jit_solution(1683591129704821700)
XLA Ops:
  0.0 4.0 %shard_map.64 = (bf16[8,272,128]{2,1,0:T(8,128)(2,1)}, bf16[8,896,128]{2,1,0:T(8,128)(2,1)}) custom-call(bf16[128,3072]{1,0:T(8,128)(2,1)} %queries_ref.1, bf16[128,3072]{1,0:T(8,128)(2,1)} %keys_ref.1, bf16[128,3072]{1,0:T(8,128)(2,1)} %values_ref.1, s32[1,128]{1,0:T(1,128)} %bitcast.58), custom_call_target="tpu_custom_call" | custom-call | tf_op jit(solution)/shard_map/pallas_call | solution.py:319
  4.0 15.3 %all_to_all.15 = bf16[8,272,128]{2,1,0:T(8,128)(2,1)S(1)} all-to-all(bf16[8,272,128]{2,1,0:T(8,128)(2,1)} %get-tuple-element.41), channel_id=1, replica_groups={{0,16,32,48,64,80,96,112},{1,17,33,49,65,81,97,113},{2,18,34,50,66,82,9..., dimensions={0} | all-to-all | bytes 1114112 | tf_op jit(solution)/shard_map/all_to_all | solution.py:302
  19.3 0.5 collective-permute-start
  19.8 2.2 collective-permute-start.1
  22.0 10.4 %collective-permute-done = bf16[8,272,128]{2,1,0:T(8,128)(2,1)S(1)} collective-permute-done((bf16[8,272,128]{2,1,0:T(8,128)(2,1)S(1)}, bf16[8,272,128]{2,1,0:T(8,128)(2,1)S(1)}, u32[]{:S(2)}, u32[]{:S(2)}) %collective-permute-start) | collective-permute-done | bytes 557088 | tf_op jit(solution)/shard_map/ppermute | solution.py:316
  32.4 0.8 slice.61
  33.1 0.0 collective-permute-start.3
  33.2 0.8 slice.60
  33.9 2.7 collective-permute-start.2
  36.6 3.6 %all-to-all-start.1 = ((bf16[8,896,128]{2,1,0:T(8,128)(2,1)}), bf16[8,896,128]{2,1,0:T(8,128)(2,1)S(1)}, u32[]{:S(2)}, u32[]{:S(2)}) async-start(bf16[8,896,128]{2,1,0:T(8,128)(2,1)} %get-tuple-element.42), calls=%async_computation.1 | async-start | bytes 3670016 | tf_op jit(solution)/shard_map/all_to_all | solution.py:302
  40.2 0.2 collective-permute-done.2
  40.4 1.1 maximum_bitcast_fusion
  41.5 3.1 pad_maximum_fusion.refs_0_
  44.6 4.3 %collective-permute-start.4 = (bf16[4,8,272,128]{3,2,1,0:T(8,128)(2,1)}, bf16[4,8,272,128]{3,2,1,0:T(8,128)(2,1)}, u32[]{:S(2)}, u32[]{:S(2)}) collective-permute-start(bf16[4,8,272,128]{3,2,1,0:T(8,128)(2,1)} %pad_maximum_fusion.refs_0_), channel_id=1, source_target_pairs={{0,8},{8,0},{16,24},{24,16},{32,40},{40,32},{48,56},{56,48},{64,72... | collective-permute-start | bytes 6684680 | tf_op jit(solution)/shard_map/ppermute | solution.py:313
  48.9 0.9 convert_reduce_fusion.1
  49.8 0.9 slice_reduce_fusion.1
  50.7 10.0 %all-to-all-done.1.own_q = bf16[8,896,128]{2,1,0:T(8,128)(2,1)S(1)} async-done(((bf16[8,896,128]{2,1,0:T(8,128)(2,1)}), bf16[8,896,128]{2,1,0:T(8,128)(2,1)S(1)}, u32[]{:S(2)}, u32[]{:S(2)}) %all-to-all-start.1) | async-done | bytes 1835040 | tf_op jit(solution)/shard_map/all_to_all | solution.py:302
  60.7 0.9 fusion.20
  61.6 1.1 fusion.19
  62.7 2.7 collective-permute-start.6
  65.4 2.5 collective-permute-start.7
  67.8 0.1 add_multiply_fusion
  67.9 0.1 broadcast_add_fusion
  68.0 4.4 %collective-permute-done.7.their_q = bf16[8,128,128]{2,1,0:T(8,128)(2,1)} collective-permute-done((bf16[8,128,128]{2,1,0:T(8,128)(2,1)}, bf16[8,128,128]{2,1,0:T(8,128)(2,1)}, u32[]{:S(2)}, u32[]{:S(2)}) %collective-permute-start.7) | collective-permute-done | bytes 262176 | tf_op jit(solution)/shard_map/ppermute | solution.py:342
  72.4 1.2 slice.66
  73.6 1.2 slice.64
  74.8 1.2 slice.65
  77.9 0.9 convert_reduce_fusion
  78.8 0.9 slice_reduce_fusion
  79.7 2.8 collective-permute-start.8
  82.5 0.1 fusion.12
  82.6 1.1 collective-permute-done.8
  83.7 0.1 compare_convert_fusion
  83.7 0.1 select_reduce_fusion
  83.9 0.1 fusion.15
  84.0 0.1 pad_add_fusion.info_ref
  84.1 0.0 collective-permute-start.11
  84.1 2.7 collective-permute-start.12
  86.8 0.0 collective-permute-start.10
  86.8 2.7 collective-permute-start.13
  89.6 67.9 %shard_map.65 = (bf16[8,144,128]{2,1,0:T(8,128)(2,1)S(1)}, bf16[8,144,128]{2,1,0:T(8,128)(2,1)S(1)}) custom-call(s32[13]{0:T(128)S(1)} %pad_add_fusion.info_ref, bf16[8,896,128]{2,1,0:T(8,128)(2,1)S(1)} %all-to-all-done.1.own_q, bf16[8,128,128]{2,1,0:T(8,128)(2,1)} %collective-permute-done.7.their_q, s32[8,1,256]{2,1,0:T(1,128)S(1)} %fusion.13.end_ref, ...), custom_call_target="tpu_custom_call" | custom-call | flops 8589934592 | bytes 5242880 | tf_op jit(solution)/shard_map/pallas_call | solution.py:177
  157.5 0.0 copy-start.2
  157.5 1.7 pad_maximum_fusion.1.refs_0_
  159.2 1.8 collective-permute-start.14
  161.1 0.2 pad_maximum_fusion.2.refs_0_
  161.3 0.1 collective-permute-start.18
  161.4 0.1 collective-permute-start.17
  161.4 0.9 collective-permute-start.16
  162.4 2.5 collective-permute-done.14.refs_1_
  164.9 67.9 %shard_map.66 = (bf16[8,144,128]{2,1,0:T(8,128)(2,1)S(1)}, bf16[8,144,128]{2,1,0:T(8,128)(2,1)S(1)}) custom-call(s32[13]{0:T(128)S(1)} %pad_add_fusion.info_ref, bf16[8,896,128]{2,1,0:T(8,128)(2,1)S(1)} %all-to-all-done.1.own_q, bf16[8,128,128]{2,1,0:T(8,128)(2,1)S(1)} %collective-permute-done.13.their_q, s32[8,1,256]{2,1,0:T(1,128)S(1)} %fusion.13.end_ref, ...), custom_call_target="tpu_custom_call" | custom-call | flops 8589934592 | bytes 5242880 | tf_op jit(solution)/shard_map/pallas_call | solution.py:177
  232.8 0.0 copy-start.7
  232.8 0.1 collective-permute-start.19
  232.9 0.1 collective-permute-start.9
  233.0 3.0 collective-permute-start.15
  235.9 67.7 %shard_map.67 = (bf16[8,144,128]{2,1,0:T(8,128)(2,1)S(1)}, bf16[8,144,128]{2,1,0:T(8,128)(2,1)S(1)}) custom-call(s32[13]{0:T(128)S(1)} %pad_add_fusion.info_ref, bf16[8,896,128]{2,1,0:T(8,128)(2,1)S(1)} %all-to-all-done.1.own_q, bf16[8,128,128]{2,1,0:T(8,128)(2,1)S(1)} %collective-permute-done.17.their_q, s32[8,1,256]{2,1,0:T(1,128)S(1)} %fusion.13.end_ref, ...), custom_call_target="tpu_custom_call" | custom-call | flops 8589934592 | bytes 5242880 | tf_op jit(solution)/shard_map/pallas_call | solution.py:177
  303.6 0.1 collective-permute-start.20
  303.8 7.0 %collective-permute-done.20.refs_5_ = bf16[8,144,128]{2,1,0:T(8,128)(2,1)S(1)} collective-permute-done((bf16[8,144,128]{2,1,0:T(8,128)(2,1)S(1)}, bf16[8,144,128]{2,1,0:T(8,128)(2,1)S(1)}, u32[]{:S(2)}, u32[]{:S(2)}) %collective-permute-start.20) | collective-permute-done | bytes 294944 | tf_op jit(solution)/shard_map/ppermute | solution.py:370
  310.8 1.2 shard_map.68
  312.0 4.5 %all-to-all-start.2 = ((bf16[8,384,128]{2,1,0:T(8,128)(2,1)}), bf16[8,384,128]{2,1,0:T(8,128)(2,1)}, u32[]{:S(2)}, u32[]{:S(2)}) async-start(bf16[8,384,128]{2,1,0:T(8,128)(2,1)} %shard_map.68), calls=%async_computation.2 | async-start | bytes 1572864 | tf_op jit(solution)/shard_map/all_to_all | solution.py:302
  316.5 0.1 fusion.2
  316.6 0.3 fusion.4
  316.9 0.8 fusion.gate_ref
  317.8 8.7 %all-to-all-done.2.mixed_ref = bf16[8,384,128]{2,1,0:T(8,128)(2,1)} async-done(((bf16[8,384,128]{2,1,0:T(8,128)(2,1)}), bf16[8,384,128]{2,1,0:T(8,128)(2,1)}, u32[]{:S(2)}, u32[]{:S(2)}) %all-to-all-start.2) | async-done | bytes 786464 | tf_op jit(solution)/shard_map/all_to_all | solution.py:302
  326.5 2.3 shard_map.69
  (42 shorter events, 0.2 us)
Async XLA Ops:
  0.0 316.6 %copy-start = (bf16[256,3072]{1,0:T(8,128)(2,1)S(1)}, bf16[256,3072]{1,0:T(8,128)(2,1)}, u32[]{:S(2)}) copy-start(bf16[256,3072]{1,0:T(8,128)(2,1)} %param.11) | copy-start | bytes 4718596
  19.3 17.3 %copy-start.1 = (bf16[8,272,128]{2,1,0:T(8,128)(2,1)}, bf16[8,272,128]{2,1,0:T(8,128)(2,1)S(1)}, u32[]{:S(2)}) copy-start(bf16[8,272,128]{2,1,0:T(8,128)(2,1)S(1)} %all_to_all.15) | copy-start | bytes 1671172
  19.3 13.1 %collective-permute-start = (bf16[8,272,128]{2,1,0:T(8,128)(2,1)S(1)}, bf16[8,272,128]{2,1,0:T(8,128)(2,1)S(1)}, u32[]{:S(2)}, u32[]{:S(2)}) collective-permute-start(bf16[8,272,128]{2,1,0:T(8,128)(2,1)S(1)} %all_to_all.15), channel_id=1, source_target_pairs={{0,6},{1,7},{2,0},{3,1},{4,2},{5,3},{6,4},{7,5},{8,14},{9,15},{10,... | collective-permute-start | bytes 1671176 | tf_op jit(solution)/shard_map/ppermute | solution.py:316
  19.8 13.4 %collective-permute-start.1 = (bf16[8,272,128]{2,1,0:T(8,128)(2,1)S(1)}, bf16[8,272,128]{2,1,0:T(8,128)(2,1)S(1)}, u32[]{:S(2)}, u32[]{:S(2)}) collective-permute-start(bf16[8,272,128]{2,1,0:T(8,128)(2,1)S(1)} %all_to_all.15), channel_id=1, source_target_pairs={{0,2},{1,3},{2,4},{3,5},{4,6},{5,7},{6,0},{7,1},{8,10},{9,11},{10,... | collective-permute-start | bytes 1671176 | tf_op jit(solution)/shard_map/ppermute | solution.py:316
  32.4 4.2 %copy-start.3 = (bf16[8,272,128]{2,1,0:T(8,128)(2,1)}, bf16[8,272,128]{2,1,0:T(8,128)(2,1)S(1)}, u32[]{:S(2)}) copy-start(bf16[8,272,128]{2,1,0:T(8,128)(2,1)S(1)} %collective-permute-done) | copy-start | bytes 1671172
  33.1 7.1 %collective-permute-start.3 = (bf16[4,272,128]{2,1,0:T(8,128)(2,1)}, bf16[4,272,128]{2,1,0:T(8,128)(2,1)}, u32[]{:S(2)}, u32[]{:S(2)}) collective-permute-start(bf16[4,272,128]{2,1,0:T(8,128)(2,1)} %slice.61), channel_id=1, source_target_pairs={{0,6},{1,7},{2,0},{3,1},{4,2},{5,3},{6,4},{7,5},{8,14},{9,15},{10,... | collective-permute-start | bytes 835592 | tf_op jit(solution)/shard_map/ppermute | solution.py:327
  33.1 3.5 %copy-start.4 = (bf16[8,272,128]{2,1,0:T(8,128)(2,1)}, bf16[8,272,128]{2,1,0:T(8,128)(2,1)S(1)}, u32[]{:S(2)}) copy-start(bf16[8,272,128]{2,1,0:T(8,128)(2,1)S(1)} %collective-permute-done.1) | copy-start | bytes 1671172
  33.9 6.5 %collective-permute-start.2 = (bf16[4,272,128]{2,1,0:T(8,128)(2,1)}, bf16[4,272,128]{2,1,0:T(8,128)(2,1)}, u32[]{:S(2)}, u32[]{:S(2)}) collective-permute-start(bf16[4,272,128]{2,1,0:T(8,128)(2,1)} %slice.60), channel_id=1, source_target_pairs={{0,2},{1,3},{2,4},{3,5},{4,6},{5,7},{6,0},{7,1},{8,10},{9,11},{10,... | collective-permute-start | bytes 835592 | tf_op jit(solution)/shard_map/ppermute | solution.py:327
  36.6 24.1 %all-to-all-start.1 = ((bf16[8,896,128]{2,1,0:T(8,128)(2,1)}), bf16[8,896,128]{2,1,0:T(8,128)(2,1)S(1)}, u32[]{:S(2)}, u32[]{:S(2)}) async-start(bf16[8,896,128]{2,1,0:T(8,128)(2,1)} %get-tuple-element.42), calls=%async_computation.1 | async-start | bytes 3670016 | tf_op jit(solution)/shard_map/all_to_all | solution.py:302
  44.6 33.3 %collective-permute-start.4 = (bf16[4,8,272,128]{3,2,1,0:T(8,128)(2,1)}, bf16[4,8,272,128]{3,2,1,0:T(8,128)(2,1)}, u32[]{:S(2)}, u32[]{:S(2)}) collective-permute-start(bf16[4,8,272,128]{3,2,1,0:T(8,128)(2,1)} %pad_maximum_fusion.refs_0_), channel_id=1, source_target_pairs={{0,8},{8,0},{16,24},{24,16},{32,40},{40,32},{48,56},{56,48},{64,72... | collective-permute-start | bytes 6684680 | tf_op jit(solution)/shard_map/ppermute | solution.py:313
  62.7 10.9 %collective-permute-start.5 = (bf16[8,256,128]{2,1,0:T(8,128)(2,1)}, bf16[8,256,128]{2,1,0:T(8,128)(2,1)}, u32[]{:S(2)}, u32[]{:S(2)}) collective-permute-start(bf16[8,256,128]{2,1,0:T(8,128)(2,1)} %get-tuple-element.46), channel_id=1, source_target_pairs={{0,6},{1,7},{2,0},{3,1},{4,2},{5,3},{6,4},{7,5},{8,14},{9,15},{10,... | collective-permute-start | bytes 1572872 | tf_op jit(solution)/shard_map/ppermute | solution.py:316
  62.7 12.1 %collective-permute-start.6 = (bf16[8,256,128]{2,1,0:T(8,128)(2,1)}, bf16[8,256,128]{2,1,0:T(8,128)(2,1)}, u32[]{:S(2)}, u32[]{:S(2)}) collective-permute-start(bf16[8,256,128]{2,1,0:T(8,128)(2,1)} %get-tuple-element.46), channel_id=1, source_target_pairs={{0,2},{1,3},{2,4},{3,5},{4,6},{5,7},{6,0},{7,1},{8,10},{9,11},{10,... | collective-permute-start | bytes 1572872 | tf_op jit(solution)/shard_map/ppermute | solution.py:316
  65.4 7.0 %collective-permute-start.7 = (bf16[8,128,128]{2,1,0:T(8,128)(2,1)}, bf16[8,128,128]{2,1,0:T(8,128)(2,1)}, u32[]{:S(2)}, u32[]{:S(2)}) collective-permute-start(bf16[8,128,128]{2,1,0:T(8,128)(2,1)} %get-tuple-element.47), channel_id=1, source_target_pairs={{0,1},{1,0},{2,3},{3,2},{4,5},{5,4},{6,7},{7,6},{8,9},{9,8},{10,11... | collective-permute-start | bytes 786440 | tf_op jit(solution)/shard_map/ppermute | solution.py:342
  79.7 4.0 %collective-permute-start.8 = (f32[1,128]{1,0:T(1,128)S(1)}, f32[1,128]{1,0:T(1,128)S(1)}, u32[]{:S(2)}, u32[]{:S(2)}) collective-permute-start(f32[1,128]{1,0:T(1,128)S(1)} %bitcast.59), channel_id=1, source_target_pairs={{0,1},{1,0},{2,3},{3,2},{4,5},{5,4},{6,7},{7,6},{8,9},{9,8},{10,11... | collective-permute-start | bytes 1544 | tf_op jit(solution)/shard_map/ppermute | solution.py:346
  84.1 73.4 %collective-permute-start.11 = (bf16[8,256,128]{2,1,0:T(8,128)(2,1)}, bf16[8,256,128]{2,1,0:T(8,128)(2,1)S(1)}, u32[]{:S(2)}, u32[]{:S(2)}) collective-permute-start(bf16[8,256,128]{2,1,0:T(8,128)(2,1)} %get-tuple-element.56), channel_id=1, source_target_pairs={{0,6},{1,7},{2,0},{3,1},{4,2},{5,3},{6,4},{7,5},{8,14},{9,15},{10,... | collective-permute-start | bytes 1572872 | tf_op jit(solution)/shard_map/ppermute | solution.py:316
  84.1 73.4 %collective-permute-start.12 = (bf16[8,256,128]{2,1,0:T(8,128)(2,1)}, bf16[8,256,128]{2,1,0:T(8,128)(2,1)S(1)}, u32[]{:S(2)}, u32[]{:S(2)}) collective-permute-start(bf16[8,256,128]{2,1,0:T(8,128)(2,1)} %get-tuple-element.56), channel_id=1, source_target_pairs={{0,2},{1,3},{2,4},{3,5},{4,6},{5,7},{6,0},{7,1},{8,10},{9,11},{10,... | collective-permute-start | bytes 1572872 | tf_op jit(solution)/shard_map/ppermute | solution.py:316
  86.8 70.7 %collective-permute-start.10 = (bf16[8,256,128]{2,1,0:T(8,128)(2,1)}, bf16[8,256,128]{2,1,0:T(8,128)(2,1)S(1)}, u32[]{:S(2)}, u32[]{:S(2)}) collective-permute-start(bf16[8,256,128]{2,1,0:T(8,128)(2,1)} %collective-permute-done.6), channel_id=1, source_target_pairs={{0,2},{1,3},{2,4},{3,5},{4,6},{5,7},{6,0},{7,1},{8,10},{9,11},{10,... | collective-permute-start | bytes 1572872 | tf_op jit(solution)/shard_map/ppermute | solution.py:374
  86.8 70.6 %collective-permute-start.13 = (bf16[8,128,128]{2,1,0:T(8,128)(2,1)}, bf16[8,128,128]{2,1,0:T(8,128)(2,1)S(1)}, u32[]{:S(2)}, u32[]{:S(2)}) collective-permute-start(bf16[8,128,128]{2,1,0:T(8,128)(2,1)} %get-tuple-element.57), channel_id=1, source_target_pairs={{0,1},{1,0},{2,3},{3,2},{4,5},{5,4},{6,7},{7,6},{8,9},{9,8},{10,11... | collective-permute-start | bytes 786440 | tf_op jit(solution)/shard_map/ppermute | solution.py:377
  157.5 3.5 %copy-start.2 = (bf16[8,256,128]{2,1,0:T(8,128)(2,1)S(1)}, bf16[8,256,128]{2,1,0:T(8,128)(2,1)}, u32[]{:S(2)}) copy-start(bf16[8,256,128]{2,1,0:T(8,128)(2,1)} %get-tuple-element.56) | copy-start | bytes 1572868
  159.2 2.1 copy-start.5
  159.2 5.6 %collective-permute-start.14 = (bf16[4,8,256,128]{3,2,1,0:T(8,128)(2,1)S(1)}, bf16[4,8,256,128]{3,2,1,0:T(8,128)(2,1)S(1)}, u32[]{:S(2)}, u32[]{:S(2)}) collective-permute-start(bf16[4,8,256,128]{3,2,1,0:T(8,128)(2,1)S(1)} %pad_maximum_fusion.1.refs_0_), channel_id=1, source_target_pairs={{0,8},{8,0},{16,24},{24,16},{32,40},{40,32},{48,56},{56,48},{64,72... | collective-permute-start | bytes 6291464 | tf_op jit(solution)/shard_map/ppermute | solution.py:313
  161.3 74.7 %collective-permute-start.18 = (bf16[3,8,256,128]{3,2,1,0:T(8,128)(2,1)S(1)}, bf16[3,8,256,128]{3,2,1,0:T(8,128)(2,1)S(1)}, u32[]{:S(2)}, u32[]{:S(2)}) collective-permute-start(bf16[3,8,256,128]{3,2,1,0:T(8,128)(2,1)S(1)} %pad_maximum_fusion.2.refs_0_), channel_id=1, source_target_pairs={{0,8},{8,0},{16,24},{24,16},{32,40},{40,32},{48,56},{56,48},{64,72... | collective-permute-start | bytes 4718600 | tf_op jit(solution)/shard_map/ppermute | solution.py:313
  161.4 71.4 %collective-permute-start.17 = (bf16[8,128,128]{2,1,0:T(8,128)(2,1)S(1)}, bf16[8,128,128]{2,1,0:T(8,128)(2,1)S(1)}, u32[]{:S(2)}, u32[]{:S(2)}) collective-permute-start(bf16[8,128,128]{2,1,0:T(8,128)(2,1)S(1)} %copy-done.5), channel_id=1, source_target_pairs={{0,1},{1,0},{2,3},{3,2},{4,5},{5,4},{6,7},{7,6},{8,9},{9,8},{10,11... | collective-permute-start | bytes 786440 | tf_op jit(solution)/shard_map/ppermute | solution.py:385
  161.4 71.3 %collective-permute-start.16 = (bf16[8,256,128]{2,1,0:T(8,128)(2,1)S(1)}, bf16[8,256,128]{2,1,0:T(8,128)(2,1)S(1)}, u32[]{:S(2)}, u32[]{:S(2)}) collective-permute-start(bf16[8,256,128]{2,1,0:T(8,128)(2,1)S(1)} %collective-permute-done.11), channel_id=1, source_target_pairs={{0,6},{1,7},{2,0},{3,1},{4,2},{5,3},{6,4},{7,5},{8,14},{9,15},{10,... | collective-permute-start | bytes 1572872 | tf_op jit(solution)/shard_map/ppermute | solution.py:383
  232.8 71.0 %copy-start.7 = (s32[24]{0:T(128)S(1)}, s32[24]{0:T(128)}, u32[]{:S(2)}) copy-start(s32[24]{0:T(128)} %param.10) | copy-start | bytes 292
  232.8 3.1 collective-permute-start.19
  232.9 70.9 %collective-permute-start.9 = (bf16[8,144,128]{2,1,0:T(8,128)(2,1)S(1)}, bf16[8,144,128]{2,1,0:T(8,128)(2,1)S(1)}, u32[]{:S(2)}, u32[]{:S(2)}) collective-permute-start(bf16[8,144,128]{2,1,0:T(8,128)(2,1)S(1)} %get-tuple-element.53), channel_id=1, source_target_pairs={{0,1},{1,0},{2,3},{3,2},{4,5},{5,4},{6,7},{7,6},{8,9},{9,8},{10,11... | collective-permute-start | bytes 884744 | tf_op jit(solution)/shard_map/ppermute | solution.py:370
  233.0 70.8 %collective-permute-start.15 = (bf16[8,144,128]{2,1,0:T(8,128)(2,1)S(1)}, bf16[8,144,128]{2,1,0:T(8,128)(2,1)S(1)}, u32[]{:S(2)}, u32[]{:S(2)}) collective-permute-start(bf16[8,144,128]{2,1,0:T(8,128)(2,1)S(1)} %get-tuple-element.64), channel_id=1, source_target_pairs={{0,1},{1,0},{2,3},{3,2},{4,5},{5,4},{6,7},{7,6},{8,9},{9,8},{10,11... | collective-permute-start | bytes 884744 | tf_op jit(solution)/shard_map/ppermute | solution.py:370
  303.6 7.2 %collective-permute-start.20 = (bf16[8,144,128]{2,1,0:T(8,128)(2,1)S(1)}, bf16[8,144,128]{2,1,0:T(8,128)(2,1)S(1)}, u32[]{:S(2)}, u32[]{:S(2)}) collective-permute-start(bf16[8,144,128]{2,1,0:T(8,128)(2,1)S(1)} %get-tuple-element.74), channel_id=1, source_target_pairs={{0,1},{1,0},{2,3},{3,2},{4,5},{5,4},{6,7},{7,6},{8,9},{9,8},{10,11... | collective-permute-start | bytes 884744 | tf_op jit(solution)/shard_map/ppermute | solution.py:370
  312.0 4.9 %copy-start.6 = (s32[128]{0:T(128)S(1)}, s32[128]{0:T(128)}, u32[]{:S(2)}) copy-start(s32[128]{0:T(128)} %param.9) | copy-start | bytes 1540
  312.0 14.4 %all-to-all-start.2 = ((bf16[8,384,128]{2,1,0:T(8,128)(2,1)}), bf16[8,384,128]{2,1,0:T(8,128)(2,1)}, u32[]{:S(2)}, u32[]{:S(2)}) async-start(bf16[8,384,128]{2,1,0:T(8,128)(2,1)} %shard_map.68), calls=%async_computation.2 | async-start | bytes 1572864 | tf_op jit(solution)/shard_map/all_to_all | solution.py:302

commit v13 on v11

--- a/solution.py
+++ b/solution.py
@@ -17,7 +17,6 @@
 KEYS = 8192
 WIDTH = 256
 ITEMS = 8
-FIRST_ZONES = 2
 K_NORM, Q_NORM = 32, 40
 NOTE = 16
 PLAIN_LIMIT = 70.0
@@ -37,7 +36,7 @@
 
     copies = []
     half = len(sources) // 2
-    for j, zones in enumerate((pl.ds(0, FIRST_ZONES), pl.ds(FIRST_ZONES, ZONES - FIRST_ZONES))):
+    for zones in (pl.ds(0, 2), pl.ds(2, 3), pl.ds(5, 3)):
         for group, c in ((sources[:half], core), (sources[half:], 1 - core)):
             pieces = [src.at[k] for src in group for k in range(src.shape[0])]
             for piece, step in zip(pieces, (0, 1, 3, 2)):
@@ -56,7 +55,7 @@
     acc_ref[...] = jnp.zeros_like(acc_ref)
     top_ref[...] = jnp.zeros_like(top_ref)
     ones = jnp.ones((NOTE, WIDTH), jnp.bfloat16)
-    for copy in copies[: len(copies) // 2]:
+    for copy in copies[:8]:
         copy.wait()
 
     def part(i, rows):
@@ -116,7 +115,12 @@
                 items.append(following(items[-1]))
             return tuple(items)
 
-        def step(_, items):
+        def step(number, items):
+            @pl.when(number == lasting)
+            def _():
+                for copy in copies[16:]:
+                    copy.wait()
+
             later = run(following(items[-1]))
             scores = score(later[0])
             for slot in range(ITEMS):
@@ -130,9 +134,10 @@
         items = run((jnp.int32(0), jnp.int32(0)))
         for slot in range(ITEMS):
             weigh(slot, items[slot], score(items[slot]))
-        for copy in copies[len(copies) // 2 :]:
+        for copy in copies[8:16]:
             copy.wait()
         total = sum(count(r) for r in range(blocks))
+        lasting = jnp.maximum(sum(count(r) for r in range(4)) // ITEMS - 1, 0)
         items = lax.fori_loop(0, (total + ITEMS - 1) // ITEMS - 1, step, items)
         for slot in range(ITEMS):
             absorb(slot, items[slot])
@@ -140,7 +145,7 @@
     @pl.when(jnp.logical_not(plain))
     def _():
         top_ref[...] = jnp.full_like(top_ref, LOW)
-        for copy in copies[len(copies) // 2 :]:
+        for copy in copies[8:]:
             copy.wait()
 
         def over_block(r, carry):
@@ -188,7 +193,7 @@
                 pltpu.VMEM((ITEMS, WIDTH, SEGMENT), jnp.bfloat16),
                 pltpu.VMEM((ZONES + 1, HEAD_DIM + NOTE, SEGMENT), jnp.float32),
                 pltpu.VMEM((ZONES, 8, SEGMENT), jnp.float32),
-                pltpu.SemaphoreType.DMA((16,)),
+                pltpu.SemaphoreType.DMA((24,)),
             ],
         ),
         out_shape=[out, out],

time: 318 us -> 323 us (1.016)
  Pallas kernels: 212 us -> 218 us
    pallas_call x3, Pallas kernels: 205 us -> 210 us  [attend(): pl.pallas_call(functools.partial(attend_kernel, head), grid_spec=pltpu.Pr...]
where the time goes in v13:
time: 323 us
  Pallas kernels  218 us (67%)
  waiting for transfers between devices  39.7 us (12%)
  starting transfers between devices  33.7 us (10%)
  blocking collectives  15.4 us (5%)
  local copies, waits for them, and re-layouts  9.79 us (3%)
  other arithmetic  4.88 us (2%)
    pallas_call x3, Pallas kernels, attend(): pl.pallas_call(functools.partial(attend_kernel, head), grid_spec=pltpu.Pr...  210 us
    all_to_all x1, blocking collectives, exchange(): lax.all_to_all(parts, BOTH, split_axis=0, concat_axis=0, axis_index_group...  15.4 us
    all_to_all x2, waiting for transfers between devices, exchange(): lax.all_to_all(parts, BOTH, split_axis=0, concat_axis=0, axis_index_group...  10.6 us
    ppermute x6, waiting for transfers between devices, sides(): return (lax.ppermute(block, 'head', down), lax.ppermute(block, 'head', up))  9.69 us
    ppermute x6, starting transfers between devices, sides(): return (lax.ppermute(block, 'head', down), lax.ppermute(block, 'head', up))  8.03 us
    all_to_all x2, starting transfers between devices, exchange(): lax.all_to_all(parts, BOTH, split_axis=0, concat_axis=0, axis_index_group...  7.95 us
    ppermute x3, waiting for transfers between devices, attended(): parts[2 * head + 1] = lax.ppermute(theirs, 'head', partner)  7.01 us
  transfers between devices with their start and end apart: 23, of which 10 were waited for; matrix products, arithmetic and copies ran while one was open for 3% of the time, Pallas kernels for 65%

profile of v13, /device:TPU:25, one launch (start us, length us, event | category | flops | bytes accessed | tf_op | source)
XLA Modules:
  0.0 322.9 jit_solution(17644729382501408191)
XLA Ops:
  0.0 4.0 %shard_map.64 = (bf16[8,272,128]{2,1,0:T(8,128)(2,1)}, bf16[8,896,128]{2,1,0:T(8,128)(2,1)}) custom-call(bf16[128,3072]{1,0:T(8,128)(2,1)} %queries_ref.1, bf16[128,3072]{1,0:T(8,128)(2,1)} %keys_ref.1, bf16[128,3072]{1,0:T(8,128)(2,1)} %values_ref.1, s32[1,128]{1,0:T(1,128)} %bitcast.55), custom_call_target="tpu_custom_call" | custom-call | tf_op jit(solution)/shard_map/pallas_call | solution.py:321
  4.0 15.4 %all_to_all.15 = bf16[8,272,128]{2,1,0:T(8,128)(2,1)} all-to-all(bf16[8,272,128]{2,1,0:T(8,128)(2,1)} %get-tuple-element.46), channel_id=1, replica_groups={{0,16,32,48,64,80,96,112},{1,17,33,49,65,81,97,113},{2,18,34,50,66,82,9..., dimensions={0} | all-to-all | bytes 1114112 | tf_op jit(solution)/shard_map/all_to_all | solution.py:307
  19.4 0.5 collective-permute-start
  19.8 2.2 collective-permute-start.1
  22.0 3.6 %all-to-all-start.1 = ((bf16[8,896,128]{2,1,0:T(8,128)(2,1)}), bf16[8,896,128]{2,1,0:T(8,128)(2,1)S(1)}, u32[]{:S(2)}, u32[]{:S(2)}) async-start(bf16[8,896,128]{2,1,0:T(8,128)(2,1)} %get-tuple-element.47), calls=%async_computation.1 | async-start | bytes 3670016 | tf_op jit(solution)/shard_map/all_to_all | solution.py:307
  25.6 7.1 %collective-permute-done = bf16[8,272,128]{2,1,0:T(8,128)(2,1)} collective-permute-done((bf16[8,272,128]{2,1,0:T(8,128)(2,1)}, bf16[8,272,128]{2,1,0:T(8,128)(2,1)}, u32[]{:S(2)}, u32[]{:S(2)}) %collective-permute-start) | collective-permute-done | bytes 557088 | tf_op jit(solution)/shard_map/ppermute | solution.py:318
  32.8 1.0 slice.49
  33.7 0.1 collective-permute-start.3
  33.8 1.0 slice.48
  34.8 2.7 collective-permute-start.2
  37.5 3.2 collective-permute-done.3
  40.7 0.3 collective-permute-done.2
  41.1 1.7 pad_maximum_fusion.refs_0_
  42.8 0.1 slice_reduce_fusion.1
  42.9 1.3 copy-done.1
  44.2 2.8 all-to-all-done.1.own_q
  46.9 3.7 %collective-permute-start.4 = (bf16[4,8,272,128]{3,2,1,0:T(8,128)(2,1)}, bf16[4,8,272,128]{3,2,1,0:T(8,128)(2,1)}, u32[]{:S(2)}, u32[]{:S(2)}) collective-permute-start(bf16[4,8,272,128]{3,2,1,0:T(8,128)(2,1)} %copy-done.1), channel_id=1, source_target_pairs={{0,8},{8,0},{16,24},{24,16},{32,40},{40,32},{48,56},{56,48},{64,72... | collective-permute-start | bytes 6684680 | tf_op jit(solution)/shard_map/ppermute | solution.py:315
  50.7 0.1 add_multiply_fusion
  50.7 0.1 broadcast_add_fusion
  50.8 0.9 fusion.19
  51.7 0.9 fusion.18
  52.6 2.7 collective-permute-start.6
  55.2 2.5 collective-permute-start.7
  57.7 0.9 convert_reduce_fusion
  58.6 0.9 slice_reduce_fusion
  59.5 4.6 %collective-permute-done.7.their_q = bf16[8,128,128]{2,1,0:T(8,128)(2,1)S(1)} collective-permute-done((bf16[8,128,128]{2,1,0:T(8,128)(2,1)S(1)}, bf16[8,128,128]{2,1,0:T(8,128)(2,1)S(1)}, u32[]{:S(2)}, u32[]{:S(2)}) %collective-permute-start.7) | collective-permute-done | bytes 262176 | tf_op jit(solution)/shard_map/ppermute | solution.py:344
  64.1 0.7 copy-done.3
  64.8 2.6 collective-permute-done.5
  67.3 0.8 copy-done.8
  68.1 2.5 collective-permute-start.8
  70.6 0.1 fusion.12
  70.7 1.4 collective-permute-done.8
  72.0 0.1 compare_convert_fusion
  72.1 0.1 select_reduce_fusion
  72.2 0.1 fusion.15
  72.4 0.1 pad_add_fusion.info_ref
  72.5 2.7 collective-permute-start.12
  75.2 0.3 collective-permute-start.10
  75.5 2.5 collective-permute-start.13
  78.0 1.6 copy-done.2
  79.6 0.9 copy-done.4
  80.6 67.8 %shard_map.65 = (bf16[8,144,128]{2,1,0:T(8,128)(2,1)S(1)}, bf16[8,144,128]{2,1,0:T(8,128)(2,1)S(1)}) custom-call(s32[13]{0:T(128)S(1)} %pad_add_fusion.info_ref, bf16[8,896,128]{2,1,0:T(8,128)(2,1)S(1)} %all-to-all-done.1.own_q, bf16[8,128,128]{2,1,0:T(8,128)(2,1)S(1)} %copy-done.4, s32[8,1,256]{2,1,0:T(1,128)S(1)} %fusion.13.end_ref, ...), custom_call_target="tpu_custom_call" | custom-call | flops 8589934592 | bytes 5242880 | tf_op jit(solution)/shard_map/pallas_call | solution.py:182
  148.5 0.3 pad_maximum_fusion.1.refs_0_
  148.8 0.1 collective-permute-start.14
  148.9 0.7 copy-done.5
  149.5 0.2 pad_maximum_fusion.2.refs_0_
  149.7 0.1 collective-permute-start.18
  149.8 0.1 collective-permute-start.17
  149.9 0.1 collective-permute-start.16
  150.0 3.0 collective-permute-done.14.refs_1_
  153.0 71.3 %shard_map.66 = (bf16[8,144,128]{2,1,0:T(8,128)(2,1)S(1)}, bf16[8,144,128]{2,1,0:T(8,128)(2,1)S(1)}) custom-call(s32[13]{0:T(128)S(1)} %pad_add_fusion.info_ref, bf16[8,896,128]{2,1,0:T(8,128)(2,1)S(1)} %all-to-all-done.1.own_q, bf16[8,128,128]{2,1,0:T(8,128)(2,1)S(1)} %collective-permute-done.13.their_q, s32[8,1,256]{2,1,0:T(1,128)S(1)} %fusion.13.end_ref, ...), custom_call_target="tpu_custom_call" | custom-call | flops 8589934592 | bytes 5242880 | tf_op jit(solution)/shard_map/pallas_call | solution.py:182
  224.4 0.1 collective-permute-start.19
  224.5 0.1 collective-permute-start.9
  224.6 3.0 collective-permute-start.15
  227.6 71.2 %shard_map.67 = (bf16[8,144,128]{2,1,0:T(8,128)(2,1)S(1)}, bf16[8,144,128]{2,1,0:T(8,128)(2,1)S(1)}) custom-call(s32[13]{0:T(128)S(1)} %pad_add_fusion.info_ref, bf16[8,896,128]{2,1,0:T(8,128)(2,1)S(1)} %all-to-all-done.1.own_q, bf16[8,128,128]{2,1,0:T(8,128)(2,1)S(1)} %collective-permute-done.17.their_q, s32[8,1,256]{2,1,0:T(1,128)S(1)} %fusion.13.end_ref, ...), custom_call_target="tpu_custom_call" | custom-call | flops 8589934592 | bytes 5242880 | tf_op jit(solution)/shard_map/pallas_call | solution.py:182
  298.7 0.1 collective-permute-start.20
  298.9 7.0 %collective-permute-done.20.refs_5_ = bf16[8,144,128]{2,1,0:T(8,128)(2,1)S(1)} collective-permute-done((bf16[8,144,128]{2,1,0:T(8,128)(2,1)S(1)}, bf16[8,144,128]{2,1,0:T(8,128)(2,1)S(1)}, u32[]{:S(2)}, u32[]{:S(2)}) %collective-permute-start.20) | collective-permute-done | bytes 294944 | tf_op jit(solution)/shard_map/ppermute | solution.py:372
  305.9 1.3 shard_map.68
  307.1 4.4 %all-to-all-start.2 = ((bf16[8,384,128]{2,1,0:T(8,128)(2,1)}), bf16[8,384,128]{2,1,0:T(8,128)(2,1)}, u32[]{:S(2)}, u32[]{:S(2)}) async-start(bf16[8,384,128]{2,1,0:T(8,128)(2,1)} %shard_map.68), calls=%async_computation.2 | async-start | bytes 1572864 | tf_op jit(solution)/shard_map/all_to_all | solution.py:307
  311.5 0.1 fusion.2
  311.6 0.3 fusion.4
  312.0 0.8 fusion.gate_ref
  312.8 7.8 %all-to-all-done.2.mixed_ref = bf16[8,384,128]{2,1,0:T(8,128)(2,1)} async-done(((bf16[8,384,128]{2,1,0:T(8,128)(2,1)}), bf16[8,384,128]{2,1,0:T(8,128)(2,1)}, u32[]{:S(2)}, u32[]{:S(2)}) %all-to-all-start.2) | async-done | bytes 786464 | tf_op jit(solution)/shard_map/all_to_all | solution.py:307
  320.6 2.3 shard_map.69
  (53 shorter events, 0.3 us)
Async XLA Ops:
  0.0 311.6 %copy-start = (bf16[256,3072]{1,0:T(8,128)(2,1)S(1)}, bf16[256,3072]{1,0:T(8,128)(2,1)}, u32[]{:S(2)}) copy-start(bf16[256,3072]{1,0:T(8,128)(2,1)} %param.11) | copy-start | bytes 4718596
  19.4 13.4 %collective-permute-start = (bf16[8,272,128]{2,1,0:T(8,128)(2,1)}, bf16[8,272,128]{2,1,0:T(8,128)(2,1)}, u32[]{:S(2)}, u32[]{:S(2)}) collective-permute-start(bf16[8,272,128]{2,1,0:T(8,128)(2,1)} %all_to_all.15), channel_id=1, source_target_pairs={{0,6},{1,7},{2,0},{3,1},{4,2},{5,3},{6,4},{7,5},{8,14},{9,15},{10,... | collective-permute-start | bytes 1671176 | tf_op jit(solution)/shard_map/ppermute | solution.py:318
  19.8 14.0 %collective-permute-start.1 = (bf16[8,272,128]{2,1,0:T(8,128)(2,1)}, bf16[8,272,128]{2,1,0:T(8,128)(2,1)}, u32[]{:S(2)}, u32[]{:S(2)}) collective-permute-start(bf16[8,272,128]{2,1,0:T(8,128)(2,1)} %all_to_all.15), channel_id=1, source_target_pairs={{0,2},{1,3},{2,4},{3,5},{4,6},{5,7},{6,0},{7,1},{8,10},{9,11},{10,... | collective-permute-start | bytes 1671176 | tf_op jit(solution)/shard_map/ppermute | solution.py:318
  22.0 24.9 %all-to-all-start.1 = ((bf16[8,896,128]{2,1,0:T(8,128)(2,1)}), bf16[8,896,128]{2,1,0:T(8,128)(2,1)S(1)}, u32[]{:S(2)}, u32[]{:S(2)}) async-start(bf16[8,896,128]{2,1,0:T(8,128)(2,1)} %get-tuple-element.47), calls=%async_computation.1 | async-start | bytes 3670016 | tf_op jit(solution)/shard_map/all_to_all | solution.py:307
  33.7 7.0 %collective-permute-start.3 = (bf16[4,272,128]{2,1,0:T(8,128)(2,1)S(1)}, bf16[4,272,128]{2,1,0:T(8,128)(2,1)S(1)}, u32[]{:S(2)}, u32[]{:S(2)}) collective-permute-start(bf16[4,272,128]{2,1,0:T(8,128)(2,1)S(1)} %slice.49), channel_id=1, source_target_pairs={{0,6},{1,7},{2,0},{3,1},{4,2},{5,3},{6,4},{7,5},{8,14},{9,15},{10,... | collective-permute-start | bytes 835592 | tf_op jit(solution)/shard_map/ppermute | solution.py:329
  34.8 6.2 %collective-permute-start.2 = (bf16[4,272,128]{2,1,0:T(8,128)(2,1)S(1)}, bf16[4,272,128]{2,1,0:T(8,128)(2,1)S(1)}, u32[]{:S(2)}, u32[]{:S(2)}) collective-permute-start(bf16[4,272,128]{2,1,0:T(8,128)(2,1)S(1)} %slice.48), channel_id=1, source_target_pairs={{0,2},{1,3},{2,4},{3,5},{4,6},{5,7},{6,0},{7,1},{8,10},{9,11},{10,... | collective-permute-start | bytes 835592 | tf_op jit(solution)/shard_map/ppermute | solution.py:329
  42.8 1.4 copy-start.1
  46.9 10.8 %collective-permute-start.4 = (bf16[4,8,272,128]{3,2,1,0:T(8,128)(2,1)}, bf16[4,8,272,128]{3,2,1,0:T(8,128)(2,1)}, u32[]{:S(2)}, u32[]{:S(2)}) collective-permute-start(bf16[4,8,272,128]{3,2,1,0:T(8,128)(2,1)} %copy-done.1), channel_id=1, source_target_pairs={{0,8},{8,0},{16,24},{24,16},{32,40},{40,32},{48,56},{56,48},{64,72... | collective-permute-start | bytes 6684680 | tf_op jit(solution)/shard_map/ppermute | solution.py:315
  52.6 11.5 %copy-start.6 = (bf16[8,256,128]{2,1,0:T(8,128)(2,1)}, bf16[8,256,128]{2,1,0:T(8,128)(2,1)S(1)}, u32[]{:S(2)}) copy-start(bf16[8,256,128]{2,1,0:T(8,128)(2,1)S(1)} %get-tuple-element.52) | copy-start | bytes 1572868
  52.6 14.8 %collective-permute-start.5 = (bf16[8,256,128]{2,1,0:T(8,128)(2,1)S(1)}, bf16[8,256,128]{2,1,0:T(8,128)(2,1)S(1)}, u32[]{:S(2)}, u32[]{:S(2)}) collective-permute-start(bf16[8,256,128]{2,1,0:T(8,128)(2,1)S(1)} %get-tuple-element.52), channel_id=1, source_target_pairs={{0,6},{1,7},{2,0},{3,1},{4,2},{5,3},{6,4},{7,5},{8,14},{9,15},{10,... | collective-permute-start | bytes 1572872 | tf_op jit(solution)/shard_map/ppermute | solution.py:318
  52.6 14.8 %collective-permute-start.6 = (bf16[8,256,128]{2,1,0:T(8,128)(2,1)S(1)}, bf16[8,256,128]{2,1,0:T(8,128)(2,1)S(1)}, u32[]{:S(2)}, u32[]{:S(2)}) collective-permute-start(bf16[8,256,128]{2,1,0:T(8,128)(2,1)S(1)} %get-tuple-element.52), channel_id=1, source_target_pairs={{0,2},{1,3},{2,4},{3,5},{4,6},{5,7},{6,0},{7,1},{8,10},{9,11},{10,... | collective-permute-start | bytes 1572872 | tf_op jit(solution)/shard_map/ppermute | solution.py:318
  55.2 8.8 %collective-permute-start.7 = (bf16[8,128,128]{2,1,0:T(8,128)(2,1)S(1)}, bf16[8,128,128]{2,1,0:T(8,128)(2,1)S(1)}, u32[]{:S(2)}, u32[]{:S(2)}) collective-permute-start(bf16[8,128,128]{2,1,0:T(8,128)(2,1)S(1)} %get-tuple-element.53), channel_id=1, source_target_pairs={{0,1},{1,0},{2,3},{3,2},{4,5},{5,4},{6,7},{7,6},{8,9},{9,8},{10,11... | collective-permute-start | bytes 786440 | tf_op jit(solution)/shard_map/ppermute | solution.py:344
  64.0 0.7 copy-start.3
  67.3 0.8 copy-start.8
  68.1 2.5 copy-start.10
  68.1 3.9 %collective-permute-start.8 = (f32[1,128]{1,0:T(1,128)S(1)}, f32[1,128]{1,0:T(1,128)S(1)}, u32[]{:S(2)}, u32[]{:S(2)}) collective-permute-start(f32[1,128]{1,0:T(1,128)S(1)} %select_bitcast_fusion), channel_id=1, source_target_pairs={{0,1},{1,0},{2,3},{3,2},{4,5},{5,4},{6,7},{7,6},{8,9},{9,8},{10,11... | collective-permute-start | bytes 1544 | tf_op jit(solution)/shard_map/ppermute | solution.py:348
  72.5 75.9 %collective-permute-start.11 = (bf16[8,256,128]{2,1,0:T(8,128)(2,1)}, bf16[8,256,128]{2,1,0:T(8,128)(2,1)S(1)}, u32[]{:S(2)}, u32[]{:S(2)}) collective-permute-start(bf16[8,256,128]{2,1,0:T(8,128)(2,1)} %get-tuple-element.66), channel_id=1, source_target_pairs={{0,6},{1,7},{2,0},{3,1},{4,2},{5,3},{6,4},{7,5},{8,14},{9,15},{10,... | collective-permute-start | bytes 1572872 | tf_op jit(solution)/shard_map/ppermute | solution.py:318
  72.5 75.9 %collective-permute-start.12 = (bf16[8,256,128]{2,1,0:T(8,128)(2,1)}, bf16[8,256,128]{2,1,0:T(8,128)(2,1)S(1)}, u32[]{:S(2)}, u32[]{:S(2)}) collective-permute-start(bf16[8,256,128]{2,1,0:T(8,128)(2,1)} %get-tuple-element.66), channel_id=1, source_target_pairs={{0,2},{1,3},{2,4},{3,5},{4,6},{5,7},{6,0},{7,1},{8,10},{9,11},{10,... | collective-permute-start | bytes 1572872 | tf_op jit(solution)/shard_map/ppermute | solution.py:318
  75.2 73.2 %collective-permute-start.10 = (bf16[8,256,128]{2,1,0:T(8,128)(2,1)}, bf16[8,256,128]{2,1,0:T(8,128)(2,1)S(1)}, u32[]{:S(2)}, u32[]{:S(2)}) collective-permute-start(bf16[8,256,128]{2,1,0:T(8,128)(2,1)} %copy-done.10), channel_id=1, source_target_pairs={{0,2},{1,3},{2,4},{3,5},{4,6},{5,7},{6,0},{7,1},{8,10},{9,11},{10,... | collective-permute-start | bytes 1572872 | tf_op jit(solution)/shard_map/ppermute | solution.py:376
  75.5 72.9 %collective-permute-start.13 = (bf16[8,128,128]{2,1,0:T(8,128)(2,1)}, bf16[8,128,128]{2,1,0:T(8,128)(2,1)S(1)}, u32[]{:S(2)}, u32[]{:S(2)}) collective-permute-start(bf16[8,128,128]{2,1,0:T(8,128)(2,1)} %get-tuple-element.67), channel_id=1, source_target_pairs={{0,1},{1,0},{2,3},{3,2},{4,5},{5,4},{6,7},{7,6},{8,9},{9,8},{10,11... | collective-permute-start | bytes 786440 | tf_op jit(solution)/shard_map/ppermute | solution.py:379
  78.0 1.6 copy-start.2
  79.6 0.9 copy-start.4
  80.6 67.9 %copy-start.7 = (bf16[8,256,128]{2,1,0:T(8,128)(2,1)S(1)}, bf16[8,256,128]{2,1,0:T(8,128)(2,1)}, u32[]{:S(2)}) copy-start(bf16[8,256,128]{2,1,0:T(8,128)(2,1)} %copy-done.6) | copy-start | bytes 1572868
  80.6 67.9 %copy-start.9 = (bf16[8,256,128]{2,1,0:T(8,128)(2,1)S(1)}, bf16[8,256,128]{2,1,0:T(8,128)(2,1)}, u32[]{:S(2)}) copy-start(bf16[8,256,128]{2,1,0:T(8,128)(2,1)} %copy-done.8) | copy-start | bytes 1572868
  80.6 67.9 %copy-start.11 = (bf16[8,256,128]{2,1,0:T(8,128)(2,1)S(1)}, bf16[8,256,128]{2,1,0:T(8,128)(2,1)}, u32[]{:S(2)}) copy-start(bf16[8,256,128]{2,1,0:T(8,128)(2,1)} %copy-done.10) | copy-start | bytes 1572868
  148.5 1.0 copy-start.5
  148.8 1.0 copy-start.12
  148.8 4.2 %collective-permute-start.14 = (bf16[4,8,256,128]{3,2,1,0:T(8,128)(2,1)S(1)}, bf16[4,8,256,128]{3,2,1,0:T(8,128)(2,1)S(1)}, u32[]{:S(2)}, u32[]{:S(2)}) collective-permute-start(bf16[4,8,256,128]{3,2,1,0:T(8,128)(2,1)S(1)} %pad_maximum_fusion.1.refs_0_), channel_id=1, source_target_pairs={{0,8},{8,0},{16,24},{24,16},{32,40},{40,32},{48,56},{56,48},{64,72... | collective-permute-start | bytes 6291464 | tf_op jit(solution)/shard_map/ppermute | solution.py:315
  149.7 77.8 %collective-permute-start.18 = (bf16[3,8,256,128]{3,2,1,0:T(8,128)(2,1)S(1)}, bf16[3,8,256,128]{3,2,1,0:T(8,128)(2,1)S(1)}, u32[]{:S(2)}, u32[]{:S(2)}) collective-permute-start(bf16[3,8,256,128]{3,2,1,0:T(8,128)(2,1)S(1)} %pad_maximum_fusion.2.refs_0_), channel_id=1, source_target_pairs={{0,8},{8,0},{16,24},{24,16},{32,40},{40,32},{48,56},{56,48},{64,72... | collective-permute-start | bytes 4718600 | tf_op jit(solution)/shard_map/ppermute | solution.py:315
  149.8 74.6 %collective-permute-start.17 = (bf16[8,128,128]{2,1,0:T(8,128)(2,1)S(1)}, bf16[8,128,128]{2,1,0:T(8,128)(2,1)S(1)}, u32[]{:S(2)}, u32[]{:S(2)}) collective-permute-start(bf16[8,128,128]{2,1,0:T(8,128)(2,1)S(1)} %copy-done.12), channel_id=1, source_target_pairs={{0,1},{1,0},{2,3},{3,2},{4,5},{5,4},{6,7},{7,6},{8,9},{9,8},{10,11... | collective-permute-start | bytes 786440 | tf_op jit(solution)/shard_map/ppermute | solution.py:387
  149.9 74.5 %collective-permute-start.16 = (bf16[8,256,128]{2,1,0:T(8,128)(2,1)S(1)}, bf16[8,256,128]{2,1,0:T(8,128)(2,1)S(1)}, u32[]{:S(2)}, u32[]{:S(2)}) collective-permute-start(bf16[8,256,128]{2,1,0:T(8,128)(2,1)S(1)} %collective-permute-done.11), channel_id=1, source_target_pairs={{0,6},{1,7},{2,0},{3,1},{4,2},{5,3},{6,4},{7,5},{8,14},{9,15},{10,... | collective-permute-start | bytes 1572872 | tf_op jit(solution)/shard_map/ppermute | solution.py:385
  224.4 74.4 %copy-start.14 = (s32[24]{0:T(128)S(1)}, s32[24]{0:T(128)}, u32[]{:S(2)}) copy-start(s32[24]{0:T(128)} %param.10) | copy-start | bytes 292
  224.4 3.1 collective-permute-start.19
  224.5 74.4 %collective-permute-start.9 = (bf16[8,144,128]{2,1,0:T(8,128)(2,1)S(1)}, bf16[8,144,128]{2,1,0:T(8,128)(2,1)S(1)}, u32[]{:S(2)}, u32[]{:S(2)}) collective-permute-start(bf16[8,144,128]{2,1,0:T(8,128)(2,1)S(1)} %get-tuple-element.63), channel_id=1, source_target_pairs={{0,1},{1,0},{2,3},{3,2},{4,5},{5,4},{6,7},{7,6},{8,9},{9,8},{10,11... | collective-permute-start | bytes 884744 | tf_op jit(solution)/shard_map/ppermute | solution.py:372
  224.6 74.3 %collective-permute-start.15 = (bf16[8,144,128]{2,1,0:T(8,128)(2,1)S(1)}, bf16[8,144,128]{2,1,0:T(8,128)(2,1)S(1)}, u32[]{:S(2)}, u32[]{:S(2)}) collective-permute-start(bf16[8,144,128]{2,1,0:T(8,128)(2,1)S(1)} %get-tuple-element.74), channel_id=1, source_target_pairs={{0,1},{1,0},{2,3},{3,2},{4,5},{5,4},{6,7},{7,6},{8,9},{9,8},{10,11... | collective-permute-start | bytes 884744 | tf_op jit(solution)/shard_map/ppermute | solution.py:372
  298.7 7.2 %collective-permute-start.20 = (bf16[8,144,128]{2,1,0:T(8,128)(2,1)S(1)}, bf16[8,144,128]{2,1,0:T(8,128)(2,1)S(1)}, u32[]{:S(2)}, u32[]{:S(2)}) collective-permute-start(bf16[8,144,128]{2,1,0:T(8,128)(2,1)S(1)} %get-tuple-element.84), channel_id=1, source_target_pairs={{0,1},{1,0},{2,3},{3,2},{4,5},{5,4},{6,7},{7,6},{8,9},{9,8},{10,11... | collective-permute-start | bytes 884744 | tf_op jit(solution)/shard_map/ppermute | solution.py:372
  307.1 4.8 %copy-start.13 = (s32[128]{0:T(128)S(1)}, s32[128]{0:T(128)}, u32[]{:S(2)}) copy-start(s32[128]{0:T(128)} %param.9) | copy-start | bytes 1540
  307.1 13.5 %all-to-all-start.2 = ((bf16[8,384,128]{2,1,0:T(8,128)(2,1)}), bf16[8,384,128]{2,1,0:T(8,128)(2,1)}, u32[]{:S(2)}, u32[]{:S(2)}) async-start(bf16[8,384,128]{2,1,0:T(8,128)(2,1)} %shard_map.68), calls=%async_computation.2 | async-start | bytes 1572864 | tf_op jit(solution)/shard_map/all_to_all | solution.py:307

commit v14 on v11

--- a/solution.py
+++ b/solution.py
@@ -17,7 +17,6 @@
 KEYS = 8192
 WIDTH = 256
 ITEMS = 8
-FIRST_ZONES = 2
 K_NORM, Q_NORM = 32, 40
 NOTE = 16
 PLAIN_LIMIT = 70.0
@@ -37,17 +36,16 @@
 
     copies = []
     half = len(sources) // 2
-    for j, zones in enumerate((pl.ds(0, FIRST_ZONES), pl.ds(FIRST_ZONES, ZONES - FIRST_ZONES))):
-        for group, c in ((sources[:half], core), (sources[half:], 1 - core)):
-            pieces = [src.at[k] for src in group for k in range(src.shape[0])]
-            for piece, step in zip(pieces, (0, 1, 3, 2)):
-                copies.append(
-                    pltpu.make_async_copy(
-                        piece.at[zones, pl.ds(0, 2 * HEAD_DIM)],
-                        kv_ref.at[(rank + step) % 4, c, zones],
-                        sems.at[len(copies)],
-                    )
+    for group, c in ((sources[:half], core), (sources[half:], 1 - core)):
+        pieces = [src.at[k] for src in group for k in range(src.shape[0])]
+        for piece, step in zip(pieces, (0, 1, 3, 2)):
+            copies.append(
+                pltpu.make_async_copy(
+                    piece.at[:, pl.ds(0, 2 * HEAD_DIM)],
+                    kv_ref.at[(rank + step) % 4, c],
+                    sems.at[len(copies)],
                 )
+            )
     for copy in copies:
         copy.start()
 
@@ -56,7 +54,7 @@
     acc_ref[...] = jnp.zeros_like(acc_ref)
     top_ref[...] = jnp.zeros_like(top_ref)
     ones = jnp.ones((NOTE, WIDTH), jnp.bfloat16)
-    for copy in copies[: len(copies) // 2]:
+    for copy in copies:
         copy.wait()
 
     def part(i, rows):
@@ -130,8 +128,6 @@
         items = run((jnp.int32(0), jnp.int32(0)))
         for slot in range(ITEMS):
             weigh(slot, items[slot], score(items[slot]))
-        for copy in copies[len(copies) // 2 :]:
-            copy.wait()
         total = sum(count(r) for r in range(blocks))
         items = lax.fori_loop(0, (total + ITEMS - 1) // ITEMS - 1, step, items)
         for slot in range(ITEMS):
@@ -140,8 +136,6 @@
     @pl.when(jnp.logical_not(plain))
     def _():
         top_ref[...] = jnp.full_like(top_ref, LOW)
-        for copy in copies[len(copies) // 2 :]:
-            copy.wait()
 
         def over_block(r, carry):
             def over_chunk(i, carry):
@@ -188,7 +182,7 @@
                 pltpu.VMEM((ITEMS, WIDTH, SEGMENT), jnp.bfloat16),
                 pltpu.VMEM((ZONES + 1, HEAD_DIM + NOTE, SEGMENT), jnp.float32),
                 pltpu.VMEM((ZONES, 8, SEGMENT), jnp.float32),
-                pltpu.SemaphoreType.DMA((16,)),
+                pltpu.SemaphoreType.DMA((8,)),
             ],
         ),
         out_shape=[out, out],

time: 318 us -> 314 us (0.987)
  transfers between devices with their start and end apart: 23 -> 23, of which waited for: 10 -> 10; matrix products, arithmetic and copies ran while one was open for 3% -> 3% of each run, Pallas kernels for 65% -> 64%
where the time goes in v14:
time: 314 us
  Pallas kernels  209 us (67%)
  waiting for transfers between devices  39.6 us (13%)
  starting transfers between devices  33.7 us (11%)
  blocking collectives  15.4 us (5%)
  local copies, waits for them, and re-layouts  9.79 us (3%)
  other arithmetic  4.88 us (2%)
    pallas_call x3, Pallas kernels, attend(): pl.pallas_call(functools.partial(attend_kernel, head), grid_spec=pltpu.Pr...  202 us
    all_to_all x1, blocking collectives, exchange(): lax.all_to_all(parts, BOTH, split_axis=0, concat_axis=0, axis_index_group...  15.4 us
    all_to_all x2, waiting for transfers between devices, exchange(): lax.all_to_all(parts, BOTH, split_axis=0, concat_axis=0, axis_index_group...  10.5 us
    ppermute x6, waiting for transfers between devices, sides(): return (lax.ppermute(block, 'head', down), lax.ppermute(block, 'head', up))  9.69 us
    ppermute x6, starting transfers between devices, sides(): return (lax.ppermute(block, 'head', down), lax.ppermute(block, 'head', up))  8.03 us
    all_to_all x2, starting transfers between devices, exchange(): lax.all_to_all(parts, BOTH, split_axis=0, concat_axis=0, axis_index_group...  7.95 us
    ppermute x3, waiting for transfers between devices, attended(): parts[2 * head + 1] = lax.ppermute(theirs, 'head', partner)  7.01 us
  transfers between devices with their start and end apart: 23, of which 10 were waited for; matrix products, arithmetic and copies ran while one was open for 3% of the time, Pallas kernels for 64%

profile of v14, /device:TPU:25, one launch (start us, length us, event | category | flops | bytes accessed | tf_op | source)
XLA Modules:
  0.0 314.0 jit_solution(12477773660910172313)
XLA Ops:
  0.0 4.0 %shard_map.64 = (bf16[8,272,128]{2,1,0:T(8,128)(2,1)}, bf16[8,896,128]{2,1,0:T(8,128)(2,1)}) custom-call(bf16[128,3072]{1,0:T(8,128)(2,1)} %queries_ref.1, bf16[128,3072]{1,0:T(8,128)(2,1)} %keys_ref.1, bf16[128,3072]{1,0:T(8,128)(2,1)} %values_ref.1, s32[1,128]{1,0:T(1,128)} %bitcast.55), custom_call_target="tpu_custom_call" | custom-call | tf_op jit(solution)/shard_map/pallas_call | solution.py:310
  4.0 15.4 %all_to_all.15 = bf16[8,272,128]{2,1,0:T(8,128)(2,1)} all-to-all(bf16[8,272,128]{2,1,0:T(8,128)(2,1)} %get-tuple-element.46), channel_id=1, replica_groups={{0,16,32,48,64,80,96,112},{1,17,33,49,65,81,97,113},{2,18,34,50,66,82,9..., dimensions={0} | all-to-all | bytes 1114112 | tf_op jit(solution)/shard_map/all_to_all | solution.py:296
  19.4 0.5 collective-permute-start
  19.8 2.2 collective-permute-start.1
  22.0 3.6 %all-to-all-start.1 = ((bf16[8,896,128]{2,1,0:T(8,128)(2,1)}), bf16[8,896,128]{2,1,0:T(8,128)(2,1)S(1)}, u32[]{:S(2)}, u32[]{:S(2)}) async-start(bf16[8,896,128]{2,1,0:T(8,128)(2,1)} %get-tuple-element.47), calls=%async_computation.1 | async-start | bytes 3670016 | tf_op jit(solution)/shard_map/all_to_all | solution.py:296
  25.6 7.1 %collective-permute-done = bf16[8,272,128]{2,1,0:T(8,128)(2,1)} collective-permute-done((bf16[8,272,128]{2,1,0:T(8,128)(2,1)}, bf16[8,272,128]{2,1,0:T(8,128)(2,1)}, u32[]{:S(2)}, u32[]{:S(2)}) %collective-permute-start) | collective-permute-done | bytes 557088 | tf_op jit(solution)/shard_map/ppermute | solution.py:307
  32.8 1.0 slice.49
  33.7 0.1 collective-permute-start.3
  33.8 1.0 slice.48
  34.8 2.7 collective-permute-start.2
  37.5 3.2 %collective-permute-done.3 = bf16[4,272,128]{2,1,0:T(8,128)(2,1)S(1)} collective-permute-done((bf16[4,272,128]{2,1,0:T(8,128)(2,1)S(1)}, bf16[4,272,128]{2,1,0:T(8,128)(2,1)S(1)}, u32[]{:S(2)}, u32[]{:S(2)}) %collective-permute-start.3) | collective-permute-done | bytes 278560 | tf_op jit(solution)/shard_map/ppermute | solution.py:318
  40.7 0.3 collective-permute-done.2
  41.1 1.7 pad_maximum_fusion.refs_0_
  42.8 0.1 slice_reduce_fusion.1
  42.9 1.3 copy-done.1
  44.2 2.8 all-to-all-done.1.own_q
  46.9 3.7 %collective-permute-start.4 = (bf16[4,8,272,128]{3,2,1,0:T(8,128)(2,1)}, bf16[4,8,272,128]{3,2,1,0:T(8,128)(2,1)}, u32[]{:S(2)}, u32[]{:S(2)}) collective-permute-start(bf16[4,8,272,128]{3,2,1,0:T(8,128)(2,1)} %copy-done.1), channel_id=1, source_target_pairs={{0,8},{8,0},{16,24},{24,16},{32,40},{40,32},{48,56},{56,48},{64,72... | collective-permute-start | bytes 6684680 | tf_op jit(solution)/shard_map/ppermute | solution.py:304
  50.7 0.1 add_multiply_fusion
  50.7 0.1 broadcast_add_fusion
  50.8 0.9 fusion.19
  51.7 0.9 fusion.18
  52.6 2.7 collective-permute-start.6
  55.2 2.5 collective-permute-start.7
  57.7 0.9 convert_reduce_fusion
  58.6 0.9 slice_reduce_fusion
  59.5 4.6 %collective-permute-done.7.their_q = bf16[8,128,128]{2,1,0:T(8,128)(2,1)S(1)} collective-permute-done((bf16[8,128,128]{2,1,0:T(8,128)(2,1)S(1)}, bf16[8,128,128]{2,1,0:T(8,128)(2,1)S(1)}, u32[]{:S(2)}, u32[]{:S(2)}) %collective-permute-start.7) | collective-permute-done | bytes 262176 | tf_op jit(solution)/shard_map/ppermute | solution.py:333
  64.1 0.7 copy-done.3
  64.8 2.6 collective-permute-done.5
  67.3 0.8 copy-done.8
  68.1 2.5 collective-permute-start.8
  70.6 0.1 fusion.12
  70.7 1.4 collective-permute-done.8
  72.0 0.1 compare_convert_fusion
  72.1 0.1 select_reduce_fusion
  72.2 0.1 fusion.15
  72.4 0.1 pad_add_fusion.info_ref
  72.5 2.7 collective-permute-start.12
  75.2 0.3 collective-permute-start.10
  75.5 2.5 collective-permute-start.13
  78.0 1.6 copy-done.2
  79.6 0.9 copy-done.4
  80.6 67.9 %shard_map.65 = (bf16[8,144,128]{2,1,0:T(8,128)(2,1)S(1)}, bf16[8,144,128]{2,1,0:T(8,128)(2,1)S(1)}) custom-call(s32[13]{0:T(128)S(1)} %pad_add_fusion.info_ref, bf16[8,896,128]{2,1,0:T(8,128)(2,1)S(1)} %all-to-all-done.1.own_q, bf16[8,128,128]{2,1,0:T(8,128)(2,1)S(1)} %copy-done.4, s32[8,1,256]{2,1,0:T(1,128)S(1)} %fusion.13.end_ref, ...), custom_call_target="tpu_custom_call" | custom-call | flops 8589934592 | bytes 5242880 | tf_op jit(solution)/shard_map/pallas_call | solution.py:171
  148.6 0.3 pad_maximum_fusion.1.refs_0_
  148.9 0.1 collective-permute-start.14
  149.0 0.7 copy-done.5
  149.6 0.2 pad_maximum_fusion.2.refs_0_
  149.8 0.1 collective-permute-start.18
  149.9 0.1 collective-permute-start.17
  150.0 0.1 collective-permute-start.16
  150.1 3.0 collective-permute-done.14.refs_1_
  153.1 66.9 %shard_map.66 = (bf16[8,144,128]{2,1,0:T(8,128)(2,1)S(1)}, bf16[8,144,128]{2,1,0:T(8,128)(2,1)S(1)}) custom-call(s32[13]{0:T(128)S(1)} %pad_add_fusion.info_ref, bf16[8,896,128]{2,1,0:T(8,128)(2,1)S(1)} %all-to-all-done.1.own_q, bf16[8,128,128]{2,1,0:T(8,128)(2,1)S(1)} %collective-permute-done.13.their_q, s32[8,1,256]{2,1,0:T(1,128)S(1)} %fusion.13.end_ref, ...), custom_call_target="tpu_custom_call" | custom-call | flops 8589934592 | bytes 5242880 | tf_op jit(solution)/shard_map/pallas_call | solution.py:171
  220.1 0.1 collective-permute-start.19
  220.2 0.1 collective-permute-start.9
  220.3 3.0 collective-permute-start.15
  223.2 66.7 %shard_map.67 = (bf16[8,144,128]{2,1,0:T(8,128)(2,1)S(1)}, bf16[8,144,128]{2,1,0:T(8,128)(2,1)S(1)}) custom-call(s32[13]{0:T(128)S(1)} %pad_add_fusion.info_ref, bf16[8,896,128]{2,1,0:T(8,128)(2,1)S(1)} %all-to-all-done.1.own_q, bf16[8,128,128]{2,1,0:T(8,128)(2,1)S(1)} %collective-permute-done.17.their_q, s32[8,1,256]{2,1,0:T(1,128)S(1)} %fusion.13.end_ref, ...), custom_call_target="tpu_custom_call" | custom-call | flops 8589934592 | bytes 5242880 | tf_op jit(solution)/shard_map/pallas_call | solution.py:171
  290.0 0.1 collective-permute-start.20
  290.1 7.0 %collective-permute-done.20.refs_5_ = bf16[8,144,128]{2,1,0:T(8,128)(2,1)S(1)} collective-permute-done((bf16[8,144,128]{2,1,0:T(8,128)(2,1)S(1)}, bf16[8,144,128]{2,1,0:T(8,128)(2,1)S(1)}, u32[]{:S(2)}, u32[]{:S(2)}) %collective-permute-start.20) | collective-permute-done | bytes 294944 | tf_op jit(solution)/shard_map/ppermute | solution.py:361
  297.1 1.3 shard_map.68
  298.4 4.4 %all-to-all-start.2 = ((bf16[8,384,128]{2,1,0:T(8,128)(2,1)}), bf16[8,384,128]{2,1,0:T(8,128)(2,1)}, u32[]{:S(2)}, u32[]{:S(2)}) async-start(bf16[8,384,128]{2,1,0:T(8,128)(2,1)} %shard_map.68), calls=%async_computation.2 | async-start | bytes 1572864 | tf_op jit(solution)/shard_map/all_to_all | solution.py:296
  302.7 0.1 fusion.2
  302.9 0.3 fusion.4
  303.2 0.8 fusion.gate_ref
  304.0 7.7 %all-to-all-done.2.mixed_ref = bf16[8,384,128]{2,1,0:T(8,128)(2,1)} async-done(((bf16[8,384,128]{2,1,0:T(8,128)(2,1)}), bf16[8,384,128]{2,1,0:T(8,128)(2,1)}, u32[]{:S(2)}, u32[]{:S(2)}) %all-to-all-start.2) | async-done | bytes 786464 | tf_op jit(solution)/shard_map/all_to_all | solution.py:296
  311.7 2.3 shard_map.69
  (53 shorter events, 0.3 us)
Async XLA Ops:
  0.0 302.9 %copy-start = (bf16[256,3072]{1,0:T(8,128)(2,1)S(1)}, bf16[256,3072]{1,0:T(8,128)(2,1)}, u32[]{:S(2)}) copy-start(bf16[256,3072]{1,0:T(8,128)(2,1)} %param.11) | copy-start | bytes 4718596
  19.4 13.4 %collective-permute-start = (bf16[8,272,128]{2,1,0:T(8,128)(2,1)}, bf16[8,272,128]{2,1,0:T(8,128)(2,1)}, u32[]{:S(2)}, u32[]{:S(2)}) collective-permute-start(bf16[8,272,128]{2,1,0:T(8,128)(2,1)} %all_to_all.15), channel_id=1, source_target_pairs={{0,6},{1,7},{2,0},{3,1},{4,2},{5,3},{6,4},{7,5},{8,14},{9,15},{10,... | collective-permute-start | bytes 1671176 | tf_op jit(solution)/shard_map/ppermute | solution.py:307
  19.8 14.0 %collective-permute-start.1 = (bf16[8,272,128]{2,1,0:T(8,128)(2,1)}, bf16[8,272,128]{2,1,0:T(8,128)(2,1)}, u32[]{:S(2)}, u32[]{:S(2)}) collective-permute-start(bf16[8,272,128]{2,1,0:T(8,128)(2,1)} %all_to_all.15), channel_id=1, source_target_pairs={{0,2},{1,3},{2,4},{3,5},{4,6},{5,7},{6,0},{7,1},{8,10},{9,11},{10,... | collective-permute-start | bytes 1671176 | tf_op jit(solution)/shard_map/ppermute | solution.py:307
  22.0 24.9 %all-to-all-start.1 = ((bf16[8,896,128]{2,1,0:T(8,128)(2,1)}), bf16[8,896,128]{2,1,0:T(8,128)(2,1)S(1)}, u32[]{:S(2)}, u32[]{:S(2)}) async-start(bf16[8,896,128]{2,1,0:T(8,128)(2,1)} %get-tuple-element.47), calls=%async_computation.1 | async-start | bytes 3670016 | tf_op jit(solution)/shard_map/all_to_all | solution.py:296
  33.7 7.0 %collective-permute-start.3 = (bf16[4,272,128]{2,1,0:T(8,128)(2,1)S(1)}, bf16[4,272,128]{2,1,0:T(8,128)(2,1)S(1)}, u32[]{:S(2)}, u32[]{:S(2)}) collective-permute-start(bf16[4,272,128]{2,1,0:T(8,128)(2,1)S(1)} %slice.49), channel_id=1, source_target_pairs={{0,6},{1,7},{2,0},{3,1},{4,2},{5,3},{6,4},{7,5},{8,14},{9,15},{10,... | collective-permute-start | bytes 835592 | tf_op jit(solution)/shard_map/ppermute | solution.py:318
  34.8 6.2 %collective-permute-start.2 = (bf16[4,272,128]{2,1,0:T(8,128)(2,1)S(1)}, bf16[4,272,128]{2,1,0:T(8,128)(2,1)S(1)}, u32[]{:S(2)}, u32[]{:S(2)}) collective-permute-start(bf16[4,272,128]{2,1,0:T(8,128)(2,1)S(1)} %slice.48), channel_id=1, source_target_pairs={{0,2},{1,3},{2,4},{3,5},{4,6},{5,7},{6,0},{7,1},{8,10},{9,11},{10,... | collective-permute-start | bytes 835592 | tf_op jit(solution)/shard_map/ppermute | solution.py:318
  42.8 1.4 copy-start.1
  46.9 10.8 %collective-permute-start.4 = (bf16[4,8,272,128]{3,2,1,0:T(8,128)(2,1)}, bf16[4,8,272,128]{3,2,1,0:T(8,128)(2,1)}, u32[]{:S(2)}, u32[]{:S(2)}) collective-permute-start(bf16[4,8,272,128]{3,2,1,0:T(8,128)(2,1)} %copy-done.1), channel_id=1, source_target_pairs={{0,8},{8,0},{16,24},{24,16},{32,40},{40,32},{48,56},{56,48},{64,72... | collective-permute-start | bytes 6684680 | tf_op jit(solution)/shard_map/ppermute | solution.py:304
  52.6 11.5 %copy-start.6 = (bf16[8,256,128]{2,1,0:T(8,128)(2,1)}, bf16[8,256,128]{2,1,0:T(8,128)(2,1)S(1)}, u32[]{:S(2)}) copy-start(bf16[8,256,128]{2,1,0:T(8,128)(2,1)S(1)} %get-tuple-element.52) | copy-start | bytes 1572868
  52.6 14.8 %collective-permute-start.5 = (bf16[8,256,128]{2,1,0:T(8,128)(2,1)S(1)}, bf16[8,256,128]{2,1,0:T(8,128)(2,1)S(1)}, u32[]{:S(2)}, u32[]{:S(2)}) collective-permute-start(bf16[8,256,128]{2,1,0:T(8,128)(2,1)S(1)} %get-tuple-element.52), channel_id=1, source_target_pairs={{0,6},{1,7},{2,0},{3,1},{4,2},{5,3},{6,4},{7,5},{8,14},{9,15},{10,... | collective-permute-start | bytes 1572872 | tf_op jit(solution)/shard_map/ppermute | solution.py:307
  52.6 14.8 %collective-permute-start.6 = (bf16[8,256,128]{2,1,0:T(8,128)(2,1)S(1)}, bf16[8,256,128]{2,1,0:T(8,128)(2,1)S(1)}, u32[]{:S(2)}, u32[]{:S(2)}) collective-permute-start(bf16[8,256,128]{2,1,0:T(8,128)(2,1)S(1)} %get-tuple-element.52), channel_id=1, source_target_pairs={{0,2},{1,3},{2,4},{3,5},{4,6},{5,7},{6,0},{7,1},{8,10},{9,11},{10,... | collective-permute-start | bytes 1572872 | tf_op jit(solution)/shard_map/ppermute | solution.py:307
  55.2 8.8 %collective-permute-start.7 = (bf16[8,128,128]{2,1,0:T(8,128)(2,1)S(1)}, bf16[8,128,128]{2,1,0:T(8,128)(2,1)S(1)}, u32[]{:S(2)}, u32[]{:S(2)}) collective-permute-start(bf16[8,128,128]{2,1,0:T(8,128)(2,1)S(1)} %get-tuple-element.53), channel_id=1, source_target_pairs={{0,1},{1,0},{2,3},{3,2},{4,5},{5,4},{6,7},{7,6},{8,9},{9,8},{10,11... | collective-permute-start | bytes 786440 | tf_op jit(solution)/shard_map/ppermute | solution.py:333
  64.0 0.7 copy-start.3
  67.3 0.8 copy-start.8
  68.1 2.5 copy-start.10
  68.1 3.9 %collective-permute-start.8 = (f32[1,128]{1,0:T(1,128)S(1)}, f32[1,128]{1,0:T(1,128)S(1)}, u32[]{:S(2)}, u32[]{:S(2)}) collective-permute-start(f32[1,128]{1,0:T(1,128)S(1)} %select_bitcast_fusion), channel_id=1, source_target_pairs={{0,1},{1,0},{2,3},{3,2},{4,5},{5,4},{6,7},{7,6},{8,9},{9,8},{10,11... | collective-permute-start | bytes 1544 | tf_op jit(solution)/shard_map/ppermute | solution.py:337
  72.5 76.0 %collective-permute-start.11 = (bf16[8,256,128]{2,1,0:T(8,128)(2,1)}, bf16[8,256,128]{2,1,0:T(8,128)(2,1)S(1)}, u32[]{:S(2)}, u32[]{:S(2)}) collective-permute-start(bf16[8,256,128]{2,1,0:T(8,128)(2,1)} %get-tuple-element.66), channel_id=1, source_target_pairs={{0,6},{1,7},{2,0},{3,1},{4,2},{5,3},{6,4},{7,5},{8,14},{9,15},{10,... | collective-permute-start | bytes 1572872 | tf_op jit(solution)/shard_map/ppermute | solution.py:307
  72.5 76.0 %collective-permute-start.12 = (bf16[8,256,128]{2,1,0:T(8,128)(2,1)}, bf16[8,256,128]{2,1,0:T(8,128)(2,1)S(1)}, u32[]{:S(2)}, u32[]{:S(2)}) collective-permute-start(bf16[8,256,128]{2,1,0:T(8,128)(2,1)} %get-tuple-element.66), channel_id=1, source_target_pairs={{0,2},{1,3},{2,4},{3,5},{4,6},{5,7},{6,0},{7,1},{8,10},{9,11},{10,... | collective-permute-start | bytes 1572872 | tf_op jit(solution)/shard_map/ppermute | solution.py:307
  75.2 73.3 %collective-permute-start.10 = (bf16[8,256,128]{2,1,0:T(8,128)(2,1)}, bf16[8,256,128]{2,1,0:T(8,128)(2,1)S(1)}, u32[]{:S(2)}, u32[]{:S(2)}) collective-permute-start(bf16[8,256,128]{2,1,0:T(8,128)(2,1)} %copy-done.10), channel_id=1, source_target_pairs={{0,2},{1,3},{2,4},{3,5},{4,6},{5,7},{6,0},{7,1},{8,10},{9,11},{10,... | collective-permute-start | bytes 1572872 | tf_op jit(solution)/shard_map/ppermute | solution.py:365
  75.5 73.0 %collective-permute-start.13 = (bf16[8,128,128]{2,1,0:T(8,128)(2,1)}, bf16[8,128,128]{2,1,0:T(8,128)(2,1)S(1)}, u32[]{:S(2)}, u32[]{:S(2)}) collective-permute-start(bf16[8,128,128]{2,1,0:T(8,128)(2,1)} %get-tuple-element.67), channel_id=1, source_target_pairs={{0,1},{1,0},{2,3},{3,2},{4,5},{5,4},{6,7},{7,6},{8,9},{9,8},{10,11... | collective-permute-start | bytes 786440 | tf_op jit(solution)/shard_map/ppermute | solution.py:368
  78.0 1.6 copy-start.2
  79.6 0.9 copy-start.4
  80.6 68.0 %copy-start.7 = (bf16[8,256,128]{2,1,0:T(8,128)(2,1)S(1)}, bf16[8,256,128]{2,1,0:T(8,128)(2,1)}, u32[]{:S(2)}) copy-start(bf16[8,256,128]{2,1,0:T(8,128)(2,1)} %copy-done.6) | copy-start | bytes 1572868
  80.6 68.0 %copy-start.9 = (bf16[8,256,128]{2,1,0:T(8,128)(2,1)S(1)}, bf16[8,256,128]{2,1,0:T(8,128)(2,1)}, u32[]{:S(2)}) copy-start(bf16[8,256,128]{2,1,0:T(8,128)(2,1)} %copy-done.8) | copy-start | bytes 1572868
  80.6 68.0 %copy-start.11 = (bf16[8,256,128]{2,1,0:T(8,128)(2,1)S(1)}, bf16[8,256,128]{2,1,0:T(8,128)(2,1)}, u32[]{:S(2)}) copy-start(bf16[8,256,128]{2,1,0:T(8,128)(2,1)} %copy-done.10) | copy-start | bytes 1572868
  148.6 1.0 copy-start.5
  148.9 1.0 copy-start.12
  148.9 4.2 %collective-permute-start.14 = (bf16[4,8,256,128]{3,2,1,0:T(8,128)(2,1)S(1)}, bf16[4,8,256,128]{3,2,1,0:T(8,128)(2,1)S(1)}, u32[]{:S(2)}, u32[]{:S(2)}) collective-permute-start(bf16[4,8,256,128]{3,2,1,0:T(8,128)(2,1)S(1)} %pad_maximum_fusion.1.refs_0_), channel_id=1, source_target_pairs={{0,8},{8,0},{16,24},{24,16},{32,40},{40,32},{48,56},{56,48},{64,72... | collective-permute-start | bytes 6291464 | tf_op jit(solution)/shard_map/ppermute | solution.py:304
  149.8 73.4 %collective-permute-start.18 = (bf16[3,8,256,128]{3,2,1,0:T(8,128)(2,1)S(1)}, bf16[3,8,256,128]{3,2,1,0:T(8,128)(2,1)S(1)}, u32[]{:S(2)}, u32[]{:S(2)}) collective-permute-start(bf16[3,8,256,128]{3,2,1,0:T(8,128)(2,1)S(1)} %pad_maximum_fusion.2.refs_0_), channel_id=1, source_target_pairs={{0,8},{8,0},{16,24},{24,16},{32,40},{40,32},{48,56},{56,48},{64,72... | collective-permute-start | bytes 4718600 | tf_op jit(solution)/shard_map/ppermute | solution.py:304
  149.9 70.1 %collective-permute-start.17 = (bf16[8,128,128]{2,1,0:T(8,128)(2,1)S(1)}, bf16[8,128,128]{2,1,0:T(8,128)(2,1)S(1)}, u32[]{:S(2)}, u32[]{:S(2)}) collective-permute-start(bf16[8,128,128]{2,1,0:T(8,128)(2,1)S(1)} %copy-done.12), channel_id=1, source_target_pairs={{0,1},{1,0},{2,3},{3,2},{4,5},{5,4},{6,7},{7,6},{8,9},{9,8},{10,11... | collective-permute-start | bytes 786440 | tf_op jit(solution)/shard_map/ppermute | solution.py:376
  150.0 70.0 %collective-permute-start.16 = (bf16[8,256,128]{2,1,0:T(8,128)(2,1)S(1)}, bf16[8,256,128]{2,1,0:T(8,128)(2,1)S(1)}, u32[]{:S(2)}, u32[]{:S(2)}) collective-permute-start(bf16[8,256,128]{2,1,0:T(8,128)(2,1)S(1)} %collective-permute-done.11), channel_id=1, source_target_pairs={{0,6},{1,7},{2,0},{3,1},{4,2},{5,3},{6,4},{7,5},{8,14},{9,15},{10,... | collective-permute-start | bytes 1572872 | tf_op jit(solution)/shard_map/ppermute | solution.py:374
  220.1 70.0 %copy-start.14 = (s32[24]{0:T(128)S(1)}, s32[24]{0:T(128)}, u32[]{:S(2)}) copy-start(s32[24]{0:T(128)} %param.10) | copy-start | bytes 292
  220.1 3.1 %collective-permute-start.19 = (bf16[1,8,256,128]{3,2,1,0:T(8,128)(2,1)S(1)}, bf16[1,8,256,128]{3,2,1,0:T(8,128)(2,1)S(1)}, u32[]{:S(2)}, u32[]{:S(2)}) collective-permute-start(bf16[1,8,256,128]{3,2,1,0:T(8,128)(2,1)S(1)} %bitcast.46), channel_id=1, source_target_pairs={{0,8},{8,0},{16,24},{24,16},{32,40},{40,32},{48,56},{56,48},{64,72... | collective-permute-start | bytes 1572872 | tf_op jit(solution)/shard_map/ppermute | solution.py:304
  220.2 69.9 %collective-permute-start.9 = (bf16[8,144,128]{2,1,0:T(8,128)(2,1)S(1)}, bf16[8,144,128]{2,1,0:T(8,128)(2,1)S(1)}, u32[]{:S(2)}, u32[]{:S(2)}) collective-permute-start(bf16[8,144,128]{2,1,0:T(8,128)(2,1)S(1)} %get-tuple-element.63), channel_id=1, source_target_pairs={{0,1},{1,0},{2,3},{3,2},{4,5},{5,4},{6,7},{7,6},{8,9},{9,8},{10,11... | collective-permute-start | bytes 884744 | tf_op jit(solution)/shard_map/ppermute | solution.py:361
  220.3 69.8 %collective-permute-start.15 = (bf16[8,144,128]{2,1,0:T(8,128)(2,1)S(1)}, bf16[8,144,128]{2,1,0:T(8,128)(2,1)S(1)}, u32[]{:S(2)}, u32[]{:S(2)}) collective-permute-start(bf16[8,144,128]{2,1,0:T(8,128)(2,1)S(1)} %get-tuple-element.74), channel_id=1, source_target_pairs={{0,1},{1,0},{2,3},{3,2},{4,5},{5,4},{6,7},{7,6},{8,9},{9,8},{10,11... | collective-permute-start | bytes 884744 | tf_op jit(solution)/shard_map/ppermute | solution.py:361
  290.0 7.2 %collective-permute-start.20 = (bf16[8,144,128]{2,1,0:T(8,128)(2,1)S(1)}, bf16[8,144,128]{2,1,0:T(8,128)(2,1)S(1)}, u32[]{:S(2)}, u32[]{:S(2)}) collective-permute-start(bf16[8,144,128]{2,1,0:T(8,128)(2,1)S(1)} %get-tuple-element.84), channel_id=1, source_target_pairs={{0,1},{1,0},{2,3},{3,2},{4,5},{5,4},{6,7},{7,6},{8,9},{9,8},{10,11... | collective-permute-start | bytes 884744 | tf_op jit(solution)/shard_map/ppermute | solution.py:361
  298.4 4.8 %copy-start.13 = (s32[128]{0:T(128)S(1)}, s32[128]{0:T(128)}, u32[]{:S(2)}) copy-start(s32[128]{0:T(128)} %param.9) | copy-start | bytes 1540
  298.4 13.4 %all-to-all-start.2 = ((bf16[8,384,128]{2,1,0:T(8,128)(2,1)}), bf16[8,384,128]{2,1,0:T(8,128)(2,1)}, u32[]{:S(2)}, u32[]{:S(2)}) async-start(bf16[8,384,128]{2,1,0:T(8,128)(2,1)} %shard_map.68), calls=%async_computation.2 | async-start | bytes 1572864 | tf_op jit(solution)/shard_map/all_to_all | solution.py:296

commit v15 on v14

--- a/solution.py
+++ b/solution.py
@@ -16,7 +16,7 @@
 SEGMENT = 2 * HEAD_DIM
 KEYS = 8192
 WIDTH = 256
-ITEMS = 8
+ITEMS = 12
 K_NORM, Q_NORM = 32, 40
 NOTE = 16
 PLAIN_LIMIT = 70.0

time: 314 us -> 310 us (0.987)
  Pallas kernels: 209 us -> 202 us
    pallas_call x3, Pallas kernels: 202 us -> 194 us  [attend(): pl.pallas_call(functools.partial(attend_kernel, head), grid_spec=pltpu.Pr...]
  transfers between devices with their start and end apart: 23 -> 23, of which waited for: 10 -> 10; matrix products, arithmetic and copies ran while one was open for 3% -> 3% of each run, Pallas kernels for 64% -> 63%
where the time goes in v15:
time: 310 us; the launch traced here: 308 us
  Pallas kernels  202 us (65%)
  waiting for transfers between devices  41.2 us (13%)
  starting transfers between devices  34.1 us (11%)
  blocking collectives  15.4 us (5%)
  local copies, waits for them, and re-layouts  9.79 us (3%)
  other arithmetic  4.88 us (2%)
    pallas_call x3, Pallas kernels, attend(): pl.pallas_call(functools.partial(attend_kernel, head), grid_spec=pltpu.Pr...  194 us
    all_to_all x1, blocking collectives, exchange(): lax.all_to_all(parts, BOTH, split_axis=0, concat_axis=0, axis_index_group...  15.4 us
    all_to_all x2, waiting for transfers between devices, exchange(): lax.all_to_all(parts, BOTH, split_axis=0, concat_axis=0, axis_index_group...  12.3 us
    ppermute x6, waiting for transfers between devices, sides(): return (lax.ppermute(block, 'head', down), lax.ppermute(block, 'head', up))  9.69 us
    ppermute x6, starting transfers between devices, sides(): return (lax.ppermute(block, 'head', down), lax.ppermute(block, 'head', up))  8.03 us
    all_to_all x2, starting transfers between devices, exchange(): lax.all_to_all(parts, BOTH, split_axis=0, concat_axis=0, axis_index_group...  7.95 us
    ppermute x3, waiting for transfers between devices, attended(): parts[2 * head + 1] = lax.ppermute(theirs, 'head', partner)  7.01 us
  transfers between devices with their start and end apart: 23, of which 10 were waited for; matrix products, arithmetic and copies ran while one was open for 3% of the time, Pallas kernels for 63%

profile of v15, /device:TPU:25, one launch (start us, length us, event | category | flops | bytes accessed | tf_op | source)
XLA Modules:
  0.0 308.3 jit_solution(12765253529012994639)
XLA Ops:
  0.0 4.0 %shard_map.64 = (bf16[8,272,128]{2,1,0:T(8,128)(2,1)}, bf16[8,896,128]{2,1,0:T(8,128)(2,1)}) custom-call(bf16[128,3072]{1,0:T(8,128)(2,1)} %queries_ref.1, bf16[128,3072]{1,0:T(8,128)(2,1)} %keys_ref.1, bf16[128,3072]{1,0:T(8,128)(2,1)} %values_ref.1, s32[1,128]{1,0:T(1,128)} %bitcast.55), custom_call_target="tpu_custom_call" | custom-call | tf_op jit(solution)/shard_map/pallas_call | solution.py:310
  4.0 15.4 %all_to_all.15 = bf16[8,272,128]{2,1,0:T(8,128)(2,1)} all-to-all(bf16[8,272,128]{2,1,0:T(8,128)(2,1)} %get-tuple-element.46), channel_id=1, replica_groups={{0,16,32,48,64,80,96,112},{1,17,33,49,65,81,97,113},{2,18,34,50,66,82,9..., dimensions={0} | all-to-all | bytes 1114112 | tf_op jit(solution)/shard_map/all_to_all | solution.py:296
  19.4 0.5 collective-permute-start
  19.8 2.2 collective-permute-start.1
  22.0 3.6 %all-to-all-start.1 = ((bf16[8,896,128]{2,1,0:T(8,128)(2,1)}), bf16[8,896,128]{2,1,0:T(8,128)(2,1)S(1)}, u32[]{:S(2)}, u32[]{:S(2)}) async-start(bf16[8,896,128]{2,1,0:T(8,128)(2,1)} %get-tuple-element.47), calls=%async_computation.1 | async-start | bytes 3670016 | tf_op jit(solution)/shard_map/all_to_all | solution.py:296
  25.6 7.1 %collective-permute-done = bf16[8,272,128]{2,1,0:T(8,128)(2,1)} collective-permute-done((bf16[8,272,128]{2,1,0:T(8,128)(2,1)}, bf16[8,272,128]{2,1,0:T(8,128)(2,1)}, u32[]{:S(2)}, u32[]{:S(2)}) %collective-permute-start) | collective-permute-done | bytes 557088 | tf_op jit(solution)/shard_map/ppermute | solution.py:307
  32.8 1.0 slice.49
  33.7 0.1 collective-permute-start.3
  33.8 1.0 slice.48
  34.8 2.7 collective-permute-start.2
  37.5 3.2 %collective-permute-done.3 = bf16[4,272,128]{2,1,0:T(8,128)(2,1)S(1)} collective-permute-done((bf16[4,272,128]{2,1,0:T(8,128)(2,1)S(1)}, bf16[4,272,128]{2,1,0:T(8,128)(2,1)S(1)}, u32[]{:S(2)}, u32[]{:S(2)}) %collective-permute-start.3) | collective-permute-done | bytes 278560 | tf_op jit(solution)/shard_map/ppermute | solution.py:318
  40.7 0.3 collective-permute-done.2
  41.1 1.7 pad_maximum_fusion.refs_0_
  42.8 0.1 slice_reduce_fusion.1
  42.9 1.3 copy-done.1
  44.2 2.8 all-to-all-done.1.own_q
  46.9 3.7 %collective-permute-start.4 = (bf16[4,8,272,128]{3,2,1,0:T(8,128)(2,1)}, bf16[4,8,272,128]{3,2,1,0:T(8,128)(2,1)}, u32[]{:S(2)}, u32[]{:S(2)}) collective-permute-start(bf16[4,8,272,128]{3,2,1,0:T(8,128)(2,1)} %copy-done.1), channel_id=1, source_target_pairs={{0,8},{8,0},{16,24},{24,16},{32,40},{40,32},{48,56},{56,48},{64,72... | collective-permute-start | bytes 6684680 | tf_op jit(solution)/shard_map/ppermute | solution.py:304
  50.7 0.1 add_multiply_fusion
  50.7 0.1 broadcast_add_fusion
  50.8 0.9 fusion.19
  51.7 0.9 fusion.18
  52.6 2.7 collective-permute-start.6
  55.2 2.5 collective-permute-start.7
  57.7 0.9 convert_reduce_fusion
  58.6 0.9 slice_reduce_fusion
  59.5 4.6 %collective-permute-done.7.their_q = bf16[8,128,128]{2,1,0:T(8,128)(2,1)S(1)} collective-permute-done((bf16[8,128,128]{2,1,0:T(8,128)(2,1)S(1)}, bf16[8,128,128]{2,1,0:T(8,128)(2,1)S(1)}, u32[]{:S(2)}, u32[]{:S(2)}) %collective-permute-start.7) | collective-permute-done | bytes 262176 | tf_op jit(solution)/shard_map/ppermute | solution.py:333
  64.1 0.7 copy-done.3
  64.8 2.6 collective-permute-done.5
  67.3 0.8 copy-done.8
  68.1 2.5 collective-permute-start.8
  70.6 0.1 fusion.12
  70.7 1.4 collective-permute-done.8
  72.0 0.1 compare_convert_fusion
  72.1 0.1 select_reduce_fusion
  72.2 0.1 fusion.15
  72.4 0.1 pad_add_fusion.info_ref
  72.5 2.7 collective-permute-start.12
  75.2 0.3 collective-permute-start.10
  75.5 2.5 collective-permute-start.13
  78.0 1.6 copy-done.2
  79.6 0.9 copy-done.4
  80.6 65.4 %shard_map.65 = (bf16[8,144,128]{2,1,0:T(8,128)(2,1)S(1)}, bf16[8,144,128]{2,1,0:T(8,128)(2,1)S(1)}) custom-call(s32[13]{0:T(128)S(1)} %pad_add_fusion.info_ref, bf16[8,896,128]{2,1,0:T(8,128)(2,1)S(1)} %all-to-all-done.1.own_q, bf16[8,128,128]{2,1,0:T(8,128)(2,1)S(1)} %copy-done.4, s32[8,1,256]{2,1,0:T(1,128)S(1)} %fusion.13.end_ref, ...), custom_call_target="tpu_custom_call" | custom-call | flops 8589934592 | bytes 5242880 | tf_op jit(solution)/shard_map/pallas_call | solution.py:171
  146.1 0.3 pad_maximum_fusion.1.refs_0_
  146.4 0.1 collective-permute-start.14
  146.5 0.7 copy-done.5
  147.1 0.2 pad_maximum_fusion.2.refs_0_
  147.3 0.1 collective-permute-start.18
  147.4 0.1 collective-permute-start.17
  147.5 0.4 collective-permute-start.16
  147.9 2.7 collective-permute-done.14.refs_1_
  150.6 64.4 %shard_map.66 = (bf16[8,144,128]{2,1,0:T(8,128)(2,1)S(1)}, bf16[8,144,128]{2,1,0:T(8,128)(2,1)S(1)}) custom-call(s32[13]{0:T(128)S(1)} %pad_add_fusion.info_ref, bf16[8,896,128]{2,1,0:T(8,128)(2,1)S(1)} %all-to-all-done.1.own_q, bf16[8,128,128]{2,1,0:T(8,128)(2,1)S(1)} %collective-permute-done.13.their_q, s32[8,1,256]{2,1,0:T(1,128)S(1)} %fusion.13.end_ref, ...), custom_call_target="tpu_custom_call" | custom-call | flops 8589934592 | bytes 5242880 | tf_op jit(solution)/shard_map/pallas_call | solution.py:171
  215.1 0.1 collective-permute-start.19
  215.2 0.1 collective-permute-start.9
  215.3 3.0 collective-permute-start.15
  218.2 64.2 %shard_map.67 = (bf16[8,144,128]{2,1,0:T(8,128)(2,1)S(1)}, bf16[8,144,128]{2,1,0:T(8,128)(2,1)S(1)}) custom-call(s32[13]{0:T(128)S(1)} %pad_add_fusion.info_ref, bf16[8,896,128]{2,1,0:T(8,128)(2,1)S(1)} %all-to-all-done.1.own_q, bf16[8,128,128]{2,1,0:T(8,128)(2,1)S(1)} %collective-permute-done.17.their_q, s32[8,1,256]{2,1,0:T(1,128)S(1)} %fusion.13.end_ref, ...), custom_call_target="tpu_custom_call" | custom-call | flops 8589934592 | bytes 5242880 | tf_op jit(solution)/shard_map/pallas_call | solution.py:171
  282.5 0.1 collective-permute-start.20
  282.6 7.0 %collective-permute-done.20.refs_5_ = bf16[8,144,128]{2,1,0:T(8,128)(2,1)S(1)} collective-permute-done((bf16[8,144,128]{2,1,0:T(8,128)(2,1)S(1)}, bf16[8,144,128]{2,1,0:T(8,128)(2,1)S(1)}, u32[]{:S(2)}, u32[]{:S(2)}) %collective-permute-start.20) | collective-permute-done | bytes 294944 | tf_op jit(solution)/shard_map/ppermute | solution.py:361
  289.6 1.3 shard_map.68
  290.9 4.4 %all-to-all-start.2 = ((bf16[8,384,128]{2,1,0:T(8,128)(2,1)}), bf16[8,384,128]{2,1,0:T(8,128)(2,1)}, u32[]{:S(2)}, u32[]{:S(2)}) async-start(bf16[8,384,128]{2,1,0:T(8,128)(2,1)} %shard_map.68), calls=%async_computation.2 | async-start | bytes 1572864 | tf_op jit(solution)/shard_map/all_to_all | solution.py:296
  295.2 0.1 fusion.2
  295.4 0.3 fusion.4
  295.7 0.8 fusion.gate_ref
  296.5 9.6 %all-to-all-done.2.mixed_ref = bf16[8,384,128]{2,1,0:T(8,128)(2,1)} async-done(((bf16[8,384,128]{2,1,0:T(8,128)(2,1)}), bf16[8,384,128]{2,1,0:T(8,128)(2,1)}, u32[]{:S(2)}, u32[]{:S(2)}) %all-to-all-start.2) | async-done | bytes 786464 | tf_op jit(solution)/shard_map/all_to_all | solution.py:296
  306.1 2.3 shard_map.69
  (53 shorter events, 0.3 us)
Async XLA Ops:
  0.0 295.4 %copy-start = (bf16[256,3072]{1,0:T(8,128)(2,1)S(1)}, bf16[256,3072]{1,0:T(8,128)(2,1)}, u32[]{:S(2)}) copy-start(bf16[256,3072]{1,0:T(8,128)(2,1)} %param.11) | copy-start | bytes 4718596
  19.4 13.4 %collective-permute-start = (bf16[8,272,128]{2,1,0:T(8,128)(2,1)}, bf16[8,272,128]{2,1,0:T(8,128)(2,1)}, u32[]{:S(2)}, u32[]{:S(2)}) collective-permute-start(bf16[8,272,128]{2,1,0:T(8,128)(2,1)} %all_to_all.15), channel_id=1, source_target_pairs={{0,6},{1,7},{2,0},{3,1},{4,2},{5,3},{6,4},{7,5},{8,14},{9,15},{10,... | collective-permute-start | bytes 1671176 | tf_op jit(solution)/shard_map/ppermute | solution.py:307
  19.8 14.0 %collective-permute-start.1 = (bf16[8,272,128]{2,1,0:T(8,128)(2,1)}, bf16[8,272,128]{2,1,0:T(8,128)(2,1)}, u32[]{:S(2)}, u32[]{:S(2)}) collective-permute-start(bf16[8,272,128]{2,1,0:T(8,128)(2,1)} %all_to_all.15), channel_id=1, source_target_pairs={{0,2},{1,3},{2,4},{3,5},{4,6},{5,7},{6,0},{7,1},{8,10},{9,11},{10,... | collective-permute-start | bytes 1671176 | tf_op jit(solution)/shard_map/ppermute | solution.py:307
  22.0 24.9 %all-to-all-start.1 = ((bf16[8,896,128]{2,1,0:T(8,128)(2,1)}), bf16[8,896,128]{2,1,0:T(8,128)(2,1)S(1)}, u32[]{:S(2)}, u32[]{:S(2)}) async-start(bf16[8,896,128]{2,1,0:T(8,128)(2,1)} %get-tuple-element.47), calls=%async_computation.1 | async-start | bytes 3670016 | tf_op jit(solution)/shard_map/all_to_all | solution.py:296
  33.7 7.0 %collective-permute-start.3 = (bf16[4,272,128]{2,1,0:T(8,128)(2,1)S(1)}, bf16[4,272,128]{2,1,0:T(8,128)(2,1)S(1)}, u32[]{:S(2)}, u32[]{:S(2)}) collective-permute-start(bf16[4,272,128]{2,1,0:T(8,128)(2,1)S(1)} %slice.49), channel_id=1, source_target_pairs={{0,6},{1,7},{2,0},{3,1},{4,2},{5,3},{6,4},{7,5},{8,14},{9,15},{10,... | collective-permute-start | bytes 835592 | tf_op jit(solution)/shard_map/ppermute | solution.py:318
  34.8 6.2 %collective-permute-start.2 = (bf16[4,272,128]{2,1,0:T(8,128)(2,1)S(1)}, bf16[4,272,128]{2,1,0:T(8,128)(2,1)S(1)}, u32[]{:S(2)}, u32[]{:S(2)}) collective-permute-start(bf16[4,272,128]{2,1,0:T(8,128)(2,1)S(1)} %slice.48), channel_id=1, source_target_pairs={{0,2},{1,3},{2,4},{3,5},{4,6},{5,7},{6,0},{7,1},{8,10},{9,11},{10,... | collective-permute-start | bytes 835592 | tf_op jit(solution)/shard_map/ppermute | solution.py:318
  42.8 1.4 copy-start.1
  46.9 10.8 %collective-permute-start.4 = (bf16[4,8,272,128]{3,2,1,0:T(8,128)(2,1)}, bf16[4,8,272,128]{3,2,1,0:T(8,128)(2,1)}, u32[]{:S(2)}, u32[]{:S(2)}) collective-permute-start(bf16[4,8,272,128]{3,2,1,0:T(8,128)(2,1)} %copy-done.1), channel_id=1, source_target_pairs={{0,8},{8,0},{16,24},{24,16},{32,40},{40,32},{48,56},{56,48},{64,72... | collective-permute-start | bytes 6684680 | tf_op jit(solution)/shard_map/ppermute | solution.py:304
  52.6 11.5 %copy-start.6 = (bf16[8,256,128]{2,1,0:T(8,128)(2,1)}, bf16[8,256,128]{2,1,0:T(8,128)(2,1)S(1)}, u32[]{:S(2)}) copy-start(bf16[8,256,128]{2,1,0:T(8,128)(2,1)S(1)} %get-tuple-element.52) | copy-start | bytes 1572868
  52.6 14.8 %collective-permute-start.5 = (bf16[8,256,128]{2,1,0:T(8,128)(2,1)S(1)}, bf16[8,256,128]{2,1,0:T(8,128)(2,1)S(1)}, u32[]{:S(2)}, u32[]{:S(2)}) collective-permute-start(bf16[8,256,128]{2,1,0:T(8,128)(2,1)S(1)} %get-tuple-element.52), channel_id=1, source_target_pairs={{0,6},{1,7},{2,0},{3,1},{4,2},{5,3},{6,4},{7,5},{8,14},{9,15},{10,... | collective-permute-start | bytes 1572872 | tf_op jit(solution)/shard_map/ppermute | solution.py:307
  52.6 14.8 %collective-permute-start.6 = (bf16[8,256,128]{2,1,0:T(8,128)(2,1)S(1)}, bf16[8,256,128]{2,1,0:T(8,128)(2,1)S(1)}, u32[]{:S(2)}, u32[]{:S(2)}) collective-permute-start(bf16[8,256,128]{2,1,0:T(8,128)(2,1)S(1)} %get-tuple-element.52), channel_id=1, source_target_pairs={{0,2},{1,3},{2,4},{3,5},{4,6},{5,7},{6,0},{7,1},{8,10},{9,11},{10,... | collective-permute-start | bytes 1572872 | tf_op jit(solution)/shard_map/ppermute | solution.py:307
  55.2 8.8 %collective-permute-start.7 = (bf16[8,128,128]{2,1,0:T(8,128)(2,1)S(1)}, bf16[8,128,128]{2,1,0:T(8,128)(2,1)S(1)}, u32[]{:S(2)}, u32[]{:S(2)}) collective-permute-start(bf16[8,128,128]{2,1,0:T(8,128)(2,1)S(1)} %get-tuple-element.53), channel_id=1, source_target_pairs={{0,1},{1,0},{2,3},{3,2},{4,5},{5,4},{6,7},{7,6},{8,9},{9,8},{10,11... | collective-permute-start | bytes 786440 | tf_op jit(solution)/shard_map/ppermute | solution.py:333
  64.0 0.7 copy-start.3
  67.3 0.8 copy-start.8
  68.1 2.5 copy-start.10
  68.1 3.9 %collective-permute-start.8 = (f32[1,128]{1,0:T(1,128)S(1)}, f32[1,128]{1,0:T(1,128)S(1)}, u32[]{:S(2)}, u32[]{:S(2)}) collective-permute-start(f32[1,128]{1,0:T(1,128)S(1)} %select_bitcast_fusion), channel_id=1, source_target_pairs={{0,1},{1,0},{2,3},{3,2},{4,5},{5,4},{6,7},{7,6},{8,9},{9,8},{10,11... | collective-permute-start | bytes 1544 | tf_op jit(solution)/shard_map/ppermute | solution.py:337
  72.5 73.5 %collective-permute-start.11 = (bf16[8,256,128]{2,1,0:T(8,128)(2,1)}, bf16[8,256,128]{2,1,0:T(8,128)(2,1)S(1)}, u32[]{:S(2)}, u32[]{:S(2)}) collective-permute-start(bf16[8,256,128]{2,1,0:T(8,128)(2,1)} %get-tuple-element.66), channel_id=1, source_target_pairs={{0,6},{1,7},{2,0},{3,1},{4,2},{5,3},{6,4},{7,5},{8,14},{9,15},{10,... | collective-permute-start | bytes 1572872 | tf_op jit(solution)/shard_map/ppermute | solution.py:307
  72.5 73.5 %collective-permute-start.12 = (bf16[8,256,128]{2,1,0:T(8,128)(2,1)}, bf16[8,256,128]{2,1,0:T(8,128)(2,1)S(1)}, u32[]{:S(2)}, u32[]{:S(2)}) collective-permute-start(bf16[8,256,128]{2,1,0:T(8,128)(2,1)} %get-tuple-element.66), channel_id=1, source_target_pairs={{0,2},{1,3},{2,4},{3,5},{4,6},{5,7},{6,0},{7,1},{8,10},{9,11},{10,... | collective-permute-start | bytes 1572872 | tf_op jit(solution)/shard_map/ppermute | solution.py:307
  75.2 70.8 %collective-permute-start.10 = (bf16[8,256,128]{2,1,0:T(8,128)(2,1)}, bf16[8,256,128]{2,1,0:T(8,128)(2,1)S(1)}, u32[]{:S(2)}, u32[]{:S(2)}) collective-permute-start(bf16[8,256,128]{2,1,0:T(8,128)(2,1)} %copy-done.10), channel_id=1, source_target_pairs={{0,2},{1,3},{2,4},{3,5},{4,6},{5,7},{6,0},{7,1},{8,10},{9,11},{10,... | collective-permute-start | bytes 1572872 | tf_op jit(solution)/shard_map/ppermute | solution.py:365
  75.5 70.5 %collective-permute-start.13 = (bf16[8,128,128]{2,1,0:T(8,128)(2,1)}, bf16[8,128,128]{2,1,0:T(8,128)(2,1)S(1)}, u32[]{:S(2)}, u32[]{:S(2)}) collective-permute-start(bf16[8,128,128]{2,1,0:T(8,128)(2,1)} %get-tuple-element.67), channel_id=1, source_target_pairs={{0,1},{1,0},{2,3},{3,2},{4,5},{5,4},{6,7},{7,6},{8,9},{9,8},{10,11... | collective-permute-start | bytes 786440 | tf_op jit(solution)/shard_map/ppermute | solution.py:368
  78.0 1.6 copy-start.2
  79.6 0.9 copy-start.4
  80.6 65.5 %copy-start.7 = (bf16[8,256,128]{2,1,0:T(8,128)(2,1)S(1)}, bf16[8,256,128]{2,1,0:T(8,128)(2,1)}, u32[]{:S(2)}) copy-start(bf16[8,256,128]{2,1,0:T(8,128)(2,1)} %copy-done.6) | copy-start | bytes 1572868
  80.6 65.5 %copy-start.9 = (bf16[8,256,128]{2,1,0:T(8,128)(2,1)S(1)}, bf16[8,256,128]{2,1,0:T(8,128)(2,1)}, u32[]{:S(2)}) copy-start(bf16[8,256,128]{2,1,0:T(8,128)(2,1)} %copy-done.8) | copy-start | bytes 1572868
  80.6 65.5 %copy-start.11 = (bf16[8,256,128]{2,1,0:T(8,128)(2,1)S(1)}, bf16[8,256,128]{2,1,0:T(8,128)(2,1)}, u32[]{:S(2)}) copy-start(bf16[8,256,128]{2,1,0:T(8,128)(2,1)} %copy-done.10) | copy-start | bytes 1572868
  146.1 1.0 copy-start.5
  146.4 1.0 copy-start.12
  146.4 4.2 %collective-permute-start.14 = (bf16[4,8,256,128]{3,2,1,0:T(8,128)(2,1)S(1)}, bf16[4,8,256,128]{3,2,1,0:T(8,128)(2,1)S(1)}, u32[]{:S(2)}, u32[]{:S(2)}) collective-permute-start(bf16[4,8,256,128]{3,2,1,0:T(8,128)(2,1)S(1)} %pad_maximum_fusion.1.refs_0_), channel_id=1, source_target_pairs={{0,8},{8,0},{16,24},{24,16},{32,40},{40,32},{48,56},{56,48},{64,72... | collective-permute-start | bytes 6291464 | tf_op jit(solution)/shard_map/ppermute | solution.py:304
  147.3 70.9 %collective-permute-start.18 = (bf16[3,8,256,128]{3,2,1,0:T(8,128)(2,1)S(1)}, bf16[3,8,256,128]{3,2,1,0:T(8,128)(2,1)S(1)}, u32[]{:S(2)}, u32[]{:S(2)}) collective-permute-start(bf16[3,8,256,128]{3,2,1,0:T(8,128)(2,1)S(1)} %pad_maximum_fusion.2.refs_0_), channel_id=1, source_target_pairs={{0,8},{8,0},{16,24},{24,16},{32,40},{40,32},{48,56},{56,48},{64,72... | collective-permute-start | bytes 4718600 | tf_op jit(solution)/shard_map/ppermute | solution.py:304
  147.4 67.6 %collective-permute-start.17 = (bf16[8,128,128]{2,1,0:T(8,128)(2,1)S(1)}, bf16[8,128,128]{2,1,0:T(8,128)(2,1)S(1)}, u32[]{:S(2)}, u32[]{:S(2)}) collective-permute-start(bf16[8,128,128]{2,1,0:T(8,128)(2,1)S(1)} %copy-done.12), channel_id=1, source_target_pairs={{0,1},{1,0},{2,3},{3,2},{4,5},{5,4},{6,7},{7,6},{8,9},{9,8},{10,11... | collective-permute-start | bytes 786440 | tf_op jit(solution)/shard_map/ppermute | solution.py:376
  147.5 67.5 %collective-permute-start.16 = (bf16[8,256,128]{2,1,0:T(8,128)(2,1)S(1)}, bf16[8,256,128]{2,1,0:T(8,128)(2,1)S(1)}, u32[]{:S(2)}, u32[]{:S(2)}) collective-permute-start(bf16[8,256,128]{2,1,0:T(8,128)(2,1)S(1)} %collective-permute-done.11), channel_id=1, source_target_pairs={{0,6},{1,7},{2,0},{3,1},{4,2},{5,3},{6,4},{7,5},{8,14},{9,15},{10,... | collective-permute-start | bytes 1572872 | tf_op jit(solution)/shard_map/ppermute | solution.py:374
  215.1 67.5 %copy-start.14 = (s32[24]{0:T(128)S(1)}, s32[24]{0:T(128)}, u32[]{:S(2)}) copy-start(s32[24]{0:T(128)} %param.10) | copy-start | bytes 292
  215.1 3.1 %collective-permute-start.19 = (bf16[1,8,256,128]{3,2,1,0:T(8,128)(2,1)S(1)}, bf16[1,8,256,128]{3,2,1,0:T(8,128)(2,1)S(1)}, u32[]{:S(2)}, u32[]{:S(2)}) collective-permute-start(bf16[1,8,256,128]{3,2,1,0:T(8,128)(2,1)S(1)} %bitcast.46), channel_id=1, source_target_pairs={{0,8},{8,0},{16,24},{24,16},{32,40},{40,32},{48,56},{56,48},{64,72... | collective-permute-start | bytes 1572872 | tf_op jit(solution)/shard_map/ppermute | solution.py:304
  215.2 67.4 %collective-permute-start.9 = (bf16[8,144,128]{2,1,0:T(8,128)(2,1)S(1)}, bf16[8,144,128]{2,1,0:T(8,128)(2,1)S(1)}, u32[]{:S(2)}, u32[]{:S(2)}) collective-permute-start(bf16[8,144,128]{2,1,0:T(8,128)(2,1)S(1)} %get-tuple-element.63), channel_id=1, source_target_pairs={{0,1},{1,0},{2,3},{3,2},{4,5},{5,4},{6,7},{7,6},{8,9},{9,8},{10,11... | collective-permute-start | bytes 884744 | tf_op jit(solution)/shard_map/ppermute | solution.py:361
  215.3 67.3 %collective-permute-start.15 = (bf16[8,144,128]{2,1,0:T(8,128)(2,1)S(1)}, bf16[8,144,128]{2,1,0:T(8,128)(2,1)S(1)}, u32[]{:S(2)}, u32[]{:S(2)}) collective-permute-start(bf16[8,144,128]{2,1,0:T(8,128)(2,1)S(1)} %get-tuple-element.74), channel_id=1, source_target_pairs={{0,1},{1,0},{2,3},{3,2},{4,5},{5,4},{6,7},{7,6},{8,9},{9,8},{10,11... | collective-permute-start | bytes 884744 | tf_op jit(solution)/shard_map/ppermute | solution.py:361
  282.5 7.2 %collective-permute-start.20 = (bf16[8,144,128]{2,1,0:T(8,128)(2,1)S(1)}, bf16[8,144,128]{2,1,0:T(8,128)(2,1)S(1)}, u32[]{:S(2)}, u32[]{:S(2)}) collective-permute-start(bf16[8,144,128]{2,1,0:T(8,128)(2,1)S(1)} %get-tuple-element.84), channel_id=1, source_target_pairs={{0,1},{1,0},{2,3},{3,2},{4,5},{5,4},{6,7},{7,6},{8,9},{9,8},{10,11... | collective-permute-start | bytes 884744 | tf_op jit(solution)/shard_map/ppermute | solution.py:361
  290.9 4.8 %copy-start.13 = (s32[128]{0:T(128)S(1)}, s32[128]{0:T(128)}, u32[]{:S(2)}) copy-start(s32[128]{0:T(128)} %param.9) | copy-start | bytes 1540
  290.9 15.2 %all-to-all-start.2 = ((bf16[8,384,128]{2,1,0:T(8,128)(2,1)}), bf16[8,384,128]{2,1,0:T(8,128)(2,1)}, u32[]{:S(2)}, u32[]{:S(2)}) async-start(bf16[8,384,128]{2,1,0:T(8,128)(2,1)} %shard_map.68), calls=%async_computation.2 | async-start | bytes 1572864 | tf_op jit(solution)/shard_map/all_to_all | solution.py:296
